TPU v7x, 32 devices: a whole 2x2x4 slice. The times are simulated.
32 devices in a mesh: dp: 16 (over z, y, x), tensor: 2 (over core).
Axes of the slice: x: 2, y: 2, z: 4, core: 2. Of those that a mesh axis runs over, the one named last changes fastest.
Arguments:
- patches: bfloat16 [16, 16, 32, 1024], P('dp'), may hold values from -6 to 6
- counts: int32 [16, 16], replicated, may hold values from 1 to 32, 256 in all within a row
- doc_ids: int32 [16, 256], P('dp'), may hold values from 0 to 3, never falling along the last dimension, each value on 1 to 128 neighbouring positions
- w_query: bfloat16 [1024, 1024], P('dp', 'tensor'), may hold values from -0.1875 to 0.1875
- w_key: bfloat16 [1024, 1024], P('dp', 'tensor'), may hold values from -0.1875 to 0.1875
- w_value: bfloat16 [1024, 1024], P('dp', 'tensor'), may hold values from -0.1875 to 0.1875
- w_output: bfloat16 [1024, 1024], P('tensor', 'dp'), may hold values from -0.75 to 0.75
- w_gate: bfloat16 [1024, 2816], P('dp', 'tensor'), may hold values from -0.1875 to 0.1875
- w_up: bfloat16 [1024, 2816], P('dp', 'tensor'), may hold values from -0.1875 to 0.1875
- w_down: bfloat16 [2816, 1024], P('tensor', 'dp'), may hold values from -0.109375 to 0.109375
- gain_attn: bfloat16 [1024], P('dp'), may hold values from 0.25 to 1.75
- gain_ffn: bfloat16 [1024], P('dp'), may hold values from 0.25 to 1.75
- cotangent: bfloat16 [16, 16, 32, 1024], P('dp'), may hold values from -6 to 6
Outputs:
- outputs: bfloat16 [16, 16, 32, 1024], P('dp')
- input_grad: bfloat16 [16, 16, 32, 1024], P('dp')
- grad_w_query: float32 [1024, 1024], P('dp', 'tensor')
- grad_w_key: float32 [1024, 1024], P('dp', 'tensor')
- grad_w_value: float32 [1024, 1024], P('dp', 'tensor')
- grad_w_output: float32 [1024, 1024], P('tensor', 'dp')
- grad_w_gate: float32 [1024, 2816], P('dp', 'tensor')
- grad_w_up: float32 [1024, 2816], P('dp', 'tensor')
- grad_w_down: float32 [2816, 1024], P('tensor', 'dp')
- grad_gain_attn: float32 [1024], P('dp')
- grad_gain_ffn: float32 [1024], P('dp')
Inputs may be any that keep to these rules, and one draw needn't show every extreme that they name: Each row of counts sums to 256 and its largest entry is 32. `doc_ids`: along each row the document numbers never fall; a document holds 1 to 128 patches of a row, and one holds exactly that many.
All inputs are finite; a program needn't handle non-finite values.
Results may differ from a plain program's by a relative error of at most 0.017.
Values may be sent and summed in bfloat16 or wider, within the bound.
No kernel may reach another device: no remote copies, remote signals or barrier semaphores. Data moves between devices by JAX's collectives and lax.ppermute only.
A program may use at most 128 MiB of HBM per device.

v0:
```python
import jax
import jax.numpy as jnp
from jax import lax
from jax.sharding import PartitionSpec as P

DH = 64


eps = 1e-05
masked_score = -1e30


def inverse_root(values):
    return lax.rsqrt(jnp.mean(values * values, axis=-1, keepdims=True) + eps)


def outer_sum(left, right):
    return lax.dot_general(
        left, right, (((0,), (0,)), ((), ())), preferred_element_type=jnp.float32
    )


def through(left, right):
    return lax.dot_general(
        left, right, (((1,), (1,)), ((), ())), preferred_element_type=jnp.float32
    )


def layout_tables(counts, my_row, tok_count, slot_cap):
    my_counts = lax.dynamic_index_in_dim(counts, my_row, 0, keepdims=False)
    offsets = jnp.cumsum(my_counts) - my_counts
    position = jnp.arange(tok_count, dtype=jnp.int32)
    reached = offsets[None, :] <= position[:, None]
    source = jnp.sum(reached.astype(jnp.int32), axis=1) - 1
    first_slot = jnp.max(jnp.where(reached, offsets[None, :], 0), axis=1)
    flat_index = source * slot_cap + position - first_slot
    places = jnp.arange(slot_cap, dtype=jnp.int32)
    back_index = jnp.minimum(offsets[:, None] + places[None, :], tok_count - 1)
    back_valid = places[None, :] < my_counts[:, None]
    return (flat_index, back_index, back_valid)


def collect(received, flat_index):
    return jnp.take(received.reshape(-1, received.shape[-1]), flat_index, axis=0)


def spread(values, back_index, back_valid):
    picked = jnp.take(values, back_index, axis=0)
    return jnp.where(back_valid[:, :, None], picked, jnp.zeros_like(picked))


def block_scores(query_heads, key_heads, doc_row, begin_row, end_row, score_scale):
    raw_scores = (
        jnp.einsum("thd,shd->hts", query_heads, key_heads, preferred_element_type=jnp.float32)
        * score_scale
    )
    query_pos = begin_row + jnp.arange(end_row - begin_row)
    key_pos = jnp.arange(end_row)
    same_doc = doc_row[begin_row:end_row, None] == doc_row[None, :end_row]
    visible = same_doc & (key_pos[None, :] <= query_pos[:, None])
    return jnp.where(visible[None], raw_scores, masked_score)


def attention_forward(query_mat, key_mat, value_mat, doc_row, block_rows, score_scale):
    tok_count, local_width = query_mat.shape
    head_count = local_width // DH
    query_heads = query_mat.reshape(tok_count, head_count, DH)
    key_heads = key_mat.reshape(tok_count, head_count, DH)
    value_heads = value_mat.reshape(tok_count, head_count, DH)
    scores = block_scores(query_heads, key_heads, doc_row, 0, block_rows, score_scale)
    row_top = jnp.max(scores, axis=-1, keepdims=True)
    lifted = jnp.exp(scores - row_top)
    row_total = jnp.sum(lifted, axis=-1, keepdims=True)
    chances = (lifted / row_total).astype(jnp.bfloat16)
    attended = jnp.einsum("hts,shd->thd", chances, value_heads, preferred_element_type=jnp.float32)
    pieces = attended.reshape(block_rows, local_width)
    log_totals = [row_top + jnp.log(row_total)]
    return (pieces.astype(jnp.bfloat16), log_totals)


def attention_backward(
    query_mat, key_mat, value_mat, grad_attended, doc_row, log_totals, block_rows, score_scale
):
    tok_count, local_width = query_mat.shape
    head_count = local_width // DH
    query_heads = query_mat.reshape(tok_count, head_count, DH)
    key_heads = key_mat.reshape(tok_count, head_count, DH)
    value_heads = value_mat.reshape(tok_count, head_count, DH)
    grad_heads = grad_attended.reshape(tok_count, head_count, DH)
    query_parts = []
    grad_key = jnp.zeros((tok_count, head_count, DH), jnp.float32)
    grad_value = jnp.zeros((tok_count, head_count, DH), jnp.float32)
    for block_no, begin_row in enumerate(range(0, tok_count, block_rows)):
        end_row = begin_row + block_rows
        scores = block_scores(query_heads, key_heads, doc_row, begin_row, end_row, score_scale)
        chances = jnp.exp(scores - log_totals[block_no])
        chances_low = chances.astype(jnp.bfloat16)
        grad_chances = jnp.einsum(
            "thd,shd->hts", grad_heads, value_heads, preferred_element_type=jnp.float32
        )
        grad_value = grad_value.at[:end_row].add(
            jnp.einsum("hts,thd->shd", chances_low, grad_heads, preferred_element_type=jnp.float32)
        )
        grad_scores = chances * (
            grad_chances - jnp.sum(grad_chances * chances, axis=-1, keepdims=True)
        )
        scores_low = grad_scores.astype(jnp.bfloat16)
        query_parts.append(
            jnp.einsum("hts,shd->thd", scores_low, key_heads, preferred_element_type=jnp.float32)
            * score_scale
        )
        grad_key = grad_key.at[:end_row].add(
            jnp.einsum("hts,thd->shd", scores_low, query_heads, preferred_element_type=jnp.float32)
            * score_scale
        )
    grad_query = query_parts[0].reshape(tok_count, local_width).astype(jnp.bfloat16)
    return (
        grad_query,
        grad_key.reshape(tok_count, local_width).astype(jnp.bfloat16),
        grad_value.reshape(tok_count, local_width).astype(jnp.bfloat16),
    )


def body(
    patches,
    counts,
    doc_ids,
    w_query,
    w_key,
    w_value,
    w_output,
    w_gate,
    w_up,
    w_down,
    gain_attn,
    gain_ffn,
    cotangent,
):
    peers = lax.axis_size("dp")
    my_row = lax.axis_index("dp")
    slot_cap = patches.shape[2]
    width = patches.shape[3]
    doc_row = doc_ids[0]
    tok_count = doc_row.shape[0]
    block_rows = min(512, tok_count)
    score_scale = DH ** (-0.5)
    flat_index, back_index, back_valid = layout_tables(counts, my_row, tok_count, slot_cap)
    received = lax.all_to_all(
        patches.reshape(peers, slot_cap, width), "dp", split_axis=0, concat_axis=0, tiled=True
    )
    row_in = collect(received, flat_index).astype(jnp.float32)
    full = (
        lax.all_gather(w_query, "dp", axis=0, tiled=True),
        lax.all_gather(w_key, "dp", axis=0, tiled=True),
        lax.all_gather(w_value, "dp", axis=0, tiled=True),
        lax.all_gather(w_output, "dp", axis=1, tiled=True),
        lax.all_gather(w_gate, "dp", axis=0, tiled=True),
        lax.all_gather(w_up, "dp", axis=0, tiled=True),
        lax.all_gather(w_down, "dp", axis=1, tiled=True),
        lax.all_gather(gain_attn, "dp", axis=0, tiled=True),
        lax.all_gather(gain_ffn, "dp", axis=0, tiled=True),
    )
    root_attn = inverse_root(row_in)
    norm_attn = row_in * root_attn
    gain_one = full[7].astype(jnp.float32)
    normed_attn = (norm_attn * gain_one).astype(jnp.bfloat16)
    query_mat = jnp.dot(normed_attn, full[0], preferred_element_type=jnp.float32).astype(
        jnp.bfloat16
    )
    key_mat = jnp.dot(normed_attn, full[1], preferred_element_type=jnp.float32).astype(jnp.bfloat16)
    value_mat = jnp.dot(normed_attn, full[2], preferred_element_type=jnp.float32).astype(
        jnp.bfloat16
    )
    attended, log_totals = attention_forward(
        query_mat, key_mat, value_mat, doc_row, block_rows, score_scale
    )
    branch_attn = lax.psum(jnp.dot(attended, full[3], preferred_element_type=jnp.float32), "tensor")
    hidden = row_in + branch_attn
    root_ffn = inverse_root(hidden)
    norm_ffn = hidden * root_ffn
    gain_two = full[8].astype(jnp.float32)
    normed_ffn = (norm_ffn * gain_two).astype(jnp.bfloat16)
    gate_pre = jnp.dot(normed_ffn, full[4], preferred_element_type=jnp.float32)
    up_proj = jnp.dot(normed_ffn, full[5], preferred_element_type=jnp.float32)
    sigmoid_gate = jax.nn.sigmoid(gate_pre)
    silu_gate = gate_pre * sigmoid_gate
    product = (silu_gate * up_proj).astype(jnp.bfloat16)
    branch_ffn = lax.psum(
        jnp.dot(product, full[6], preferred_element_type=jnp.float32).astype(jnp.bfloat16), "tensor"
    ).astype(jnp.float32)
    final = hidden + branch_ffn
    sent = lax.all_to_all(
        spread(final.astype(jnp.bfloat16), back_index, back_valid),
        "dp",
        split_axis=0,
        concat_axis=0,
        tiled=True,
    )
    outputs = sent.reshape(patches.shape)
    arrived = lax.all_to_all(
        cotangent.reshape(peers, slot_cap, width), "dp", split_axis=0, concat_axis=0, tiled=True
    )
    grad_low = collect(arrived, flat_index)
    grad_final = grad_low.astype(jnp.float32)
    back_full = (
        lax.all_gather(w_query, "dp", axis=0, tiled=True),
        lax.all_gather(w_key, "dp", axis=0, tiled=True),
        lax.all_gather(w_value, "dp", axis=0, tiled=True),
        lax.all_gather(w_output, "dp", axis=1, tiled=True),
        lax.all_gather(w_gate, "dp", axis=0, tiled=True),
        lax.all_gather(w_up, "dp", axis=0, tiled=True),
        lax.all_gather(w_down, "dp", axis=1, tiled=True),
        lax.all_gather(gain_attn, "dp", axis=0, tiled=True),
        lax.all_gather(gain_ffn, "dp", axis=0, tiled=True),
    )
    grad_down = outer_sum(product, grad_low)
    grad_product = through(grad_low, back_full[6])
    grad_gate_low = (
        grad_product * up_proj * sigmoid_gate * (1.0 + gate_pre * (1.0 - sigmoid_gate))
    ).astype(jnp.bfloat16)
    grad_up_low = (grad_product * silu_gate).astype(jnp.bfloat16)
    grad_gate = outer_sum(normed_ffn, grad_gate_low)
    grad_up = outer_sum(normed_ffn, grad_up_low)
    partial_ffn = through(grad_gate_low, back_full[4]) + through(grad_up_low, back_full[5])
    grad_normed_ffn = lax.psum(partial_ffn.astype(jnp.bfloat16), "tensor").astype(jnp.float32)
    grad_gain_two = jnp.sum(grad_normed_ffn * norm_ffn, axis=0)
    scaled_two = grad_normed_ffn * back_full[8].astype(jnp.float32)
    grad_hidden = grad_final + root_ffn * (
        scaled_two - norm_ffn * jnp.mean(scaled_two * norm_ffn, axis=-1, keepdims=True)
    )
    grad_branch = grad_hidden.astype(jnp.bfloat16)
    grad_output = outer_sum(attended, grad_branch)
    grad_attended = through(grad_branch, back_full[3]).astype(jnp.bfloat16)
    grad_query_low, grad_key_low, grad_value_low = attention_backward(
        query_mat, key_mat, value_mat, grad_attended, doc_row, log_totals, block_rows, score_scale
    )
    grad_query = outer_sum(normed_attn, grad_query_low)
    grad_key = outer_sum(normed_attn, grad_key_low)
    grad_value = outer_sum(normed_attn, grad_value_low)
    partial_attn = (
        through(grad_query_low, back_full[0])
        + through(grad_key_low, back_full[1])
        + through(grad_value_low, back_full[2])
    )
    grad_normed_attn = lax.psum(partial_attn.astype(jnp.bfloat16), "tensor").astype(jnp.float32)
    grad_gain_one = jnp.sum(grad_normed_attn * norm_attn, axis=0)
    scaled_one = grad_normed_attn * back_full[7].astype(jnp.float32)
    grad_input = grad_hidden + root_attn * (
        scaled_one - norm_attn * jnp.mean(scaled_one * norm_attn, axis=-1, keepdims=True)
    )
    returned = lax.all_to_all(
        spread(grad_input.astype(jnp.bfloat16), back_index, back_valid),
        "dp",
        split_axis=0,
        concat_axis=0,
        tiled=True,
    )
    input_grad = returned.reshape(patches.shape)
    summed = (
        lax.psum_scatter(grad_query, "dp", scatter_dimension=0, tiled=True),
        lax.psum_scatter(grad_key, "dp", scatter_dimension=0, tiled=True),
        lax.psum_scatter(grad_value, "dp", scatter_dimension=0, tiled=True),
        lax.psum_scatter(grad_output, "dp", scatter_dimension=1, tiled=True),
        lax.psum_scatter(grad_gate, "dp", scatter_dimension=0, tiled=True),
        lax.psum_scatter(grad_up, "dp", scatter_dimension=0, tiled=True),
        lax.psum_scatter(grad_down, "dp", scatter_dimension=1, tiled=True),
        lax.psum_scatter(grad_gain_one, "dp", scatter_dimension=0, tiled=True),
        lax.psum_scatter(grad_gain_two, "dp", scatter_dimension=0, tiled=True),
    )
    return (
        outputs,
        input_grad,
        summed[0],
        summed[1],
        summed[2],
        summed[3],
        summed[4],
        summed[5],
        summed[6],
        summed[7],
        summed[8],
    )


def solution(mesh):
    in_specs = (
        P("dp", None, None, None),
        P(),
        P("dp", None),
        P("dp", "tensor"),
        P("dp", "tensor"),
        P("dp", "tensor"),
        P("tensor", "dp"),
        P("dp", "tensor"),
        P("dp", "tensor"),
        P("tensor", "dp"),
        P("dp"),
        P("dp"),
        P("dp", None, None, None),
    )
    out_specs = (
        P("dp", None, None, None),
        P("dp", None, None, None),
        P("dp", "tensor"),
        P("dp", "tensor"),
        P("dp", "tensor"),
        P("tensor", "dp"),
        P("dp", "tensor"),
        P("dp", "tensor"),
        P("tensor", "dp"),
        P("dp"),
        P("dp"),
    )
    return jax.shard_map(body, mesh=mesh, in_specs=in_specs, out_specs=out_specs, check_vma=False)
```

profile of v0, /device:TPU:9, one launch (start us, length us, event | category | flops | bytes accessed | tf_op | source)
XLA Modules:
  0.0 1261.4 jit_solution(13559703428642343478)
XLA Ops:
  9.4 6.7 all-to-all-start
  18.5 41.2 %all-reduce.5 = (bf16[1024]{0:T(1024)(128)(2,1)S(1)}, bf16[1024]{0:T(1024)(128)(2,1)S(1)}) all-reduce(bf16[1024]{0:T(1024)(128)(2,1)S(1)} %dynamic-update-slice.4, bf16[1024]{0:T(1024)(128)(2,1)S(1)} %dynamic-update-slice.5), channel_id=1, replica_groups=mesh['dp'=16,'tensor'=2] {'dp'}, use_global_device_ids=true, to_apply=%add | all-reduce | flops 2048 | bytes 8192
  63.0 7.5 all-gather.12.cloned.1.call-done
  70.5 1.7 convolution_convert_fusion.4
  72.4 54.9 %all-gather.10.cloned.1.call-done = bf16[1024,512]{1,0:T(8,128)(2,1)} async-done(((bf16[64,512]{1,0:T(8,128)(2,1)}), bf16[1024,512]{1,0:T(8,128)(2,1)}) %all-gather.10.cloned.1.call-update) | async-done | bytes 1048592 | tf_op jit(solution)/shard_map/all_gather | solution.py:153
  127.3 1.7 convolution_convert_fusion.5
  129.2 55.0 %all-gather.8.cloned.1.call-done = bf16[1024,512]{1,0:T(8,128)(2,1)} async-done(((bf16[64,512]{1,0:T(8,128)(2,1)}), bf16[1024,512]{1,0:T(8,128)(2,1)}) %all-gather.8.cloned.1.call-update) | async-done | bytes 1048592 | tf_op jit(solution)/shard_map/all_gather | solution.py:155
  184.2 1.7 convolution_convert_fusion.6
  187.4 53.5 %all-gather.14.cloned.1.call-done = bf16[512,1024]{0,1:T(8,128)(2,1)} async-done(((bf16[512,64]{0,1:T(8,128)(2,1)}), bf16[512,1024]{0,1:T(8,128)(2,1)}) %all-gather.14.cloned.1.call-update) | async-done | bytes 1048592 | tf_op jit(solution)/shard_map/all_gather | solution.py:156
  240.9 2.7 fusion.45
  245.7 5.4 all-to-all-start.2
  251.1 24.4 %all-to-all-done.2 = bf16[16,32,1024]{2,1,0:T(8,128)(2,1)} async-done(((bf16[16,32,1024]{2,1,0:T(8,128)(2,1)}), bf16[16,32,1024]{2,1,0:T(8,128)(2,1)}, u32[]{:S(2)}, u32[]{:S(2)}) %all-to-all-start.2) | async-done | bytes 1048608 | tf_op jit(solution)/shard_map/all_to_all | solution.py:200
  275.5 3.7 gather_fusion.2
  279.2 1.5 multiply_reduce_fusion.1
  281.9 52.4 %all-gather.18.cloned.1.call-done = bf16[1024,1408]{1,0:T(8,128)(2,1)} async-done(((bf16[64,1408]{1,0:T(8,128)(2,1)}), bf16[1024,1408]{1,0:T(8,128)(2,1)}) %all-gather.18.cloned.1.call-update) | async-done | bytes 2883600 | tf_op jit(solution)/shard_map/all_gather | solution.py:158
  334.3 3.9 fusion.47
  338.2 64.2 %all-gather.16.cloned.1.call-done = bf16[1024,1408]{1,0:T(8,128)(2,1)} async-done(((bf16[64,1408]{1,0:T(8,128)(2,1)}), bf16[1024,1408]{1,0:T(8,128)(2,1)}) %all-gather.16.cloned.1.call-update) | async-done | bytes 2883600 | tf_op jit(solution)/shard_map/all_gather | solution.py:157
  402.4 3.9 fusion.46
  406.3 64.2 %all-gather.20.cloned.1.call-done = bf16[1408,1024]{0,1:T(8,128)(2,1)} async-done(((bf16[1408,64]{0,1:T(8,128)(2,1)}), bf16[1408,1024]{0,1:T(8,128)(2,1)}) %all-gather.20.cloned.1.call-update) | async-done | bytes 2883600 | tf_op jit(solution)/shard_map/all_gather | solution.py:159
  470.5 5.2 multiply_convert_fusion.1
  476.9 1.2 copy-done.8
  478.1 1.8 fusion.7
  480.2 3.9 convolution_convert_fusion
  484.0 14.7 %all-reduce.13.cloned.1.call-done = bf16[256,1024]{1,0:T(8,128)(2,1)} async-done(((bf16[256,1024]{1,0:T(8,128)(2,1)}), bf16[256,1024]{1,0:T(8,128)(2,1)}) %all-reduce.13.cloned.1.call-update) | async-done | bytes 524304 | tf_op jit(solution)/shard_map/psum | solution.py:225
  498.7 2.0 fusion.20
  500.7 1.6 fusion.19
  510.9 1.3 fusion.8
  512.3 1.9 fusion.27
  514.3 2.0 fusion.34
  516.3 2.0 fusion.36
  518.4 2.0 fusion.38
  521.5 3.6 fusion.32
  526.2 3.5 fusion.51
  530.9 3.5 fusion.50
  536.1 1.5 fusion.23
  537.6 1.5 fusion.16
  539.1 2.8 gather_fusion.3
  542.0 2.1 gather_fusion.1
  544.1 1.3 select_select_fusion
  545.4 39.7 %all_to_all.20 = bf16[16,32,1024]{2,1,0:T(8,128)(2,1)S(1)} all-to-all(bf16[16,32,1024]{2,1,0:T(8,128)(2,1)S(1)} %get-tuple-element.72), channel_id=1, replica_groups=mesh['dp'=16,'tensor'=2] {'dp'}, dimensions={0} | all-to-all | bytes 2097152 | tf_op jit(solution)/shard_map/all_to_all | solution.py:251
  585.2 4.1 all-to-all-start.1
  589.9 48.9 %all-reduce.4 = (f32[1024]{0:T(1024)S(1)}, f32[1024]{0:T(1024)S(1)}) all-reduce(f32[1024]{0:T(1024)S(1)} %get-tuple-element.55, f32[1024]{0:T(1024)S(1)} %get-tuple-element.53), channel_id=9, replica_groups=mesh['dp'=16,'tensor'=2] {'dp'}, use_global_device_ids=true, to_apply=%region_22.25.clone | all-reduce | flops 2048 | bytes 16384
  640.0 51.1 %reduce-scatter.12.cloned.1.call-done = f32[64,512]{1,0:T(8,128)} async-done(((f32[1024,512]{1,0:T(8,128)}), f32[64,512]{1,0:T(8,128)}) %reduce-scatter.12.cloned.1.call-update) | async-done | bytes 131088 | tf_op jit(solution)/shard_map/reduce_scatter | solution.py:262
  691.1 80.9 %reduce-scatter.10.cloned.1.call-done = f32[64,512]{1,0:T(8,128)} async-done(((f32[1024,512]{1,0:T(8,128)}), f32[64,512]{1,0:T(8,128)}) %reduce-scatter.10.cloned.1.call-update) | async-done | bytes 131088 | tf_op jit(solution)/shard_map/reduce_scatter | solution.py:261
  771.9 80.6 %reduce-scatter.8.cloned.1.call-done = f32[64,512]{1,0:T(8,128)} async-done(((f32[1024,512]{1,0:T(8,128)}), f32[64,512]{1,0:T(8,128)}) %reduce-scatter.8.cloned.1.call-update) | async-done | bytes 131088 | tf_op jit(solution)/shard_map/reduce_scatter | solution.py:260
  852.5 140.8 %reduce-scatter.20.cloned.1.call-done = f32[1408,64]{0,1:T(8,128)} async-done(((f32[1408,1024]{0,1:T(8,128)}), f32[1408,64]{0,1:T(8,128)}) %reduce-scatter.20.cloned.1.call-update) | async-done | bytes 360464 | tf_op jit(solution)/shard_map/reduce_scatter | solution.py:266
  993.3 129.8 %reduce-scatter.18.cloned.1.call-done = f32[64,1408]{1,0:T(8,128)} async-done(((f32[1024,1408]{1,0:T(8,128)}), f32[64,1408]{1,0:T(8,128)}) %reduce-scatter.18.cloned.1.call-update) | async-done | bytes 360464 | tf_op jit(solution)/shard_map/reduce_scatter | solution.py:265
  1123.1 129.8 %reduce-scatter.16.cloned.1.call-done = f32[64,1408]{1,0:T(8,128)} async-done(((f32[1024,1408]{1,0:T(8,128)}), f32[64,1408]{1,0:T(8,128)}) %reduce-scatter.16.cloned.1.call-update) | async-done | bytes 360464 | tf_op jit(solution)/shard_map/reduce_scatter | solution.py:264
  (155 shorter events, 30.5 us)
Async XLA Ops:
  7.2 9.6 copy-start.30
  7.2 10.8 copy-start.31
  7.2 11.1 copy-start.32
  7.2 54.2 %copy-start.29 = (s32[1,256]{1,0:T(1,128)S(1)}, s32[1,256]{1,0:T(1,128)}, u32[]{:S(2)}) copy-start(s32[1,256]{1,0:T(1,128)} %param.27) | copy-start | bytes 3076
  7.2 63.3 %all-gather.12.cloned.1.call-start = ((), (), s32[]{:S(2)}) async-start(), calls=%async_computation.13 | async-start | bytes 1114112 | tf_op jit(solution)/shard_map/all_gather | solution.py:154
  8.0 119.3 %all-gather.10.cloned.1.call-start = ((), (), s32[]{:S(2)}) async-start(), calls=%async_computation.12 | async-start | bytes 1114112 | tf_op jit(solution)/shard_map/all_gather | solution.py:153
  8.7 175.5 %all-gather.8.cloned.1.call-start = ((), (), s32[]{:S(2)}) async-start(), calls=%async_computation.11 | async-start | bytes 1114112 | tf_op jit(solution)/shard_map/all_gather | solution.py:155
  9.4 52.1 %all-to-all-start = ((bf16[16,32,1024]{2,1,0:T(8,128)(2,1)}), bf16[16,32,1024]{2,1,0:T(8,128)(2,1)S(1)}, u32[]{:S(2)}, u32[]{:S(2)}) async-start(bf16[16,32,1024]{2,1,0:T(8,128)(2,1)} %bitcast.99), calls=%async_computation | async-start | bytes 2097152 | tf_op jit(solution)/shard_map/all_to_all | solution.py:148
  16.1 224.8 %all-gather.14.cloned.1.call-start = ((), (), s32[]{:S(2)}) async-start(), calls=%async_computation.14 | async-start | bytes 1114112 | tf_op jit(solution)/shard_map/all_gather | solution.py:156
  16.7 262.5 %all-reduce.11.cloned.1.call-start = ((), (), s32[]{:S(2)}) async-start(), calls=%async_computation.15 | async-start | bytes 2097152 | tf_op jit(solution)/shard_map/psum | solution.py:177
  72.3 113.7 %copy-start.12 = (bf16[256,512]{0,1:T(8,128)(2,1)}, bf16[256,512]{0,1:T(8,128)(2,1)S(1)}, u32[]{:S(2)}) copy-start(bf16[256,512]{0,1:T(8,128)(2,1)S(1)} %copy.58) | copy-start | bytes 786436
  129.1 57.4 %copy-start.14 = (bf16[256,512]{0,1:T(8,128)(2,1)}, bf16[256,512]{0,1:T(8,128)(2,1)S(1)}, u32[]{:S(2)}) copy-start(bf16[256,512]{0,1:T(8,128)(2,1)S(1)} %copy.57) | copy-start | bytes 786436
  187.4 58.3 %copy-start.22 = (bf16[8,64,256]{2,1,0:T(8,128)(2,1)}, bf16[8,64,256]{2,1,0:T(8,128)(2,1)S(1)}, u32[]{:S(2)}) copy-start(bf16[8,64,256]{2,1,0:T(8,128)(2,1)S(1)} %convolution_convert_fusion.3) | copy-start | bytes 786436
  243.6 90.7 %all-gather.18.cloned.1.call-start = ((), (), s32[]{:S(2)}) async-start(), calls=%async_computation.17 | async-start | bytes 3063808 | tf_op jit(solution)/shard_map/all_gather | solution.py:158
  244.2 158.3 %all-gather.16.cloned.1.call-start = ((), (), s32[]{:S(2)}) async-start(), calls=%async_computation.16 | async-start | bytes 3063808 | tf_op jit(solution)/shard_map/all_gather | solution.py:157
  244.9 225.6 %all-gather.20.cloned.1.call-start = ((), (), s32[]{:S(2)}) async-start(), calls=%async_computation.18 | async-start | bytes 3063808 | tf_op jit(solution)/shard_map/all_gather | solution.py:159
  245.7 29.8 %all-to-all-start.2 = ((bf16[16,32,1024]{2,1,0:T(8,128)(2,1)}), bf16[16,32,1024]{2,1,0:T(8,128)(2,1)}, u32[]{:S(2)}, u32[]{:S(2)}) async-start(bf16[16,32,1024]{2,1,0:T(8,128)(2,1)} %bitcast.100), calls=%async_computation.2 | async-start | bytes 2097152 | tf_op jit(solution)/shard_map/all_to_all | solution.py:200
  251.1 247.6 %all-reduce.13.cloned.1.call-start = ((), (), s32[]{:S(2)}) async-start(), calls=%async_computation.19 | async-start | bytes 1048576 | tf_op jit(solution)/shard_map/psum | solution.py:225
  470.5 5.2 copy-start.9
  475.7 1.0 copy-start.24
  475.7 1.2 copy-start.26
  475.7 2.3 copy-start.8
  479.9 56.2 %all-reduce.15.cloned.1.call-start = ((), (), s32[]{:S(2)}) async-start(), calls=%async_computation.27 | async-start | bytes 2097152 | tf_op jit(solution)/shard_map/psum | solution.py:188
  498.7 2.0 copy-start.1
  498.7 4.6 copy-start.6
  506.4 3.8 copy-start.10
  507.0 1.4 copy-start.13
  508.0 1.2 copy-start.20
  508.4 1.3 copy-start.19
  509.7 1.2 copy-start.21
  510.2 2.1 copy-start.4
  510.2 2.1 copy-start.23
  512.2 2.0 copy-start.11
  512.2 127.7 %reduce-scatter.14.cloned.1.call-start = ((), (), s32[]{:S(2)}) async-start(), calls=%async_computation.23 | async-start | bytes 2228224 | tf_op jit(solution)/shard_map/reduce_scatter | solution.py:263
  514.2 176.9 %reduce-scatter.12.cloned.1.call-start = ((), (), s32[]{:S(2)}) async-start(), calls=%async_computation.22 | async-start | bytes 2228224 | tf_op jit(solution)/shard_map/reduce_scatter | solution.py:262
  516.3 255.6 %reduce-scatter.10.cloned.1.call-start = ((), (), s32[]{:S(2)}) async-start(), calls=%async_computation.21 | async-start | bytes 2228224 | tf_op jit(solution)/shard_map/reduce_scatter | solution.py:261
  518.3 2.1 copy-start.5
  518.4 334.1 %reduce-scatter.8.cloned.1.call-start = ((), (), s32[]{:S(2)}) async-start(), calls=%async_computation.20 | async-start | bytes 2228224 | tf_op jit(solution)/shard_map/reduce_scatter | solution.py:260
  520.4 1.1 copy-start.16
  520.4 472.9 %reduce-scatter.20.cloned.1.call-start = ((), (), s32[]{:S(2)}) async-start(), calls=%async_computation.26 | async-start | bytes 6127616 | tf_op jit(solution)/shard_map/reduce_scatter | solution.py:266
  525.1 1.1 copy-start.27
  525.1 598.0 %reduce-scatter.18.cloned.1.call-start = ((), (), s32[]{:S(2)}) async-start(), calls=%async_computation.25 | async-start | bytes 6127616 | tf_op jit(solution)/shard_map/reduce_scatter | solution.py:265
  529.8 1.1 copy-start.25
  529.8 723.2 %reduce-scatter.16.cloned.1.call-start = ((), (), s32[]{:S(2)}) async-start(), calls=%async_computation.24 | async-start | bytes 6127616 | tf_op jit(solution)/shard_map/reduce_scatter | solution.py:264
  539.1 2.8 copy-start.2
  539.1 2.8 copy-start.28
  542.0 2.1 copy-start.7
  585.2 54.8 %all-to-all-start.1 = ((bf16[16,32,1024]{2,1,0:T(8,128)(2,1)}), bf16[16,32,1024]{2,1,0:T(8,128)(2,1)S(1)}, u32[]{:S(2)}, u32[]{:S(2)}) async-start(bf16[16,32,1024]{2,1,0:T(8,128)(2,1)} %get-tuple-element.73), calls=%async_computation.1 | async-start | bytes 2097152 | tf_op jit(solution)/shard_map/all_to_all | solution.py:192
  (5 other events, 4.7 us)
Sparse Core Ops, SparseCore 0:
  10.8 59.6 all-gather.11
  73.2 54.0 all-gather.9
  130.1 54.0 all-gather.7
  186.8 54.0 all-gather.13
  243.7 21.3 all-reduce.10
  268.1 66.2 all-gather.17
  337.5 64.9 all-gather.15
  405.6 64.9 all-gather.19
  480.0 18.6 all-reduce.12
  512.4 20.8 all-reduce.14
  536.2 79.8 reduce-scatter.13
  618.9 72.1 reduce-scatter.11
  694.0 77.8 reduce-scatter.9
  774.7 77.7 reduce-scatter.7
  855.3 137.8 reduce-scatter.19
  996.1 126.9 reduce-scatter.17
  1126.0 126.9 reduce-scatter.15
where the time goes:
time: 1270 us; the launch traced here: 1260 us
  waiting for transfers between devices  1010 us (80%)
  blocking collectives  130 us (10%)
  matrix products  52.1 us (4%)
  local copies, waits for them, and re-layouts  25.3 us (2%)
  starting transfers between devices  17.2 us (1%)
  between operations  15.9 us (1%)
    reduce_scatter x1, waiting for transfers between devices, body(): lax.psum_scatter(grad_down, 'dp', scatter_dimension=1, tiled=True)  141 us
    reduce_scatter x1, waiting for transfers between devices, body(): lax.psum_scatter(grad_up, 'dp', scatter_dimension=0, tiled=True)  130 us
    reduce_scatter x1, waiting for transfers between devices, body(): lax.psum_scatter(grad_gate, 'dp', scatter_dimension=0, tiled=True)  130 us
    unnamed x2, blocking collectives  90.1 us
    reduce_scatter x1, waiting for transfers between devices, body(): lax.psum_scatter(grad_key, 'dp', scatter_dimension=0, tiled=True)  80.9 us
    reduce_scatter x1, waiting for transfers between devices, body(): lax.psum_scatter(grad_query, 'dp', scatter_dimension=0, tiled=True)  80.6 us
    all_gather x1, waiting for transfers between devices, body(): lax.all_gather(w_down, 'dp', axis=1, tiled=True)  64.2 us
    all_gather x1, waiting for transfers between devices, body(): lax.all_gather(w_gate, 'dp', axis=0, tiled=True)  64.2 us
  transfers between devices with their start and end apart: 20, of which 15 were waited for; matrix products, arithmetic and copies ran while one was open for 5% of the time, Pallas kernels for 0%

commit v1 on v0

v1 whole, which is shorter than its diff:
```python
import jax
import jax.numpy as jnp
import numpy as np
from jax import lax
from jax.sharding import Mesh, PartitionSpec as P

DH = 64
eps = 1e-05
masked_score = -1e30
bf16 = jnp.bfloat16
f32 = jnp.float32

DP = ("z", "yh", "yl", "xh", "xl")
FAR = ("z", "yh", "xh")
NEAR = ("yl", "xl")
CORE = "c"


def mm(left, right):
    return lax.dot_general(left, right, (((1,), (0,)), ((), ())), preferred_element_type=f32)


def mm_t(left, right):
    return lax.dot_general(left, right, (((1,), (1,)), ((), ())), preferred_element_type=f32)


def outer_sum(left, right):
    return lax.dot_general(left, right, (((0,), (0,)), ((), ())), preferred_element_type=f32)


def swap(value):
    return lax.ppermute(value, CORE, [(0, 1), (1, 0)])


def near(value, k):
    return lax.ppermute(value, NEAR, [(i, i ^ k) for i in range(4)])


def gather_near(value):
    return jnp.concatenate([value] + [near(value, k) for k in (1, 2, 3)], axis=0)


def scatter_near(partial):
    low = partial.astype(bf16)
    total = partial[0]
    for k in (1, 2, 3):
        total = total + near(low[k], k).astype(f32)
    return total


def inverse_root(values):
    return lax.rsqrt(jnp.mean(values * values, axis=-1, keepdims=True) + eps)


def natural_rows(weight, far_sizes, rows):
    nz, nyh, nxh = far_sizes
    if nyh * nxh == 1:
        return weight
    cols = weight.shape[-1]
    split = weight.reshape(nz, nyh, nxh, 2, 2, rows, cols)
    return split.transpose(0, 1, 3, 2, 4, 5, 6).reshape(-1, cols)


def far_rows(weight, far_sizes, rows):
    nz, nyh, nxh = far_sizes
    if nyh * nxh == 1:
        return weight
    cols = weight.shape[-1]
    split = weight.reshape(nz, nyh, 2, nxh, 2, rows, cols)
    return split.transpose(0, 1, 3, 2, 4, 5, 6).reshape(-1, cols)


def spread_pack(pieces):
    rows = pieces[0].shape[0]
    blocks = [p.reshape(rows, 4, -1) for p in pieces]
    return jnp.concatenate(blocks, axis=-1).transpose(1, 0, 2)


def body(patches, counts, doc_ids, w_query, w_key, w_value, w_output, w_gate, w_up, w_down, gain_attn, gain_ffn, cotangent):
    core = lax.axis_index(CORE)
    my_row = lax.axis_index(DP)
    peers, slot_cap, width = patches.shape[1:]
    half_width = width // 2
    tok_count = doc_ids.shape[1]
    toks = tok_count // 2
    rows = w_query.shape[0]
    far_sizes = tuple(lax.axis_size(a) for a in FAR)
    score_scale = DH ** (-0.5)
    heads_part = w_query.shape[1] // 4
    ff_part = w_gate.shape[1] // 4
    ff_pad = -(-ff_part // 128) * 128

    gain_a = gain_attn.astype(f32)[:, None]
    gain_f = gain_ffn.astype(f32)[:, None]

    def scaled(weight, gain):
        return (weight.astype(f32) * gain).astype(bf16)

    attn_pack = spread_pack([scaled(w_query, gain_a), scaled(w_key, gain_a), scaled(w_value, gain_a), w_output.T])

    def padded(weight):
        quarter = weight.reshape(rows, 4, ff_part)
        return jnp.pad(quarter, ((0, 0), (0, 0), (0, ff_pad - ff_part))).reshape(rows, -1)

    ffn_pack = spread_pack([padded(scaled(w_gate, gain_f)), padded(scaled(w_up, gain_f)), padded(w_down.T)])

    def exchange(pack):
        moved = lax.all_to_all(pack, NEAR, 0, 0, tiled=True)
        flat = moved.reshape(4 * rows, -1)
        whole = lax.all_gather(flat, FAR, axis=0, tiled=True)
        return natural_rows(whole, far_sizes, rows)

    def half_features(blocks):
        return lax.dynamic_slice_in_dim(blocks, core * half_width, half_width, 2)

    def to_rows(blocks):
        return lax.all_to_all(half_features(blocks[0]), DP, 0, 0, tiled=True).reshape(peers * slot_cap, half_width)

    received = to_rows(patches)
    attn_own = exchange(attn_pack)
    arrived = to_rows(cotangent)
    ffn_own = exchange(ffn_pack)
    attn_oth = swap(attn_own)
    ffn_oth = swap(ffn_own)

    my_counts = lax.dynamic_index_in_dim(counts, my_row, 0, keepdims=False)
    offsets = jnp.cumsum(my_counts) - my_counts
    slots = jnp.arange(slot_cap, dtype=jnp.int32)
    slot_token = jnp.where(slots[None, :] < my_counts[:, None], offsets[:, None] + slots[None, :], -1).reshape(-1)
    token_ids = jnp.arange(tok_count, dtype=jnp.int32)
    place = (token_ids[:, None] == slot_token[None, :]).astype(bf16)

    def join_features(own, other):
        first = jnp.where(core == 0, own, other)
        second = jnp.where(core == 0, other, own)
        return jnp.concatenate([first, second], axis=-1)

    def collect(slots_in):
        mine = mm(place, slots_in).astype(bf16)
        own = lax.dynamic_slice_in_dim(mine, core * toks, toks, 0)
        give = lax.dynamic_slice_in_dim(mine, (1 - core) * toks, toks, 0)
        return join_features(own, swap(give))

    def deliver(values):
        own = lax.dynamic_slice_in_dim(values, core * half_width, half_width, 1)
        give = lax.dynamic_slice_in_dim(values, (1 - core) * half_width, half_width, 1)
        other = swap(give)
        both = jnp.concatenate([jnp.where(core == 0, own, other), jnp.where(core == 0, other, own)], axis=0)
        spread = outer_sum(place, both).astype(bf16).reshape(peers, slot_cap, half_width)
        back = lax.all_to_all(spread, DP, 0, 0, tiled=True)
        return join_features(back, swap(back))[None]

    doc_rows = gather_near(doc_ids)
    doc_own = lax.dynamic_slice_in_dim(doc_rows, core * toks, toks, 1)
    doc_oth = lax.dynamic_slice_in_dim(doc_rows, (1 - core) * toks, toks, 1)
    pos = jnp.arange(toks)
    visible_own = (doc_own[:, :, None] == doc_own[:, None, :]) & (pos[None, :] <= pos[:, None])[None]
    visible_oth = (doc_own[:, :, None] == doc_oth[:, None, :]) & (core == 1)
    visible = jnp.concatenate([visible_own, visible_oth], axis=-1)

    x = collect(received).astype(f32)
    root_attn = inverse_root(x)
    norm_attn = x * root_attn
    norm_a = gather_near(norm_attn.astype(bf16))

    n3 = 3 * heads_part
    qkv_own = mm(norm_a, attn_own[:, :n3]).astype(bf16)
    qkv_oth = mm(norm_a, attn_oth[:, :n3]).astype(bf16)
    kv_own = qkv_own[:, heads_part:]
    kv_oth = qkv_oth[:, heads_part:]
    kv_own_far = swap(kv_oth)
    kv_oth_far = swap(kv_own)

    def heads(own, oth):
        both = jnp.concatenate([own, oth], axis=-1)
        return both.reshape(4, toks, -1, DH)

    hp = heads_part
    q = heads(qkv_own[:, :hp], qkv_oth[:, :hp])
    k = jnp.concatenate([heads(kv_own[:, :hp], kv_oth[:, :hp]), heads(kv_own_far[:, :hp], kv_oth_far[:, :hp])], axis=1)
    v = jnp.concatenate([heads(kv_own[:, hp:], kv_oth[:, hp:]), heads(kv_own_far[:, hp:], kv_oth_far[:, hp:])], axis=1)
    scores = jnp.einsum("rthd,rshd->rhts", q, k, preferred_element_type=f32) * score_scale
    scores = jnp.where(visible[:, None], scores, masked_score)
    lifted = jnp.exp(scores - jnp.max(scores, axis=-1, keepdims=True))
    probs = lifted / jnp.sum(lifted, axis=-1, keepdims=True)
    probs_low = probs.astype(bf16)
    attended = jnp.einsum("rhts,rshd->rthd", probs_low, v, preferred_element_type=f32).astype(bf16)
    attended = attended.reshape(4 * toks, -1)
    att_own, att_oth = attended[:, :hp], attended[:, hp:]
    out_own, out_oth = attn_own[:, n3:], attn_oth[:, n3:]
    branch = mm_t(att_own, out_own) + mm_t(att_oth, out_oth)
    hidden = x + scatter_near(branch.reshape(4, toks, width))

    root_ffn = inverse_root(hidden)
    norm_ffn = hidden * root_ffn
    norm_f = gather_near(norm_ffn.astype(bf16))
    grad_low = collect(arrived)
    grad_y = gather_near(grad_low)

    def ffn_half(weights):
        gate_w, up_w, down_w = (weights[:, i * ff_pad : (i + 1) * ff_pad] for i in range(3))
        gate = mm(norm_f, gate_w)
        up = mm(norm_f, up_w)
        sig = jax.nn.sigmoid(gate)
        silu = gate * sig
        product = (silu * up).astype(bf16)
        grad_product = mm(grad_y, down_w)
        grad_gate = (grad_product * up * sig * (1.0 + gate * (1.0 - sig))).astype(bf16)
        grad_up = (grad_product * silu).astype(bf16)
        branch = mm_t(product, down_w)
        grad_norm = mm_t(grad_gate, gate_w) + mm_t(grad_up, up_w)
        grads = jnp.concatenate(
            [outer_sum(norm_f, grad_gate), outer_sum(norm_f, grad_up), outer_sum(grad_y, product)], axis=-1
        ).astype(bf16)
        return branch, grad_norm, grads

    branch_own, grad_norm_own, ffn_grads_own = ffn_half(ffn_own)
    branch_oth, grad_norm_oth, ffn_grads_oth = ffn_half(ffn_oth)
    scaled_two = scatter_near((grad_norm_own + grad_norm_oth).reshape(4, toks, width))
    grad_hidden = grad_low.astype(f32) + root_ffn * (
        scaled_two - norm_ffn * jnp.mean(scaled_two * norm_ffn, axis=-1, keepdims=True)
    )
    grad_branch = gather_near(grad_hidden.astype(bf16))

    final = hidden + scatter_near((branch_own + branch_oth).reshape(4, toks, width))
    outputs = deliver(final.astype(bf16))

    def reduce_far(own, other):
        total = (own.astype(f32) + swap(other).astype(f32)).astype(bf16)
        part = lax.psum_scatter(far_rows(total, far_sizes, rows), FAR, scatter_dimension=0, tiled=True)
        cols = part.shape[-1]
        return lax.all_to_all(part.reshape(4, rows, cols), NEAR, 0, 0, tiled=True)

    ffn_grads = reduce_far(ffn_grads_own, ffn_grads_oth)

    grad_att_own = mm(grad_branch, out_own).astype(bf16)
    grad_att_oth = mm(grad_branch, out_oth).astype(bf16)
    grad_heads = heads(grad_att_own, grad_att_oth)
    grad_probs = jnp.einsum("rthd,rshd->rhts", grad_heads, v, preferred_element_type=f32)
    grad_v = jnp.einsum("rhts,rthd->rshd", probs_low, grad_heads, preferred_element_type=f32)
    grad_scores = probs * (grad_probs - jnp.sum(grad_probs * probs, axis=-1, keepdims=True))
    scores_low = grad_scores.astype(bf16)
    grad_q = (jnp.einsum("rhts,rshd->rthd", scores_low, k, preferred_element_type=f32) * score_scale).astype(bf16)
    grad_k = jnp.einsum("rhts,rthd->rshd", scores_low, q, preferred_element_type=f32) * score_scale
    grad_q = grad_q.reshape(4 * toks, -1)

    def halves(grad):
        near_part = grad[:, :toks].reshape(4 * toks, -1)
        far_part = grad[:, toks:].reshape(4 * toks, -1)
        return near_part[:, :hp], near_part[:, hp:], far_part[:, :hp], far_part[:, hp:]

    k_own, k_oth, k_own_far, k_oth_far = halves(grad_k)
    v_own, v_oth, v_own_far, v_oth_far = halves(grad_v)
    far_grads = jnp.concatenate([k_oth_far, v_oth_far, k_own_far, v_own_far], axis=-1).astype(bf16)
    back = swap(far_grads).astype(f32)
    gqkv_own = jnp.concatenate(
        [grad_q[:, :hp], (k_own + back[:, :hp]).astype(bf16), (v_own + back[:, hp : 2 * hp]).astype(bf16)], axis=-1
    )
    gqkv_oth = jnp.concatenate(
        [grad_q[:, hp:], (k_oth + back[:, 2 * hp : 3 * hp]).astype(bf16), (v_oth + back[:, 3 * hp :]).astype(bf16)], axis=-1
    )
    grad_norm_a = mm_t(gqkv_own, attn_own[:, :n3]) + mm_t(gqkv_oth, attn_oth[:, :n3])
    scaled_one = scatter_near(grad_norm_a.reshape(4, toks, width))
    grad_input = grad_hidden + root_attn * (
        scaled_one - norm_attn * jnp.mean(scaled_one * norm_attn, axis=-1, keepdims=True)
    )
    input_grad = deliver(grad_input.astype(bf16))

    attn_grads = reduce_far(
        jnp.concatenate([outer_sum(norm_a, gqkv_own), outer_sum(grad_branch, att_own)], axis=-1).astype(bf16),
        jnp.concatenate([outer_sum(norm_a, gqkv_oth), outer_sum(grad_branch, att_oth)], axis=-1).astype(bf16),
    )

    def unpack(blocks, start, size, total):
        piece = blocks[:, :, start : start + size].astype(f32)
        return piece.transpose(1, 0, 2).reshape(rows, total)

    raw_q, raw_k, raw_v, raw_o = (unpack(attn_grads, i * hp, hp, 4 * hp) for i in range(4))
    raw_g, raw_u, raw_d = (unpack(ffn_grads, i * ff_pad, ff_part, 4 * ff_part) for i in range(3))

    def gain_sum(raws, weights):
        return sum(jnp.sum(r * w.astype(f32), axis=1) for r, w in zip(raws, weights))

    gains = jnp.stack([gain_sum([raw_q, raw_k, raw_v], [w_query, w_key, w_value]), gain_sum([raw_g, raw_u], [w_gate, w_up])])
    gains = gains + swap(gains)
    return (
        outputs,
        input_grad,
        raw_q * gain_a,
        raw_k * gain_a,
        raw_v * gain_a,
        raw_o.T,
        raw_g * gain_f,
        raw_u * gain_f,
        raw_d.T,
        gains[0],
        gains[1],
    )


def solution(mesh):
    dp_size = mesh.shape["dp"]
    side = round((dp_size / 2) ** (1 / 3))
    grid = (2 * side, side // 2, 2, side // 2, 2, 2)
    inner = Mesh(np.asarray(mesh.devices).reshape(grid), ("z", "yh", "yl", "xh", "xl", "c"))
    rows_first = P(DP, "c")
    cols_first = P("c", DP)
    blocks = P(DP, None, None, None)
    weights = (rows_first, rows_first, rows_first, cols_first, rows_first, rows_first, cols_first, P(DP), P(DP))
    in_specs = (blocks, P(), P(DP, None)) + weights + (blocks,)
    out_specs = (blocks, blocks) + weights
    return jax.shard_map(body, mesh=inner, in_specs=in_specs, out_specs=out_specs, check_vma=False)
```

time: 1270 us -> 348 us (0.27)
  waiting for transfers between devices: 1010 us -> 138 us
  blocking collectives: 130 us -> 0 us
  starting transfers between devices: 17.2 us -> 91.1 us
  other arithmetic: 12.6 us -> 27.6 us
    reduce_scatter x7 -> x2, waiting for transfers between devices: 613 us -> 0.02 us  [reduce_far(): lax.psum_scatter(far_rows(total, far_sizes, rows), FAR, scatter_dimension...]
    all_gather x7 -> x2, waiting for transfers between devices: 352 us -> 30.9 us  [exchange(): whole = lax.all_gather(flat, FAR, axis=0, tiled=True)]
    unnamed x2 -> x0, blocking collectives: 90.1 us -> none
    ppermute x0 -> x41, waiting for transfers between devices: none -> 63.2 us  [the longest x27 60.4 us: near(): return lax.ppermute(value, NEAR, [(i, i ^ k) for i in range(4)])]
    ppermute x0 -> x41, starting transfers between devices: none -> 52.2 us  [the longest x27 27.5 us: near(): return lax.ppermute(value, NEAR, [(i, i ^ k) for i in range(4)])]
    all_to_all x1 -> x0, blocking collectives: 39.7 us -> none  [body(): lax.all_to_all(spread(grad_input.astype(jnp.bfloat16), back_index, back_v...]
    all_to_all x3 -> x8, starting transfers between devices: 16.1 us -> 38 us  [the longest x2 12.6 us: deliver(): back = lax.all_to_all(spread, DP, 0, 0, tiled=True)]
    all_to_all x3 -> x8, waiting for transfers between devices: 24.4 us -> 42.8 us  [the longest x2 22.2 us: deliver(): back = lax.all_to_all(spread, DP, 0, 0, tiled=True)]
  transfers between devices with their start and end apart: 20 -> 53, of which waited for: 15 -> 25; matrix products, arithmetic and copies ran while one was open for 5% -> 20% of each run, Pallas kernels for 0% -> 0%
where the time goes in v1:
time: 348 us; the launch traced here: 342 us
  waiting for transfers between devices  138 us (40%)
  starting transfers between devices  91.1 us (26%)
  matrix products  43.4 us (12%)
  other arithmetic  27.6 us (8%)
  local copies, waits for them, and re-layouts  26.3 us (8%)
  between operations  15.7 us (5%)
    ppermute x27, waiting for transfers between devices, near(): return lax.ppermute(value, NEAR, [(i, i ^ k) for i in range(4)])  60.4 us
    all_gather x2, waiting for transfers between devices, exchange(): whole = lax.all_gather(flat, FAR, axis=0, tiled=True)  30.9 us
    ppermute x27, starting transfers between devices, near(): return lax.ppermute(value, NEAR, [(i, i ^ k) for i in range(4)])  27.5 us
    ppermute x14, starting transfers between devices, swap(): return lax.ppermute(value, CORE, [(0, 1), (1, 0)])  24.7 us
    all_to_all x2, waiting for transfers between devices, deliver(): back = lax.all_to_all(spread, DP, 0, 0, tiled=True)  22.2 us
    dot_general x12, matrix products, mm(): lax.dot_general(left, right, (((1,), (0,)), ((), ())), preferred_element_...  15 us
    all_to_all x2, starting transfers between devices, deliver(): back = lax.all_to_all(spread, DP, 0, 0, tiled=True)  12.6 us
    dot_general x12, matrix products, outer_sum(): lax.dot_general(left, right, (((0,), (0,)), ((), ())), preferred_element_...  11.4 us
  transfers between devices with their start and end apart: 53, of which 25 were waited for; matrix products, arithmetic and copies ran while one was open for 20% of the time, Pallas kernels for 0%

profile of v1, /device:TPU:9, one launch (start us, length us, event | category | flops | bytes accessed | tf_op | source)
XLA Modules:
  0.0 341.8 jit_solution(9248975378159011909)
XLA Ops:
  7.2 2.2 collective-permute-start.9
  13.5 3.4 %all-to-all-start.1 = ((bf16[4,64,512]{2,1,0:T(8,128)(2,1)}), bf16[4,64,512]{2,1,0:T(8,128)(2,1)S(1)}, u32[]{:S(2)}, u32[]{:S(2)}) async-start(bf16[4,64,512]{2,1,0:T(8,128)(2,1)} %copy.84), calls=%async_computation.1 | async-start | bytes 524288 | tf_op jit(solution)/shard_map/all_to_all | solution.py:108
  21.1 5.8 %all-to-all-start = ((bf16[16,32,512]{2,1,0:T(8,128)(2,1)}), bf16[16,32,512]{2,1,0:T(8,128)(2,1)S(1)}, u32[]{:S(2)}, u32[]{:S(2)}) async-start(bf16[16,32,512]{2,1,0:T(8,128)(2,1)} %dynamic-slice_bitcast_fusion.1), calls=%async_computation | async-start | bytes 1048576 | tf_op jit(solution)/shard_map/all_to_all | solution.py:117
  29.9 8.2 %all-to-all-done = bf16[16,32,512]{2,1,0:T(8,128)(2,1)S(1)} async-done(((bf16[16,32,512]{2,1,0:T(8,128)(2,1)}), bf16[16,32,512]{2,1,0:T(8,128)(2,1)S(1)}, u32[]{:S(2)}, u32[]{:S(2)}) %all-to-all-start) | async-done | bytes 524320 | tf_op jit(solution)/shard_map/all_to_all | solution.py:117
  38.1 4.0 %all-to-all-start.2 = ((bf16[4,64,1152]{2,1,0:T(8,128)(2,1)}), bf16[4,64,1152]{2,1,0:T(8,128)(2,1)S(1)}, u32[]{:S(2)}, u32[]{:S(2)}) async-start(bf16[4,64,1152]{2,1,0:T(8,128)(2,1)} %copy.91), calls=%async_computation.2 | async-start | bytes 1179648 | tf_op jit(solution)/shard_map/all_to_all | solution.py:108
  42.5 4.0 %collective-permute-start = (bf16[128,512]{1,0:T(8,128)(2,1)S(1)}, bf16[128,512]{1,0:T(8,128)(2,1)S(1)}, u32[]{:S(2)}, u32[]{:S(2)}) collective-permute-start(bf16[128,512]{1,0:T(8,128)(2,1)S(1)} %constant_dynamic-slice_fusion.5), channel_id=1, source_target_pairs={{0,1},{1,0},{2,3},{3,2},{4,5},{5,4},{6,7},{7,6},{8,9},{9,8},{10,11... | collective-permute-start | bytes 393224 | tf_op jit(solution)/shard_map/ppermute | solution.py:32
  47.8 2.7 collective-permute-start.3
  50.9 10.1 %all-gather.3.cloned.1.call-done = bf16[1024,512]{1,0:T(8,128)(2,1)} async-done(((bf16[256,512]{1,0:T(8,128)(2,1)}), bf16[1024,512]{1,0:T(8,128)(2,1)}) %all-gather.3.cloned.1.call-update) | async-done | bytes 1048592 | tf_op jit(solution)/shard_map/all_gather | solution.py:110
  63.5 1.9 convolution_convert_fusion.11
  66.4 4.5 %all-to-all-start.4 = ((bf16[16,32,512]{2,1,0:T(8,128)(2,1)}), bf16[16,32,512]{2,1,0:T(8,128)(2,1)}, u32[]{:S(2)}, u32[]{:S(2)}) async-start(bf16[16,32,512]{2,1,0:T(8,128)(2,1)} %dynamic-slice_bitcast_fusion), calls=%async_computation.4 | async-start | bytes 1048576 | tf_op jit(solution)/shard_map/all_to_all | solution.py:117
  72.3 2.1 convolution_convert_fusion.10
  78.6 2.0 fusion.8
  84.6 2.1 collective-permute-start.12
  90.0 3.5 %collective-permute-done.12 = bf16[128,1024]{1,0:T(8,128)(2,1)S(1)} collective-permute-done((bf16[128,1024]{1,0:T(8,128)(2,1)}, bf16[128,1024]{1,0:T(8,128)(2,1)S(1)}, u32[]{:S(2)}, u32[]{:S(2)}) %collective-permute-start.12) | collective-permute-done | bytes 262176 | tf_op jit(solution)/shard_map/ppermute | solution.py:36
  93.4 6.3 %collective-permute-done.11 = bf16[128,1024]{1,0:T(8,128)(2,1)S(1)} collective-permute-done((bf16[128,1024]{1,0:T(8,128)(2,1)}, bf16[128,1024]{1,0:T(8,128)(2,1)S(1)}, u32[]{:S(2)}, u32[]{:S(2)}) %collective-permute-start.11) | collective-permute-done | bytes 262176 | tf_op jit(solution)/shard_map/ppermute | solution.py:36
  102.4 20.8 %all-gather.5.cloned.1.call-done = bf16[1024,1152]{1,0:T(8,128)(2,1)} async-done(((bf16[256,1152]{1,0:T(8,128)(2,1)}), bf16[1024,1152]{1,0:T(8,128)(2,1)}) %all-gather.5.cloned.1.call-update) | async-done | bytes 2359312 | tf_op jit(solution)/shard_map/all_gather | solution.py:110
  124.3 2.2 collective-permute-start.15
  128.0 2.2 collective-permute-start.25
  130.2 3.0 collective-permute-done.15
  134.4 5.0 %collective-permute-done.14 = bf16[128,1024]{1,0:T(8,128)(2,1)S(1)} collective-permute-done((bf16[128,1024]{1,0:T(8,128)(2,1)S(1)}, bf16[128,1024]{1,0:T(8,128)(2,1)S(1)}, u32[]{:S(2)}, u32[]{:S(2)}) %collective-permute-start.14) | collective-permute-done | bytes 262176 | tf_op jit(solution)/shard_map/ppermute | solution.py:36
  140.6 1.9 fusion.38
  144.5 5.8 %collective-permute-done.24 = bf16[128,1024]{1,0:T(8,128)(2,1)S(1)} collective-permute-done((bf16[128,1024]{1,0:T(8,128)(2,1)S(1)}, bf16[128,1024]{1,0:T(8,128)(2,1)S(1)}, u32[]{:S(2)}, u32[]{:S(2)}) %collective-permute-start.24) | collective-permute-done | bytes 262176 | tf_op jit(solution)/shard_map/ppermute | solution.py:36
  162.2 1.6 collective-permute-start.18
  163.8 2.2 collective-permute-done.28
  167.2 6.2 %collective-permute-done.27 = bf16[128,1024]{1,0:T(8,128)(2,1)S(1)} collective-permute-done((bf16[128,1024]{1,0:T(8,128)(2,1)S(1)}, bf16[128,1024]{1,0:T(8,128)(2,1)S(1)}, u32[]{:S(2)}, u32[]{:S(2)}) %collective-permute-start.27) | collective-permute-done | bytes 262176 | tf_op jit(solution)/shard_map/ppermute | solution.py:36
  173.6 3.7 %collective-permute-done.19 = bf16[128,1024]{1,0:T(8,128)(2,1)S(1)} collective-permute-done((bf16[128,1024]{1,0:T(8,128)(2,1)S(1)}, bf16[128,1024]{1,0:T(8,128)(2,1)S(1)}, u32[]{:S(2)}, u32[]{:S(2)}) %collective-permute-start.19) | collective-permute-done | bytes 262176 | tf_op jit(solution)/shard_map/ppermute | solution.py:36
  177.3 6.4 %collective-permute-done.18 = bf16[128,1024]{1,0:T(8,128)(2,1)S(1)} collective-permute-done((bf16[128,1024]{1,0:T(8,128)(2,1)S(1)}, bf16[128,1024]{1,0:T(8,128)(2,1)S(1)}, u32[]{:S(2)}, u32[]{:S(2)}) %collective-permute-start.18) | collective-permute-done | bytes 262176 | tf_op jit(solution)/shard_map/ppermute | solution.py:36
  190.8 2.5 collective-permute-done.31
  193.3 6.5 %collective-permute-done.30 = bf16[128,1024]{1,0:T(8,128)(2,1)S(1)} collective-permute-done((bf16[128,1024]{1,0:T(8,128)(2,1)S(1)}, bf16[128,1024]{1,0:T(8,128)(2,1)S(1)}, u32[]{:S(2)}, u32[]{:S(2)}) %collective-permute-start.30) | collective-permute-done | bytes 262176 | tf_op jit(solution)/shard_map/ppermute | solution.py:36
  199.8 1.6 convolution_convert_fusion.17
  201.5 1.6 convolution_convert_fusion.18
  215.7 1.6 pad_maximum_fusion
  226.0 4.4 %add_convert_fusion = bf16[1024,1152]{0,1:T(8,128)(2,1)} fusion(bf16[1024,1152]{0,1:T(8,128)(2,1)} %collective-permute-done.39, bf16[1024,384]{0,1:T(8,128)(2,1)S(1)} %convolution_convert_fusion.5, bf16[1024,384]{0,1:T(8,128)(2,1)S(1)} %convolution_convert_fusion.6, bf16[1024,384]{0,1:T(8,128)(2,1)S(1)} %convolution_convert_fusion.7), kind=kLoop, calls=%fused_computation.1 | loop fusion | flops 10616832 | bytes 7077888 | tf_op jit(solution)/shard_map/convert_element_type | solution.py:229
  231.3 3.3 fusion.142
  240.3 5.1 %all-to-all-start.3 = ((bf16[16,32,512]{2,1,0:T(8,128)(2,1)}), bf16[16,32,512]{2,1,0:T(8,128)(2,1)S(1)}, u32[]{:S(2)}, u32[]{:S(2)}) async-start(bf16[16,32,512]{2,1,0:T(8,128)(2,1)} %bitcast.168), calls=%async_computation.3 | async-start | bytes 1048576 | tf_op jit(solution)/shard_map/all_to_all | solution.py:150
  245.4 6.6 %collective-permute-done.34 = bf16[128,1024]{1,0:T(8,128)(2,1)S(1)} collective-permute-done((bf16[128,1024]{1,0:T(8,128)(2,1)}, bf16[128,1024]{1,0:T(8,128)(2,1)S(1)}, u32[]{:S(2)}, u32[]{:S(2)}) %collective-permute-start.34) | collective-permute-done | bytes 262176 | tf_op jit(solution)/shard_map/ppermute | solution.py:36
  257.6 3.4 all-to-all-done.3
  261.0 7.5 %all-to-all-start.5 = ((bf16[16,32,512]{2,1,0:T(8,128)(2,1)}), bf16[16,32,512]{2,1,0:T(8,128)(2,1)S(1)}, u32[]{:S(2)}, u32[]{:S(2)}) async-start(bf16[16,32,512]{2,1,0:T(8,128)(2,1)} %bitcast.18), calls=%async_computation.5 | async-start | bytes 1048576 | tf_op jit(solution)/shard_map/all_to_all | solution.py:150
  268.5 6.0 %collective-permute-start.21 = (bf16[16,32,512]{2,1,0:T(8,128)(2,1)S(1)}, bf16[16,32,512]{2,1,0:T(8,128)(2,1)S(1)}, u32[]{:S(2)}, u32[]{:S(2)}) collective-permute-start(bf16[16,32,512]{2,1,0:T(8,128)(2,1)S(1)} %all-to-all-done.3), channel_id=1, source_target_pairs={{0,1},{1,0},{2,3},{3,2},{4,5},{5,4},{6,7},{7,6},{8,9},{9,8},{10,11... | collective-permute-start | bytes 1572872 | tf_op jit(solution)/shard_map/ppermute | solution.py:32
  274.5 18.8 %all-to-all-done.5 = bf16[16,32,512]{2,1,0:T(8,128)(2,1)S(1)} async-done(((bf16[16,32,512]{2,1,0:T(8,128)(2,1)}), bf16[16,32,512]{2,1,0:T(8,128)(2,1)S(1)}, u32[]{:S(2)}, u32[]{:S(2)}) %all-to-all-start.5) | async-done | bytes 524320 | tf_op jit(solution)/shard_map/all_to_all | solution.py:150
  293.3 6.5 %collective-permute-start.37 = (bf16[16,32,512]{2,1,0:T(8,128)(2,1)S(1)}, bf16[16,32,512]{2,1,0:T(8,128)(2,1)}, u32[]{:S(2)}, u32[]{:S(2)}) collective-permute-start(bf16[16,32,512]{2,1,0:T(8,128)(2,1)S(1)} %all-to-all-done.5), channel_id=1, source_target_pairs={{0,1},{1,0},{2,3},{3,2},{4,5},{5,4},{6,7},{7,6},{8,9},{9,8},{10,11... | collective-permute-start | bytes 1572872 | tf_op jit(solution)/shard_map/ppermute | solution.py:32
  299.8 1.8 copy.100
  301.6 4.2 %all-to-all-start.6 = ((bf16[4,64,512]{2,1,0:T(8,128)(2,1)}), bf16[4,64,512]{2,1,0:T(8,128)(2,1)S(1)}, u32[]{:S(2)}, u32[]{:S(2)}) async-start(bf16[4,64,512]{2,1,0:T(8,128)(2,1)} %bitcast.20), calls=%async_computation.7 | async-start | bytes 524288 | tf_op jit(solution)/shard_map/all_to_all | solution.py:232
  308.1 3.9 %all-to-all-done.6 = bf16[4,64,512]{2,1,0:T(8,128)(2,1)S(1)} async-done(((bf16[4,64,512]{2,1,0:T(8,128)(2,1)}), bf16[4,64,512]{2,1,0:T(8,128)(2,1)S(1)}, u32[]{:S(2)}, u32[]{:S(2)}) %all-to-all-start.6) | async-done | bytes 262176 | tf_op jit(solution)/shard_map/all_to_all | solution.py:232
  313.0 2.1 copy.105
  315.1 3.5 %all-to-all-start.7 = ((bf16[4,64,1152]{2,1,0:T(8,128)(2,1)}), bf16[4,64,1152]{2,1,0:T(8,128)(2,1)S(1)}, u32[]{:S(2)}, u32[]{:S(2)}) async-start(bf16[4,64,1152]{2,1,0:T(8,128)(2,1)} %bitcast.26), calls=%async_computation.9 | async-start | bytes 1179648 | tf_op jit(solution)/shard_map/all_to_all | solution.py:232
  319.5 7.4 %all-to-all-done.7 = bf16[4,64,1152]{2,1,0:T(8,128)(2,1)S(1)} async-done(((bf16[4,64,1152]{2,1,0:T(8,128)(2,1)}), bf16[4,64,1152]{2,1,0:T(8,128)(2,1)S(1)}, u32[]{:S(2)}, u32[]{:S(2)}) %all-to-all-start.7) | async-done | bytes 589856 | tf_op jit(solution)/shard_map/all_to_all | solution.py:232
  327.9 2.1 fusion.67
  (396 shorter events, 102.0 us)
Async XLA Ops:
  7.2 39.3 %collective-permute-start.9 = (s32[1,256]{1,0:T(1,128)}, s32[1,256]{1,0:T(1,128)S(1)}, u32[]{:S(2)}, u32[]{:S(2)}) collective-permute-start(s32[1,256]{1,0:T(1,128)} %param.15), channel_id=1, source_target_pairs={{0,6},{2,4},{4,2},{6,0},{1,7},{3,5},{5,3},{7,1},{8,14},{10,12},{12... | collective-permute-start | bytes 3080 | tf_op jit(solution)/shard_map/ppermute | solution.py:36
  9.5 37.1 %collective-permute-start.8 = (s32[1,256]{1,0:T(1,128)}, s32[1,256]{1,0:T(1,128)S(1)}, u32[]{:S(2)}, u32[]{:S(2)}) collective-permute-start(s32[1,256]{1,0:T(1,128)} %param.15), channel_id=1, source_target_pairs={{0,4},{2,6},{4,0},{6,2},{1,5},{3,7},{5,1},{7,3},{8,12},{10,14},{12... | collective-permute-start | bytes 3080 | tf_op jit(solution)/shard_map/ppermute | solution.py:36
  9.7 36.9 %collective-permute-start.7 = (s32[1,256]{1,0:T(1,128)}, s32[1,256]{1,0:T(1,128)S(1)}, u32[]{:S(2)}, u32[]{:S(2)}) collective-permute-start(s32[1,256]{1,0:T(1,128)} %param.15), channel_id=1, source_target_pairs={{0,2},{2,0},{4,6},{6,4},{1,3},{3,1},{5,7},{7,5},{8,10},{10,8},{12,... | collective-permute-start | bytes 3080 | tf_op jit(solution)/shard_map/ppermute | solution.py:36
  13.5 7.7 %all-to-all-start.1 = ((bf16[4,64,512]{2,1,0:T(8,128)(2,1)}), bf16[4,64,512]{2,1,0:T(8,128)(2,1)S(1)}, u32[]{:S(2)}, u32[]{:S(2)}) async-start(bf16[4,64,512]{2,1,0:T(8,128)(2,1)} %copy.84), calls=%async_computation.1 | async-start | bytes 524288 | tf_op jit(solution)/shard_map/all_to_all | solution.py:108
  21.1 16.9 %all-to-all-start = ((bf16[16,32,512]{2,1,0:T(8,128)(2,1)}), bf16[16,32,512]{2,1,0:T(8,128)(2,1)S(1)}, u32[]{:S(2)}, u32[]{:S(2)}) async-start(bf16[16,32,512]{2,1,0:T(8,128)(2,1)} %dynamic-slice_bitcast_fusion.1), calls=%async_computation | async-start | bytes 1048576 | tf_op jit(solution)/shard_map/all_to_all | solution.py:117
  26.9 34.1 %all-gather.3.cloned.1.call-start = ((), (), s32[]{:S(2)}) async-start(), calls=%async_computation.10 | async-start | bytes 1310720 | tf_op jit(solution)/shard_map/all_gather | solution.py:110
  38.1 28.4 %all-to-all-start.2 = ((bf16[4,64,1152]{2,1,0:T(8,128)(2,1)}), bf16[4,64,1152]{2,1,0:T(8,128)(2,1)S(1)}, u32[]{:S(2)}, u32[]{:S(2)}) async-start(bf16[4,64,1152]{2,1,0:T(8,128)(2,1)} %copy.91), calls=%async_computation.2 | async-start | bytes 1179648 | tf_op jit(solution)/shard_map/all_to_all | solution.py:108
  47.8 14.2 %collective-permute-start.3 = (bf16[128,1024]{1,0:T(8,128)(2,1)S(1)}, bf16[128,1024]{1,0:T(8,128)(2,1)S(1)}, u32[]{:S(2)}, u32[]{:S(2)}) collective-permute-start(bf16[128,1024]{1,0:T(8,128)(2,1)S(1)} %fusion.17), channel_id=1, source_target_pairs={{0,6},{2,4},{4,2},{6,0},{1,7},{3,5},{5,3},{7,1},{8,14},{10,12},{12... | collective-permute-start | bytes 786440 | tf_op jit(solution)/shard_map/ppermute | solution.py:36
  50.5 13.0 %collective-permute-start.2 = (bf16[128,1024]{1,0:T(8,128)(2,1)S(1)}, bf16[128,1024]{1,0:T(8,128)(2,1)S(1)}, u32[]{:S(2)}, u32[]{:S(2)}) collective-permute-start(bf16[128,1024]{1,0:T(8,128)(2,1)S(1)} %fusion.17), channel_id=1, source_target_pairs={{0,4},{2,6},{4,0},{6,2},{1,5},{3,7},{5,1},{7,3},{8,12},{10,14},{12... | collective-permute-start | bytes 786440 | tf_op jit(solution)/shard_map/ppermute | solution.py:36
  50.8 12.7 %collective-permute-start.1 = (bf16[128,1024]{1,0:T(8,128)(2,1)S(1)}, bf16[128,1024]{1,0:T(8,128)(2,1)}, u32[]{:S(2)}, u32[]{:S(2)}) collective-permute-start(bf16[128,1024]{1,0:T(8,128)(2,1)S(1)} %fusion.17), channel_id=1, source_target_pairs={{0,2},{2,0},{4,6},{6,4},{1,3},{3,1},{5,7},{7,5},{8,10},{10,8},{12,... | collective-permute-start | bytes 786440 | tf_op jit(solution)/shard_map/ppermute | solution.py:36
  61.0 11.3 %collective-permute-start.4 = (bf16[1024,512]{1,0:T(8,128)(2,1)}, bf16[1024,512]{1,0:T(8,128)(2,1)S(1)}, u32[]{:S(2)}, u32[]{:S(2)}) collective-permute-start(bf16[1024,512]{1,0:T(8,128)(2,1)} %all-gather.3.cloned.1.call-done), channel_id=1, source_target_pairs={{0,1},{1,0},{2,3},{3,2},{4,5},{5,4},{6,7},{7,6},{8,9},{9,8},{10,11... | collective-permute-start | bytes 3145736 | tf_op jit(solution)/shard_map/ppermute | solution.py:32
  65.5 6.8 %collective-permute-start.6 = (bf16[512,256]{0,1:T(8,128)(2,1)S(1)}, bf16[512,256]{0,1:T(8,128)(2,1)S(1)}, u32[]{:S(2)}, u32[]{:S(2)}) collective-permute-start(bf16[512,256]{0,1:T(8,128)(2,1)S(1)} %slice.300), channel_id=1, source_target_pairs={{0,1},{1,0},{2,3},{3,2},{4,5},{5,4},{6,7},{7,6},{8,9},{9,8},{10,11... | collective-permute-start | bytes 786440 | tf_op jit(solution)/shard_map/ppermute | solution.py:32
  66.4 20.9 %all-to-all-start.4 = ((bf16[16,32,512]{2,1,0:T(8,128)(2,1)}), bf16[16,32,512]{2,1,0:T(8,128)(2,1)}, u32[]{:S(2)}, u32[]{:S(2)}) async-start(bf16[16,32,512]{2,1,0:T(8,128)(2,1)} %dynamic-slice_bitcast_fusion), calls=%async_computation.4 | async-start | bytes 1048576 | tf_op jit(solution)/shard_map/all_to_all | solution.py:117
  70.9 52.3 %all-gather.5.cloned.1.call-start = ((), (), s32[]{:S(2)}) async-start(), calls=%async_computation.11 | async-start | bytes 2949120 | tf_op jit(solution)/shard_map/all_gather | solution.py:110
  71.7 228.1 %reduce-scatter.3.cloned.1.call-start = ((), (), s32[]{:S(2)}) async-start(), calls=%async_computation.12 | async-start | bytes 1310720 | tf_op jit(solution)/shard_map/reduce_scatter | solution.py:230
  84.6 8.8 %collective-permute-start.12 = (bf16[128,1024]{1,0:T(8,128)(2,1)}, bf16[128,1024]{1,0:T(8,128)(2,1)S(1)}, u32[]{:S(2)}, u32[]{:S(2)}) collective-permute-start(bf16[128,1024]{1,0:T(8,128)(2,1)} %get-tuple-element.43), channel_id=1, source_target_pairs={{0,6},{2,4},{4,2},{6,0},{1,7},{3,5},{5,3},{7,1},{8,14},{10,12},{12... | collective-permute-start | bytes 786440 | tf_op jit(solution)/shard_map/ppermute | solution.py:36
  86.7 13.0 %collective-permute-start.11 = (bf16[128,1024]{1,0:T(8,128)(2,1)}, bf16[128,1024]{1,0:T(8,128)(2,1)S(1)}, u32[]{:S(2)}, u32[]{:S(2)}) collective-permute-start(bf16[128,1024]{1,0:T(8,128)(2,1)} %get-tuple-element.44), channel_id=1, source_target_pairs={{0,4},{2,6},{4,0},{6,2},{1,5},{3,7},{5,1},{7,3},{8,12},{10,14},{12... | collective-permute-start | bytes 786440 | tf_op jit(solution)/shard_map/ppermute | solution.py:36
  87.0 12.7 %collective-permute-start.10 = (bf16[128,1024]{1,0:T(8,128)(2,1)}, bf16[128,1024]{1,0:T(8,128)(2,1)S(1)}, u32[]{:S(2)}, u32[]{:S(2)}) collective-permute-start(bf16[128,1024]{1,0:T(8,128)(2,1)} %get-tuple-element.42), channel_id=1, source_target_pairs={{0,2},{2,0},{4,6},{6,4},{1,3},{3,1},{5,7},{7,5},{8,10},{10,8},{12,... | collective-permute-start | bytes 786440 | tf_op jit(solution)/shard_map/ppermute | solution.py:36
  88.7 38.3 %collective-permute-start.22 = (bf16[128,512]{1,0:T(8,128)(2,1)S(1)}, bf16[128,512]{1,0:T(8,128)(2,1)}, u32[]{:S(2)}, u32[]{:S(2)}) collective-permute-start(bf16[128,512]{1,0:T(8,128)(2,1)S(1)} %constant_dynamic-slice_fusion.1), channel_id=1, source_target_pairs={{0,1},{1,0},{2,3},{3,2},{4,5},{5,4},{6,7},{7,6},{8,9},{9,8},{10,11... | collective-permute-start | bytes 393224 | tf_op jit(solution)/shard_map/ppermute | solution.py:32
  123.2 30.3 %collective-permute-start.16 = (bf16[1024,1152]{1,0:T(8,128)(2,1)}, bf16[1024,1152]{1,0:T(8,128)(2,1)S(1)}, u32[]{:S(2)}, u32[]{:S(2)}) collective-permute-start(bf16[1024,1152]{1,0:T(8,128)(2,1)} %all-gather.5.cloned.1.call-done), channel_id=1, source_target_pairs={{0,1},{1,0},{2,3},{3,2},{4,5},{5,4},{6,7},{7,6},{8,9},{9,8},{10,11... | collective-permute-start | bytes 7077896 | tf_op jit(solution)/shard_map/ppermute | solution.py:32
  124.3 8.9 %collective-permute-start.15 = (bf16[128,1024]{1,0:T(8,128)(2,1)S(1)}, bf16[128,1024]{1,0:T(8,128)(2,1)S(1)}, u32[]{:S(2)}, u32[]{:S(2)}) collective-permute-start(bf16[128,1024]{1,0:T(8,128)(2,1)S(1)} %multiply_convert_fusion.7), channel_id=1, source_target_pairs={{0,6},{2,4},{4,2},{6,0},{1,7},{3,5},{5,3},{7,1},{8,14},{10,12},{12... | collective-permute-start | bytes 786440 | tf_op jit(solution)/shard_map/ppermute | solution.py:36
  126.4 12.9 %collective-permute-start.14 = (bf16[128,1024]{1,0:T(8,128)(2,1)S(1)}, bf16[128,1024]{1,0:T(8,128)(2,1)S(1)}, u32[]{:S(2)}, u32[]{:S(2)}) collective-permute-start(bf16[128,1024]{1,0:T(8,128)(2,1)S(1)} %multiply_convert_fusion.7), channel_id=1, source_target_pairs={{0,4},{2,6},{4,0},{6,2},{1,5},{3,7},{5,1},{7,3},{8,12},{10,14},{12... | collective-permute-start | bytes 786440 | tf_op jit(solution)/shard_map/ppermute | solution.py:36
  126.7 13.9 %collective-permute-start.13 = (bf16[128,1024]{1,0:T(8,128)(2,1)S(1)}, bf16[128,1024]{1,0:T(8,128)(2,1)S(1)}, u32[]{:S(2)}, u32[]{:S(2)}) collective-permute-start(bf16[128,1024]{1,0:T(8,128)(2,1)S(1)} %multiply_convert_fusion.7), channel_id=1, source_target_pairs={{0,2},{2,0},{4,6},{6,4},{1,3},{3,1},{5,7},{7,5},{8,10},{10,8},{12,... | collective-permute-start | bytes 786440 | tf_op jit(solution)/shard_map/ppermute | solution.py:36
  128.0 16.4 %collective-permute-start.25 = (bf16[128,1024]{1,0:T(8,128)(2,1)S(1)}, bf16[128,1024]{1,0:T(8,128)(2,1)S(1)}, u32[]{:S(2)}, u32[]{:S(2)}) collective-permute-start(bf16[128,1024]{1,0:T(8,128)(2,1)S(1)} %pad_maximum_fusion.15), channel_id=1, source_target_pairs={{0,6},{2,4},{4,2},{6,0},{1,7},{3,5},{5,3},{7,1},{8,14},{10,12},{12... | collective-permute-start | bytes 786440 | tf_op jit(solution)/shard_map/ppermute | solution.py:36
  133.2 17.1 %collective-permute-start.24 = (bf16[128,1024]{1,0:T(8,128)(2,1)S(1)}, bf16[128,1024]{1,0:T(8,128)(2,1)S(1)}, u32[]{:S(2)}, u32[]{:S(2)}) collective-permute-start(bf16[128,1024]{1,0:T(8,128)(2,1)S(1)} %pad_maximum_fusion.15), channel_id=1, source_target_pairs={{0,4},{2,6},{4,0},{6,2},{1,5},{3,7},{5,1},{7,3},{8,12},{10,14},{12... | collective-permute-start | bytes 786440 | tf_op jit(solution)/shard_map/ppermute | solution.py:36
  139.4 11.0 %collective-permute-start.23 = (bf16[128,1024]{1,0:T(8,128)(2,1)S(1)}, bf16[128,1024]{1,0:T(8,128)(2,1)S(1)}, u32[]{:S(2)}, u32[]{:S(2)}) collective-permute-start(bf16[128,1024]{1,0:T(8,128)(2,1)S(1)} %pad_maximum_fusion.15), channel_id=1, source_target_pairs={{0,2},{2,0},{4,6},{6,4},{1,3},{3,1},{5,7},{7,5},{8,10},{10,8},{12,... | collective-permute-start | bytes 786440 | tf_op jit(solution)/shard_map/ppermute | solution.py:36
  157.7 8.3 %collective-permute-start.28 = (bf16[128,1024]{1,0:T(8,128)(2,1)S(1)}, bf16[128,1024]{1,0:T(8,128)(2,1)S(1)}, u32[]{:S(2)}, u32[]{:S(2)}) collective-permute-start(bf16[128,1024]{1,0:T(8,128)(2,1)S(1)} %get-tuple-element.35), channel_id=1, source_target_pairs={{0,6},{2,4},{4,2},{6,0},{1,7},{3,5},{5,3},{7,1},{8,14},{10,12},{12... | collective-permute-start | bytes 786440 | tf_op jit(solution)/shard_map/ppermute | solution.py:36
  158.7 14.7 %collective-permute-start.27 = (bf16[128,1024]{1,0:T(8,128)(2,1)S(1)}, bf16[128,1024]{1,0:T(8,128)(2,1)S(1)}, u32[]{:S(2)}, u32[]{:S(2)}) collective-permute-start(bf16[128,1024]{1,0:T(8,128)(2,1)S(1)} %get-tuple-element.36), channel_id=1, source_target_pairs={{0,4},{2,6},{4,0},{6,2},{1,5},{3,7},{5,1},{7,3},{8,12},{10,14},{12... | collective-permute-start | bytes 786440 | tf_op jit(solution)/shard_map/ppermute | solution.py:36
  160.1 13.2 %collective-permute-start.26 = (bf16[128,1024]{1,0:T(8,128)(2,1)S(1)}, bf16[128,1024]{1,0:T(8,128)(2,1)S(1)}, u32[]{:S(2)}, u32[]{:S(2)}) collective-permute-start(bf16[128,1024]{1,0:T(8,128)(2,1)S(1)} %get-tuple-element.34), channel_id=1, source_target_pairs={{0,2},{2,0},{4,6},{6,4},{1,3},{3,1},{5,7},{7,5},{8,10},{10,8},{12,... | collective-permute-start | bytes 786440 | tf_op jit(solution)/shard_map/ppermute | solution.py:36
  161.2 16.1 %collective-permute-start.19 = (bf16[128,1024]{1,0:T(8,128)(2,1)S(1)}, bf16[128,1024]{1,0:T(8,128)(2,1)S(1)}, u32[]{:S(2)}, u32[]{:S(2)}) collective-permute-start(bf16[128,1024]{1,0:T(8,128)(2,1)S(1)} %get-tuple-element.40), channel_id=1, source_target_pairs={{0,6},{2,4},{4,2},{6,0},{1,7},{3,5},{5,3},{7,1},{8,14},{10,12},{12... | collective-permute-start | bytes 786440 | tf_op jit(solution)/shard_map/ppermute | solution.py:36
  162.2 21.5 %collective-permute-start.18 = (bf16[128,1024]{1,0:T(8,128)(2,1)S(1)}, bf16[128,1024]{1,0:T(8,128)(2,1)S(1)}, u32[]{:S(2)}, u32[]{:S(2)}) collective-permute-start(bf16[128,1024]{1,0:T(8,128)(2,1)S(1)} %get-tuple-element.41), channel_id=1, source_target_pairs={{0,4},{2,6},{4,0},{6,2},{1,5},{3,7},{5,1},{7,3},{8,12},{10,14},{12... | collective-permute-start | bytes 786440 | tf_op jit(solution)/shard_map/ppermute | solution.py:36
  166.0 17.7 %collective-permute-start.17 = (bf16[128,1024]{1,0:T(8,128)(2,1)S(1)}, bf16[128,1024]{1,0:T(8,128)(2,1)S(1)}, u32[]{:S(2)}, u32[]{:S(2)}) collective-permute-start(bf16[128,1024]{1,0:T(8,128)(2,1)S(1)} %get-tuple-element.39), channel_id=1, source_target_pairs={{0,2},{2,0},{4,6},{6,4},{1,3},{3,1},{5,7},{7,5},{8,10},{10,8},{12,... | collective-permute-start | bytes 786440 | tf_op jit(solution)/shard_map/ppermute | solution.py:36
  185.1 8.2 %collective-permute-start.31 = (bf16[128,1024]{1,0:T(8,128)(2,1)S(1)}, bf16[128,1024]{1,0:T(8,128)(2,1)S(1)}, u32[]{:S(2)}, u32[]{:S(2)}) collective-permute-start(bf16[128,1024]{1,0:T(8,128)(2,1)S(1)} %get-tuple-element.11), channel_id=1, source_target_pairs={{0,6},{2,4},{4,2},{6,0},{1,7},{3,5},{5,3},{7,1},{8,14},{10,12},{12... | collective-permute-start | bytes 786440 | tf_op jit(solution)/shard_map/ppermute | solution.py:36
  186.0 13.8 %collective-permute-start.30 = (bf16[128,1024]{1,0:T(8,128)(2,1)S(1)}, bf16[128,1024]{1,0:T(8,128)(2,1)S(1)}, u32[]{:S(2)}, u32[]{:S(2)}) collective-permute-start(bf16[128,1024]{1,0:T(8,128)(2,1)S(1)} %get-tuple-element.11), channel_id=1, source_target_pairs={{0,4},{2,6},{4,0},{6,2},{1,5},{3,7},{5,1},{7,3},{8,12},{10,14},{12... | collective-permute-start | bytes 786440 | tf_op jit(solution)/shard_map/ppermute | solution.py:36
  187.5 12.4 %collective-permute-start.29 = (bf16[128,1024]{1,0:T(8,128)(2,1)S(1)}, bf16[128,1024]{1,0:T(8,128)(2,1)S(1)}, u32[]{:S(2)}, u32[]{:S(2)}) collective-permute-start(bf16[128,1024]{1,0:T(8,128)(2,1)S(1)} %get-tuple-element.11), channel_id=1, source_target_pairs={{0,2},{2,0},{4,6},{6,4},{1,3},{3,1},{5,7},{7,5},{8,10},{10,8},{12,... | collective-permute-start | bytes 786440 | tf_op jit(solution)/shard_map/ppermute | solution.py:36
  213.9 5.8 %collective-permute-start.38 = (bf16[1024,512]{0,1:T(8,128)(2,1)S(1)}, bf16[1024,512]{0,1:T(8,128)(2,1)S(1)}, u32[]{:S(2)}, u32[]{:S(2)}) collective-permute-start(bf16[1024,512]{0,1:T(8,128)(2,1)S(1)} %pad_maximum_fusion.5), channel_id=1, source_target_pairs={{0,1},{1,0},{2,3},{3,2},{4,5},{5,4},{6,7},{7,6},{8,9},{9,8},{10,11... | collective-permute-start | bytes 3145736 | tf_op jit(solution)/shard_map/ppermute | solution.py:32
  217.3 8.7 %collective-permute-start.39 = (bf16[1024,1152]{0,1:T(8,128)(2,1)}, bf16[1024,1152]{0,1:T(8,128)(2,1)}, u32[]{:S(2)}, u32[]{:S(2)}) collective-permute-start(bf16[1024,1152]{0,1:T(8,128)(2,1)} %pad_maximum_fusion), channel_id=1, source_target_pairs={{0,1},{1,0},{2,3},{3,2},{4,5},{5,4},{6,7},{7,6},{8,9},{9,8},{10,11... | collective-permute-start | bytes 7077896 | tf_op jit(solution)/shard_map/ppermute | solution.py:32
  221.1 91.9 %reduce-scatter.5.cloned.1.call-start = ((), (), s32[]{:S(2)}) async-start(), calls=%async_computation.13 | async-start | bytes 2949120 | tf_op jit(solution)/shard_map/reduce_scatter | solution.py:230
  225.2 13.0 %collective-permute-start.20 = (bf16[128,512]{1,0:T(8,128)(2,1)}, bf16[128,512]{1,0:T(8,128)(2,1)}, u32[]{:S(2)}, u32[]{:S(2)}) collective-permute-start(bf16[128,512]{1,0:T(8,128)(2,1)} %constant_dynamic-slice_fusion.2), channel_id=1, source_target_pairs={{0,1},{1,0},{2,3},{3,2},{4,5},{5,4},{6,7},{7,6},{8,9},{9,8},{10,11... | collective-permute-start | bytes 393224 | tf_op jit(solution)/shard_map/ppermute | solution.py:32
  235.5 9.8 %collective-permute-start.35 = (bf16[128,1024]{1,0:T(8,128)(2,1)}, bf16[128,1024]{1,0:T(8,128)(2,1)S(1)}, u32[]{:S(2)}, u32[]{:S(2)}) collective-permute-start(bf16[128,1024]{1,0:T(8,128)(2,1)} %get-tuple-element.30), channel_id=1, source_target_pairs={{0,6},{2,4},{4,2},{6,0},{1,7},{3,5},{5,3},{7,1},{8,14},{10,12},{12... | collective-permute-start | bytes 786440 | tf_op jit(solution)/shard_map/ppermute | solution.py:36
  236.5 15.5 %collective-permute-start.34 = (bf16[128,1024]{1,0:T(8,128)(2,1)}, bf16[128,1024]{1,0:T(8,128)(2,1)S(1)}, u32[]{:S(2)}, u32[]{:S(2)}) collective-permute-start(bf16[128,1024]{1,0:T(8,128)(2,1)} %get-tuple-element.31), channel_id=1, source_target_pairs={{0,4},{2,6},{4,0},{6,2},{1,5},{3,7},{5,1},{7,3},{8,12},{10,14},{12... | collective-permute-start | bytes 786440 | tf_op jit(solution)/shard_map/ppermute | solution.py:36
  237.9 14.1 %collective-permute-start.33 = (bf16[128,1024]{1,0:T(8,128)(2,1)}, bf16[128,1024]{1,0:T(8,128)(2,1)}, u32[]{:S(2)}, u32[]{:S(2)}) collective-permute-start(bf16[128,1024]{1,0:T(8,128)(2,1)} %get-tuple-element.29), channel_id=1, source_target_pairs={{0,2},{2,0},{4,6},{6,4},{1,3},{3,1},{5,7},{7,5},{8,10},{10,8},{12,... | collective-permute-start | bytes 786440 | tf_op jit(solution)/shard_map/ppermute | solution.py:36
  240.3 20.7 %all-to-all-start.3 = ((bf16[16,32,512]{2,1,0:T(8,128)(2,1)}), bf16[16,32,512]{2,1,0:T(8,128)(2,1)S(1)}, u32[]{:S(2)}, u32[]{:S(2)}) async-start(bf16[16,32,512]{2,1,0:T(8,128)(2,1)} %bitcast.168), calls=%async_computation.3 | async-start | bytes 1048576 | tf_op jit(solution)/shard_map/all_to_all | solution.py:150
  261.0 32.3 %all-to-all-start.5 = ((bf16[16,32,512]{2,1,0:T(8,128)(2,1)}), bf16[16,32,512]{2,1,0:T(8,128)(2,1)S(1)}, u32[]{:S(2)}, u32[]{:S(2)}) async-start(bf16[16,32,512]{2,1,0:T(8,128)(2,1)} %bitcast.18), calls=%async_computation.5 | async-start | bytes 1048576 | tf_op jit(solution)/shard_map/all_to_all | solution.py:150
  268.5 37.3 %collective-permute-start.21 = (bf16[16,32,512]{2,1,0:T(8,128)(2,1)S(1)}, bf16[16,32,512]{2,1,0:T(8,128)(2,1)S(1)}, u32[]{:S(2)}, u32[]{:S(2)}) collective-permute-start(bf16[16,32,512]{2,1,0:T(8,128)(2,1)S(1)} %all-to-all-done.3), channel_id=1, source_target_pairs={{0,1},{1,0},{2,3},{3,2},{4,5},{5,4},{6,7},{7,6},{8,9},{9,8},{10,11... | collective-permute-start | bytes 1572872 | tf_op jit(solution)/shard_map/ppermute | solution.py:32
  293.3 12.5 %collective-permute-start.37 = (bf16[16,32,512]{2,1,0:T(8,128)(2,1)S(1)}, bf16[16,32,512]{2,1,0:T(8,128)(2,1)}, u32[]{:S(2)}, u32[]{:S(2)}) collective-permute-start(bf16[16,32,512]{2,1,0:T(8,128)(2,1)S(1)} %all-to-all-done.5), channel_id=1, source_target_pairs={{0,1},{1,0},{2,3},{3,2},{4,5},{5,4},{6,7},{7,6},{8,9},{9,8},{10,11... | collective-permute-start | bytes 1572872 | tf_op jit(solution)/shard_map/ppermute | solution.py:32
  301.6 10.4 %all-to-all-start.6 = ((bf16[4,64,512]{2,1,0:T(8,128)(2,1)}), bf16[4,64,512]{2,1,0:T(8,128)(2,1)S(1)}, u32[]{:S(2)}, u32[]{:S(2)}) async-start(bf16[4,64,512]{2,1,0:T(8,128)(2,1)} %bitcast.20), calls=%async_computation.7 | async-start | bytes 524288 | tf_op jit(solution)/shard_map/all_to_all | solution.py:232
  315.1 11.7 %all-to-all-start.7 = ((bf16[4,64,1152]{2,1,0:T(8,128)(2,1)}), bf16[4,64,1152]{2,1,0:T(8,128)(2,1)S(1)}, u32[]{:S(2)}, u32[]{:S(2)}) async-start(bf16[4,64,1152]{2,1,0:T(8,128)(2,1)} %bitcast.26), calls=%async_computation.9 | async-start | bytes 1179648 | tf_op jit(solution)/shard_map/all_to_all | solution.py:232
  (90 other events, 741.7 us)
Sparse Core Ops, SparseCore 0:
  29.9 31.0 all-gather.2
  73.9 49.2 all-gather.4
  221.2 24.1 reduce-scatter.2
  247.6 61.8 reduce-scatter.4

commit v2 on v1

v2 whole, which is shorter than its diff:
```python
import functools

import jax
import jax.numpy as jnp
import numpy as np
from jax import lax
from jax.experimental import pallas as pl
from jax.experimental.pallas import tpu as pltpu
from jax.sharding import Mesh, PartitionSpec as P

DH = 64
eps = 1e-05
masked_score = -1e30
bf16 = jnp.bfloat16
f32 = jnp.float32

DP = ("z", "yh", "yl", "xh", "xl")
FAR = ("z", "yh", "xh")
NEAR = ("yl", "xl")
CORE = "c"


def mm(left, right):
    return lax.dot_general(left, right, (((1,), (0,)), ((), ())), preferred_element_type=f32)


def mm_t(left, right):
    return lax.dot_general(left, right, (((1,), (1,)), ((), ())), preferred_element_type=f32)


def outer_sum(left, right):
    return lax.dot_general(left, right, (((0,), (0,)), ((), ())), preferred_element_type=f32)


def swap(value):
    return lax.ppermute(value, CORE, [(0, 1), (1, 0)])


def near(value, k):
    return lax.ppermute(value, NEAR, [(i, i ^ k) for i in range(4)])


def gather_near(value):
    return [value] + [near(value, k) for k in (1, 2, 3)]


def scatter_near(low):
    return [near(low[k - 1], k) for k in (1, 2, 3)]


def after(value, *tokens):
    return lax.optimization_barrier((value, tokens))[0]


def inverse_root(values):
    return lax.rsqrt(jnp.mean(values * values, axis=-1, keepdims=True) + eps)


def call(kernel, outs, args, scratch=(), limit=4, us=1.0):
    in_specs = [pl.BlockSpec(memory_space=pltpu.SMEM if a.ndim == 1 else pltpu.VMEM) for a in args]
    out_specs = [pl.BlockSpec(memory_space=pltpu.VMEM) for _ in outs]
    return pl.pallas_call(
        kernel,
        out_shape=[jax.ShapeDtypeStruct(shape, kind) for shape, kind in outs],
        in_specs=in_specs,
        out_specs=out_specs,
        scratch_shapes=list(scratch),
        compiler_params=pltpu.CompilerParams(vmem_limit_bytes=limit << 20),
        cost_estimate=pl.CostEstimate(flops=int(us * 1e9), bytes_accessed=int(us * 1e6), transcendentals=0),
    )(*args)


def lane_half(value, half):
    lanes = lax.broadcasted_iota(jnp.int32, value.shape, 1)
    keep = (lanes < DH) if half == 0 else (lanes >= DH)
    return jnp.where(keep, value, jnp.zeros_like(value))


def flipped(value):
    n = value.shape[1]
    eye = (
        lax.broadcasted_iota(jnp.int32, (n, n), 0) == lax.broadcasted_iota(jnp.int32, (n, n), 1)
    ).astype(bf16)
    return mm_t(eye, value).astype(bf16)


def pack_kernel(part, me, gain, *refs):
    n = len(refs) - 5
    weights, outs, blocks = refs[:n], refs[n : n + 4], refs[n + 4]
    size = blocks.shape[2] // n
    if size != part:
        blocks[...] = jnp.zeros(blocks.shape, blocks.dtype)
    for m, ref in enumerate(weights):
        w = ref[...].astype(f32)
        if m < n - 1:
            w = w * gain[...]
        w = w.astype(bf16)
        for i in range(4):
            blocks[i, :, m * size : m * size + part] = w[:, i * part : (i + 1) * part]
    for k, out in enumerate(outs):
        out[...] = blocks[me[0] ^ k]


def place_kernel(me, b0, b1, b2, b3, out):
    for k, ref in enumerate((b0, b1, b2, b3)):
        out[me[0] ^ k] = ref[...]


def place_far_kernel(me, far, b0, b1, b2, b3, out):
    for k, ref in enumerate((b0, b1, b2, b3)):
        plane = lax.rem(far[0] + (4 - k), 4)
        for i in range(4):
            out[plane * 4 + (me[0] ^ i)] = ref[i]


def collect_kernel(core, slot_row, slots, own, give):
    toks = own.shape[0]
    token = lax.broadcasted_iota(jnp.int32, (toks, slots.shape[0]), 0)
    for ref, half in ((own, core[0]), (give, 1 - core[0])):
        place = ((token + half * toks) == slot_row[...]).astype(bf16)
        ref[...] = mm(place, slots[...]).astype(bf16)


def normed(x):
    return x * inverse_root(x)


def enter_kernel(core, own, other, x_ref, y_ref, norm_ref):
    half = own.shape[1] // 2
    first = core[0] == 0
    for ref, at in ((x_ref, slice(0, half)), (y_ref, slice(half, 2 * half))):
        ref[:, :half] = jnp.where(first, own[:, at], other[:, at])
        ref[:, half:] = jnp.where(first, other[:, at], own[:, at])
    norm_ref[...] = normed(x_ref[...].astype(f32)).astype(bf16)


def project_kernel(n0, n1, n2, n3, w, q_ref, kv_ref, all_n):
    toks = n0.shape[0]
    hp = w.shape[2] // 4
    for r, ref in enumerate((n0, n1, n2, n3)):
        all_n[r * toks : (r + 1) * toks, :] = ref[...]
    for j in range(2):
        q_ref[:, j * hp : (j + 1) * hp] = mm(all_n[...], w[j, :, :hp]).astype(bf16)
        kv = mm(all_n[...], w[j, :, hp : 3 * hp]).astype(bf16)
        kv_ref[:, 2 * j * hp : 2 * (j + 1) * hp] = kv


def attend_kernel(scale, core, q_ref, kv, kvf, doc_q, doc_kn, doc_kf, w, p_ref, att_ref, own_ref, b1, b2, b3):
    hp = q_ref.shape[1] // 2
    rows = doc_q.shape[0]
    toks = q_ref.shape[0] // rows
    key_pos = lax.broadcasted_iota(jnp.int32, (toks, toks), 0)
    query_pos = lax.broadcasted_iota(jnp.int32, (toks, toks), 1)
    causal = key_pos <= query_pos
    later = core[0] == 1
    for r in range(rows):
        at = slice(r * toks, (r + 1) * toks)
        dq = doc_q[r : r + 1, :]
        near_ok = causal & (doc_kn[:, r : r + 1] == dq)
        far_ok = (doc_kf[:, r : r + 1] == dq) & later
        for j in range(2):
            base = 2 * j * hp
            q2 = q_ref[at, j * hp : (j + 1) * hp]
            kn, kf = kv[at, base : base + hp], kvf[at, base : base + hp]
            v_t = jnp.concatenate(
                [flipped(kv[at, base + hp : base + 2 * hp]), flipped(kvf[at, base + hp : base + 2 * hp])], axis=1
            )
            pieces = []
            for h in range(2):
                qh = lane_half(q2, h)
                sn = jnp.where(near_ok, mm_t(kn, qh) * scale, masked_score)
                sf = jnp.where(far_ok, mm_t(kf, qh) * scale, masked_score)
                top = jnp.maximum(jnp.max(sn, axis=0, keepdims=True), jnp.max(sf, axis=0, keepdims=True))
                en, ef = jnp.exp(sn - top), jnp.exp(sf - top)
                total = jnp.sum(en, axis=0, keepdims=True) + jnp.sum(ef, axis=0, keepdims=True)
                inv = 1.0 / total
                p = (jnp.concatenate([en, ef], axis=0) * inv).astype(bf16)
                p_ref[(r * 2 + j) * 2 + h] = p
                pieces.append(mm(v_t[h * DH : (h + 1) * DH, :], p))
            att_ref[at, j * hp : (j + 1) * hp] = flipped(jnp.concatenate(pieces, axis=0).astype(bf16)).astype(bf16)
        out = mm_t(att_ref[at, :hp], w[0, :, 3 * hp :]) + mm_t(att_ref[at, hp:], w[1, :, 3 * hp :])
        if r == 0:
            own_ref[...] = out
        else:
            (b1, b2, b3)[r - 1][...] = out.astype(bf16)


def attend_back_kernel(scale, g0, g1, g2, g3, w, q_ref, kv, kvf, p_ref, dq_ref, near_ref, far_ref, all_g, ga_ref):
    hp = q_ref.shape[1] // 2
    toks = g0.shape[0]
    for r, g_ref in enumerate((g0, g1, g2, g3)):
        at = slice(r * toks, (r + 1) * toks)
        all_g[at, :] = g_ref[...]
        for j in range(2):
            ga_ref[...] = mm(g_ref[...], w[j, :, 3 * hp :]).astype(bf16)
            g = ga_ref[...]
            base = 2 * j * hp
            q2 = q_ref[at, j * hp : (j + 1) * hp]
            v = jnp.concatenate([kv[at, base + hp : base + 2 * hp], kvf[at, base + hp : base + 2 * hp]], axis=0)
            k_t = jnp.concatenate([flipped(kv[at, base : base + hp]), flipped(kvf[at, base : base + hp])], axis=1)
            dqs, ps, dss, gs, qs = [], [], [], [], []
            for h in range(2):
                gh = lane_half(g, h)
                dp = mm_t(v, gh)
                p_low = p_ref[(r * 2 + j) * 2 + h]
                p = p_low.astype(f32)
                ds = p * (dp - jnp.sum(dp * p, axis=0, keepdims=True))
                ds = ds.astype(bf16)
                dqs.append(mm(k_t[h * DH : (h + 1) * DH, :], ds))
                ps.append(p_low)
                dss.append(ds)
                gs.append(gh)
                qs.append(lane_half(q2, h))
            dq = (jnp.concatenate(dqs, axis=0) * scale).astype(bf16)
            dq_ref[at, j * hp : (j + 1) * hp] = flipped(dq)
            dv = mm(jnp.concatenate(ps, axis=1), jnp.concatenate(gs, axis=0))
            dk = mm(jnp.concatenate(dss, axis=1), jnp.concatenate(qs, axis=0)) * scale
            near_ref[at, base : base + hp] = dk[:toks]
            near_ref[at, base + hp : base + 2 * hp] = dv[:toks]
            far_ref[at, base : base + hp] = dk[toks:].astype(bf16)
            far_ref[at, base + hp : base + 2 * hp] = dv[toks:].astype(bf16)


def project_back_kernel(dq, near_g, back, w, gown, goth, own_ref, b1, b2, b3, acc):
    hp = dq.shape[1] // 2
    toks = own_ref.shape[0]
    for j, g in enumerate((gown, goth)):
        g[:, :hp] = dq[:, j * hp : (j + 1) * hp]
        both = slice(2 * j * hp, 2 * (j + 1) * hp)
        g[:, hp:] = (near_g[:, both] + back[:, both].astype(f32)).astype(bf16)
    acc[...] = mm_t(gown[...], w[0, :, : 3 * hp]) + mm_t(goth[...], w[1, :, : 3 * hp])
    own_ref[...] = acc[:toks]
    for r, ref in enumerate((b1, b2, b3)):
        ref[...] = acc[(r + 1) * toks : (r + 2) * toks].astype(bf16)


def total_of(refs):
    total = refs[0][...]
    for ref in refs[1:]:
        total = total + ref[...].astype(f32)
    return total


def middle_kernel(x, b0, b1, b2, b3, hidden, norm_ref):
    value = x[...].astype(f32) + total_of((b0, b1, b2, b3))
    hidden[...] = value
    norm_ref[...] = normed(value).astype(bf16)


def ffn_kernel(n0, n1, n2, n3, y0, y1, y2, y3, w, mid, own_ref, b1, b2, b3, all_n, all_y, acc):
    toks = n0.shape[0]
    ff = w.shape[2] // 3
    for r in range(4):
        all_n[r * toks : (r + 1) * toks, :] = (n0, n1, n2, n3)[r][...]
        all_y[r * toks : (r + 1) * toks, :] = (y0, y1, y2, y3)[r][...]
    for j in range(2):
        gate = mm(all_n[...], w[j, :, :ff])
        up = mm(all_n[...], w[j, :, ff : 2 * ff])
        sig = jax.nn.sigmoid(gate)
        silu = gate * sig
        mid[j, :, 2 * ff :] = (silu * up).astype(bf16)
        grad_product = mm(all_y[...], w[j, :, 2 * ff :])
        mid[j, :, :ff] = (grad_product * up * sig * (1.0 + gate * (1.0 - sig))).astype(bf16)
        mid[j, :, ff : 2 * ff] = (grad_product * silu).astype(bf16)
        part = mm_t(mid[j, :, : 2 * ff], w[j, :, : 2 * ff])
        if j == 0:
            acc[...] = part
        else:
            acc[...] += part
    own_ref[...] = acc[:toks]
    for r, ref in enumerate((b1, b2, b3)):
        ref[...] = acc[(r + 1) * toks : (r + 2) * toks].astype(bf16)


def ffn_out_kernel(mid, w, own_ref, b1, b2, b3, acc):
    toks = own_ref.shape[0]
    ff = w.shape[2] // 3
    acc[...] = mm_t(mid[0, :, 2 * ff :], w[0, :, 2 * ff :]) + mm_t(mid[1, :, 2 * ff :], w[1, :, 2 * ff :])
    own_ref[...] = acc[:toks]
    for r, ref in enumerate((b1, b2, b3)):
        ref[...] = acc[(r + 1) * toks : (r + 2) * toks].astype(bf16)


def ffn_grads_kernel(all_n, all_y, mid, out):
    rows = out.shape[2]
    ff = out.shape[3] // 3
    for i in range(4):
        at = slice(i * rows, (i + 1) * rows)
        for j in range(2):
            out[i, j, :, : 2 * ff] = outer_sum(all_n[:, at], mid[j, :, : 2 * ff]).astype(bf16)
            out[i, j, :, 2 * ff :] = outer_sum(all_y[:, at], mid[j, :, 2 * ff :]).astype(bf16)


def split_halves(core, value, own, give):
    half = own.shape[1]
    first = core[0] == 0
    own[...] = jnp.where(first, value[:, :half], value[:, half:])
    give[...] = jnp.where(first, value[:, half:], value[:, :half])


def final_kernel(core, hidden, b0, b1, b2, b3, own, give):
    split_halves(core, (hidden[...] + total_of((b0, b1, b2, b3))).astype(bf16), own, give)


def norm_back(x, grad):
    root = inverse_root(x)
    norm = x * root
    return root * (grad - norm * jnp.mean(grad * norm, axis=-1, keepdims=True))


def middle_back_kernel(hidden, grad_low, b0, b1, b2, b3, out, low):
    grad = grad_low[...].astype(f32) + norm_back(hidden[...], total_of((b0, b1, b2, b3)))
    out[...] = grad
    low[...] = grad.astype(bf16)


def leave_kernel(core, x, grad_hidden, b0, b1, b2, b3, out_own, out_give, own, give):
    half = out_own.shape[1]
    own[:, :half] = out_own[...]
    give[:, :half] = out_give[...]
    grad = grad_hidden[...] + norm_back(x[...].astype(f32), total_of((b0, b1, b2, b3)))
    split_halves(core, grad.astype(bf16), own.at[:, half:], give.at[:, half:])


def spread_kernel(core, slot_col, own, other, out):
    toks = own.shape[0]
    first = core[0] == 0
    token = lax.broadcasted_iota(jnp.int32, (slot_col.shape[0], toks), 1)
    low = (token == slot_col[...]).astype(bf16)
    high = ((token + toks) == slot_col[...]).astype(bf16)
    own, other = own[...], other[...]
    out[...] = (mm(low, jnp.where(first, own, other)) + mm(high, jnp.where(first, other, own))).astype(bf16)


def join_kernel(core, own, other, out, grad):
    half = own.shape[1] // 2
    first = core[0] == 0
    for ref, at in ((out, slice(0, half)), (grad, slice(half, 2 * half))):
        ref[:, :half] = jnp.where(first, own[:, at], other[:, at])
        ref[:, half:] = jnp.where(first, other[:, at], own[:, at])


def attn_grads_kernel(core, all_n, all_g, g0, g1, att, own, oth):
    hp = att.shape[1] // 2
    first = core[0] == 0
    for j, out in enumerate((own, oth)):
        mine = first if j == 0 else core[0] == 1
        out[:, : 3 * hp] = outer_sum(all_n[...], jnp.where(mine, g0[...], g1[...])).astype(bf16)
        out[:, 3 * hp :] = outer_sum(all_g[...], jnp.where(mine, att[:, :hp], att[:, hp:])).astype(bf16)


def core_sum_kernel(far, own, other, t0, t1, t2, t3):
    rows = t0.shape[0]
    for k, ref in enumerate((t0, t1, t2, t3)):
        at = pl.ds(pl.multiple_of(lax.rem(far[0] + k, 4) * rows, rows), rows)
        ref[...] = (own[at, :].astype(f32) + other[at, :].astype(f32)).astype(bf16)


def far_sum_kernel(me, t0, t1, t2, t3, s0, s1, s2, s3):
    rows = s0.shape[0]
    for k, ref in enumerate((s0, s1, s2, s3)):
        at = pl.ds(pl.multiple_of((me[0] ^ k) * rows, rows), rows)
        total = t0[at, :].astype(f32)
        for other in (t1, t2, t3):
            total = total + other[at, :].astype(f32)
        ref[...] = total.astype(bf16)


def pick_kernel(me, part, s0, s1, s2, s3):
    rows = s0.shape[0]
    for k, ref in enumerate((s0, s1, s2, s3)):
        ref[...] = part[pl.ds(pl.multiple_of((me[0] ^ k) * rows, rows), rows), :]


def unpack_kernel(part, me, gain, s0, s1, s2, s3, *refs):
    n = (len(refs) - 1) // 2
    weights, outs, gain_sum, blocks = refs[: n - 1], refs[n - 1 : 2 * n - 1], refs[2 * n - 1], refs[2 * n]
    for k, ref in enumerate((s0, s1, s2, s3)):
        blocks[me[0] ^ k] = ref[...]
    size = blocks.shape[2] // n
    total = jnp.zeros(gain_sum.shape, f32)
    for m, out in enumerate(outs):
        for i in range(4):
            raw = blocks[i, :, m * size : m * size + part].astype(f32)
            at = slice(i * part, (i + 1) * part)
            if m < n - 1:
                total = total + jnp.sum(raw * weights[m][:, at].astype(f32), axis=1, keepdims=True)
                raw = raw * gain[...]
            out[:, at] = raw
    gain_sum[...] = total


def natural_rows(weight, far_sizes, rows):
    nz, nyh, nxh = far_sizes
    if nyh * nxh == 1:
        return weight
    cols = weight.shape[-1]
    split = weight.reshape(nz, nyh, nxh, 2, 2, rows, cols)
    return split.transpose(0, 1, 3, 2, 4, 5, 6).reshape(-1, cols)


def far_rows(weight, far_sizes, rows):
    nz, nyh, nxh = far_sizes
    if nyh * nxh == 1:
        return weight
    cols = weight.shape[-1]
    split = weight.reshape(nz, nyh, 2, nxh, 2, rows, cols)
    return split.transpose(0, 1, 3, 2, 4, 5, 6).reshape(-1, cols)


def spread_pack(pieces):
    rows = pieces[0].shape[0]
    blocks = [p.reshape(rows, 4, -1) for p in pieces]
    return jnp.concatenate(blocks, axis=-1).transpose(1, 0, 2)


def near_exchange(blocks, my_near):
    got = jnp.zeros(blocks.shape, blocks.dtype)
    for k in range(4):
        give = lax.dynamic_index_in_dim(blocks, my_near ^ k, 0, keepdims=True)
        got = lax.dynamic_update_slice_in_dim(got, near(give, k) if k else give, my_near ^ k, 0)
    return got


def body(patches, counts, doc_ids, w_query, w_key, w_value, w_output, w_gate, w_up, w_down, gain_attn, gain_ffn, cotangent):
    core = lax.axis_index(CORE)
    my_row = lax.axis_index(DP)
    my_near = lax.axis_index(NEAR)
    my_far = lax.axis_index(FAR)
    core_ref, near_ref, far_ref = core.reshape(1), my_near.reshape(1), my_far.reshape(1)
    peers, slot_cap, width = patches.shape[1:]
    half_width = width // 2
    slot_count = peers * slot_cap
    tok_count = doc_ids.shape[1]
    toks = tok_count // 2
    group = 4 * toks
    rows = w_query.shape[0]
    far_sizes = tuple(lax.axis_size(a) for a in FAR)
    far = far_sizes[0] * far_sizes[1] * far_sizes[2]
    direct = far == 4 and rows % 16 == 0
    score_scale = DH ** (-0.5)
    hp = w_query.shape[1] // 4
    ff_part = w_gate.shape[1] // 4
    ff_pad = -(-ff_part // 128) * 128
    gain_a = gain_attn.astype(f32)[:, None]
    gain_f = gain_ffn.astype(f32)[:, None]

    def far_shift(value, k):
        return lax.ppermute(value, FAR, [(i, (i + k) % far) for i in range(far)])

    def half_features(blocks):
        return lax.dynamic_slice_in_dim(blocks[0], core * half_width, half_width, 2)

    both = jnp.concatenate([half_features(patches), half_features(cotangent)], axis=-1)
    received = lax.all_to_all(both, DP, 0, 0, tiled=True).reshape(slot_count, width)

    def packed(weights, gain, part, size, token):
        weights = after(weights, token)
        if direct:
            return call(
                functools.partial(pack_kernel, part),
                [((rows, size * len(weights)), bf16)] * 4,
                [near_ref, gain, *weights],
                [pltpu.VMEM((4, rows, size * len(weights)), bf16)],
            )
        scaled = [(w.astype(f32) * gain).astype(bf16) for w in weights[:-1]] + [weights[-1]]
        return [jnp.pad(w.reshape(rows, 4, part), ((0, 0), (0, 0), (0, size - part))).reshape(rows, -1) for w in scaled]

    attn_weights = [w_query, w_key, w_value, w_output.T]
    ffn_weights = [w_gate, w_up, w_down.T]
    def gathered(pack, *tokens):
        if direct:
            got = scatter_near(pack[1:])
            (flat,) = call(place_kernel, [((4,) + pack[0].shape, bf16)], [near_ref, pack[0], *got])
        else:
            flat = near_exchange(spread_pack(pack), my_near)
        cols = flat.shape[-1]
        flat = flat.reshape(4 * rows, cols)
        return flat, lambda operand: lax.all_gather(operand, (CORE,) + FAR, axis=0, tiled=True).reshape(2, width, cols)

    attn_flat, gather_attn = gathered(packed(attn_weights, gain_a, hp, hp, both))
    attn_w = gather_attn(attn_flat)
    ffn_flat, gather_ffn = gathered(packed(ffn_weights, gain_f, ff_part, ff_pad, attn_flat))
    doc_rows = jnp.concatenate(gather_near(after(doc_ids, attn_flat)), axis=0)
    my_counts = lax.dynamic_index_in_dim(counts, my_row, 0, keepdims=False)
    offsets = jnp.cumsum(my_counts) - my_counts
    slots = jnp.arange(slot_cap, dtype=jnp.int32)
    slot_token = jnp.where(slots[None, :] < my_counts[:, None], offsets[:, None] + slots[None, :], -1).reshape(-1)
    slot_row, slot_col = slot_token[None, :], slot_token[:, None]
    received, slot_row, slot_col, doc_rows, ffn_flat = lax.optimization_barrier(
        (received, slot_row, slot_col, doc_rows, ffn_flat)
    )
    ffn_w = gather_ffn(ffn_flat)
    if not direct:
        attn_w, ffn_w = (jnp.stack([natural_rows(w[i], far_sizes, rows) for i in range(2)]) for w in (attn_w, ffn_w))
    doc_own = lax.dynamic_slice_in_dim(doc_rows, core * toks, toks, 1)
    doc_oth = lax.dynamic_slice_in_dim(doc_rows, (1 - core) * toks, toks, 1)

    docs = (doc_own, doc_own.T, doc_oth.T)
    slab = ((toks, width), f32), ((toks, width), bf16), ((toks, width), bf16), ((toks, width), bf16)
    token_low = ((toks, width), bf16)
    half_low = ((toks, half_width), bf16)
    whole = ((group, width), bf16)
    acc = pltpu.VMEM((group, width), f32)

    own, give = call(collect_kernel, [token_low, token_low], [core_ref, slot_row, received])
    x, grad_low, norm = call(enter_kernel, [token_low] * 3, [core_ref, own, swap(give)])
    norm_a = gather_near(norm)
    grad_y = gather_near(grad_low)
    q, kv, norm_a_all = call(
        project_kernel,
        [((group, 2 * hp), bf16), ((group, 4 * hp), bf16), whole],
        [after(norm, docs, ffn_flat), *norm_a[1:], attn_w],
        us=2,
    )
    kv_far = swap(kv)
    probs, attended, *branch = call(
        functools.partial(attend_kernel, score_scale),
        [((4 * 2 * hp // DH, 2 * toks, toks), bf16), ((group, 2 * hp), bf16), *slab],
        [core_ref, q, kv, kv_far, *docs, attn_w],
        us=6,
    )
    branch = after(branch, grad_y)
    hidden, norm = call(middle_kernel, [slab[0], token_low], [x, branch[0], *scatter_near(branch[1:])])
    norm_f = gather_near(norm)
    mid, grad_norm, *grad_norm_low, norm_f_all, grad_y_all = call(
        ffn_kernel, [((2, group, 3 * ff_pad), bf16), *slab, whole, whole], [*norm_f, *grad_y, ffn_w], [acc], 12, 7
    )
    branch = call(ffn_out_kernel, slab, [mid, ffn_w], [acc], us=2)
    (ffn_grads,) = call(
        ffn_grads_kernel, [((4, 2, width // 4, 3 * ff_pad), bf16)], [norm_f_all, grad_y_all, mid], (), 12, 4
    )
    grad_hidden, grad_hidden_low = call(
        middle_back_kernel, [slab[0], token_low], [hidden, grad_low, grad_norm, *scatter_near(grad_norm_low)]
    )
    grad_branch = gather_near(grad_hidden_low)
    final_parts = scatter_near(after(branch[1:], grad_hidden_low))

    if direct:
        ffn_part = lax.psum_scatter(ffn_grads.reshape(-1, 3 * ff_pad), FAR + (CORE,), scatter_dimension=0, tiled=True)
    else:
        ordered = jnp.moveaxis(ffn_grads, 1, 0).reshape(2, width, 3 * ff_pad)
        ordered = jnp.stack([far_rows(ordered[i], far_sizes, rows).reshape(far, -1, 3 * ff_pad) for i in range(2)], axis=1)
        ffn_part = lax.psum_scatter(ordered.reshape(-1, 3 * ff_pad), FAR + (CORE,), scatter_dimension=0, tiled=True)

    grad_q, grad_kv, far_give, grad_branch_all = call(
        functools.partial(attend_back_kernel, score_scale),
        [((group, 2 * hp), bf16), ((group, 4 * hp), f32), ((group, 4 * hp), bf16), whole],
        [*grad_branch, attn_w, q, kv, kv_far, probs],
        [pltpu.VMEM((toks, hp), bf16)],
        us=7,
    )
    out_own, out_give = call(final_kernel, [half_low, half_low], [core_ref, hidden, branch[0], *final_parts])
    gqkv_own, gqkv_oth, *grad_norm = call(
        project_back_kernel,
        [((group, 3 * hp), bf16), ((group, 3 * hp), bf16), *slab],
        [grad_q, grad_kv, swap(after(far_give, out_own)), attn_w],
        [acc],
        us=2,
    )
    arriving = scatter_near(grad_norm[1:])
    grads_own, grads_oth = call(
        attn_grads_kernel,
        [((width, 4 * hp), bf16)] * 2,
        [core_ref, norm_a_all, grad_branch_all, gqkv_own, gqkv_oth, attended],
        us=3,
    )
    other = swap(grads_oth)
    own, give = call(
        leave_kernel, [token_low, token_low], [core_ref, x, grad_hidden, grad_norm[0], *arriving, out_own, out_give]
    )

    def finished(pieces, weights, gain, part, size):
        n = len(weights)
        return call(
            functools.partial(unpack_kernel, part),
            [((rows, 4 * part), f32)] * n + [((rows, 1), f32)],
            [near_ref, gain, *pieces, *weights[:-1]],
            [pltpu.VMEM((4, rows, n * size), bf16)],
        )

    def finished_plain(blocks, weights, gain, part, size):
        blocks = near_exchange(blocks.reshape(4, rows, -1), my_near)
        raws = []
        for m in range(len(weights)):
            piece = blocks[:, :, m * size : m * size + part].astype(f32)
            raws.append(piece.transpose(1, 0, 2).reshape(rows, 4 * part))
        total = sum(jnp.sum(r * w.astype(f32), axis=1, keepdims=True) for r, w in zip(raws[:-1], weights[:-1]))
        return [r * gain for r in raws[:-1]] + [raws[-1], total]

    def returned(own, *tokens):
        (spread,) = call(spread_kernel, [((slot_count, width), bf16)], [core_ref, slot_col, after(own, tokens), swap(give)])
        back = lax.all_to_all(spread.reshape(peers, slot_cap, width), DP, 0, 0, tiled=True)
        return back.reshape(slot_count, width)

    if direct:
        planes = call(core_sum_kernel, [((4 * rows, 4 * hp), bf16)] * 4, [far_ref, grads_own, other])
        back = returned(own, planes)
        planes = [planes[0]] + [far_shift(planes[k], k) for k in range(1, 4)]
        pieces = call(far_sum_kernel, [((rows, 4 * hp), bf16)] * 4, [near_ref, *planes])
        pieces = [pieces[0]] + scatter_near(pieces[1:])
        *attn_grads, sum_a = finished(pieces, attn_weights, gain_a, hp, hp)
        pieces = call(pick_kernel, [((rows, 3 * ff_pad), bf16)] * 4, [near_ref, ffn_part])
        pieces = [pieces[0]] + scatter_near(pieces[1:])
        *ffn_grads, sum_f = finished(pieces, ffn_weights, gain_f, ff_part, ff_pad)
        back = after(back, ffn_grads, attn_grads)
    else:
        back = returned(own)
        total = far_rows((grads_own.astype(f32) + other.astype(f32)).astype(bf16), far_sizes, rows)
        attn_part = lax.psum_scatter(total, FAR, scatter_dimension=0, tiled=True)
        *attn_grads, sum_a = finished_plain(attn_part, attn_weights, gain_a, hp, hp)
        *ffn_grads, sum_f = finished_plain(ffn_part, ffn_weights, gain_f, ff_part, ff_pad)
    gains = jnp.concatenate([sum_a, sum_f], axis=1).T
    gains = gains + swap(gains)
    outputs, input_grad = call(join_kernel, [((slot_count, width), bf16)] * 2, [core_ref, back, swap(back)])
    grad_q, grad_k, grad_v, grad_o = attn_grads
    grad_g, grad_u, grad_d = ffn_grads
    return (
        outputs.reshape(patches.shape),
        input_grad.reshape(patches.shape),
        grad_q,
        grad_k,
        grad_v,
        grad_o.T,
        grad_g,
        grad_u,
        grad_d.T,
        gains[0],
        gains[1],
    )


def solution(mesh):
    dp_size = mesh.shape["dp"]
    side = round((dp_size / 2) ** (1 / 3))
    grid = (2 * side, side // 2, 2, side // 2, 2, 2)
    inner = Mesh(np.asarray(mesh.devices).reshape(grid), ("z", "yh", "yl", "xh", "xl", "c"))
    rows_first = P(DP, "c")
    cols_first = P("c", DP)
    blocks = P(DP, None, None, None)
    weights = (rows_first, rows_first, rows_first, cols_first, rows_first, rows_first, cols_first, P(DP), P(DP))
    in_specs = (blocks, P(), P(DP, None)) + weights + (blocks,)
    out_specs = (blocks, blocks) + weights
    return jax.shard_map(body, mesh=inner, in_specs=in_specs, out_specs=out_specs, check_vma=False)
```

time: 348 us -> 306 us (0.88); the launches traced: 342 us -> 305 us
  matrix products: 43.4 us -> 0 us
  Pallas kernels: 0 us -> 40.7 us
  other arithmetic: 27.6 us -> 2.07 us
  starting transfers between devices: 91.1 us -> 66.3 us
  local copies, waits for them, and re-layouts: 26.3 us -> 38.4 us
  waiting for transfers between devices: 138 us -> 143 us
    ppermute x0 -> x3, waiting for transfers between devices: none -> 43 us  [far_shift(): return lax.ppermute(value, FAR, [(i, (i + k) % far) for i in range(far)])]
    dot_general x39 -> x0, matrix products: 42.3 us -> none  [the longest x12 15 us: mm(): lax.dot_general(left, right, (((1,), (0,)), ((), ())), preferred_element_...]
    pallas_call x0 -> x25, Pallas kernels: none -> 40.7 us  [call(): pl.pallas_call(kernel, out_shape=[jax.ShapeDtypeStruct(shape, kind) for s...]
    all_gather x2, waiting for transfers between devices: 30.9 us -> 0.01 us  [gathered(): lax.all_gather(operand, (CORE,) + FAR, axis=0, tiled=True)]
    all_to_all x8 -> x2, starting transfers between devices: 38 us -> 9.4 us  [the longest x1 5.34 us: body(): lax.all_to_all(both, DP, 0, 0, tiled=True).reshape(slot_count, width)]
    unnamed x176 -> x130, local copies, waits for them, and re-layouts: 7.61 us -> 34.9 us
    all_to_all x8 -> x2, waiting for transfers between devices: 42.8 us -> 24.9 us  [the longest x1 24.9 us: body(): lax.all_to_all(both, DP, 0, 0, tiled=True).reshape(slot_count, width)]
    convert_element_type x13 -> x0, other arithmetic: 11.7 us -> none  [the longest x2 5.78 us: reduce_far(): total = (own.astype(f32) + swap(other).astype(f32)).astype(bf16)]
  transfers between devices with their start and end apart: 53 -> 54, of which waited for: 25 -> 37; matrix products, arithmetic and copies ran while one was open for 20% -> 1% of each run, Pallas kernels for 0% -> 10%
where the time goes in v2:
time: 306 us; the launch traced here: 305 us
  waiting for transfers between devices  143 us (47%)
  starting transfers between devices  66.3 us (22%)
  Pallas kernels  40.7 us (13%)
  local copies, waits for them, and re-layouts  38.4 us (13%)
  between operations  14.3 us (5%)
    ppermute x39, waiting for transfers between devices, near(): return lax.ppermute(value, NEAR, [(i, i ^ k) for i in range(4)])  70.7 us
    ppermute x3, waiting for transfers between devices, far_shift(): return lax.ppermute(value, FAR, [(i, (i + k) % far) for i in range(far)])  43 us
    pallas_call x25, Pallas kernels, call(): pl.pallas_call(kernel, out_shape=[jax.ShapeDtypeStruct(shape, kind) for s...  40.7 us
    ppermute x39, starting transfers between devices, near(): return lax.ppermute(value, NEAR, [(i, i ^ k) for i in range(4)])  37.9 us
    unnamed x130, local copies, waits for them, and re-layouts  34.9 us
    all_to_all x1, waiting for transfers between devices, body(): lax.all_to_all(both, DP, 0, 0, tiled=True).reshape(slot_count, width)  24.9 us
    ppermute x7, starting transfers between devices, swap(): return lax.ppermute(value, CORE, [(0, 1), (1, 0)])  15.3 us
  transfers between devices with their start and end apart: 54, of which 37 were waited for; matrix products, arithmetic and copies ran while one was open for 1% of the time, Pallas kernels for 10%

profile of v2, /device:TPU:9, one launch (start us, length us, event | category | flops | bytes accessed | tf_op | source)
XLA Modules:
  0.0 305.2 jit_solution(3698041695782690398)
XLA Ops:
  13.2 1.4 collective-permute-done.1.b2
  14.6 1.9 collective-permute-done.2.b3
  17.3 5.3 %all-to-all-start = ((bf16[16,32,1024]{2,1,0:T(8,128)(2,1)}), bf16[16,32,1024]{2,1,0:T(8,128)(2,1)S(1)}, u32[]{:S(2)}, u32[]{:S(2)}) async-start(bf16[16,32,1024]{2,1,0:T(8,128)(2,1)} %pad_maximum_fusion), calls=%async_computation | async-start | bytes 2097152 | tf_op jit(solution)/shard_map/all_to_all | solution.py:455
  31.8 5.1 %collective-permute-done.7.b2 = bf16[64,1152]{1,0:T(8,128)(2,1)S(1)} collective-permute-done((bf16[64,1152]{1,0:T(8,128)(2,1)S(1)}, bf16[64,1152]{1,0:T(8,128)(2,1)S(1)}, u32[]{:S(2)}, u32[]{:S(2)}) %collective-permute-start.7) | collective-permute-done | bytes 147488 | tf_op jit(solution)/shard_map/ppermute | solution.py:40
  37.8 24.9 %all-to-all-done = bf16[16,32,1024]{2,1,0:T(8,128)(2,1)S(1)} async-done(((bf16[16,32,1024]{2,1,0:T(8,128)(2,1)}), bf16[16,32,1024]{2,1,0:T(8,128)(2,1)S(1)}, u32[]{:S(2)}, u32[]{:S(2)}) %all-to-all-start) | async-done | bytes 1048608 | tf_op jit(solution)/shard_map/all_to_all | solution.py:455
  63.2 3.7 %collective-permute-start.9 = (bf16[128,1024]{1,0:T(8,128)(2,1)S(1)}, bf16[128,1024]{1,0:T(8,128)(2,1)S(1)}, u32[]{:S(2)}, u32[]{:S(2)}) collective-permute-start(bf16[128,1024]{1,0:T(8,128)(2,1)S(1)} %get-tuple-element.131), channel_id=1, source_target_pairs={{0,1},{1,0},{2,3},{3,2},{4,5},{5,4},{6,7},{7,6},{8,9},{9,8},{10,11... | collective-permute-start | bytes 786440 | tf_op jit(solution)/shard_map/ppermute | solution.py:36
  71.7 4.7 %collective-permute-done.10.n1 = bf16[128,1024]{1,0:T(8,128)(2,1)S(1)} collective-permute-done((bf16[128,1024]{1,0:T(8,128)(2,1)S(1)}, bf16[128,1024]{1,0:T(8,128)(2,1)S(1)}, u32[]{:S(2)}, u32[]{:S(2)}) %collective-permute-start.10) | collective-permute-done | bytes 262176 | tf_op jit(solution)/shard_map/ppermute | solution.py:40
  77.8 5.0 %collective-permute-done.12.n3 = bf16[128,1024]{1,0:T(8,128)(2,1)S(1)} collective-permute-done((bf16[128,1024]{1,0:T(8,128)(2,1)S(1)}, bf16[128,1024]{1,0:T(8,128)(2,1)S(1)}, u32[]{:S(2)}, u32[]{:S(2)}) %collective-permute-start.12) | collective-permute-done | bytes 262176 | tf_op jit(solution)/shard_map/ppermute | solution.py:40
  83.5 1.6 copy-done.3
  92.1 1.5 collective-permute-start.14
  95.8 7.5 %shard_map.219 = (bf16[16,256,128]{2,1,0:T(8,128)(2,1)S(1)}, bf16[512,256]{1,0:T(8,128)(2,1)S(1)}, f32[128,1024]{1,0:T(8,128)S(1)}, bf16[128,1024]{1,0:T(8,128)(...) custom-call(s32[1]{0:T(128)} %bitcast.core, bf16[512,256]{1,0:T(8,128)(2,1)S(1)} %copy-done.56, ...), custom_call_target="tpu_custom_call" | custom-call | flops 6000000000 | bytes 6000000 | tf_op jit(solution)/shard_map/pallas_call | solution.py:62
  110.5 2.9 collective-permute-done.17.b1
  113.4 1.9 collective-permute-done.18.b2
  115.3 6.2 %collective-permute-done.19.b3 = bf16[128,1024]{1,0:T(8,128)(2,1)S(1)} collective-permute-done((bf16[128,1024]{1,0:T(8,128)(2,1)S(1)}, bf16[128,1024]{1,0:T(8,128)(2,1)S(1)}, u32[]{:S(2)}, u32[]{:S(2)}) %collective-permute-start.19) | collective-permute-done | bytes 262176 | tf_op jit(solution)/shard_map/ppermute | solution.py:40
  123.6 1.7 collective-permute-start.22
  125.9 2.5 collective-permute-done.20.n1
  129.2 2.5 collective-permute-done.21.n2
  133.0 2.3 copy-done.1
  141.1 5.4 %shard_map.221 = (bf16[2,512,1152]{2,1,0:T(8,128)(2,1)S(1)}, f32[128,1024]{1,0:T(8,128)S(1)}, bf16[128,1024]{1,0:T(8,128)(2,1)S(1)}, bf16[128,1024]{1,0:T(8,128)...) custom-call(bf16[128,1024]{1,0:T(8,128)(2,1)S(1)} %copy-done.19, ...), custom_call_target="tpu_custom_call" | custom-call | flops 7000000000 | bytes 7000000 | tf_op jit(solution)/shard_map/pallas_call | solution.py:62
  146.5 3.1 %shard_map.231 = bf16[4,2,256,1152]{3,2,1,0:T(8,128)(2,1)S(1)} custom-call(bf16[512,1024]{1,0:T(8,128)(2,1)S(1)} %get-tuple-element.189.all_n, bf16[512,1024]{1,0:T(8,128)(2,1)S(1)} %get-tuple-element.190.all_y, bf16[2,512,1152]{2,1,0:T(8,128)(2,1)S(1)} %get-tuple-element.160.mid), custom_call_target="tpu_custom_call" | custom-call | flops 4000000000 | bytes 4000000 | tf_op jit(solution)/shard_map/pallas_call | solution.py:62
  149.7 2.2 copy-done
  153.4 2.0 collective-permute-start.24
  156.1 2.3 copy-done.2
  158.4 1.7 copy-done.39
  168.6 1.4 collective-permute-done.29.b1
  170.1 2.1 collective-permute-start.28
  172.2 1.7 collective-permute-done.30.b2
  175.3 2.4 collective-permute-done.26.g1
  177.7 5.9 %collective-permute-done.27.g2 = bf16[128,1024]{1,0:T(8,128)(2,1)S(1)} collective-permute-done((bf16[128,1024]{1,0:T(8,128)(2,1)S(1)}, bf16[128,1024]{1,0:T(8,128)(2,1)S(1)}, u32[]{:S(2)}, u32[]{:S(2)}) %collective-permute-start.27) | collective-permute-done | bytes 262176 | tf_op jit(solution)/shard_map/ppermute | solution.py:40
  183.5 2.8 collective-permute-done.28.g3
  186.4 7.3 %shard_map.223 = (bf16[512,256]{1,0:T(8,128)(2,1)S(1)}, f32[512,512]{1,0:T(8,128)S(1)}, bf16[512,512]{1,0:T(8,128)(2,1)S(1)}, bf16[512,1024]{1,0:T(8,128)(2,1)S(1)}) custom-call(bf16[128,1024]{1,0:T(8,128)(2,1)S(1)} %get-tuple-element.155.g0, bf16[128,1024]{1,0:T(8,128)(2,1)S(1)} %collective-permute-done.26.g1, ...), custom_call_target="tpu_custom_call" | custom-call | flops 7000000000 | bytes 7000000 | tf_op jit(solution)/shard_map/pallas_call | solution.py:62
  193.7 5.5 %collective-permute-start.32 = (bf16[512,512]{1,0:T(8,128)(2,1)S(1)}, bf16[512,512]{1,0:T(8,128)(2,1)S(1)}, u32[]{:S(2)}, u32[]{:S(2)}) collective-permute-start(bf16[512,512]{1,0:T(8,128)(2,1)S(1)} %get-tuple-element.169), channel_id=1, source_target_pairs={{0,1},{1,0},{2,3},{3,2},{4,5},{5,4},{6,7},{7,6},{8,9},{9,8},{10,11... | collective-permute-start | bytes 1572872 | tf_op jit(solution)/shard_map/ppermute | solution.py:36
  199.3 1.5 collective-permute-done.32.back
  202.1 1.8 shard_map.228
  208.0 5.1 %collective-permute-done.33.b1 = bf16[128,1024]{1,0:T(8,128)(2,1)S(1)} collective-permute-done((bf16[128,1024]{1,0:T(8,128)(2,1)S(1)}, bf16[128,1024]{1,0:T(8,128)(2,1)S(1)}, u32[]{:S(2)}, u32[]{:S(2)}) %collective-permute-start.33) | collective-permute-done | bytes 262176 | tf_op jit(solution)/shard_map/ppermute | solution.py:40
  213.8 5.1 %collective-permute-done.35.b3 = bf16[128,1024]{1,0:T(8,128)(2,1)S(1)} collective-permute-done((bf16[128,1024]{1,0:T(8,128)(2,1)S(1)}, bf16[128,1024]{1,0:T(8,128)(2,1)S(1)}, u32[]{:S(2)}, u32[]{:S(2)}) %collective-permute-start.35) | collective-permute-done | bytes 262176 | tf_op jit(solution)/shard_map/ppermute | solution.py:40
  219.2 1.6 collective-permute-start.37
  223.1 2.7 shard_map.230
  225.8 4.1 %all-to-all-start.1 = ((bf16[16,32,1024]{2,1,0:T(8,128)(2,1)}), bf16[16,32,1024]{2,1,0:T(8,128)(2,1)S(1)}, u32[]{:S(2)}, u32[]{:S(2)}) async-start(bf16[16,32,1024]{2,1,0:T(8,128)(2,1)} %bitcast.18), calls=%async_computation.1 | async-start | bytes 2097152 | tf_op jit(solution)/shard_map/all_to_all | solution.py:593
  233.4 35.3 %collective-permute-done.41.t1 = bf16[256,512]{1,0:T(8,128)(2,1)S(1)} collective-permute-done((bf16[256,512]{1,0:T(8,128)(2,1)S(1)}, bf16[256,512]{1,0:T(8,128)(2,1)S(1)}, u32[]{:S(2)}, u32[]{:S(2)}) %collective-permute-start.41) | collective-permute-done | bytes 262176 | tf_op jit(solution)/shard_map/ppermute | solution.py:449
  268.8 5.6 %collective-permute-done.42.t2 = bf16[256,512]{1,0:T(8,128)(2,1)S(1)} collective-permute-done((bf16[256,512]{1,0:T(8,128)(2,1)S(1)}, bf16[256,512]{1,0:T(8,128)(2,1)S(1)}, u32[]{:S(2)}, u32[]{:S(2)}) %collective-permute-start.42) | collective-permute-done | bytes 262176 | tf_op jit(solution)/shard_map/ppermute | solution.py:449
  274.4 2.1 collective-permute-done.43.t3
  285.4 1.7 collective-permute-done.39.s2
  287.1 2.0 collective-permute-done.40.s3
  289.1 2.3 shard_map.233
  291.4 2.9 collective-permute-start.47
  294.5 2.0 collective-permute-done.48
  297.1 1.5 shard_map.236
  (242 shorter events, 85.0 us)
Async XLA Ops:
  7.2 76.3 %all-gather.3.cloned.1.call-start = ((), (), s32[]{:S(2)}) async-start(), calls=%async_computation.3 | async-start | bytes 2359296 | tf_op jit(solution)/shard_map/all_gather | solution.py:479
  12.5 4.0 %collective-permute-start.2 = (bf16[64,512]{1,0:T(8,128)(2,1)S(1)}, bf16[64,512]{1,0:T(8,128)(2,1)S(1)}, u32[]{:S(2)}, u32[]{:S(2)}) collective-permute-start(bf16[64,512]{1,0:T(8,128)(2,1)S(1)} %get-tuple-element.118), channel_id=1, source_target_pairs={{0,6},{2,4},{4,2},{6,0},{1,7},{3,5},{5,3},{7,1},{8,14},{10,12},{12... | collective-permute-start | bytes 196616 | tf_op jit(solution)/shard_map/ppermute | solution.py:40
  17.3 45.3 %all-to-all-start = ((bf16[16,32,1024]{2,1,0:T(8,128)(2,1)}), bf16[16,32,1024]{2,1,0:T(8,128)(2,1)S(1)}, u32[]{:S(2)}, u32[]{:S(2)}) async-start(bf16[16,32,1024]{2,1,0:T(8,128)(2,1)} %pad_maximum_fusion), calls=%async_computation | async-start | bytes 2097152 | tf_op jit(solution)/shard_map/all_to_all | solution.py:455
  22.7 110.4 %all-gather.5.cloned.1.call-start = ((), (), s32[]{:S(2)}) async-start(), calls=%async_computation.4 | async-start | bytes 5308416 | tf_op jit(solution)/shard_map/all_gather | solution.py:479
  24.5 5.4 %collective-permute-start.3 = (s32[1,256]{1,0:T(1,128)S(1)}, s32[1,256]{1,0:T(1,128)S(1)}, u32[]{:S(2)}, u32[]{:S(2)}) collective-permute-start(s32[1,256]{1,0:T(1,128)S(1)} %copy-done.62), channel_id=1, source_target_pairs={{0,2},{2,0},{4,6},{6,4},{1,3},{3,1},{5,7},{7,5},{8,10},{10,8},{12,... | collective-permute-start | bytes 3080 | tf_op jit(solution)/shard_map/ppermute | solution.py:40
  25.6 4.8 %collective-permute-start.4 = (s32[1,256]{1,0:T(1,128)S(1)}, s32[1,256]{1,0:T(1,128)S(1)}, u32[]{:S(2)}, u32[]{:S(2)}) collective-permute-start(s32[1,256]{1,0:T(1,128)S(1)} %copy-done.62), channel_id=1, source_target_pairs={{0,4},{2,6},{4,0},{6,2},{1,5},{3,7},{5,1},{7,3},{8,12},{10,14},{12... | collective-permute-start | bytes 3080 | tf_op jit(solution)/shard_map/ppermute | solution.py:40
  27.5 4.4 %collective-permute-start.6 = (bf16[64,1152]{1,0:T(8,128)(2,1)S(1)}, bf16[64,1152]{1,0:T(8,128)(2,1)S(1)}, u32[]{:S(2)}, u32[]{:S(2)}) collective-permute-start(bf16[64,1152]{1,0:T(8,128)(2,1)S(1)} %get-tuple-element.124), channel_id=1, source_target_pairs={{0,2},{2,0},{4,6},{6,4},{1,3},{3,1},{5,7},{7,5},{8,10},{10,8},{12,... | collective-permute-start | bytes 442376 | tf_op jit(solution)/shard_map/ppermute | solution.py:40
  28.7 8.2 %collective-permute-start.7 = (bf16[64,1152]{1,0:T(8,128)(2,1)S(1)}, bf16[64,1152]{1,0:T(8,128)(2,1)S(1)}, u32[]{:S(2)}, u32[]{:S(2)}) collective-permute-start(bf16[64,1152]{1,0:T(8,128)(2,1)S(1)} %get-tuple-element.125), channel_id=1, source_target_pairs={{0,4},{2,6},{4,0},{6,2},{1,5},{3,7},{5,1},{7,3},{8,12},{10,14},{12... | collective-permute-start | bytes 442376 | tf_op jit(solution)/shard_map/ppermute | solution.py:40
  29.9 7.0 %collective-permute-start.8 = (bf16[64,1152]{1,0:T(8,128)(2,1)S(1)}, bf16[64,1152]{1,0:T(8,128)(2,1)S(1)}, u32[]{:S(2)}, u32[]{:S(2)}) collective-permute-start(bf16[64,1152]{1,0:T(8,128)(2,1)S(1)} %get-tuple-element.126), channel_id=1, source_target_pairs={{0,6},{2,4},{4,2},{6,0},{1,7},{3,5},{5,3},{7,1},{8,14},{10,12},{12... | collective-permute-start | bytes 442376 | tf_op jit(solution)/shard_map/ppermute | solution.py:40
  62.7 216.6 %reduce-scatter.2.cloned.1.call-start = ((), (), s32[]{:S(2)}) async-start(), calls=%async_computation.5 | async-start | bytes 5308416 | tf_op jit(solution)/shard_map/reduce_scatter | solution.py:540
  63.2 4.9 %collective-permute-start.9 = (bf16[128,1024]{1,0:T(8,128)(2,1)S(1)}, bf16[128,1024]{1,0:T(8,128)(2,1)S(1)}, u32[]{:S(2)}, u32[]{:S(2)}) collective-permute-start(bf16[128,1024]{1,0:T(8,128)(2,1)S(1)} %get-tuple-element.131), channel_id=1, source_target_pairs={{0,1},{1,0},{2,3},{3,2},{4,5},{5,4},{6,7},{7,6},{8,9},{9,8},{10,11... | collective-permute-start | bytes 786440 | tf_op jit(solution)/shard_map/ppermute | solution.py:36
  68.9 7.5 %collective-permute-start.10 = (bf16[128,1024]{1,0:T(8,128)(2,1)S(1)}, bf16[128,1024]{1,0:T(8,128)(2,1)S(1)}, u32[]{:S(2)}, u32[]{:S(2)}) collective-permute-start(bf16[128,1024]{1,0:T(8,128)(2,1)S(1)} %get-tuple-element.136.n0), channel_id=1, source_target_pairs={{0,2},{2,0},{4,6},{6,4},{1,3},{3,1},{5,7},{7,5},{8,10},{10,8},{12,... | collective-permute-start | bytes 786440 | tf_op jit(solution)/shard_map/ppermute | solution.py:40
  69.2 7.9 %collective-permute-start.11 = (bf16[128,1024]{1,0:T(8,128)(2,1)S(1)}, bf16[128,1024]{1,0:T(8,128)(2,1)S(1)}, u32[]{:S(2)}, u32[]{:S(2)}) collective-permute-start(bf16[128,1024]{1,0:T(8,128)(2,1)S(1)} %get-tuple-element.136.n0), channel_id=1, source_target_pairs={{0,4},{2,6},{4,0},{6,2},{1,5},{3,7},{5,1},{7,3},{8,12},{10,14},{12... | collective-permute-start | bytes 786440 | tf_op jit(solution)/shard_map/ppermute | solution.py:40
  70.2 12.6 %collective-permute-start.12 = (bf16[128,1024]{1,0:T(8,128)(2,1)S(1)}, bf16[128,1024]{1,0:T(8,128)(2,1)S(1)}, u32[]{:S(2)}, u32[]{:S(2)}) collective-permute-start(bf16[128,1024]{1,0:T(8,128)(2,1)S(1)} %get-tuple-element.136.n0), channel_id=1, source_target_pairs={{0,6},{2,4},{4,2},{6,0},{1,7},{3,5},{5,3},{7,1},{8,14},{10,12},{12... | collective-permute-start | bytes 786440 | tf_op jit(solution)/shard_map/ppermute | solution.py:40
  92.1 12.9 %collective-permute-start.14 = (bf16[128,1024]{1,0:T(8,128)(2,1)S(1)}, bf16[128,1024]{1,0:T(8,128)(2,1)S(1)}, u32[]{:S(2)}, u32[]{:S(2)}) collective-permute-start(bf16[128,1024]{1,0:T(8,128)(2,1)S(1)} %get-tuple-element.143.y0.grad_low), channel_id=1, source_target_pairs={{0,2},{2,0},{4,6},{6,4},{1,3},{3,1},{5,7},{7,5},{8,10},{10,8},{12,... | collective-permute-start | bytes 786440 | tf_op jit(solution)/shard_map/ppermute | solution.py:40
  93.6 11.9 %collective-permute-start.15 = (bf16[128,1024]{1,0:T(8,128)(2,1)S(1)}, bf16[128,1024]{1,0:T(8,128)(2,1)S(1)}, u32[]{:S(2)}, u32[]{:S(2)}) collective-permute-start(bf16[128,1024]{1,0:T(8,128)(2,1)S(1)} %get-tuple-element.143.y0.grad_low), channel_id=1, source_target_pairs={{0,4},{2,6},{4,0},{6,2},{1,5},{3,7},{5,1},{7,3},{8,12},{10,14},{12... | collective-permute-start | bytes 786440 | tf_op jit(solution)/shard_map/ppermute | solution.py:40
  94.6 12.1 %collective-permute-start.16 = (bf16[128,1024]{1,0:T(8,128)(2,1)S(1)}, bf16[128,1024]{1,0:T(8,128)(2,1)S(1)}, u32[]{:S(2)}, u32[]{:S(2)}) collective-permute-start(bf16[128,1024]{1,0:T(8,128)(2,1)S(1)} %get-tuple-element.143.y0.grad_low), channel_id=1, source_target_pairs={{0,6},{2,4},{4,2},{6,0},{1,7},{3,5},{5,3},{7,1},{8,14},{10,12},{12... | collective-permute-start | bytes 786440 | tf_op jit(solution)/shard_map/ppermute | solution.py:40
  107.3 6.1 %collective-permute-start.17 = (bf16[128,1024]{1,0:T(8,128)(2,1)S(1)}, bf16[128,1024]{1,0:T(8,128)(2,1)S(1)}, u32[]{:S(2)}, u32[]{:S(2)}) collective-permute-start(bf16[128,1024]{1,0:T(8,128)(2,1)S(1)} %get-tuple-element.145), channel_id=1, source_target_pairs={{0,2},{2,0},{4,6},{6,4},{1,3},{3,1},{5,7},{7,5},{8,10},{10,8},{12,... | collective-permute-start | bytes 786440 | tf_op jit(solution)/shard_map/ppermute | solution.py:40
  108.6 6.7 %collective-permute-start.18 = (bf16[128,1024]{1,0:T(8,128)(2,1)S(1)}, bf16[128,1024]{1,0:T(8,128)(2,1)S(1)}, u32[]{:S(2)}, u32[]{:S(2)}) collective-permute-start(bf16[128,1024]{1,0:T(8,128)(2,1)S(1)} %get-tuple-element.146), channel_id=1, source_target_pairs={{0,4},{2,6},{4,0},{6,2},{1,5},{3,7},{5,1},{7,3},{8,12},{10,14},{12... | collective-permute-start | bytes 786440 | tf_op jit(solution)/shard_map/ppermute | solution.py:40
  109.3 12.1 %collective-permute-start.19 = (bf16[128,1024]{1,0:T(8,128)(2,1)S(1)}, bf16[128,1024]{1,0:T(8,128)(2,1)S(1)}, u32[]{:S(2)}, u32[]{:S(2)}) collective-permute-start(bf16[128,1024]{1,0:T(8,128)(2,1)S(1)} %get-tuple-element.147), channel_id=1, source_target_pairs={{0,6},{2,4},{4,2},{6,0},{1,7},{3,5},{5,3},{7,1},{8,14},{10,12},{12... | collective-permute-start | bytes 786440 | tf_op jit(solution)/shard_map/ppermute | solution.py:40
  122.6 5.9 %collective-permute-start.20 = (bf16[128,1024]{1,0:T(8,128)(2,1)S(1)}, bf16[128,1024]{1,0:T(8,128)(2,1)S(1)}, u32[]{:S(2)}, u32[]{:S(2)}) collective-permute-start(bf16[128,1024]{1,0:T(8,128)(2,1)S(1)} %get-tuple-element.149.n0), channel_id=1, source_target_pairs={{0,2},{2,0},{4,6},{6,4},{1,3},{3,1},{5,7},{7,5},{8,10},{10,8},{12,... | collective-permute-start | bytes 786440 | tf_op jit(solution)/shard_map/ppermute | solution.py:40
  122.9 8.7 %collective-permute-start.21 = (bf16[128,1024]{1,0:T(8,128)(2,1)S(1)}, bf16[128,1024]{1,0:T(8,128)(2,1)S(1)}, u32[]{:S(2)}, u32[]{:S(2)}) collective-permute-start(bf16[128,1024]{1,0:T(8,128)(2,1)S(1)} %get-tuple-element.149.n0), channel_id=1, source_target_pairs={{0,4},{2,6},{4,0},{6,2},{1,5},{3,7},{5,1},{7,3},{8,12},{10,14},{12... | collective-permute-start | bytes 786440 | tf_op jit(solution)/shard_map/ppermute | solution.py:40
  123.6 8.8 %collective-permute-start.22 = (bf16[128,1024]{1,0:T(8,128)(2,1)S(1)}, bf16[128,1024]{1,0:T(8,128)(2,1)S(1)}, u32[]{:S(2)}, u32[]{:S(2)}) collective-permute-start(bf16[128,1024]{1,0:T(8,128)(2,1)S(1)} %get-tuple-element.149.n0), channel_id=1, source_target_pairs={{0,6},{2,4},{4,2},{6,0},{1,7},{3,5},{5,3},{7,1},{8,14},{10,12},{12... | collective-permute-start | bytes 786440 | tf_op jit(solution)/shard_map/ppermute | solution.py:40
  152.0 9.4 %collective-permute-start.23 = (bf16[128,1024]{1,0:T(8,128)(2,1)}, bf16[128,1024]{1,0:T(8,128)(2,1)S(1)}, u32[]{:S(2)}, u32[]{:S(2)}) collective-permute-start(bf16[128,1024]{1,0:T(8,128)(2,1)} %copy-done.20), channel_id=1, source_target_pairs={{0,2},{2,0},{4,6},{6,4},{1,3},{3,1},{5,7},{7,5},{8,10},{10,8},{12,... | collective-permute-start | bytes 786440 | tf_op jit(solution)/shard_map/ppermute | solution.py:40
  153.4 9.5 %collective-permute-start.24 = (bf16[128,1024]{1,0:T(8,128)(2,1)S(1)}, bf16[128,1024]{1,0:T(8,128)(2,1)S(1)}, u32[]{:S(2)}, u32[]{:S(2)}) collective-permute-start(bf16[128,1024]{1,0:T(8,128)(2,1)S(1)} %get-tuple-element.152), channel_id=1, source_target_pairs={{0,4},{2,6},{4,0},{6,2},{1,5},{3,7},{5,1},{7,3},{8,12},{10,14},{12... | collective-permute-start | bytes 786440 | tf_op jit(solution)/shard_map/ppermute | solution.py:40
  155.4 8.7 %collective-permute-start.25 = (bf16[128,1024]{1,0:T(8,128)(2,1)S(1)}, bf16[128,1024]{1,0:T(8,128)(2,1)S(1)}, u32[]{:S(2)}, u32[]{:S(2)}) collective-permute-start(bf16[128,1024]{1,0:T(8,128)(2,1)S(1)} %copy-done.17), channel_id=1, source_target_pairs={{0,6},{2,4},{4,2},{6,0},{1,7},{3,5},{5,3},{7,1},{8,14},{10,12},{12... | collective-permute-start | bytes 786440 | tf_op jit(solution)/shard_map/ppermute | solution.py:40
  164.4 5.7 %collective-permute-start.29 = (bf16[128,1024]{1,0:T(8,128)(2,1)S(1)}, bf16[128,1024]{1,0:T(8,128)(2,1)S(1)}, u32[]{:S(2)}, u32[]{:S(2)}) collective-permute-start(bf16[128,1024]{1,0:T(8,128)(2,1)S(1)} %get-tuple-element.165), channel_id=1, source_target_pairs={{0,2},{2,0},{4,6},{6,4},{1,3},{3,1},{5,7},{7,5},{8,10},{10,8},{12,... | collective-permute-start | bytes 786440 | tf_op jit(solution)/shard_map/ppermute | solution.py:40
  165.6 8.3 %collective-permute-start.30 = (bf16[128,1024]{1,0:T(8,128)(2,1)S(1)}, bf16[128,1024]{1,0:T(8,128)(2,1)S(1)}, u32[]{:S(2)}, u32[]{:S(2)}) collective-permute-start(bf16[128,1024]{1,0:T(8,128)(2,1)S(1)} %get-tuple-element.166), channel_id=1, source_target_pairs={{0,4},{2,6},{4,0},{6,2},{1,5},{3,7},{5,1},{7,3},{8,12},{10,14},{12... | collective-permute-start | bytes 786440 | tf_op jit(solution)/shard_map/ppermute | solution.py:40
  166.0 9.1 %collective-permute-start.31 = (bf16[128,1024]{1,0:T(8,128)(2,1)S(1)}, bf16[128,1024]{1,0:T(8,128)(2,1)S(1)}, u32[]{:S(2)}, u32[]{:S(2)}) collective-permute-start(bf16[128,1024]{1,0:T(8,128)(2,1)S(1)} %get-tuple-element.167), channel_id=1, source_target_pairs={{0,6},{2,4},{4,2},{6,0},{1,7},{3,5},{5,3},{7,1},{8,14},{10,12},{12... | collective-permute-start | bytes 786440 | tf_op jit(solution)/shard_map/ppermute | solution.py:40
  167.1 10.6 %collective-permute-start.26 = (bf16[128,1024]{1,0:T(8,128)(2,1)S(1)}, bf16[128,1024]{1,0:T(8,128)(2,1)S(1)}, u32[]{:S(2)}, u32[]{:S(2)}) collective-permute-start(bf16[128,1024]{1,0:T(8,128)(2,1)S(1)} %get-tuple-element.155.g0), channel_id=1, source_target_pairs={{0,2},{2,0},{4,6},{6,4},{1,3},{3,1},{5,7},{7,5},{8,10},{10,8},{12,... | collective-permute-start | bytes 786440 | tf_op jit(solution)/shard_map/ppermute | solution.py:40
  168.2 15.3 %collective-permute-start.27 = (bf16[128,1024]{1,0:T(8,128)(2,1)S(1)}, bf16[128,1024]{1,0:T(8,128)(2,1)S(1)}, u32[]{:S(2)}, u32[]{:S(2)}) collective-permute-start(bf16[128,1024]{1,0:T(8,128)(2,1)S(1)} %get-tuple-element.155.g0), channel_id=1, source_target_pairs={{0,4},{2,6},{4,0},{6,2},{1,5},{3,7},{5,1},{7,3},{8,12},{10,14},{12... | collective-permute-start | bytes 786440 | tf_op jit(solution)/shard_map/ppermute | solution.py:40
  170.1 16.3 %collective-permute-start.28 = (bf16[128,1024]{1,0:T(8,128)(2,1)S(1)}, bf16[128,1024]{1,0:T(8,128)(2,1)S(1)}, u32[]{:S(2)}, u32[]{:S(2)}) collective-permute-start(bf16[128,1024]{1,0:T(8,128)(2,1)S(1)} %get-tuple-element.155.g0), channel_id=1, source_target_pairs={{0,6},{2,4},{4,2},{6,0},{1,7},{3,5},{5,3},{7,1},{8,14},{10,12},{12... | collective-permute-start | bytes 786440 | tf_op jit(solution)/shard_map/ppermute | solution.py:40
  193.7 7.1 %collective-permute-start.32 = (bf16[512,512]{1,0:T(8,128)(2,1)S(1)}, bf16[512,512]{1,0:T(8,128)(2,1)S(1)}, u32[]{:S(2)}, u32[]{:S(2)}) collective-permute-start(bf16[512,512]{1,0:T(8,128)(2,1)S(1)} %get-tuple-element.169), channel_id=1, source_target_pairs={{0,1},{1,0},{2,3},{3,2},{4,5},{5,4},{6,7},{7,6},{8,9},{9,8},{10,11... | collective-permute-start | bytes 1572872 | tf_op jit(solution)/shard_map/ppermute | solution.py:36
  204.9 16.0 %collective-permute-start.36 = (bf16[1024,512]{1,0:T(8,128)(2,1)S(1)}, bf16[1024,512]{1,0:T(8,128)(2,1)S(1)}, u32[]{:S(2)}, u32[]{:S(2)}) collective-permute-start(bf16[1024,512]{1,0:T(8,128)(2,1)S(1)} %get-tuple-element.182), channel_id=1, source_target_pairs={{0,1},{1,0},{2,3},{3,2},{4,5},{5,4},{6,7},{7,6},{8,9},{9,8},{10,11... | collective-permute-start | bytes 3145736 | tf_op jit(solution)/shard_map/ppermute | solution.py:36
  205.3 7.8 %collective-permute-start.33 = (bf16[128,1024]{1,0:T(8,128)(2,1)S(1)}, bf16[128,1024]{1,0:T(8,128)(2,1)S(1)}, u32[]{:S(2)}, u32[]{:S(2)}) collective-permute-start(bf16[128,1024]{1,0:T(8,128)(2,1)S(1)} %get-tuple-element.171), channel_id=1, source_target_pairs={{0,2},{2,0},{4,6},{6,4},{1,3},{3,1},{5,7},{7,5},{8,10},{10,8},{12,... | collective-permute-start | bytes 786440 | tf_op jit(solution)/shard_map/ppermute | solution.py:40
  206.0 7.7 %collective-permute-start.34 = (bf16[128,1024]{1,0:T(8,128)(2,1)S(1)}, bf16[128,1024]{1,0:T(8,128)(2,1)S(1)}, u32[]{:S(2)}, u32[]{:S(2)}) collective-permute-start(bf16[128,1024]{1,0:T(8,128)(2,1)S(1)} %get-tuple-element.172), channel_id=1, source_target_pairs={{0,4},{2,6},{4,0},{6,2},{1,5},{3,7},{5,1},{7,3},{8,12},{10,14},{12... | collective-permute-start | bytes 786440 | tf_op jit(solution)/shard_map/ppermute | solution.py:40
  206.7 12.1 %collective-permute-start.35 = (bf16[128,1024]{1,0:T(8,128)(2,1)S(1)}, bf16[128,1024]{1,0:T(8,128)(2,1)S(1)}, u32[]{:S(2)}, u32[]{:S(2)}) collective-permute-start(bf16[128,1024]{1,0:T(8,128)(2,1)S(1)} %get-tuple-element.173), channel_id=1, source_target_pairs={{0,6},{2,4},{4,2},{6,0},{1,7},{3,5},{5,3},{7,1},{8,14},{10,12},{12... | collective-permute-start | bytes 786440 | tf_op jit(solution)/shard_map/ppermute | solution.py:40
  225.8 65.6 %all-to-all-start.1 = ((bf16[16,32,1024]{2,1,0:T(8,128)(2,1)}), bf16[16,32,1024]{2,1,0:T(8,128)(2,1)S(1)}, u32[]{:S(2)}, u32[]{:S(2)}) async-start(bf16[16,32,1024]{2,1,0:T(8,128)(2,1)} %bitcast.18), calls=%async_computation.1 | async-start | bytes 2097152 | tf_op jit(solution)/shard_map/all_to_all | solution.py:593
  229.9 38.9 %collective-permute-start.41 = (bf16[256,512]{1,0:T(8,128)(2,1)S(1)}, bf16[256,512]{1,0:T(8,128)(2,1)S(1)}, u32[]{:S(2)}, u32[]{:S(2)}) collective-permute-start(bf16[256,512]{1,0:T(8,128)(2,1)S(1)} %get-tuple-element.184), channel_id=1, source_target_pairs={{0,8},{8,16},{16,24},{24,0},{1,9},{9,17},{17,25},{25,1},{2,10},{10... | collective-permute-start | bytes 786440 | tf_op jit(solution)/shard_map/ppermute | solution.py:449
  231.1 43.3 %collective-permute-start.42 = (bf16[256,512]{1,0:T(8,128)(2,1)S(1)}, bf16[256,512]{1,0:T(8,128)(2,1)S(1)}, u32[]{:S(2)}, u32[]{:S(2)}) collective-permute-start(bf16[256,512]{1,0:T(8,128)(2,1)S(1)} %get-tuple-element.185), channel_id=1, source_target_pairs={{0,16},{8,24},{16,0},{24,8},{1,17},{9,25},{17,1},{25,9},{2,18},{10... | collective-permute-start | bytes 786440 | tf_op jit(solution)/shard_map/ppermute | solution.py:449
  232.1 44.4 %collective-permute-start.43 = (bf16[256,512]{1,0:T(8,128)(2,1)S(1)}, bf16[256,512]{1,0:T(8,128)(2,1)S(1)}, u32[]{:S(2)}, u32[]{:S(2)}) collective-permute-start(bf16[256,512]{1,0:T(8,128)(2,1)S(1)} %get-tuple-element.186), channel_id=1, source_target_pairs={{0,24},{8,0},{16,8},{24,16},{1,25},{9,1},{17,9},{25,17},{2,26},{10... | collective-permute-start | bytes 786440 | tf_op jit(solution)/shard_map/ppermute | solution.py:449
  276.6 6.4 %collective-permute-start.44 = (bf16[64,512]{1,0:T(8,128)(2,1)S(1)}, bf16[64,512]{1,0:T(8,128)(2,1)S(1)}, u32[]{:S(2)}, u32[]{:S(2)}) collective-permute-start(bf16[64,512]{1,0:T(8,128)(2,1)S(1)} %get-tuple-element.199), channel_id=1, source_target_pairs={{0,2},{2,0},{4,6},{6,4},{1,3},{3,1},{5,7},{7,5},{8,10},{10,8},{12,... | collective-permute-start | bytes 196616 | tf_op jit(solution)/shard_map/ppermute | solution.py:40
  277.9 5.3 %collective-permute-start.45 = (bf16[64,512]{1,0:T(8,128)(2,1)S(1)}, bf16[64,512]{1,0:T(8,128)(2,1)S(1)}, u32[]{:S(2)}, u32[]{:S(2)}) collective-permute-start(bf16[64,512]{1,0:T(8,128)(2,1)S(1)} %get-tuple-element.200), channel_id=1, source_target_pairs={{0,4},{2,6},{4,0},{6,2},{1,5},{3,7},{5,1},{7,3},{8,12},{10,14},{12... | collective-permute-start | bytes 196616 | tf_op jit(solution)/shard_map/ppermute | solution.py:40
  279.1 4.3 %collective-permute-start.46 = (bf16[64,512]{1,0:T(8,128)(2,1)S(1)}, bf16[64,512]{1,0:T(8,128)(2,1)S(1)}, u32[]{:S(2)}, u32[]{:S(2)}) collective-permute-start(bf16[64,512]{1,0:T(8,128)(2,1)S(1)} %get-tuple-element.201), channel_id=1, source_target_pairs={{0,6},{2,4},{4,2},{6,0},{1,7},{3,5},{5,3},{7,1},{8,14},{10,12},{12... | collective-permute-start | bytes 196616 | tf_op jit(solution)/shard_map/ppermute | solution.py:40
  280.5 5.0 %collective-permute-start.38 = (bf16[64,1152]{1,0:T(8,128)(2,1)S(1)}, bf16[64,1152]{1,0:T(8,128)(2,1)S(1)}, u32[]{:S(2)}, u32[]{:S(2)}) collective-permute-start(bf16[64,1152]{1,0:T(8,128)(2,1)S(1)} %get-tuple-element.192), channel_id=1, source_target_pairs={{0,2},{2,0},{4,6},{6,4},{1,3},{3,1},{5,7},{7,5},{8,10},{10,8},{12,... | collective-permute-start | bytes 442376 | tf_op jit(solution)/shard_map/ppermute | solution.py:40
  281.7 5.4 %collective-permute-start.39 = (bf16[64,1152]{1,0:T(8,128)(2,1)S(1)}, bf16[64,1152]{1,0:T(8,128)(2,1)S(1)}, u32[]{:S(2)}, u32[]{:S(2)}) collective-permute-start(bf16[64,1152]{1,0:T(8,128)(2,1)S(1)} %get-tuple-element.193), channel_id=1, source_target_pairs={{0,4},{2,6},{4,0},{6,2},{1,5},{3,7},{5,1},{7,3},{8,12},{10,14},{12... | collective-permute-start | bytes 442376 | tf_op jit(solution)/shard_map/ppermute | solution.py:40
  283.0 6.1 %collective-permute-start.40 = (bf16[64,1152]{1,0:T(8,128)(2,1)S(1)}, bf16[64,1152]{1,0:T(8,128)(2,1)S(1)}, u32[]{:S(2)}, u32[]{:S(2)}) collective-permute-start(bf16[64,1152]{1,0:T(8,128)(2,1)S(1)} %get-tuple-element.194), channel_id=1, source_target_pairs={{0,6},{2,4},{4,2},{6,0},{1,7},{3,5},{5,3},{7,1},{8,14},{10,12},{12... | collective-permute-start | bytes 442376 | tf_op jit(solution)/shard_map/ppermute | solution.py:40
  291.4 5.7 %collective-permute-start.47 = (bf16[512,1024]{1,0:T(8,128)(2,1)S(1)}, bf16[512,1024]{1,0:T(8,128)(2,1)S(1)}, u32[]{:S(2)}, u32[]{:S(2)}) collective-permute-start(bf16[512,1024]{1,0:T(8,128)(2,1)S(1)} %bitcast.44), channel_id=1, source_target_pairs={{0,1},{1,0},{2,3},{3,2},{4,5},{5,4},{6,7},{7,6},{8,9},{9,8},{10,11... | collective-permute-start | bytes 3145736 | tf_op jit(solution)/shard_map/ppermute | solution.py:36
  (71 other events, 316.8 us)
Sparse Core Ops, SparseCore 0:
  17.4 44.0 all-gather.2
  63.2 53.2 all-gather.4
  152.1 57.2 reduce-scatter.1

commit v3 on v2

--- a/solution.py
+++ b/solution.py
@@ -56,18 +56,42 @@
     return lax.rsqrt(jnp.mean(values * values, axis=-1, keepdims=True) + eps)
 
 
-def call(kernel, outs, args, scratch=(), limit=4, us=1.0):
-    in_specs = [pl.BlockSpec(memory_space=pltpu.SMEM if a.ndim == 1 else pltpu.VMEM) for a in args]
-    out_specs = [pl.BlockSpec(memory_space=pltpu.VMEM) for _ in outs]
+def call(kernel, outs, args, scratch=(), limit=4, us=1.0, far_args=(), far_outs=()):
+    def space(i, ndim, left):
+        if i in left:
+            return pl.BlockSpec(memory_space=pltpu.HBM)
+        return pl.BlockSpec(memory_space=pltpu.SMEM if ndim == 1 else pltpu.VMEM)
+
+    args = [pltpu.with_memory_space_constraint(a, pltpu.HBM) if i in far_args else a for i, a in enumerate(args)]
     return pl.pallas_call(
         kernel,
-        out_shape=[jax.ShapeDtypeStruct(shape, kind) for shape, kind in outs],
-        in_specs=in_specs,
-        out_specs=out_specs,
+        out_shape=[
+            pltpu.HBM(shape, kind) if i in far_outs else jax.ShapeDtypeStruct(shape, kind)
+            for i, (shape, kind) in enumerate(outs)
+        ],
+        in_specs=[space(i, a.ndim, far_args) for i, a in enumerate(args)],
+        out_specs=[space(i, 2, far_outs) for i in range(len(outs))],
         scratch_shapes=list(scratch),
         compiler_params=pltpu.CompilerParams(vmem_limit_bytes=limit << 20),
         cost_estimate=pl.CostEstimate(flops=int(us * 1e9), bytes_accessed=int(us * 1e6), transcendentals=0),
     )(*args)
+
+
+def bring(pairs, sems, first=0):
+    copies = [pltpu.make_async_copy(a, b, sems.at[first + i]) for i, (a, b) in enumerate(pairs)]
+    for copy in copies:
+        copy.start()
+    return copies
+
+
+def wait(copies):
+    for copy in copies:
+        copy.wait()
+
+
+def stacked(refs, whole, first=0):
+    rows = refs[0].shape[0]
+    return [(ref, whole.at[pl.ds((first + r) * rows, rows)]) for r, ref in enumerate(refs)]
 
 
 def lane_half(value, half):
@@ -82,6 +106,16 @@
         lax.broadcasted_iota(jnp.int32, (n, n), 0) == lax.broadcasted_iota(jnp.int32, (n, n), 1)
     ).astype(bf16)
     return mm_t(eye, value).astype(bf16)
+
+
+def fetch_kernel(*refs):
+    n = (len(refs) - 1) // 2
+    wait(bring(list(zip(refs[:n], refs[n : 2 * n])), refs[2 * n]))
+
+
+def fetch(arrays, us=1.0):
+    outs = [(a.shape, a.dtype) for a in arrays]
+    return call(fetch_kernel, outs, arrays, [pltpu.SemaphoreType.DMA((len(arrays),))], 2, us, range(len(arrays)))
 
 
 def pack_kernel(part, me, gain, *refs):
@@ -125,28 +159,35 @@
     return x * inverse_root(x)
 
 
-def enter_kernel(core, own, other, x_ref, y_ref, norm_ref):
+def enter_kernel(core, own, other, x_ref, y_ref, norm_ref, x_far, sems):
     half = own.shape[1] // 2
     first = core[0] == 0
     for ref, at in ((x_ref, slice(0, half)), (y_ref, slice(half, 2 * half))):
         ref[:, :half] = jnp.where(first, own[:, at], other[:, at])
         ref[:, half:] = jnp.where(first, other[:, at], own[:, at])
+    kept = bring([(x_ref, x_far)], sems)
     norm_ref[...] = normed(x_ref[...].astype(f32)).astype(bf16)
-
-
-def project_kernel(n0, n1, n2, n3, w, q_ref, kv_ref, all_n):
+    wait(kept)
+
+
+def project_kernel(n0, n1, n2, n3, w, q_ref, kv_ref, n_far, all_n, sems):
+    hp = w.shape[2] // 4
     toks = n0.shape[0]
-    hp = w.shape[2] // 4
-    for r, ref in enumerate((n0, n1, n2, n3)):
-        all_n[r * toks : (r + 1) * toks, :] = ref[...]
+    blocks = bring(stacked((n1, n2, n3), all_n, 1), sems)
+    all_n[:toks, :] = n0[...]
+    wait(blocks)
+    kept = bring([(all_n, n_far)], sems, 3)
     for j in range(2):
-        q_ref[:, j * hp : (j + 1) * hp] = mm(all_n[...], w[j, :, :hp]).astype(bf16)
-        kv = mm(all_n[...], w[j, :, hp : 3 * hp]).astype(bf16)
-        kv_ref[:, 2 * j * hp : 2 * (j + 1) * hp] = kv
-
-
-def attend_kernel(scale, core, q_ref, kv, kvf, doc_q, doc_kn, doc_kf, w, p_ref, att_ref, own_ref, b1, b2, b3):
+        out = mm(all_n[...], w[j, :, : 3 * hp])
+        q_ref[:, j * hp : (j + 1) * hp] = out[:, :hp].astype(bf16)
+        kv_ref[:, 2 * j * hp : 2 * (j + 1) * hp] = out[:, hp:].astype(bf16)
+    wait(kept)
+
+
+def attend_kernel(scale, core, q_ref, kv, kvf, doc_q, doc_kn, doc_kf, w_far, p_far, q_far, kv_far, kvf_far, att_far, own_ref, b1, b2, b3, p_ref, att_ref, w, sems, p_sems):
     hp = q_ref.shape[1] // 2
+    weights = bring([(w_far.at[j, :, pl.ds(3 * hp, hp)], w.at[j]) for j in range(2)], sems)
+    kept = bring([(q_ref, q_far), (kv, kv_far), (kvf, kvf_far)], sems, 2)
     rows = doc_q.shape[0]
     toks = q_ref.shape[0] // rows
     key_pos = lax.broadcasted_iota(jnp.int32, (toks, toks), 0)
@@ -175,25 +216,34 @@
                 total = jnp.sum(en, axis=0, keepdims=True) + jnp.sum(ef, axis=0, keepdims=True)
                 inv = 1.0 / total
                 p = (jnp.concatenate([en, ef], axis=0) * inv).astype(bf16)
-                p_ref[(r * 2 + j) * 2 + h] = p
+                at_head = (r * 2 + j) * 2 + h
+                p_ref[at_head] = p
+                kept += bring([(p_ref.at[at_head], p_far.at[at_head])], p_sems, at_head)
                 pieces.append(mm(v_t[h * DH : (h + 1) * DH, :], p))
             att_ref[at, j * hp : (j + 1) * hp] = flipped(jnp.concatenate(pieces, axis=0).astype(bf16)).astype(bf16)
-        out = mm_t(att_ref[at, :hp], w[0, :, 3 * hp :]) + mm_t(att_ref[at, hp:], w[1, :, 3 * hp :])
+        if r == 0:
+            wait(weights)
+        out = mm_t(att_ref[at, :hp], w[0]) + mm_t(att_ref[at, hp:], w[1])
         if r == 0:
             own_ref[...] = out
         else:
             (b1, b2, b3)[r - 1][...] = out.astype(bf16)
-
-
-def attend_back_kernel(scale, g0, g1, g2, g3, w, q_ref, kv, kvf, p_ref, dq_ref, near_ref, far_ref, all_g, ga_ref):
+    wait(kept + bring([(att_ref, att_far)], sems, 5))
+
+
+def attend_back_kernel(scale, g0, g1, g2, g3, w_out, q_ref, kv, kvf, p_ref, hidden_ref, w_far, dq_ref, near_ref, far_ref, w, g_far, hidden_far, all_g, ga_ref, sems):
     hp = q_ref.shape[1] // 2
     toks = g0.shape[0]
-    for r, g_ref in enumerate((g0, g1, g2, g3)):
+    out = bring([(w_far.at[j, :, pl.ds(0, 3 * hp)], w.at[j]) for j in range(2)] + [(hidden_ref, hidden_far)], sems)
+    for r, ref in enumerate((g0, g1, g2, g3)):
+        all_g[r * toks : (r + 1) * toks, :] = ref[...]
+    out += bring([(all_g, g_far)], sems, 3)
+    for j in range(2):
+        ga_ref[:, j * hp : (j + 1) * hp] = mm(all_g[...], w_out[j]).astype(bf16)
+    for r in range(4):
         at = slice(r * toks, (r + 1) * toks)
-        all_g[at, :] = g_ref[...]
         for j in range(2):
-            ga_ref[...] = mm(g_ref[...], w[j, :, 3 * hp :]).astype(bf16)
-            g = ga_ref[...]
+            g = ga_ref[at, j * hp : (j + 1) * hp]
             base = 2 * j * hp
             q2 = q_ref[at, j * hp : (j + 1) * hp]
             v = jnp.concatenate([kv[at, base + hp : base + 2 * hp], kvf[at, base + hp : base + 2 * hp]], axis=0)
@@ -219,19 +269,23 @@
             near_ref[at, base + hp : base + 2 * hp] = dv[:toks]
             far_ref[at, base : base + hp] = dk[toks:].astype(bf16)
             far_ref[at, base + hp : base + 2 * hp] = dv[toks:].astype(bf16)
-
-
-def project_back_kernel(dq, near_g, back, w, gown, goth, own_ref, b1, b2, b3, acc):
+    wait(out)
+
+
+def project_back_kernel(dq, near_g, back, w, n_far, g_far, att_far, gown, goth, own_ref, b1, b2, b3, n_ref, g_ref, att_ref, acc, sems):
     hp = dq.shape[1] // 2
     toks = own_ref.shape[0]
+    got = bring([(n_far, n_ref), (g_far, g_ref), (att_far, att_ref)], sems)
     for j, g in enumerate((gown, goth)):
         g[:, :hp] = dq[:, j * hp : (j + 1) * hp]
         both = slice(2 * j * hp, 2 * (j + 1) * hp)
         g[:, hp:] = (near_g[:, both] + back[:, both].astype(f32)).astype(bf16)
-    acc[...] = mm_t(gown[...], w[0, :, : 3 * hp]) + mm_t(goth[...], w[1, :, : 3 * hp])
+    acc[...] = mm_t(gown[...], w[0])
+    acc[...] += mm_t(goth[...], w[1])
     own_ref[...] = acc[:toks]
     for r, ref in enumerate((b1, b2, b3)):
         ref[...] = acc[(r + 1) * toks : (r + 2) * toks].astype(bf16)
+    wait(got)
 
 
 def total_of(refs):
@@ -247,12 +301,13 @@
     norm_ref[...] = normed(value).astype(bf16)
 
 
-def ffn_kernel(n0, n1, n2, n3, y0, y1, y2, y3, w, mid, own_ref, b1, b2, b3, all_n, all_y, acc):
+def ffn_kernel(n0, n1, n2, n3, all_y, w, hidden, mid, all_n, hidden_far, own_far, b1, b2, b3, acc, sems):
     toks = n0.shape[0]
     ff = w.shape[2] // 3
-    for r in range(4):
-        all_n[r * toks : (r + 1) * toks, :] = (n0, n1, n2, n3)[r][...]
-        all_y[r * toks : (r + 1) * toks, :] = (y0, y1, y2, y3)[r][...]
+    blocks_n = bring(stacked((n1, n2, n3), all_n, 1), sems)
+    kept = bring([(hidden, hidden_far)], sems, 3)
+    all_n[:toks, :] = n0[...]
+    wait(blocks_n)
     for j in range(2):
         gate = mm(all_n[...], w[j, :, :ff])
         up = mm(all_n[...], w[j, :, ff : 2 * ff])
@@ -267,28 +322,49 @@
             acc[...] = part
         else:
             acc[...] += part
-    own_ref[...] = acc[:toks]
+    kept += bring([(acc.at[pl.ds(0, toks)], own_far)], sems, 4)
     for r, ref in enumerate((b1, b2, b3)):
         ref[...] = acc[(r + 1) * toks : (r + 2) * toks].astype(bf16)
-
-
-def ffn_out_kernel(mid, w, own_ref, b1, b2, b3, acc):
-    toks = own_ref.shape[0]
-    ff = w.shape[2] // 3
-    acc[...] = mm_t(mid[0, :, 2 * ff :], w[0, :, 2 * ff :]) + mm_t(mid[1, :, 2 * ff :], w[1, :, 2 * ff :])
-    own_ref[...] = acc[:toks]
+    wait(kept)
+
+
+def fetch_ffn_kernel(y0, y1, y2, y3, w_far, all_y, w, sems):
+    wait(bring(stacked((y0, y1, y2, y3), all_y) + [(w_far, w)], sems))
+
+
+def fetch_back_kernel(w_far, w, sems):
+    hp = w.shape[2]
+    wait(bring([(w_far.at[j, :, pl.ds(3 * hp, hp)], w.at[j]) for j in range(2)], sems))
+
+
+def ffn_out_kernel(mid, w_far, own_far, b1, b2, b3, w, acc, sems):
+    toks = b1.shape[0]
+    ff = w.shape[2]
+    weights = bring([(w_far.at[j, :, pl.ds(2 * ff, ff)], w.at[j]) for j in range(2)], sems)
+    weights[0].wait()
+    acc[...] = mm_t(mid[0, :, 2 * ff :], w[0])
+    weights[1].wait()
+    acc[...] += mm_t(mid[1, :, 2 * ff :], w[1])
+    kept = bring([(acc.at[pl.ds(0, toks)], own_far)], sems, 2)
     for r, ref in enumerate((b1, b2, b3)):
         ref[...] = acc[(r + 1) * toks : (r + 2) * toks].astype(bf16)
-
-
-def ffn_grads_kernel(all_n, all_y, mid, out):
+    wait(kept)
+
+
+def ffn_grads_kernel(all_n, y0, y1, y2, y3, mid, out_far, all_y, out, sems, out_sems):
     rows = out.shape[2]
     ff = out.shape[3] // 3
+    copies = bring(stacked((y0, y1, y2, y3), all_y), sems)
+    kept = []
     for i in range(4):
-        at = slice(i * rows, (i + 1) * rows)
         for j in range(2):
-            out[i, j, :, : 2 * ff] = outer_sum(all_n[:, at], mid[j, :, : 2 * ff]).astype(bf16)
-            out[i, j, :, 2 * ff :] = outer_sum(all_y[:, at], mid[j, :, 2 * ff :]).astype(bf16)
+            out[i, j, :, : 2 * ff] = outer_sum(all_n[:, i * rows : (i + 1) * rows], mid[j, :, : 2 * ff]).astype(bf16)
+    wait(copies)
+    for i in range(4):
+        for j in range(2):
+            out[i, j, :, 2 * ff :] = outer_sum(all_y[:, i * rows : (i + 1) * rows], mid[j, :, 2 * ff :]).astype(bf16)
+            kept += bring([(out.at[i, j], out_far.at[i, j])], out_sems, 2 * i + j)
+    wait(kept)
 
 
 def split_halves(core, value, own, give):
@@ -298,8 +374,9 @@
     give[...] = jnp.where(first, value[:, half:], value[:, :half])
 
 
-def final_kernel(core, hidden, b0, b1, b2, b3, own, give):
-    split_halves(core, (hidden[...] + total_of((b0, b1, b2, b3))).astype(bf16), own, give)
+def final_kernel(core, hidden_far, own_far, b1, b2, b3, own, give, hidden, part, sems):
+    wait(bring([(hidden_far, hidden), (own_far, part)], sems))
+    split_halves(core, (hidden[...] + total_of((part, b1, b2, b3))).astype(bf16), own, give)
 
 
 def norm_back(x, grad):
@@ -340,30 +417,17 @@
         ref[:, half:] = jnp.where(first, other[:, at], own[:, at])
 
 
-def attn_grads_kernel(core, all_n, all_g, g0, g1, att, own, oth):
-    hp = att.shape[1] // 2
-    first = core[0] == 0
-    for j, out in enumerate((own, oth)):
-        mine = first if j == 0 else core[0] == 1
-        out[:, : 3 * hp] = outer_sum(all_n[...], jnp.where(mine, g0[...], g1[...])).astype(bf16)
-        out[:, 3 * hp :] = outer_sum(all_g[...], jnp.where(mine, att[:, :hp], att[:, hp:])).astype(bf16)
-
-
-def core_sum_kernel(far, own, other, t0, t1, t2, t3):
-    rows = t0.shape[0]
-    for k, ref in enumerate((t0, t1, t2, t3)):
-        at = pl.ds(pl.multiple_of(lax.rem(far[0] + k, 4) * rows, rows), rows)
-        ref[...] = (own[at, :].astype(f32) + other[at, :].astype(f32)).astype(bf16)
-
-
-def far_sum_kernel(me, t0, t1, t2, t3, s0, s1, s2, s3):
-    rows = s0.shape[0]
-    for k, ref in enumerate((s0, s1, s2, s3)):
-        at = pl.ds(pl.multiple_of((me[0] ^ k) * rows, rows), rows)
-        total = t0[at, :].astype(f32)
-        for other in (t1, t2, t3):
-            total = total + other[at, :].astype(f32)
-        ref[...] = total.astype(bf16)
+def attn_grads_kernel(all_n, all_g, g0, g1, att, out_far, out, sems):
+    rows = out.shape[2]
+    hp = out.shape[3] // 4
+    kept = []
+    for i in range(4):
+        at = slice(i * rows, (i + 1) * rows)
+        for j, g in enumerate((g0, g1)):
+            out[i, j, :, : 3 * hp] = outer_sum(all_n[:, at], g[...]).astype(bf16)
+            out[i, j, :, 3 * hp :] = outer_sum(all_g[:, at], att[:, j * hp : (j + 1) * hp]).astype(bf16)
+            kept += bring([(out.at[i, j], out_far.at[i, j])], sems, 2 * i + j)
+    wait(kept)
 
 
 def pick_kernel(me, part, s0, s1, s2, s3):
@@ -501,73 +565,136 @@
     token_low = ((toks, width), bf16)
     half_low = ((toks, half_width), bf16)
     whole = ((group, width), bf16)
+    sems = pltpu.SemaphoreType.DMA
+    slab_low, slab_full, all_low = pltpu.VMEM((toks, width), bf16), pltpu.VMEM((toks, width), f32), pltpu.VMEM(*whole)
     acc = pltpu.VMEM((group, width), f32)
+    attn_cols = pltpu.VMEM((2, width, 3 * hp), bf16)
+    out_cols = pltpu.VMEM((2, width, hp), bf16)
+    q_shape, kv_shape = ((group, 2 * hp), bf16), ((group, 4 * hp), bf16)
+    head_count = 4 * 2 * hp // DH
+    probs_shape = ((head_count, 2 * toks, toks), bf16)
+    ffn_w_shape = ((2, width, 3 * ff_pad), bf16)
 
     own, give = call(collect_kernel, [token_low, token_low], [core_ref, slot_row, received])
-    x, grad_low, norm = call(enter_kernel, [token_low] * 3, [core_ref, own, swap(give)])
+    x, grad_low, norm, x_far = call(
+        enter_kernel, [token_low] * 4, [core_ref, own, swap(give)], [sems((1,))], far_outs=(3,)
+    )
     norm_a = gather_near(norm)
     grad_y = gather_near(grad_low)
+    (attn_near,) = fetch([attn_w])
     q, kv, norm_a_all = call(
         project_kernel,
-        [((group, 2 * hp), bf16), ((group, 4 * hp), bf16), whole],
-        [after(norm, docs, ffn_flat), *norm_a[1:], attn_w],
-        us=2,
-    )
-    kv_far = swap(kv)
-    probs, attended, *branch = call(
+        [q_shape, kv_shape, whole],
+        [after(norm, docs, ffn_flat), *norm_a[1:], attn_near],
+        [all_low, sems((4,))],
+        us=0,
+        far_args=range(1, 4),
+        far_outs=(2,),
+    )
+    probs, q_far, kv_far, kvf_far, attended, *branch = call(
         functools.partial(attend_kernel, score_scale),
-        [((4 * 2 * hp // DH, 2 * toks, toks), bf16), ((group, 2 * hp), bf16), *slab],
-        [core_ref, q, kv, kv_far, *docs, attn_w],
-        us=6,
+        [probs_shape, q_shape, kv_shape, kv_shape, q_shape, *slab],
+        [core_ref, q, kv, swap(kv), *docs, attn_w],
+        [pltpu.VMEM(*probs_shape), pltpu.VMEM(*q_shape), out_cols, sems((6,)), sems((head_count,))],
+        us=0,
+        far_args=(7,),
+        far_outs=range(5),
     )
     branch = after(branch, grad_y)
     hidden, norm = call(middle_kernel, [slab[0], token_low], [x, branch[0], *scatter_near(branch[1:])])
     norm_f = gather_near(norm)
-    mid, grad_norm, *grad_norm_low, norm_f_all, grad_y_all = call(
-        ffn_kernel, [((2, group, 3 * ff_pad), bf16), *slab, whole, whole], [*norm_f, *grad_y, ffn_w], [acc], 12, 7
-    )
-    branch = call(ffn_out_kernel, slab, [mid, ffn_w], [acc], us=2)
+    y_all, ffn_near = call(
+        fetch_ffn_kernel, [whole, ffn_w_shape], [*grad_y, ffn_w], [sems((5,))], us=2, far_args=range(5)
+    )
+    mid, norm_f_all, hidden, grad_norm, *grad_norm_low = call(
+        ffn_kernel,
+        [((2, group, 3 * ff_pad), bf16), whole, slab[0], *slab],
+        [*norm_f, y_all, ffn_near, hidden],
+        [acc, sems((5,))],
+        12,
+        7,
+        range(1, 4),
+        (2, 3),
+    )
+    branch = call(
+        ffn_out_kernel,
+        slab,
+        [mid, ffn_w],
+        [pltpu.VMEM((2, width, ff_pad), bf16), acc, sems((3,))],
+        6,
+        2,
+        (1,),
+        (0,),
+    )
+    ffn_grads_shape = ((4, 2, width // 4, 3 * ff_pad), bf16)
     (ffn_grads,) = call(
-        ffn_grads_kernel, [((4, 2, width // 4, 3 * ff_pad), bf16)], [norm_f_all, grad_y_all, mid], (), 12, 4
+        ffn_grads_kernel,
+        [ffn_grads_shape],
+        [norm_f_all, *grad_y, mid],
+        [all_low, pltpu.VMEM(*ffn_grads_shape), sems((4,)), sems((8,))],
+        12,
+        4,
+        range(1, 5),
+        (0,),
     )
     grad_hidden, grad_hidden_low = call(
-        middle_back_kernel, [slab[0], token_low], [hidden, grad_low, grad_norm, *scatter_near(grad_norm_low)]
+        middle_back_kernel,
+        [slab[0], token_low],
+        [*fetch([hidden, grad_low]), *fetch([grad_norm]), *scatter_near(grad_norm_low)],
     )
     grad_branch = gather_near(grad_hidden_low)
     final_parts = scatter_near(after(branch[1:], grad_hidden_low))
 
-    if direct:
-        ffn_part = lax.psum_scatter(ffn_grads.reshape(-1, 3 * ff_pad), FAR + (CORE,), scatter_dimension=0, tiled=True)
-    else:
-        ordered = jnp.moveaxis(ffn_grads, 1, 0).reshape(2, width, 3 * ff_pad)
-        ordered = jnp.stack([far_rows(ordered[i], far_sizes, rows).reshape(far, -1, 3 * ff_pad) for i in range(2)], axis=1)
-        ffn_part = lax.psum_scatter(ordered.reshape(-1, 3 * ff_pad), FAR + (CORE,), scatter_dimension=0, tiled=True)
-
-    grad_q, grad_kv, far_give, grad_branch_all = call(
+    def reduced(grads):
+        cols = grads.shape[-1]
+        if not direct:
+            halves = jnp.moveaxis(grads, 1, 0).reshape(2, width, cols)
+            grads = jnp.stack([far_rows(half, far_sizes, rows).reshape(far, -1, cols) for half in halves], axis=1)
+        return lax.psum_scatter(grads.reshape(-1, cols), FAR + (CORE,), scatter_dimension=0, tiled=True)
+
+    ffn_part = reduced(ffn_grads)
+
+    grad_q, grad_kv, far_give, attn_near, grad_branch_all, grad_hidden = call(
         functools.partial(attend_back_kernel, score_scale),
-        [((group, 2 * hp), bf16), ((group, 4 * hp), f32), ((group, 4 * hp), bf16), whole],
-        [*grad_branch, attn_w, q, kv, kv_far, probs],
-        [pltpu.VMEM((toks, hp), bf16)],
+        [q_shape, ((group, 4 * hp), f32), kv_shape, ((2, width, 3 * hp), bf16), whole, slab[0]],
+        [*grad_branch, *call(fetch_back_kernel, [((2, width, hp), bf16)], [attn_w], [sems((2,))], far_args=(0,)),
+         *fetch([q_far, kv_far, kvf_far, probs]), grad_hidden, attn_w],
+        [all_low, pltpu.VMEM(*q_shape), sems((4,))],
         us=7,
-    )
-    out_own, out_give = call(final_kernel, [half_low, half_low], [core_ref, hidden, branch[0], *final_parts])
-    gqkv_own, gqkv_oth, *grad_norm = call(
+        far_args=(10,),
+        far_outs=(4, 5),
+    )
+    out_own, out_give = call(
+        final_kernel,
+        [half_low, half_low],
+        [core_ref, hidden, branch[0], *after(final_parts, grad_q)],
+        [slab_full, slab_full, sems((2,))],
+        far_args=(1, 2),
+    )
+    gqkv_own, gqkv_oth, own_norm, *grad_norm, n_all, g_all, att = call(
         project_back_kernel,
-        [((group, 3 * hp), bf16), ((group, 3 * hp), bf16), *slab],
-        [grad_q, grad_kv, swap(after(far_give, out_own)), attn_w],
-        [acc],
+        [((group, 3 * hp), bf16), ((group, 3 * hp), bf16), *slab, whole, whole, q_shape],
+        [grad_q, grad_kv, swap(after(far_give, out_own)), attn_near, norm_a_all, grad_branch_all, attended],
+        [acc, sems((3,))],
         us=2,
-    )
-    arriving = scatter_near(grad_norm[1:])
-    grads_own, grads_oth = call(
+        far_args=(4, 5, 6),
+    )
+    arriving = scatter_near(grad_norm)
+    attn_grads_shape = ((4, 2, width // 4, 4 * hp), bf16)
+    (attn_grads,) = call(
         attn_grads_kernel,
-        [((width, 4 * hp), bf16)] * 2,
-        [core_ref, norm_a_all, grad_branch_all, gqkv_own, gqkv_oth, attended],
-        us=3,
-    )
-    other = swap(grads_oth)
+        [attn_grads_shape],
+        [n_all, g_all, gqkv_own, gqkv_oth, att],
+        [pltpu.VMEM(*attn_grads_shape), sems((8,))],
+        8,
+        3,
+        far_outs=(0,),
+    )
+    attn_part = reduced(after(attn_grads, ffn_part, arriving))
     own, give = call(
-        leave_kernel, [token_low, token_low], [core_ref, x, grad_hidden, grad_norm[0], *arriving, out_own, out_give]
+        leave_kernel,
+        [token_low, token_low],
+        [core_ref, *fetch([x_far, grad_hidden]), own_norm, *arriving, out_own, out_give],
     )
 
     def finished(pieces, weights, gain, part, size):
@@ -594,20 +721,17 @@
         return back.reshape(slot_count, width)
 
     if direct:
-        planes = call(core_sum_kernel, [((4 * rows, 4 * hp), bf16)] * 4, [far_ref, grads_own, other])
-        back = returned(own, planes)
-        planes = [planes[0]] + [far_shift(planes[k], k) for k in range(1, 4)]
-        pieces = call(far_sum_kernel, [((rows, 4 * hp), bf16)] * 4, [near_ref, *planes])
-        pieces = [pieces[0]] + scatter_near(pieces[1:])
-        *attn_grads, sum_a = finished(pieces, attn_weights, gain_a, hp, hp)
-        pieces = call(pick_kernel, [((rows, 3 * ff_pad), bf16)] * 4, [near_ref, ffn_part])
-        pieces = [pieces[0]] + scatter_near(pieces[1:])
-        *ffn_grads, sum_f = finished(pieces, ffn_weights, gain_f, ff_part, ff_pad)
+        back = returned(own)
+
+        def pieces_of(part):
+            pieces = call(pick_kernel, [((rows, part.shape[1]), bf16)] * 4, [near_ref, part])
+            return [pieces[0]] + scatter_near(pieces[1:])
+
+        *ffn_grads, sum_f = finished(pieces_of(ffn_part), ffn_weights, gain_f, ff_part, ff_pad)
+        *attn_grads, sum_a = finished(pieces_of(attn_part), attn_weights, gain_a, hp, hp)
         back = after(back, ffn_grads, attn_grads)
     else:
         back = returned(own)
-        total = far_rows((grads_own.astype(f32) + other.astype(f32)).astype(bf16), far_sizes, rows)
-        attn_part = lax.psum_scatter(total, FAR, scatter_dimension=0, tiled=True)
         *attn_grads, sum_a = finished_plain(attn_part, attn_weights, gain_a, hp, hp)
         *ffn_grads, sum_f = finished_plain(ffn_part, ffn_weights, gain_f, ff_part, ff_pad)
     gains = jnp.concatenate([sum_a, sum_f], axis=1).T

time: 306 us -> 272 us (0.89)
  local copies, waits for them, and re-layouts: 38.4 us -> 5.91 us
  Pallas kernels: 40.7 us -> 59.1 us
  waiting for transfers between devices: 143 us -> 130 us
  starting transfers between devices: 66.3 us -> 58.6 us
    ppermute x3 -> x0, waiting for transfers between devices: 43 us -> none  [far_shift(): return lax.ppermute(value, FAR, [(i, (i + k) % far) for i in range(far)])]
    reduce_scatter x1 -> x2, waiting for transfers between devices: 0.01 us -> 40.4 us  [reduced(): lax.psum_scatter(grads.reshape(-1, cols), FAR + (CORE,), scatter_dimensio...]
    unnamed x130 -> x44, local copies, waits for them, and re-layouts: 34.9 us -> 2.42 us
    pallas_call x25 -> x31, Pallas kernels: 40.7 us -> 59.1 us  [call(): pl.pallas_call(kernel, out_shape=[pltpu.HBM(shape, kind) if i in far_outs...]
    ppermute x39, waiting for transfers between devices: 70.7 us -> 59.4 us  [near(): return lax.ppermute(value, NEAR, [(i, i ^ k) for i in range(4)])]
    ppermute x3 -> x0, starting transfers between devices: 3.55 us -> none  [far_shift(): return lax.ppermute(value, FAR, [(i, (i + k) % far) for i in range(far)])]
    ppermute x7 -> x6, starting transfers between devices: 15.3 us -> 12.2 us  [swap(): return lax.ppermute(value, CORE, [(0, 1), (1, 0)])]
  transfers between devices with their start and end apart: 54 -> 51, of which waited for: 37 -> 28; matrix products, arithmetic and copies ran while one was open for 1% -> 1% of each run, Pallas kernels for 10% -> 16%
where the time goes in v3:
time: 272 us; the launch traced here: 270 us
  waiting for transfers between devices  130 us (48%)
  Pallas kernels  59.1 us (22%)
  starting transfers between devices  58.6 us (22%)
  between operations  14.3 us (5%)
  local copies, waits for them, and re-layouts  5.91 us (2%)
    ppermute x39, waiting for transfers between devices, near(): return lax.ppermute(value, NEAR, [(i, i ^ k) for i in range(4)])  59.4 us
    pallas_call x31, Pallas kernels, call(): pl.pallas_call(kernel, out_shape=[pltpu.HBM(shape, kind) if i in far_outs...  59.1 us
    reduce_scatter x2, waiting for transfers between devices, reduced(): lax.psum_scatter(grads.reshape(-1, cols), FAR + (CORE,), scatter_dimensio...  40.4 us
    ppermute x39, starting transfers between devices, near(): return lax.ppermute(value, NEAR, [(i, i ^ k) for i in range(4)])  36 us
    all_to_all x1, waiting for transfers between devices, body(): lax.all_to_all(both, DP, 0, 0, tiled=True).reshape(slot_count, width)  24.9 us
    ppermute x6, starting transfers between devices, swap(): return lax.ppermute(value, CORE, [(0, 1), (1, 0)])  12.2 us
    ppermute x6, waiting for transfers between devices, swap(): return lax.ppermute(value, CORE, [(0, 1), (1, 0)])  5.62 us
  transfers between devices with their start and end apart: 51, of which 28 were waited for; matrix products, arithmetic and copies ran while one was open for 1% of the time, Pallas kernels for 16%

profile of v3, /device:TPU:9, one launch (start us, length us, event | category | flops | bytes accessed | tf_op | source)
XLA Modules:
  0.0 270.4 jit_solution(18406113498698161246)
XLA Ops:
  7.3 1.3 dynamic-slice_bitcast_fusion
  10.0 1.3 collective-permute-start
  13.2 1.4 collective-permute-done.1.b2
  14.6 1.9 collective-permute-done.2.b3
  17.3 5.3 %all-to-all-start = ((bf16[16,32,1024]{2,1,0:T(8,128)(2,1)}), bf16[16,32,1024]{2,1,0:T(8,128)(2,1)S(1)}, u32[]{:S(2)}, u32[]{:S(2)}) async-start(bf16[16,32,1024]{2,1,0:T(8,128)(2,1)} %pad_maximum_fusion), calls=%async_computation | async-start | bytes 2097152 | tf_op jit(solution)/shard_map/all_to_all | solution.py:519
  30.5 1.3 collective-permute-done.6.b1
  31.8 5.1 %collective-permute-done.7.b2 = bf16[64,1152]{1,0:T(8,128)(2,1)S(1)} collective-permute-done((bf16[64,1152]{1,0:T(8,128)(2,1)S(1)}, bf16[64,1152]{1,0:T(8,128)(2,1)S(1)}, u32[]{:S(2)}, u32[]{:S(2)}) %collective-permute-start.7) | collective-permute-done | bytes 147488 | tf_op jit(solution)/shard_map/ppermute | solution.py:40
  37.8 24.9 %all-to-all-done = bf16[16,32,1024]{2,1,0:T(8,128)(2,1)S(1)} async-done(((bf16[16,32,1024]{2,1,0:T(8,128)(2,1)}), bf16[16,32,1024]{2,1,0:T(8,128)(2,1)S(1)}, u32[]{:S(2)}, u32[]{:S(2)}) %all-to-all-start) | async-done | bytes 1048608 | tf_op jit(solution)/shard_map/all_to_all | solution.py:519
  63.2 3.7 %collective-permute-start.9 = (bf16[128,1024]{1,0:T(8,128)(2,1)S(1)}, bf16[128,1024]{1,0:T(8,128)(2,1)S(1)}, u32[]{:S(2)}, u32[]{:S(2)}) collective-permute-start(bf16[128,1024]{1,0:T(8,128)(2,1)S(1)} %get-tuple-element.147), channel_id=1, source_target_pairs={{0,1},{1,0},{2,3},{3,2},{4,5},{5,4},{6,7},{7,6},{8,9},{9,8},{10,11... | collective-permute-start | bytes 786440 | tf_op jit(solution)/shard_map/ppermute | solution.py:36
  70.1 1.4 collective-permute-start.12
  71.7 1.7 shard_map.218.w
  73.4 3.0 %collective-permute-done.10.n1 = bf16[128,1024]{1,0:T(8,128)(2,1)S(1)} collective-permute-done((bf16[128,1024]{1,0:T(8,128)(2,1)S(1)}, bf16[128,1024]{1,0:T(8,128)(2,1)S(1)}, u32[]{:S(2)}, u32[]{:S(2)}) %collective-permute-start.10) | collective-permute-done | bytes 262176 | tf_op jit(solution)/shard_map/ppermute | solution.py:40
  76.4 6.4 %collective-permute-done.12.n3 = bf16[128,1024]{1,0:T(8,128)(2,1)S(1)} collective-permute-done((bf16[128,1024]{1,0:T(8,128)(2,1)S(1)}, bf16[128,1024]{1,0:T(8,128)(2,1)S(1)}, u32[]{:S(2)}, u32[]{:S(2)}) %collective-permute-start.12) | collective-permute-done | bytes 262176 | tf_op jit(solution)/shard_map/ppermute | solution.py:40
  83.5 2.4 shard_map.219
  87.1 1.5 collective-permute-start.14
  89.8 8.1 %shard_map.220 = (bf16[16,256,128]{2,1,0:T(8,128)(2,1)}, bf16[512,256]{1,0:T(8,128)(2,1)}, bf16[512,512]{1,0:T(8,128)(2,1)}, bf16[512,512]{1,0:T(8,128)(2,1)}, b...) custom-call(s32[1]{0:T(128)} %bitcast.core, ...), custom_call_target="tpu_custom_call" | custom-call | tf_op jit(solution)/shard_map/pallas_call | solution.py:66
  97.9 2.5 collective-permute-done.15.y2
  104.3 3.9 %collective-permute-done.17.b1 = bf16[128,1024]{1,0:T(8,128)(2,1)S(1)} collective-permute-done((bf16[128,1024]{1,0:T(8,128)(2,1)S(1)}, bf16[128,1024]{1,0:T(8,128)(2,1)S(1)}, u32[]{:S(2)}, u32[]{:S(2)}) %collective-permute-start.17) | collective-permute-done | bytes 262176 | tf_op jit(solution)/shard_map/ppermute | solution.py:40
  108.1 1.9 collective-permute-done.18.b2
  110.0 4.8 %collective-permute-done.19.b3 = bf16[128,1024]{1,0:T(8,128)(2,1)S(1)} collective-permute-done((bf16[128,1024]{1,0:T(8,128)(2,1)S(1)}, bf16[128,1024]{1,0:T(8,128)(2,1)S(1)}, u32[]{:S(2)}, u32[]{:S(2)}) %collective-permute-start.19) | collective-permute-done | bytes 262176 | tf_op jit(solution)/shard_map/ppermute | solution.py:40
  117.8 2.7 %shard_map.222 = (bf16[512,1024]{1,0:T(8,128)(2,1)S(1)}, bf16[2,1024,1152]{2,1,0:T(8,128)(2,1)S(1)}) custom-call(bf16[128,1024]{1,0:T(8,128)(2,1)} %copy-done.1, bf16[128,1024]{1,0:T(8,128)(2,1)} %copy-done.16, bf16[128,1024]{1,0:T(8,128)(2,1)} %collective-permute-done.15.y2, bf16[128,1024]{1,0:T(8,128)(2,1)} %collective-permute-done.16.y3, ...), custom_call_target="tpu_custom_call" | custom-call | flops 2000000000 | bytes 2000000 | tf_op jit(solution)/shard_map/pallas_call | solution.py:66
  120.6 2.9 %collective-permute-done.21.n2 = bf16[128,1024]{1,0:T(8,128)(2,1)S(1)} collective-permute-done((bf16[128,1024]{1,0:T(8,128)(2,1)S(1)}, bf16[128,1024]{1,0:T(8,128)(2,1)S(1)}, u32[]{:S(2)}, u32[]{:S(2)}) %collective-permute-start.21) | collective-permute-done | bytes 262176 | tf_op jit(solution)/shard_map/ppermute | solution.py:40
  123.4 2.7 %collective-permute-done.22.n3 = bf16[128,1024]{1,0:T(8,128)(2,1)S(1)} collective-permute-done((bf16[128,1024]{1,0:T(8,128)(2,1)S(1)}, bf16[128,1024]{1,0:T(8,128)(2,1)S(1)}, u32[]{:S(2)}, u32[]{:S(2)}) %collective-permute-start.22) | collective-permute-done | bytes 262176 | tf_op jit(solution)/shard_map/ppermute | solution.py:40
  126.8 7.5 %shard_map.223 = (bf16[2,512,1152]{2,1,0:T(8,128)(2,1)S(1)}, bf16[512,1024]{1,0:T(8,128)(2,1)S(1)}, f32[128,1024]{1,0:T(8,128)}, f32[128,1024]{1,0:T(8,128)}, bf...) custom-call(bf16[128,1024]{1,0:T(8,128)(2,1)S(1)} %get-tuple-element.165.n0, ...), custom_call_target="tpu_custom_call" | custom-call | flops 7000000000 | bytes 7000000 | tf_op jit(solution)/shard_map/pallas_call | solution.py:66
  134.4 4.7 %shard_map.236 = bf16[4,2,256,1152]{3,2,1,0:T(8,128)(2,1)} custom-call(bf16[512,1024]{1,0:T(8,128)(2,1)S(1)} %get-tuple-element.216.all_n, bf16[128,1024]{1,0:T(8,128)(2,1)} %copy-done.1, bf16[128,1024]{1,0:T(8,128)(2,1)} %copy-done.16, bf16[128,1024]{1,0:T(8,128)(2,1)} %collective-permute-done.15.y2, bf16[128,1024]{1,0:T(8,128)(2,1)} %collective-permute-done.16.y3, ...), custom_call_target="tpu_custom_call" | custom-call | flops 4000000000 | bytes 4000000 | tf_op jit(solution)/shard_map/pallas_call | solution.py:66
  139.1 2.3 collective-permute-start.23
  146.0 4.8 %collective-permute-done.24.b2 = bf16[128,1024]{1,0:T(8,128)(2,1)S(1)} collective-permute-done((bf16[128,1024]{1,0:T(8,128)(2,1)S(1)}, bf16[128,1024]{1,0:T(8,128)(2,1)S(1)}, u32[]{:S(2)}, u32[]{:S(2)}) %collective-permute-start.24) | collective-permute-done | bytes 262176 | tf_op jit(solution)/shard_map/ppermute | solution.py:40
  151.1 1.4 collective-permute-start.26
  153.8 1.7 shard_map.228
  155.5 3.4 %shard_map.231 = (f32[128,1024]{1,0:T(8,128)}, bf16[128,1024]{1,0:T(8,128)(2,1)S(1)}, bf16[128,1024]{1,0:T(8,128)(2,1)S(1)}, bf16[128,1024]{1,0:T(8,128)(2,1)S(1)}) custom-call(bf16[2,512,1152]{2,1,0:T(8,128)(2,1)S(1)} %copy-done.11, bf16[2,1024,1152]{2,1,0:T(8,128)(2,1)} %bitcast.56), custom_call_target="tpu_custom_call" | custom-call | flops 2000000000 | bytes 2000000 | tf_op jit(solution)/shard_map/pallas_call | solution.py:66
  158.9 1.4 collective-permute-start.29
  161.6 6.2 %shard_map.229 = (bf16[512,256]{1,0:T(8,128)(2,1)S(1)}, f32[512,512]{1,0:T(8,128)S(1)}, bf16[512,512]{1,0:T(8,128)(2,1)S(1)}, bf16[2,1024,384]{2,1,0:T(8,128)(2,...) custom-call(bf16[128,1024]{1,0:T(8,128)(2,1)S(1)} %get-tuple-element.176.g0, ...), custom_call_target="tpu_custom_call" | custom-call | flops 7000000000 | bytes 7000000 | tf_op jit(solution)/shard_map/pallas_call | solution.py:66
  167.8 4.9 %collective-permute-done.30.b2 = bf16[128,1024]{1,0:T(8,128)(2,1)S(1)} collective-permute-done((bf16[128,1024]{1,0:T(8,128)(2,1)S(1)}, bf16[128,1024]{1,0:T(8,128)(2,1)S(1)}, u32[]{:S(2)}, u32[]{:S(2)}) %collective-permute-start.30) | collective-permute-done | bytes 262176 | tf_op jit(solution)/shard_map/ppermute | solution.py:40
  173.2 1.4 shard_map.232
  174.5 5.2 %collective-permute-start.32 = (bf16[512,512]{1,0:T(8,128)(2,1)S(1)}, bf16[512,512]{1,0:T(8,128)(2,1)S(1)}, u32[]{:S(2)}, u32[]{:S(2)}) collective-permute-start(bf16[512,512]{1,0:T(8,128)(2,1)S(1)} %get-tuple-element.204), channel_id=1, source_target_pairs={{0,1},{1,0},{2,3},{3,2},{4,5},{5,4},{6,7},{7,6},{8,9},{9,8},{10,11... | collective-permute-start | bytes 1572872 | tf_op jit(solution)/shard_map/ppermute | solution.py:36
  179.7 1.5 collective-permute-done.32.back
  181.2 1.6 shard_map.233
  185.6 2.7 shard_map.239
  188.3 2.3 collective-permute-done.33.b1
  190.9 5.6 %collective-permute-done.35.b3 = bf16[128,1024]{1,0:T(8,128)(2,1)S(1)} collective-permute-done((bf16[128,1024]{1,0:T(8,128)(2,1)S(1)}, bf16[128,1024]{1,0:T(8,128)(2,1)S(1)}, u32[]{:S(2)}, u32[]{:S(2)}) %collective-permute-start.35) | collective-permute-done | bytes 262176 | tf_op jit(solution)/shard_map/ppermute | solution.py:40
  198.0 1.6 collective-permute-start.36
  200.7 1.7 shard_map.235
  202.5 5.0 %all-to-all-start.1 = ((bf16[16,32,1024]{2,1,0:T(8,128)(2,1)}), bf16[16,32,1024]{2,1,0:T(8,128)(2,1)S(1)}, u32[]{:S(2)}, u32[]{:S(2)}) async-start(bf16[16,32,1024]{2,1,0:T(8,128)(2,1)} %bitcast.17), calls=%async_computation.1 | async-start | bytes 2097152 | tf_op jit(solution)/shard_map/all_to_all | solution.py:720
  210.2 40.4 %reduce-scatter.5.cloned.1.call-done.part = bf16[256,512]{1,0:T(8,128)(2,1)} async-done(((bf16[2048,512]{1,0:T(8,128)(2,1)}), bf16[256,512]{1,0:T(8,128)(2,1)}) %reduce-scatter.5.cloned.1.call-update) | async-done | bytes 262160 | tf_op jit(solution)/shard_map/reduce_scatter | solution.py:653
  254.3 2.3 shard_map.238
  256.6 1.4 collective-permute-done.42.s3
  259.8 1.9 collective-permute-done.44
  262.3 1.5 shard_map.242
  (157 shorter events, 49.8 us)
Async XLA Ops:
  7.2 64.5 %all-gather.3.cloned.1.call-start = ((), (), s32[]{:S(2)}) async-start(), calls=%async_computation.4 | async-start | bytes 2359296 | tf_op jit(solution)/shard_map/all_gather | solution.py:543
  11.3 3.3 %collective-permute-start.1 = (bf16[64,512]{1,0:T(8,128)(2,1)S(1)}, bf16[64,512]{1,0:T(8,128)(2,1)S(1)}, u32[]{:S(2)}, u32[]{:S(2)}) collective-permute-start(bf16[64,512]{1,0:T(8,128)(2,1)S(1)} %get-tuple-element.133), channel_id=1, source_target_pairs={{0,4},{2,6},{4,0},{6,2},{1,5},{3,7},{5,1},{7,3},{8,12},{10,14},{12... | collective-permute-start | bytes 196616 | tf_op jit(solution)/shard_map/ppermute | solution.py:40
  12.5 4.0 %collective-permute-start.2 = (bf16[64,512]{1,0:T(8,128)(2,1)S(1)}, bf16[64,512]{1,0:T(8,128)(2,1)S(1)}, u32[]{:S(2)}, u32[]{:S(2)}) collective-permute-start(bf16[64,512]{1,0:T(8,128)(2,1)S(1)} %get-tuple-element.134), channel_id=1, source_target_pairs={{0,6},{2,4},{4,2},{6,0},{1,7},{3,5},{5,3},{7,1},{8,14},{10,12},{12... | collective-permute-start | bytes 196616 | tf_op jit(solution)/shard_map/ppermute | solution.py:40
  17.3 45.3 %all-to-all-start = ((bf16[16,32,1024]{2,1,0:T(8,128)(2,1)}), bf16[16,32,1024]{2,1,0:T(8,128)(2,1)S(1)}, u32[]{:S(2)}, u32[]{:S(2)}) async-start(bf16[16,32,1024]{2,1,0:T(8,128)(2,1)} %pad_maximum_fusion), calls=%async_computation | async-start | bytes 2097152 | tf_op jit(solution)/shard_map/all_to_all | solution.py:519
  22.6 95.2 %all-gather.5.cloned.1.call-start = ((), (), s32[]{:S(2)}) async-start(), calls=%async_computation.5 | async-start | bytes 5308416 | tf_op jit(solution)/shard_map/all_gather | solution.py:543
  24.4 5.4 %collective-permute-start.3 = (s32[1,256]{1,0:T(1,128)S(1)}, s32[1,256]{1,0:T(1,128)S(1)}, u32[]{:S(2)}, u32[]{:S(2)}) collective-permute-start(s32[1,256]{1,0:T(1,128)S(1)} %copy-done.15), channel_id=1, source_target_pairs={{0,2},{2,0},{4,6},{6,4},{1,3},{3,1},{5,7},{7,5},{8,10},{10,8},{12,... | collective-permute-start | bytes 3080 | tf_op jit(solution)/shard_map/ppermute | solution.py:40
  25.6 4.8 %collective-permute-start.4 = (s32[1,256]{1,0:T(1,128)S(1)}, s32[1,256]{1,0:T(1,128)S(1)}, u32[]{:S(2)}, u32[]{:S(2)}) collective-permute-start(s32[1,256]{1,0:T(1,128)S(1)} %copy-done.15), channel_id=1, source_target_pairs={{0,4},{2,6},{4,0},{6,2},{1,5},{3,7},{5,1},{7,3},{8,12},{10,14},{12... | collective-permute-start | bytes 3080 | tf_op jit(solution)/shard_map/ppermute | solution.py:40
  26.8 3.7 %collective-permute-start.5 = (s32[1,256]{1,0:T(1,128)S(1)}, s32[1,256]{1,0:T(1,128)S(1)}, u32[]{:S(2)}, u32[]{:S(2)}) collective-permute-start(s32[1,256]{1,0:T(1,128)S(1)} %copy-done.15), channel_id=1, source_target_pairs={{0,6},{2,4},{4,2},{6,0},{1,7},{3,5},{5,3},{7,1},{8,14},{10,12},{12... | collective-permute-start | bytes 3080 | tf_op jit(solution)/shard_map/ppermute | solution.py:40
  27.4 4.4 %collective-permute-start.6 = (bf16[64,1152]{1,0:T(8,128)(2,1)S(1)}, bf16[64,1152]{1,0:T(8,128)(2,1)S(1)}, u32[]{:S(2)}, u32[]{:S(2)}) collective-permute-start(bf16[64,1152]{1,0:T(8,128)(2,1)S(1)} %get-tuple-element.140), channel_id=1, source_target_pairs={{0,2},{2,0},{4,6},{6,4},{1,3},{3,1},{5,7},{7,5},{8,10},{10,8},{12,... | collective-permute-start | bytes 442376 | tf_op jit(solution)/shard_map/ppermute | solution.py:40
  28.7 8.2 %collective-permute-start.7 = (bf16[64,1152]{1,0:T(8,128)(2,1)S(1)}, bf16[64,1152]{1,0:T(8,128)(2,1)S(1)}, u32[]{:S(2)}, u32[]{:S(2)}) collective-permute-start(bf16[64,1152]{1,0:T(8,128)(2,1)S(1)} %get-tuple-element.141), channel_id=1, source_target_pairs={{0,4},{2,6},{4,0},{6,2},{1,5},{3,7},{5,1},{7,3},{8,12},{10,14},{12... | collective-permute-start | bytes 442376 | tf_op jit(solution)/shard_map/ppermute | solution.py:40
  29.9 7.0 %collective-permute-start.8 = (bf16[64,1152]{1,0:T(8,128)(2,1)S(1)}, bf16[64,1152]{1,0:T(8,128)(2,1)S(1)}, u32[]{:S(2)}, u32[]{:S(2)}) collective-permute-start(bf16[64,1152]{1,0:T(8,128)(2,1)S(1)} %get-tuple-element.142), channel_id=1, source_target_pairs={{0,6},{2,4},{4,2},{6,0},{1,7},{3,5},{5,3},{7,1},{8,14},{10,12},{12... | collective-permute-start | bytes 442376 | tf_op jit(solution)/shard_map/ppermute | solution.py:40
  62.7 133.8 %reduce-scatter.3.cloned.1.call-start = ((), (), s32[]{:S(2)}) async-start(), calls=%async_computation.6 | async-start | bytes 5308416 | tf_op jit(solution)/shard_map/reduce_scatter | solution.py:653
  63.2 4.9 %collective-permute-start.9 = (bf16[128,1024]{1,0:T(8,128)(2,1)S(1)}, bf16[128,1024]{1,0:T(8,128)(2,1)S(1)}, u32[]{:S(2)}, u32[]{:S(2)}) collective-permute-start(bf16[128,1024]{1,0:T(8,128)(2,1)S(1)} %get-tuple-element.147), channel_id=1, source_target_pairs={{0,1},{1,0},{2,3},{3,2},{4,5},{5,4},{6,7},{7,6},{8,9},{9,8},{10,11... | collective-permute-start | bytes 786440 | tf_op jit(solution)/shard_map/ppermute | solution.py:36
  68.8 7.6 %collective-permute-start.10 = (bf16[128,1024]{1,0:T(8,128)(2,1)S(1)}, bf16[128,1024]{1,0:T(8,128)(2,1)S(1)}, u32[]{:S(2)}, u32[]{:S(2)}) collective-permute-start(bf16[128,1024]{1,0:T(8,128)(2,1)S(1)} %get-tuple-element.153.n0), channel_id=1, source_target_pairs={{0,2},{2,0},{4,6},{6,4},{1,3},{3,1},{5,7},{7,5},{8,10},{10,8},{12,... | collective-permute-start | bytes 786440 | tf_op jit(solution)/shard_map/ppermute | solution.py:40
  69.2 7.2 %collective-permute-start.11 = (bf16[128,1024]{1,0:T(8,128)(2,1)S(1)}, bf16[128,1024]{1,0:T(8,128)(2,1)S(1)}, u32[]{:S(2)}, u32[]{:S(2)}) collective-permute-start(bf16[128,1024]{1,0:T(8,128)(2,1)S(1)} %get-tuple-element.153.n0), channel_id=1, source_target_pairs={{0,4},{2,6},{4,0},{6,2},{1,5},{3,7},{5,1},{7,3},{8,12},{10,14},{12... | collective-permute-start | bytes 786440 | tf_op jit(solution)/shard_map/ppermute | solution.py:40
  70.1 12.6 %collective-permute-start.12 = (bf16[128,1024]{1,0:T(8,128)(2,1)S(1)}, bf16[128,1024]{1,0:T(8,128)(2,1)S(1)}, u32[]{:S(2)}, u32[]{:S(2)}) collective-permute-start(bf16[128,1024]{1,0:T(8,128)(2,1)S(1)} %get-tuple-element.153.n0), channel_id=1, source_target_pairs={{0,6},{2,4},{4,2},{6,0},{1,7},{3,5},{5,3},{7,1},{8,14},{10,12},{12... | collective-permute-start | bytes 786440 | tf_op jit(solution)/shard_map/ppermute | solution.py:40
  85.9 3.9 %collective-permute-start.13 = (bf16[512,512]{1,0:T(8,128)(2,1)S(1)}, bf16[512,512]{1,0:T(8,128)(2,1)S(1)}, u32[]{:S(2)}, u32[]{:S(2)}) collective-permute-start(bf16[512,512]{1,0:T(8,128)(2,1)S(1)} %get-tuple-element.155.kv), channel_id=1, source_target_pairs={{0,1},{1,0},{2,3},{3,2},{4,5},{5,4},{6,7},{7,6},{8,9},{9,8},{10,11... | collective-permute-start | bytes 1572872 | tf_op jit(solution)/shard_map/ppermute | solution.py:36
  87.1 10.8 %collective-permute-start.14 = (bf16[128,1024]{1,0:T(8,128)(2,1)S(1)}, bf16[128,1024]{1,0:T(8,128)(2,1)S(1)}, u32[]{:S(2)}, u32[]{:S(2)}) collective-permute-start(bf16[128,1024]{1,0:T(8,128)(2,1)S(1)} %get-tuple-element.160.y0.refs_1_), channel_id=1, source_target_pairs={{0,2},{2,0},{4,6},{6,4},{1,3},{3,1},{5,7},{7,5},{8,10},{10,8},{12,... | collective-permute-start | bytes 786440 | tf_op jit(solution)/shard_map/ppermute | solution.py:40
  88.6 11.8 %collective-permute-start.15 = (bf16[128,1024]{1,0:T(8,128)(2,1)S(1)}, bf16[128,1024]{1,0:T(8,128)(2,1)}, u32[]{:S(2)}, u32[]{:S(2)}) collective-permute-start(bf16[128,1024]{1,0:T(8,128)(2,1)S(1)} %get-tuple-element.160.y0.refs_1_), channel_id=1, source_target_pairs={{0,4},{2,6},{4,0},{6,2},{1,5},{3,7},{5,1},{7,3},{8,12},{10,14},{12... | collective-permute-start | bytes 786440 | tf_op jit(solution)/shard_map/ppermute | solution.py:40
  89.6 12.1 %collective-permute-start.16 = (bf16[128,1024]{1,0:T(8,128)(2,1)S(1)}, bf16[128,1024]{1,0:T(8,128)(2,1)}, u32[]{:S(2)}, u32[]{:S(2)}) collective-permute-start(bf16[128,1024]{1,0:T(8,128)(2,1)S(1)} %get-tuple-element.160.y0.refs_1_), channel_id=1, source_target_pairs={{0,6},{2,4},{4,2},{6,0},{1,7},{3,5},{5,3},{7,1},{8,14},{10,12},{12... | collective-permute-start | bytes 786440 | tf_op jit(solution)/shard_map/ppermute | solution.py:40
  101.6 6.5 %collective-permute-start.17 = (bf16[128,1024]{1,0:T(8,128)(2,1)S(1)}, bf16[128,1024]{1,0:T(8,128)(2,1)S(1)}, u32[]{:S(2)}, u32[]{:S(2)}) collective-permute-start(bf16[128,1024]{1,0:T(8,128)(2,1)S(1)} %get-tuple-element.162), channel_id=1, source_target_pairs={{0,2},{2,0},{4,6},{6,4},{1,3},{3,1},{5,7},{7,5},{8,10},{10,8},{12,... | collective-permute-start | bytes 786440 | tf_op jit(solution)/shard_map/ppermute | solution.py:40
  102.9 7.1 %collective-permute-start.18 = (bf16[128,1024]{1,0:T(8,128)(2,1)S(1)}, bf16[128,1024]{1,0:T(8,128)(2,1)S(1)}, u32[]{:S(2)}, u32[]{:S(2)}) collective-permute-start(bf16[128,1024]{1,0:T(8,128)(2,1)S(1)} %get-tuple-element.163), channel_id=1, source_target_pairs={{0,4},{2,6},{4,0},{6,2},{1,5},{3,7},{5,1},{7,3},{8,12},{10,14},{12... | collective-permute-start | bytes 786440 | tf_op jit(solution)/shard_map/ppermute | solution.py:40
  103.4 11.5 %collective-permute-start.19 = (bf16[128,1024]{1,0:T(8,128)(2,1)S(1)}, bf16[128,1024]{1,0:T(8,128)(2,1)S(1)}, u32[]{:S(2)}, u32[]{:S(2)}) collective-permute-start(bf16[128,1024]{1,0:T(8,128)(2,1)S(1)} %get-tuple-element.164), channel_id=1, source_target_pairs={{0,6},{2,4},{4,2},{6,0},{1,7},{3,5},{5,3},{7,1},{8,14},{10,12},{12... | collective-permute-start | bytes 786440 | tf_op jit(solution)/shard_map/ppermute | solution.py:40
  115.1 5.4 %collective-permute-start.20 = (bf16[128,1024]{1,0:T(8,128)(2,1)S(1)}, bf16[128,1024]{1,0:T(8,128)(2,1)S(1)}, u32[]{:S(2)}, u32[]{:S(2)}) collective-permute-start(bf16[128,1024]{1,0:T(8,128)(2,1)S(1)} %get-tuple-element.165.n0), channel_id=1, source_target_pairs={{0,2},{2,0},{4,6},{6,4},{1,3},{3,1},{5,7},{7,5},{8,10},{10,8},{12,... | collective-permute-start | bytes 786440 | tf_op jit(solution)/shard_map/ppermute | solution.py:40
  116.1 7.3 %collective-permute-start.21 = (bf16[128,1024]{1,0:T(8,128)(2,1)S(1)}, bf16[128,1024]{1,0:T(8,128)(2,1)S(1)}, u32[]{:S(2)}, u32[]{:S(2)}) collective-permute-start(bf16[128,1024]{1,0:T(8,128)(2,1)S(1)} %get-tuple-element.165.n0), channel_id=1, source_target_pairs={{0,4},{2,6},{4,0},{6,2},{1,5},{3,7},{5,1},{7,3},{8,12},{10,14},{12... | collective-permute-start | bytes 786440 | tf_op jit(solution)/shard_map/ppermute | solution.py:40
  117.1 9.0 %collective-permute-start.22 = (bf16[128,1024]{1,0:T(8,128)(2,1)S(1)}, bf16[128,1024]{1,0:T(8,128)(2,1)S(1)}, u32[]{:S(2)}, u32[]{:S(2)}) collective-permute-start(bf16[128,1024]{1,0:T(8,128)(2,1)S(1)} %get-tuple-element.165.n0), channel_id=1, source_target_pairs={{0,6},{2,4},{4,2},{6,0},{1,7},{3,5},{5,3},{7,1},{8,14},{10,12},{12... | collective-permute-start | bytes 786440 | tf_op jit(solution)/shard_map/ppermute | solution.py:40
  139.1 111.6 %reduce-scatter.5.cloned.1.call-start = ((), (), s32[]{:S(2)}) async-start(), calls=%async_computation.7 | async-start | bytes 2359296 | tf_op jit(solution)/shard_map/reduce_scatter | solution.py:653
  139.1 6.8 %collective-permute-start.23 = (bf16[128,1024]{1,0:T(8,128)(2,1)S(1)}, bf16[128,1024]{1,0:T(8,128)(2,1)S(1)}, u32[]{:S(2)}, u32[]{:S(2)}) collective-permute-start(bf16[128,1024]{1,0:T(8,128)(2,1)S(1)} %get-tuple-element.173), channel_id=1, source_target_pairs={{0,2},{2,0},{4,6},{6,4},{1,3},{3,1},{5,7},{7,5},{8,10},{10,8},{12,... | collective-permute-start | bytes 786440 | tf_op jit(solution)/shard_map/ppermute | solution.py:40
  141.4 9.3 %collective-permute-start.24 = (bf16[128,1024]{1,0:T(8,128)(2,1)S(1)}, bf16[128,1024]{1,0:T(8,128)(2,1)S(1)}, u32[]{:S(2)}, u32[]{:S(2)}) collective-permute-start(bf16[128,1024]{1,0:T(8,128)(2,1)S(1)} %get-tuple-element.174), channel_id=1, source_target_pairs={{0,4},{2,6},{4,0},{6,2},{1,5},{3,7},{5,1},{7,3},{8,12},{10,14},{12... | collective-permute-start | bytes 786440 | tf_op jit(solution)/shard_map/ppermute | solution.py:40
  142.1 8.7 %collective-permute-start.25 = (bf16[128,1024]{1,0:T(8,128)(2,1)S(1)}, bf16[128,1024]{1,0:T(8,128)(2,1)S(1)}, u32[]{:S(2)}, u32[]{:S(2)}) collective-permute-start(bf16[128,1024]{1,0:T(8,128)(2,1)S(1)} %get-tuple-element.175), channel_id=1, source_target_pairs={{0,6},{2,4},{4,2},{6,0},{1,7},{3,5},{5,3},{7,1},{8,14},{10,12},{12... | collective-permute-start | bytes 786440 | tf_op jit(solution)/shard_map/ppermute | solution.py:40
  151.1 10.0 %collective-permute-start.26 = (bf16[128,1024]{1,0:T(8,128)(2,1)S(1)}, bf16[128,1024]{1,0:T(8,128)(2,1)S(1)}, u32[]{:S(2)}, u32[]{:S(2)}) collective-permute-start(bf16[128,1024]{1,0:T(8,128)(2,1)S(1)} %get-tuple-element.176.g0), channel_id=1, source_target_pairs={{0,2},{2,0},{4,6},{6,4},{1,3},{3,1},{5,7},{7,5},{8,10},{10,8},{12,... | collective-permute-start | bytes 786440 | tf_op jit(solution)/shard_map/ppermute | solution.py:40
  152.5 9.1 %collective-permute-start.27 = (bf16[128,1024]{1,0:T(8,128)(2,1)S(1)}, bf16[128,1024]{1,0:T(8,128)(2,1)S(1)}, u32[]{:S(2)}, u32[]{:S(2)}) collective-permute-start(bf16[128,1024]{1,0:T(8,128)(2,1)S(1)} %get-tuple-element.176.g0), channel_id=1, source_target_pairs={{0,4},{2,6},{4,0},{6,2},{1,5},{3,7},{5,1},{7,3},{8,12},{10,14},{12... | collective-permute-start | bytes 786440 | tf_op jit(solution)/shard_map/ppermute | solution.py:40
  153.3 8.3 %collective-permute-start.28 = (bf16[128,1024]{1,0:T(8,128)(2,1)S(1)}, bf16[128,1024]{1,0:T(8,128)(2,1)S(1)}, u32[]{:S(2)}, u32[]{:S(2)}) collective-permute-start(bf16[128,1024]{1,0:T(8,128)(2,1)S(1)} %get-tuple-element.176.g0), channel_id=1, source_target_pairs={{0,6},{2,4},{4,2},{6,0},{1,7},{3,5},{5,3},{7,1},{8,14},{10,12},{12... | collective-permute-start | bytes 786440 | tf_op jit(solution)/shard_map/ppermute | solution.py:40
  158.9 8.9 %collective-permute-start.29 = (bf16[128,1024]{1,0:T(8,128)(2,1)S(1)}, bf16[128,1024]{1,0:T(8,128)(2,1)S(1)}, u32[]{:S(2)}, u32[]{:S(2)}) collective-permute-start(bf16[128,1024]{1,0:T(8,128)(2,1)S(1)} %get-tuple-element.197), channel_id=1, source_target_pairs={{0,2},{2,0},{4,6},{6,4},{1,3},{3,1},{5,7},{7,5},{8,10},{10,8},{12,... | collective-permute-start | bytes 786440 | tf_op jit(solution)/shard_map/ppermute | solution.py:40
  160.3 12.4 %collective-permute-start.30 = (bf16[128,1024]{1,0:T(8,128)(2,1)S(1)}, bf16[128,1024]{1,0:T(8,128)(2,1)S(1)}, u32[]{:S(2)}, u32[]{:S(2)}) collective-permute-start(bf16[128,1024]{1,0:T(8,128)(2,1)S(1)} %get-tuple-element.198), channel_id=1, source_target_pairs={{0,4},{2,6},{4,0},{6,2},{1,5},{3,7},{5,1},{7,3},{8,12},{10,14},{12... | collective-permute-start | bytes 786440 | tf_op jit(solution)/shard_map/ppermute | solution.py:40
  161.1 12.1 %collective-permute-start.31 = (bf16[128,1024]{1,0:T(8,128)(2,1)S(1)}, bf16[128,1024]{1,0:T(8,128)(2,1)S(1)}, u32[]{:S(2)}, u32[]{:S(2)}) collective-permute-start(bf16[128,1024]{1,0:T(8,128)(2,1)S(1)} %get-tuple-element.199), channel_id=1, source_target_pairs={{0,6},{2,4},{4,2},{6,0},{1,7},{3,5},{5,3},{7,1},{8,14},{10,12},{12... | collective-permute-start | bytes 786440 | tf_op jit(solution)/shard_map/ppermute | solution.py:40
  174.5 6.7 %collective-permute-start.32 = (bf16[512,512]{1,0:T(8,128)(2,1)S(1)}, bf16[512,512]{1,0:T(8,128)(2,1)S(1)}, u32[]{:S(2)}, u32[]{:S(2)}) collective-permute-start(bf16[512,512]{1,0:T(8,128)(2,1)S(1)} %get-tuple-element.204), channel_id=1, source_target_pairs={{0,1},{1,0},{2,3},{3,2},{4,5},{5,4},{6,7},{7,6},{8,9},{9,8},{10,11... | collective-permute-start | bytes 1572872 | tf_op jit(solution)/shard_map/ppermute | solution.py:36
  182.9 7.7 %collective-permute-start.33 = (bf16[128,1024]{1,0:T(8,128)(2,1)S(1)}, bf16[128,1024]{1,0:T(8,128)(2,1)S(1)}, u32[]{:S(2)}, u32[]{:S(2)}) collective-permute-start(bf16[128,1024]{1,0:T(8,128)(2,1)S(1)} %get-tuple-element.210), channel_id=1, source_target_pairs={{0,2},{2,0},{4,6},{6,4},{1,3},{3,1},{5,7},{7,5},{8,10},{10,8},{12,... | collective-permute-start | bytes 786440 | tf_op jit(solution)/shard_map/ppermute | solution.py:40
  183.6 7.3 %collective-permute-start.34 = (bf16[128,1024]{1,0:T(8,128)(2,1)S(1)}, bf16[128,1024]{1,0:T(8,128)(2,1)S(1)}, u32[]{:S(2)}, u32[]{:S(2)}) collective-permute-start(bf16[128,1024]{1,0:T(8,128)(2,1)S(1)} %get-tuple-element.211), channel_id=1, source_target_pairs={{0,4},{2,6},{4,0},{6,2},{1,5},{3,7},{5,1},{7,3},{8,12},{10,14},{12... | collective-permute-start | bytes 786440 | tf_op jit(solution)/shard_map/ppermute | solution.py:40
  184.5 12.0 %collective-permute-start.35 = (bf16[128,1024]{1,0:T(8,128)(2,1)S(1)}, bf16[128,1024]{1,0:T(8,128)(2,1)S(1)}, u32[]{:S(2)}, u32[]{:S(2)}) collective-permute-start(bf16[128,1024]{1,0:T(8,128)(2,1)S(1)} %get-tuple-element.212), channel_id=1, source_target_pairs={{0,6},{2,4},{4,2},{6,0},{1,7},{3,5},{5,3},{7,1},{8,14},{10,12},{12... | collective-permute-start | bytes 786440 | tf_op jit(solution)/shard_map/ppermute | solution.py:40
  202.5 56.6 %all-to-all-start.1 = ((bf16[16,32,1024]{2,1,0:T(8,128)(2,1)}), bf16[16,32,1024]{2,1,0:T(8,128)(2,1)S(1)}, u32[]{:S(2)}, u32[]{:S(2)}) async-start(bf16[16,32,1024]{2,1,0:T(8,128)(2,1)} %bitcast.17), calls=%async_computation.1 | async-start | bytes 2097152 | tf_op jit(solution)/shard_map/all_to_all | solution.py:720
  207.5 46.5 %collective-permute-start.37 = (bf16[64,1152]{1,0:T(8,128)(2,1)S(1)}, bf16[64,1152]{1,0:T(8,128)(2,1)S(1)}, u32[]{:S(2)}, u32[]{:S(2)}) collective-permute-start(bf16[64,1152]{1,0:T(8,128)(2,1)S(1)} %get-tuple-element.218), channel_id=1, source_target_pairs={{0,2},{2,0},{4,6},{6,4},{1,3},{3,1},{5,7},{7,5},{8,10},{10,8},{12,... | collective-permute-start | bytes 442376 | tf_op jit(solution)/shard_map/ppermute | solution.py:40
  208.8 45.5 %collective-permute-start.38 = (bf16[64,1152]{1,0:T(8,128)(2,1)S(1)}, bf16[64,1152]{1,0:T(8,128)(2,1)S(1)}, u32[]{:S(2)}, u32[]{:S(2)}) collective-permute-start(bf16[64,1152]{1,0:T(8,128)(2,1)S(1)} %get-tuple-element.219), channel_id=1, source_target_pairs={{0,4},{2,6},{4,0},{6,2},{1,5},{3,7},{5,1},{7,3},{8,12},{10,14},{12... | collective-permute-start | bytes 442376 | tf_op jit(solution)/shard_map/ppermute | solution.py:40
  210.0 44.4 %collective-permute-start.39 = (bf16[64,1152]{1,0:T(8,128)(2,1)S(1)}, bf16[64,1152]{1,0:T(8,128)(2,1)S(1)}, u32[]{:S(2)}, u32[]{:S(2)}) collective-permute-start(bf16[64,1152]{1,0:T(8,128)(2,1)S(1)} %get-tuple-element.220), channel_id=1, source_target_pairs={{0,6},{2,4},{4,2},{6,0},{1,7},{3,5},{5,3},{7,1},{8,14},{10,12},{12... | collective-permute-start | bytes 442376 | tf_op jit(solution)/shard_map/ppermute | solution.py:40
  251.6 5.0 %collective-permute-start.40 = (bf16[64,512]{1,0:T(8,128)(2,1)S(1)}, bf16[64,512]{1,0:T(8,128)(2,1)S(1)}, u32[]{:S(2)}, u32[]{:S(2)}) collective-permute-start(bf16[64,512]{1,0:T(8,128)(2,1)S(1)} %get-tuple-element.231), channel_id=1, source_target_pairs={{0,2},{2,0},{4,6},{6,4},{1,3},{3,1},{5,7},{7,5},{8,10},{10,8},{12,... | collective-permute-start | bytes 196616 | tf_op jit(solution)/shard_map/ppermute | solution.py:40
  252.8 3.8 %collective-permute-start.41 = (bf16[64,512]{1,0:T(8,128)(2,1)S(1)}, bf16[64,512]{1,0:T(8,128)(2,1)S(1)}, u32[]{:S(2)}, u32[]{:S(2)}) collective-permute-start(bf16[64,512]{1,0:T(8,128)(2,1)S(1)} %get-tuple-element.232), channel_id=1, source_target_pairs={{0,4},{2,6},{4,0},{6,2},{1,5},{3,7},{5,1},{7,3},{8,12},{10,14},{12... | collective-permute-start | bytes 196616 | tf_op jit(solution)/shard_map/ppermute | solution.py:40
  254.0 4.0 %collective-permute-start.42 = (bf16[64,512]{1,0:T(8,128)(2,1)S(1)}, bf16[64,512]{1,0:T(8,128)(2,1)S(1)}, u32[]{:S(2)}, u32[]{:S(2)}) collective-permute-start(bf16[64,512]{1,0:T(8,128)(2,1)S(1)} %get-tuple-element.233), channel_id=1, source_target_pairs={{0,6},{2,4},{4,2},{6,0},{1,7},{3,5},{5,3},{7,1},{8,14},{10,12},{12... | collective-permute-start | bytes 196616 | tf_op jit(solution)/shard_map/ppermute | solution.py:40
  259.1 3.2 %collective-permute-start.43 = (bf16[512,1024]{1,0:T(8,128)(2,1)S(1)}, bf16[512,1024]{1,0:T(8,128)(2,1)S(1)}, u32[]{:S(2)}, u32[]{:S(2)}) collective-permute-start(bf16[512,1024]{1,0:T(8,128)(2,1)S(1)} %bitcast.43), channel_id=1, source_target_pairs={{0,1},{1,0},{2,3},{3,2},{4,5},{5,4},{6,7},{7,6},{8,9},{9,8},{10,11... | collective-permute-start | bytes 3145736 | tf_op jit(solution)/shard_map/ppermute | solution.py:36
  (25 other events, 144.3 us)
Sparse Core Ops, SparseCore 0:
  17.4 44.0 all-gather.2
  63.1 53.2 all-gather.4
  139.2 56.0 reduce-scatter.2
  197.4 53.1 reduce-scatter.4

commit v4 on v3

--- a/solution.py
+++ b/solution.py
@@ -56,7 +56,7 @@
     return lax.rsqrt(jnp.mean(values * values, axis=-1, keepdims=True) + eps)
 
 
-def call(kernel, outs, args, scratch=(), limit=4, us=1.0, far_args=(), far_outs=()):
+def call(kernel, outs, args, scratch=(), limit=4, us=1.0, far_args=(), far_outs=(), aliases=None):
     def space(i, ndim, left):
         if i in left:
             return pl.BlockSpec(memory_space=pltpu.HBM)
@@ -72,6 +72,7 @@
         in_specs=[space(i, a.ndim, far_args) for i, a in enumerate(args)],
         out_specs=[space(i, 2, far_outs) for i in range(len(outs))],
         scratch_shapes=list(scratch),
+        input_output_aliases=aliases or {},
         compiler_params=pltpu.CompilerParams(vmem_limit_bytes=limit << 20),
         cost_estimate=pl.CostEstimate(flops=int(us * 1e9), bytes_accessed=int(us * 1e6), transcendentals=0),
     )(*args)
@@ -221,6 +222,7 @@
                 kept += bring([(p_ref.at[at_head], p_far.at[at_head])], p_sems, at_head)
                 pieces.append(mm(v_t[h * DH : (h + 1) * DH, :], p))
             att_ref[at, j * hp : (j + 1) * hp] = flipped(jnp.concatenate(pieces, axis=0).astype(bf16)).astype(bf16)
+        kept += bring([(att_ref.at[pl.ds(r * toks, toks)], att_far.at[pl.ds(r * toks, toks)])], sems, 5 + r)
         if r == 0:
             wait(weights)
         out = mm_t(att_ref[at, :hp], w[0]) + mm_t(att_ref[at, hp:], w[1])
@@ -228,7 +230,7 @@
             own_ref[...] = out
         else:
             (b1, b2, b3)[r - 1][...] = out.astype(bf16)
-    wait(kept + bring([(att_ref, att_far)], sems, 5))
+    wait(kept)
 
 
 def attend_back_kernel(scale, g0, g1, g2, g3, w_out, q_ref, kv, kvf, p_ref, hidden_ref, w_far, dq_ref, near_ref, far_ref, w, g_far, hidden_far, all_g, ga_ref, sems):
@@ -301,35 +303,40 @@
     norm_ref[...] = normed(value).astype(bf16)
 
 
-def ffn_kernel(n0, n1, n2, n3, all_y, w, hidden, mid, all_n, hidden_far, own_far, b1, b2, b3, acc, sems):
+def ffn_kernel(second, n0, n1, y, w, *refs):
+    if second:
+        mid, all_n, b0, b1, acc = refs[2:]
+    else:
+        hidden, mid, all_n, hidden_far, b0, b1, acc, sems = refs
+        kept = bring([(hidden, hidden_far)], sems)
     toks = n0.shape[0]
     ff = w.shape[2] // 3
-    blocks_n = bring(stacked((n1, n2, n3), all_n, 1), sems)
-    kept = bring([(hidden, hidden_far)], sems, 3)
-    all_n[:toks, :] = n0[...]
-    wait(blocks_n)
+    rows = pl.ds(2 * toks if second else 0, 2 * toks)
+    for r, ref in enumerate((n0, n1)):
+        all_n[pl.ds((2 * second + r) * toks, toks), :] = ref[...]
     for j in range(2):
-        gate = mm(all_n[...], w[j, :, :ff])
-        up = mm(all_n[...], w[j, :, ff : 2 * ff])
+        gate = mm(all_n[rows, :], w[j, :, :ff])
+        up = mm(all_n[rows, :], w[j, :, ff : 2 * ff])
         sig = jax.nn.sigmoid(gate)
         silu = gate * sig
-        mid[j, :, 2 * ff :] = (silu * up).astype(bf16)
-        grad_product = mm(all_y[...], w[j, :, 2 * ff :])
-        mid[j, :, :ff] = (grad_product * up * sig * (1.0 + gate * (1.0 - sig))).astype(bf16)
-        mid[j, :, ff : 2 * ff] = (grad_product * silu).astype(bf16)
-        part = mm_t(mid[j, :, : 2 * ff], w[j, :, : 2 * ff])
+        mid[rows, (4 + j) * ff : (5 + j) * ff] = (silu * up).astype(bf16)
+        grad_product = mm(y[...], w[j, :, 2 * ff :])
+        at = 2 * j * ff
+        mid[rows, at : at + ff] = (grad_product * up * sig * (1.0 + gate * (1.0 - sig))).astype(bf16)
+        mid[rows, at + ff : at + 2 * ff] = (grad_product * silu).astype(bf16)
+        part = mm_t(mid[rows, at : at + 2 * ff], w[j, :, : 2 * ff])
         if j == 0:
             acc[...] = part
         else:
             acc[...] += part
-    kept += bring([(acc.at[pl.ds(0, toks)], own_far)], sems, 4)
-    for r, ref in enumerate((b1, b2, b3)):
-        ref[...] = acc[(r + 1) * toks : (r + 2) * toks].astype(bf16)
-    wait(kept)
-
-
-def fetch_ffn_kernel(y0, y1, y2, y3, w_far, all_y, w, sems):
-    wait(bring(stacked((y0, y1, y2, y3), all_y) + [(w_far, w)], sems))
+    b0[...] = acc[:toks].astype(b0.dtype)
+    b1[...] = acc[toks:].astype(bf16)
+    if not second:
+        wait(kept)
+
+
+def fetch_ffn_kernel(y0, y1, y2, y3, w_far, y_first, y_second, w, sems):
+    wait(bring(stacked((y0, y1), y_first) + stacked((y2, y3), y_second) + [(w_far, w)], sems))
 
 
 def fetch_back_kernel(w_far, w, sems):
@@ -342,28 +349,30 @@
     ff = w.shape[2]
     weights = bring([(w_far.at[j, :, pl.ds(2 * ff, ff)], w.at[j]) for j in range(2)], sems)
     weights[0].wait()
-    acc[...] = mm_t(mid[0, :, 2 * ff :], w[0])
+    acc[...] = mm_t(mid[:, 4 * ff : 5 * ff], w[0])
     weights[1].wait()
-    acc[...] += mm_t(mid[1, :, 2 * ff :], w[1])
+    acc[...] += mm_t(mid[:, 5 * ff :], w[1])
     kept = bring([(acc.at[pl.ds(0, toks)], own_far)], sems, 2)
     for r, ref in enumerate((b1, b2, b3)):
         ref[...] = acc[(r + 1) * toks : (r + 2) * toks].astype(bf16)
     wait(kept)
 
 
-def ffn_grads_kernel(all_n, y0, y1, y2, y3, mid, out_far, all_y, out, sems, out_sems):
+def ffn_grads_kernel(all_n, y0, y1, y2, y3, mid, own_ref, out_far, own_far, all_y, out, sems, out_sems):
     rows = out.shape[2]
     ff = out.shape[3] // 3
     copies = bring(stacked((y0, y1, y2, y3), all_y), sems)
-    kept = []
+    kept = bring([(own_ref, own_far)], sems, 4)
     for i in range(4):
+        grads = outer_sum(all_n[:, i * rows : (i + 1) * rows], mid[:, : 4 * ff]).astype(bf16)
         for j in range(2):
-            out[i, j, :, : 2 * ff] = outer_sum(all_n[:, i * rows : (i + 1) * rows], mid[j, :, : 2 * ff]).astype(bf16)
-    wait(copies)
-    for i in range(4):
+            out[i, j, :, : 2 * ff] = grads[:, 2 * j * ff : 2 * (j + 1) * ff]
+        if i == 0:
+            wait(copies)
+        grads = outer_sum(all_y[:, i * rows : (i + 1) * rows], mid[:, 4 * ff :]).astype(bf16)
         for j in range(2):
-            out[i, j, :, 2 * ff :] = outer_sum(all_y[:, i * rows : (i + 1) * rows], mid[j, :, 2 * ff :]).astype(bf16)
-            kept += bring([(out.at[i, j], out_far.at[i, j])], out_sems, 2 * i + j)
+            out[i, j, :, 2 * ff :] = grads[:, j * ff : (j + 1) * ff]
+        kept += bring([(out.at[i], out_far.at[i])], out_sems, i)
     wait(kept)
 
 
@@ -417,23 +426,35 @@
         ref[:, half:] = jnp.where(first, other[:, at], own[:, at])
 
 
-def attn_grads_kernel(all_n, all_g, g0, g1, att, out_far, out, sems):
-    rows = out.shape[2]
-    hp = out.shape[3] // 4
-    kept = []
-    for i in range(4):
-        at = slice(i * rows, (i + 1) * rows)
-        for j, g in enumerate((g0, g1)):
-            out[i, j, :, : 3 * hp] = outer_sum(all_n[:, at], g[...]).astype(bf16)
-            out[i, j, :, 3 * hp :] = outer_sum(all_g[:, at], att[:, j * hp : (j + 1) * hp]).astype(bf16)
-            kept += bring([(out.at[i, j], out_far.at[i, j])], sems, 2 * i + j)
-    wait(kept)
-
-
-def pick_kernel(me, part, s0, s1, s2, s3):
+def attn_grads_kernel(core, all_n, all_g, g0, g1, att, own, oth):
+    hp = att.shape[1] // 2
+    for j, out in enumerate((own, oth)):
+        mine = core[0] == j
+        out[:, : 3 * hp] = outer_sum(all_n[...], jnp.where(mine, g0[...], g1[...])).astype(bf16)
+        out[:, 3 * hp :] = outer_sum(all_g[...], jnp.where(mine, att[:, :hp], att[:, hp:])).astype(bf16)
+
+
+def core_sum_kernel(far, own, other, t0, t1, t2, t3):
+    rows = t0.shape[0]
+    for k, ref in enumerate((t0, t1, t2, t3)):
+        at = pl.ds(pl.multiple_of(lax.rem(far[0] + k, 4) * rows, rows), rows)
+        ref[...] = (own[at, :].astype(f32) + other[at, :].astype(f32)).astype(bf16)
+
+
+def far_sum_kernel(me, t0, t1, t2, t3, s0, s1, s2, s3):
     rows = s0.shape[0]
     for k, ref in enumerate((s0, s1, s2, s3)):
-        ref[...] = part[pl.ds(pl.multiple_of((me[0] ^ k) * rows, rows), rows), :]
+        at = pl.ds(pl.multiple_of((me[0] ^ k) * rows, rows), rows)
+        total = t0[at, :].astype(f32)
+        for other in (t1, t2, t3):
+            total = total + other[at, :].astype(f32)
+        ref[...] = total.astype(bf16)
+
+
+def pick_kernel(me, part, s0, s1, s2, s3, sems):
+    rows = s0.shape[0]
+    pairs = [(part.at[pl.ds(pl.multiple_of((me[0] ^ k) * rows, rows), rows)], ref) for k, ref in enumerate((s0, s1, s2, s3))]
+    wait(bring(pairs, sems))
 
 
 def unpack_kernel(part, me, gain, s0, s1, s2, s3, *refs):
@@ -595,7 +616,7 @@
         functools.partial(attend_kernel, score_scale),
         [probs_shape, q_shape, kv_shape, kv_shape, q_shape, *slab],
         [core_ref, q, kv, swap(kv), *docs, attn_w],
-        [pltpu.VMEM(*probs_shape), pltpu.VMEM(*q_shape), out_cols, sems((6,)), sems((head_count,))],
+        [pltpu.VMEM(*probs_shape), pltpu.VMEM(*q_shape), out_cols, sems((9,)), sems((head_count,))],
         us=0,
         far_args=(7,),
         far_outs=range(5),
@@ -603,19 +624,38 @@
     branch = after(branch, grad_y)
     hidden, norm = call(middle_kernel, [slab[0], token_low], [x, branch[0], *scatter_near(branch[1:])])
     norm_f = gather_near(norm)
-    y_all, ffn_near = call(
-        fetch_ffn_kernel, [whole, ffn_w_shape], [*grad_y, ffn_w], [sems((5,))], us=2, far_args=range(5)
-    )
+    half_group = group // 2
+    half_whole = ((half_group, width), bf16)
+    y_first, y_second, ffn_near = call(
+        fetch_ffn_kernel,
+        [half_whole, half_whole, ffn_w_shape],
+        [*grad_y, ffn_w],
+        [sems((5,))],
+        us=2,
+        far_args=range(5),
+    )
+    mid_shape = ((group, 6 * ff_pad), bf16)
+    half_acc = pltpu.VMEM((half_group, width), f32)
     mid, norm_f_all, hidden, grad_norm, *grad_norm_low = call(
-        ffn_kernel,
-        [((2, group, 3 * ff_pad), bf16), whole, slab[0], *slab],
-        [*norm_f, y_all, ffn_near, hidden],
-        [acc, sems((5,))],
-        12,
-        7,
-        range(1, 4),
-        (2, 3),
-    )
+        functools.partial(ffn_kernel, False),
+        [mid_shape, whole, slab[0], slab[0], slab[1]],
+        [*norm_f[:2], y_first, ffn_near, hidden],
+        [half_acc, sems((1,))],
+        8,
+        3,
+        (),
+        (2,),
+    )
+    mid, norm_f_all, *more = call(
+        functools.partial(ffn_kernel, True),
+        [mid_shape, whole, slab[1], slab[1]],
+        [*norm_f[2:], y_second, ffn_near, mid, norm_f_all],
+        [half_acc],
+        8,
+        3,
+        aliases={4: 0, 5: 1},
+    )
+    grad_norm_low += more
     branch = call(
         ffn_out_kernel,
         slab,
@@ -627,20 +667,20 @@
         (0,),
     )
     ffn_grads_shape = ((4, 2, width // 4, 3 * ff_pad), bf16)
-    (ffn_grads,) = call(
+    ffn_grads, grad_norm = call(
         ffn_grads_kernel,
-        [ffn_grads_shape],
-        [norm_f_all, *grad_y, mid],
-        [all_low, pltpu.VMEM(*ffn_grads_shape), sems((4,)), sems((8,))],
+        [ffn_grads_shape, slab[0]],
+        [norm_f_all, *grad_y, mid, grad_norm],
+        [all_low, pltpu.VMEM(*ffn_grads_shape), sems((5,)), sems((4,))],
         12,
         4,
         range(1, 5),
-        (0,),
+        (0, 1),
     )
     grad_hidden, grad_hidden_low = call(
         middle_back_kernel,
         [slab[0], token_low],
-        [*fetch([hidden, grad_low]), *fetch([grad_norm]), *scatter_near(grad_norm_low)],
+        [*fetch([hidden, grad_low]), *fetch([after(grad_norm, branch[1:])]), *scatter_near(grad_norm_low)],
     )
     grad_branch = gather_near(grad_hidden_low)
     final_parts = scatter_near(after(branch[1:], grad_hidden_low))
@@ -674,27 +714,26 @@
     gqkv_own, gqkv_oth, own_norm, *grad_norm, n_all, g_all, att = call(
         project_back_kernel,
         [((group, 3 * hp), bf16), ((group, 3 * hp), bf16), *slab, whole, whole, q_shape],
-        [grad_q, grad_kv, swap(after(far_give, out_own)), attn_near, norm_a_all, grad_branch_all, attended],
+        [grad_q, grad_kv, swap(after(far_give, final_parts)), attn_near, norm_a_all, grad_branch_all, attended],
         [acc, sems((3,))],
         us=2,
         far_args=(4, 5, 6),
     )
     arriving = scatter_near(grad_norm)
-    attn_grads_shape = ((4, 2, width // 4, 4 * hp), bf16)
-    (attn_grads,) = call(
+    grads_own, grads_oth = call(
         attn_grads_kernel,
-        [attn_grads_shape],
-        [n_all, g_all, gqkv_own, gqkv_oth, att],
-        [pltpu.VMEM(*attn_grads_shape), sems((8,))],
-        8,
-        3,
-        far_outs=(0,),
-    )
-    attn_part = reduced(after(attn_grads, ffn_part, arriving))
+        [((width, 4 * hp), bf16)] * 2,
+        [core_ref, n_all, g_all, gqkv_own, gqkv_oth, att],
+        us=3,
+    )
+    other = swap(grads_oth)
+    planes = ()
+    if direct:
+        planes = call(core_sum_kernel, [((4 * rows, 4 * hp), bf16)] * 4, [far_ref, grads_own, other])
     own, give = call(
         leave_kernel,
         [token_low, token_low],
-        [core_ref, *fetch([x_far, grad_hidden]), own_norm, *arriving, out_own, out_give],
+        [core_ref, *fetch([x_far, grad_hidden]), after(own_norm, planes), *arriving, out_own, out_give],
     )
 
     def finished(pieces, weights, gain, part, size):
@@ -722,16 +761,22 @@
 
     if direct:
         back = returned(own)
+        planes = [planes[0]] + [far_shift(planes[k], k) for k in range(1, 4)]
 
         def pieces_of(part):
-            pieces = call(pick_kernel, [((rows, part.shape[1]), bf16)] * 4, [near_ref, part])
+            pieces = call(pick_kernel, [((rows, part.shape[1]), bf16)] * 4, [near_ref, part], [sems((4,))], far_args=(1,))
             return [pieces[0]] + scatter_near(pieces[1:])
 
-        *ffn_grads, sum_f = finished(pieces_of(ffn_part), ffn_weights, gain_f, ff_part, ff_pad)
-        *attn_grads, sum_a = finished(pieces_of(attn_part), attn_weights, gain_a, hp, hp)
+        *ffn_grads, sum_f = finished(pieces_of(after(ffn_part, planes[1])), ffn_weights, gain_f, ff_part, ff_pad)
+        planes[0] = after(planes[0], ffn_grads)
+        pieces = call(far_sum_kernel, [((rows, 4 * hp), bf16)] * 4, [near_ref, *planes], us=23)
+        pieces = [pieces[0]] + scatter_near(pieces[1:])
+        *attn_grads, sum_a = finished(pieces, attn_weights, gain_a, hp, hp)
         back = after(back, ffn_grads, attn_grads)
     else:
         back = returned(own)
+        total = far_rows((grads_own.astype(f32) + other.astype(f32)).astype(bf16), far_sizes, rows)
+        attn_part = lax.psum_scatter(total, FAR, scatter_dimension=0, tiled=True)
         *attn_grads, sum_a = finished_plain(attn_part, attn_weights, gain_a, hp, hp)
         *ffn_grads, sum_f = finished_plain(ffn_part, ffn_weights, gain_f, ff_part, ff_pad)
     gains = jnp.concatenate([sum_a, sum_f], axis=1).T

time: 272 us -> 251 us (0.923)
  waiting for transfers between devices: 130 us -> 100 us
  starting transfers between devices: 58.6 us -> 63.9 us
    reduce_scatter x2 -> x1, waiting for transfers between devices: 40.4 us -> 0.02 us  [reduced(): lax.psum_scatter(grads.reshape(-1, cols), FAR + (CORE,), scatter_dimensio...]
    all_to_all x1, waiting for transfers between devices: 0.01 us -> 7.68 us  [returned(): lax.all_to_all(spread.reshape(peers, slot_cap, width), DP, 0, 0, tiled=True)]
    ppermute x0 -> x3, waiting for transfers between devices: none -> 5.16 us  [far_shift(): return lax.ppermute(value, FAR, [(i, (i + k) % far) for i in range(far)])]
    pallas_call x31 -> x33, Pallas kernels: 59.1 us -> 60.5 us  [call(): pl.pallas_call(kernel, out_shape=[pltpu.HBM(shape, kind) if i in far_outs...]
    ppermute x6 -> x7, waiting for transfers between devices: 5.62 us -> 4.75 us  [swap(): return lax.ppermute(value, CORE, [(0, 1), (1, 0)])]
    ppermute x6 -> x7, starting transfers between devices: 12.2 us -> 12.6 us  [swap(): return lax.ppermute(value, CORE, [(0, 1), (1, 0)])]
  transfers between devices with their start and end apart: 51 -> 54, of which waited for: 28 -> 33; matrix products, arithmetic and copies ran while one was open for 1% -> 1% of each run, Pallas kernels for 16% -> 20%
where the time goes in v4:
time: 251 us; the launch traced here: 249 us
  waiting for transfers between devices  100 us (40%)
  starting transfers between devices  63.9 us (25%)
  Pallas kernels  60.5 us (24%)
  between operations  14.3 us (6%)
  local copies, waits for them, and re-layouts  7.56 us (3%)
    pallas_call x33, Pallas kernels, call(): pl.pallas_call(kernel, out_shape=[pltpu.HBM(shape, kind) if i in far_outs...  60.5 us
    ppermute x39, waiting for transfers between devices, near(): return lax.ppermute(value, NEAR, [(i, i ^ k) for i in range(4)])  57.9 us
    ppermute x39, starting transfers between devices, near(): return lax.ppermute(value, NEAR, [(i, i ^ k) for i in range(4)])  37.8 us
    all_to_all x1, waiting for transfers between devices, body(): lax.all_to_all(both, DP, 0, 0, tiled=True).reshape(slot_count, width)  24.9 us
    ppermute x7, starting transfers between devices, swap(): return lax.ppermute(value, CORE, [(0, 1), (1, 0)])  12.6 us
    all_to_all x1, waiting for transfers between devices, returned(): lax.all_to_all(spread.reshape(peers, slot_cap, width), DP, 0, 0, tiled=True)  7.68 us
    all_to_all x1, starting transfers between devices, returned(): lax.all_to_all(spread.reshape(peers, slot_cap, width), DP, 0, 0, tiled=True)  5.4 us
    all_to_all x1, starting transfers between devices, body(): lax.all_to_all(both, DP, 0, 0, tiled=True).reshape(slot_count, width)  5.34 us
  transfers between devices with their start and end apart: 54, of which 33 were waited for; matrix products, arithmetic and copies ran while one was open for 1% of the time, Pallas kernels for 20%

profile of v4, /device:TPU:9, one launch (start us, length us, event | category | flops | bytes accessed | tf_op | source)
XLA Modules:
  0.0 248.8 jit_solution(2689462329508430319)
XLA Ops:
  13.2 1.4 collective-permute-done.1.b2
  14.6 1.9 collective-permute-done.2.b3
  17.3 5.3 %all-to-all-start = ((bf16[16,32,1024]{2,1,0:T(8,128)(2,1)}), bf16[16,32,1024]{2,1,0:T(8,128)(2,1)S(1)}, u32[]{:S(2)}, u32[]{:S(2)}) async-start(bf16[16,32,1024]{2,1,0:T(8,128)(2,1)} %pad_maximum_fusion), calls=%async_computation | async-start | bytes 2097152 | tf_op jit(solution)/shard_map/all_to_all | solution.py:540
  31.8 5.1 %collective-permute-done.7.b2 = bf16[64,1152]{1,0:T(8,128)(2,1)S(1)} collective-permute-done((bf16[64,1152]{1,0:T(8,128)(2,1)S(1)}, bf16[64,1152]{1,0:T(8,128)(2,1)S(1)}, u32[]{:S(2)}, u32[]{:S(2)}) %collective-permute-start.7) | collective-permute-done | bytes 147488 | tf_op jit(solution)/shard_map/ppermute | solution.py:40
  37.8 24.9 %all-to-all-done = bf16[16,32,1024]{2,1,0:T(8,128)(2,1)S(1)} async-done(((bf16[16,32,1024]{2,1,0:T(8,128)(2,1)}), bf16[16,32,1024]{2,1,0:T(8,128)(2,1)S(1)}, u32[]{:S(2)}, u32[]{:S(2)}) %all-to-all-start) | async-done | bytes 1048608 | tf_op jit(solution)/shard_map/all_to_all | solution.py:540
  63.2 3.7 %collective-permute-start.9 = (bf16[128,1024]{1,0:T(8,128)(2,1)S(1)}, bf16[128,1024]{1,0:T(8,128)(2,1)S(1)}, u32[]{:S(2)}, u32[]{:S(2)}) collective-permute-start(bf16[128,1024]{1,0:T(8,128)(2,1)S(1)} %get-tuple-element.161), channel_id=1, source_target_pairs={{0,1},{1,0},{2,3},{3,2},{4,5},{5,4},{6,7},{7,6},{8,9},{9,8},{10,11... | collective-permute-start | bytes 786440 | tf_op jit(solution)/shard_map/ppermute | solution.py:36
  70.2 1.4 collective-permute-start.12
  71.7 1.7 shard_map.218.w
  73.4 3.0 %collective-permute-done.10.n1 = bf16[128,1024]{1,0:T(8,128)(2,1)S(1)} collective-permute-done((bf16[128,1024]{1,0:T(8,128)(2,1)S(1)}, bf16[128,1024]{1,0:T(8,128)(2,1)S(1)}, u32[]{:S(2)}, u32[]{:S(2)}) %collective-permute-start.10) | collective-permute-done | bytes 262176 | tf_op jit(solution)/shard_map/ppermute | solution.py:40
  76.4 6.4 %collective-permute-done.12.n3 = bf16[128,1024]{1,0:T(8,128)(2,1)S(1)} collective-permute-done((bf16[128,1024]{1,0:T(8,128)(2,1)S(1)}, bf16[128,1024]{1,0:T(8,128)(2,1)S(1)}, u32[]{:S(2)}, u32[]{:S(2)}) %collective-permute-start.12) | collective-permute-done | bytes 262176 | tf_op jit(solution)/shard_map/ppermute | solution.py:40
  83.5 2.4 shard_map.219
  87.1 1.5 collective-permute-start.14
  89.8 8.0 %shard_map.220 = (bf16[16,256,128]{2,1,0:T(8,128)(2,1)}, bf16[512,256]{1,0:T(8,128)(2,1)}, bf16[512,512]{1,0:T(8,128)(2,1)}, bf16[512,512]{1,0:T(8,128)(2,1)}, b...) custom-call(s32[1]{0:T(128)} %bitcast.core, ...), custom_call_target="tpu_custom_call" | custom-call | tf_op jit(solution)/shard_map/pallas_call | solution.py:66
  97.9 2.5 %collective-permute-done.15.y2 = bf16[128,1024]{1,0:T(8,128)(2,1)S(1)} collective-permute-done((bf16[128,1024]{1,0:T(8,128)(2,1)S(1)}, bf16[128,1024]{1,0:T(8,128)(2,1)S(1)}, u32[]{:S(2)}, u32[]{:S(2)}) %collective-permute-start.15) | collective-permute-done | bytes 262176 | tf_op jit(solution)/shard_map/ppermute | solution.py:40
  104.3 3.9 %collective-permute-done.17.b1 = bf16[128,1024]{1,0:T(8,128)(2,1)S(1)} collective-permute-done((bf16[128,1024]{1,0:T(8,128)(2,1)S(1)}, bf16[128,1024]{1,0:T(8,128)(2,1)S(1)}, u32[]{:S(2)}, u32[]{:S(2)}) %collective-permute-start.17) | collective-permute-done | bytes 262176 | tf_op jit(solution)/shard_map/ppermute | solution.py:40
  108.2 1.9 collective-permute-done.18.b2
  110.1 5.0 %collective-permute-done.19.b3 = bf16[128,1024]{1,0:T(8,128)(2,1)S(1)} collective-permute-done((bf16[128,1024]{1,0:T(8,128)(2,1)S(1)}, bf16[128,1024]{1,0:T(8,128)(2,1)S(1)}, u32[]{:S(2)}, u32[]{:S(2)}) %collective-permute-start.19) | collective-permute-done | bytes 262176 | tf_op jit(solution)/shard_map/ppermute | solution.py:40
  118.0 2.7 %shard_map.222 = (bf16[256,1024]{1,0:T(8,128)(2,1)S(1)}, bf16[256,1024]{1,0:T(8,128)(2,1)S(1)}, bf16[2,1024,1152]{2,1,0:T(8,128)(2,1)S(1)}) custom-call(bf16[128,1024]{1,0:T(8,128)(2,1)} %copy-done, bf16[128,1024]{1,0:T(8,128)(2,1)} %copy-done.21, bf16[128,1024]{1,0:T(8,128)(2,1)} %copy-done.22, bf16[128,1024]{1,0:T(8,128)(2,1)} %copy-done.23, ...), custom_call_target="tpu_custom_call" | custom-call | flops 2000000000 | bytes 2000000 | tf_op jit(solution)/shard_map/pallas_call | solution.py:66
  120.9 2.9 %shard_map.223 = (bf16[512,2304]{1,0:T(8,128)(2,1)S(1)}, bf16[512,1024]{1,0:T(8,128)(2,1)S(1)}, f32[128,1024]{1,0:T(8,128)}, f32[128,1024]{1,0:T(8,128)S(1)}, bf16[128,1024]{1,0:T(8,128)(2,1)S(1)}) custom-call(bf16[128,1024]{1,0:T(8,128)(2,1)S(1)} %get-tuple-element.179.n0, bf16[128,1024]{1,0:T(8,128)(2,1)S(1)} %collective-permute-done.20.n1, ...), custom_call_target="tpu_custom_call" | custom-call | flops 3000000000 | bytes 3000000 | tf_op jit(solution)/shard_map/pallas_call | solution.py:66
  123.9 2.8 %collective-permute-done.22.n1 = bf16[128,1024]{1,0:T(8,128)(2,1)S(1)} collective-permute-done((bf16[128,1024]{1,0:T(8,128)(2,1)S(1)}, bf16[128,1024]{1,0:T(8,128)(2,1)S(1)}, u32[]{:S(2)}, u32[]{:S(2)}) %collective-permute-start.22) | collective-permute-done | bytes 262176 | tf_op jit(solution)/shard_map/ppermute | solution.py:40
  126.7 2.9 %shard_map.225 = (bf16[512,2304]{1,0:T(8,128)(2,1)S(1)}, bf16[512,1024]{1,0:T(8,128)(2,1)S(1)}, bf16[128,1024]{1,0:T(8,128)(2,1)S(1)}, bf16[128,1024]{1,0:T(8,128)(2,1)S(1)}) custom-call(bf16[128,1024]{1,0:T(8,128)(2,1)S(1)} %collective-permute-done.21.n0, ...), custom_call_target="tpu_custom_call", output_to_operand_aliasing={{0}: (4, {}), {1}: (5, {})} | custom-call | flops 3000000000 | bytes 3000000 | tf_op jit(solution)/shard_map/pallas_call | solution.py:66
  129.6 5.5 %shard_map.226 = (bf16[4,2,256,1152]{3,2,1,0:T(8,128)(2,1)}, f32[128,1024]{1,0:T(8,128)}) custom-call(bf16[512,1024]{1,0:T(8,128)(2,1)S(1)} %get-tuple-element.189.all_n, bf16[128,1024]{1,0:T(8,128)(2,1)} %copy-done, bf16[128,1024]{1,0:T(8,128)(2,1)} %copy-done.21, bf16[128,1024]{1,0:T(8,128)(2,1)} %copy-done.22, bf16[128,1024]{1,0:T(8,128)(2,1)} %copy-done.23, ...), custom_call_target="tpu_custom_call" | custom-call | flops 4000000000 | bytes 4000000 | tf_op jit(solution)/shard_map/pallas_call | solution.py:66
  136.3 2.0 collective-permute-start.25
  138.3 1.7 copy-done.12
  140.0 3.3 %shard_map.227 = (f32[128,1024]{1,0:T(8,128)}, bf16[128,1024]{1,0:T(8,128)(2,1)S(1)}, bf16[128,1024]{1,0:T(8,128)(2,1)S(1)}, bf16[128,1024]{1,0:T(8,128)(2,1)S(1)}) custom-call(bf16[512,2304]{1,0:T(8,128)(2,1)S(1)} %copy-done.12, bf16[2,1024,1152]{2,1,0:T(8,128)(2,1)} %bitcast.55), custom_call_target="tpu_custom_call" | custom-call | flops 2000000000 | bytes 2000000 | tf_op jit(solution)/shard_map/pallas_call | solution.py:66
  146.9 2.4 collective-permute-start.26
  151.6 1.7 shard_map.231
  153.3 1.5 collective-permute-start.29
  156.8 1.5 collective-permute-done.28.g3
  158.3 6.2 %shard_map.232 = (bf16[512,256]{1,0:T(8,128)(2,1)S(1)}, f32[512,512]{1,0:T(8,128)S(1)}, bf16[512,512]{1,0:T(8,128)(2,1)S(1)}, bf16[2,1024,384]{2,1,0:T(8,128)(2,...) custom-call(bf16[128,1024]{1,0:T(8,128)(2,1)S(1)} %get-tuple-element.200.g0, ...), custom_call_target="tpu_custom_call" | custom-call | flops 7000000000 | bytes 7000000 | tf_op jit(solution)/shard_map/pallas_call | solution.py:66
  164.4 4.2 %collective-permute-done.30.b2 = bf16[128,1024]{1,0:T(8,128)(2,1)S(1)} collective-permute-done((bf16[128,1024]{1,0:T(8,128)(2,1)S(1)}, bf16[128,1024]{1,0:T(8,128)(2,1)S(1)}, u32[]{:S(2)}, u32[]{:S(2)}) %collective-permute-start.30) | collective-permute-done | bytes 262176 | tf_op jit(solution)/shard_map/ppermute | solution.py:40
  169.5 5.4 %collective-permute-start.32 = (bf16[512,512]{1,0:T(8,128)(2,1)S(1)}, bf16[512,512]{1,0:T(8,128)(2,1)S(1)}, u32[]{:S(2)}, u32[]{:S(2)}) collective-permute-start(bf16[512,512]{1,0:T(8,128)(2,1)S(1)} %get-tuple-element.219), channel_id=1, source_target_pairs={{0,1},{1,0},{2,3},{3,2},{4,5},{5,4},{6,7},{7,6},{8,9},{9,8},{10,11... | collective-permute-start | bytes 1572872 | tf_op jit(solution)/shard_map/ppermute | solution.py:36
  174.9 1.5 collective-permute-done.32.back
  176.4 1.6 shard_map.234
  178.1 1.9 shard_map.235
  184.2 1.4 shard_map.237
  188.6 5.9 %collective-permute-done.36.b3 = bf16[128,1024]{1,0:T(8,128)(2,1)S(1)} collective-permute-done((bf16[128,1024]{1,0:T(8,128)(2,1)S(1)}, bf16[128,1024]{1,0:T(8,128)(2,1)S(1)}, u32[]{:S(2)}, u32[]{:S(2)}) %collective-permute-start.36) | collective-permute-done | bytes 262176 | tf_op jit(solution)/shard_map/ppermute | solution.py:40
  195.9 1.6 collective-permute-start.42
  197.5 1.8 shard_map.240
  202.8 1.7 shard_map.239
  204.5 5.4 %all-to-all-start.1 = ((bf16[16,32,1024]{2,1,0:T(8,128)(2,1)}), bf16[16,32,1024]{2,1,0:T(8,128)(2,1)S(1)}, u32[]{:S(2)}, u32[]{:S(2)}) async-start(bf16[16,32,1024]{2,1,0:T(8,128)(2,1)} %bitcast.18), calls=%async_computation.1 | async-start | bytes 2097152 | tf_op jit(solution)/shard_map/all_to_all | solution.py:759
  210.9 3.2 %shard_map.241 = (f32[64,1408]{1,0:T(8,128)}, f32[64,1408]{1,0:T(8,128)}, f32[64,1408]{1,0:T(8,128)}, f32[64,1]{1,0:T(8,128)S(1)}) custom-call(s32[1]{0:T(128)} %bitcast.6.me, f32[64,1]{1,0:T(8,128)S(1)} %copy.49.gain, bf16[64,1152]{1,0:T(8,128)(2,1)S(1)} %copy-done.16, bf16[64,1152]{1,0:T(8,128)(2,1)S(1)} %collective-permute-done.39.s1, ...), custom_call_target="tpu_custom_call" | custom-call | flops 1000000000 | bytes 1000000 | tf_op jit(solution)/shard_map/pallas_call | solution.py:66
  214.1 4.8 %collective-permute-done.42.t2 = bf16[256,512]{1,0:T(8,128)(2,1)S(1)} collective-permute-done((bf16[256,512]{1,0:T(8,128)(2,1)S(1)}, bf16[256,512]{1,0:T(8,128)(2,1)S(1)}, u32[]{:S(2)}, u32[]{:S(2)}) %collective-permute-start.42) | collective-permute-done | bytes 262176 | tf_op jit(solution)/shard_map/ppermute | solution.py:534
  220.7 1.8 collective-permute-start.45
  224.7 3.7 %collective-permute-done.46.s3 = bf16[64,512]{1,0:T(8,128)(2,1)S(1)} collective-permute-done((bf16[64,512]{1,0:T(8,128)(2,1)S(1)}, bf16[64,512]{1,0:T(8,128)(2,1)S(1)}, u32[]{:S(2)}, u32[]{:S(2)}) %collective-permute-start.46) | collective-permute-done | bytes 65568 | tf_op jit(solution)/shard_map/ppermute | solution.py:40
  229.5 7.7 %all-to-all-done.1 = bf16[16,32,1024]{2,1,0:T(8,128)(2,1)S(1)} async-done(((bf16[16,32,1024]{2,1,0:T(8,128)(2,1)}), bf16[16,32,1024]{2,1,0:T(8,128)(2,1)S(1)}, u32[]{:S(2)}, u32[]{:S(2)}) %all-to-all-start.1) | async-done | bytes 1048608 | tf_op jit(solution)/shard_map/all_to_all | solution.py:759
  238.1 2.0 collective-permute-done.48
  240.7 1.5 shard_map.244
  (172 shorter events, 60.3 us)
Async XLA Ops:
  7.2 64.6 %all-gather.3.cloned.1.call-start = ((), (), s32[]{:S(2)}) async-start(), calls=%async_computation.3 | async-start | bytes 2359296 | tf_op jit(solution)/shard_map/all_gather | solution.py:564
  12.5 4.0 %collective-permute-start.2 = (bf16[64,512]{1,0:T(8,128)(2,1)S(1)}, bf16[64,512]{1,0:T(8,128)(2,1)S(1)}, u32[]{:S(2)}, u32[]{:S(2)}) collective-permute-start(bf16[64,512]{1,0:T(8,128)(2,1)S(1)} %get-tuple-element.148), channel_id=1, source_target_pairs={{0,6},{2,4},{4,2},{6,0},{1,7},{3,5},{5,3},{7,1},{8,14},{10,12},{12... | collective-permute-start | bytes 196616 | tf_op jit(solution)/shard_map/ppermute | solution.py:40
  17.3 45.3 %all-to-all-start = ((bf16[16,32,1024]{2,1,0:T(8,128)(2,1)}), bf16[16,32,1024]{2,1,0:T(8,128)(2,1)S(1)}, u32[]{:S(2)}, u32[]{:S(2)}) async-start(bf16[16,32,1024]{2,1,0:T(8,128)(2,1)} %pad_maximum_fusion), calls=%async_computation | async-start | bytes 2097152 | tf_op jit(solution)/shard_map/all_to_all | solution.py:540
  22.7 95.3 %all-gather.5.cloned.1.call-start = ((), (), s32[]{:S(2)}) async-start(), calls=%async_computation.4 | async-start | bytes 5308416 | tf_op jit(solution)/shard_map/all_gather | solution.py:564
  24.4 5.4 %collective-permute-start.3 = (s32[1,256]{1,0:T(1,128)S(1)}, s32[1,256]{1,0:T(1,128)S(1)}, u32[]{:S(2)}, u32[]{:S(2)}) collective-permute-start(s32[1,256]{1,0:T(1,128)S(1)} %copy-done.20), channel_id=1, source_target_pairs={{0,2},{2,0},{4,6},{6,4},{1,3},{3,1},{5,7},{7,5},{8,10},{10,8},{12,... | collective-permute-start | bytes 3080 | tf_op jit(solution)/shard_map/ppermute | solution.py:40
  25.6 4.8 %collective-permute-start.4 = (s32[1,256]{1,0:T(1,128)S(1)}, s32[1,256]{1,0:T(1,128)S(1)}, u32[]{:S(2)}, u32[]{:S(2)}) collective-permute-start(s32[1,256]{1,0:T(1,128)S(1)} %copy-done.20), channel_id=1, source_target_pairs={{0,4},{2,6},{4,0},{6,2},{1,5},{3,7},{5,1},{7,3},{8,12},{10,14},{12... | collective-permute-start | bytes 3080 | tf_op jit(solution)/shard_map/ppermute | solution.py:40
  27.4 4.4 %collective-permute-start.6 = (bf16[64,1152]{1,0:T(8,128)(2,1)S(1)}, bf16[64,1152]{1,0:T(8,128)(2,1)S(1)}, u32[]{:S(2)}, u32[]{:S(2)}) collective-permute-start(bf16[64,1152]{1,0:T(8,128)(2,1)S(1)} %get-tuple-element.154), channel_id=1, source_target_pairs={{0,2},{2,0},{4,6},{6,4},{1,3},{3,1},{5,7},{7,5},{8,10},{10,8},{12,... | collective-permute-start | bytes 442376 | tf_op jit(solution)/shard_map/ppermute | solution.py:40
  28.7 8.2 %collective-permute-start.7 = (bf16[64,1152]{1,0:T(8,128)(2,1)S(1)}, bf16[64,1152]{1,0:T(8,128)(2,1)S(1)}, u32[]{:S(2)}, u32[]{:S(2)}) collective-permute-start(bf16[64,1152]{1,0:T(8,128)(2,1)S(1)} %get-tuple-element.155), channel_id=1, source_target_pairs={{0,4},{2,6},{4,0},{6,2},{1,5},{3,7},{5,1},{7,3},{8,12},{10,14},{12... | collective-permute-start | bytes 442376 | tf_op jit(solution)/shard_map/ppermute | solution.py:40
  29.9 7.0 %collective-permute-start.8 = (bf16[64,1152]{1,0:T(8,128)(2,1)S(1)}, bf16[64,1152]{1,0:T(8,128)(2,1)S(1)}, u32[]{:S(2)}, u32[]{:S(2)}) collective-permute-start(bf16[64,1152]{1,0:T(8,128)(2,1)S(1)} %get-tuple-element.156), channel_id=1, source_target_pairs={{0,6},{2,4},{4,2},{6,0},{1,7},{3,5},{5,3},{7,1},{8,14},{10,12},{12... | collective-permute-start | bytes 442376 | tf_op jit(solution)/shard_map/ppermute | solution.py:40
  62.7 134.8 %reduce-scatter.2.cloned.1.call-start = ((), (), s32[]{:S(2)}) async-start(), calls=%async_computation.5 | async-start | bytes 5308416 | tf_op jit(solution)/shard_map/reduce_scatter | solution.py:693
  63.2 4.9 %collective-permute-start.9 = (bf16[128,1024]{1,0:T(8,128)(2,1)S(1)}, bf16[128,1024]{1,0:T(8,128)(2,1)S(1)}, u32[]{:S(2)}, u32[]{:S(2)}) collective-permute-start(bf16[128,1024]{1,0:T(8,128)(2,1)S(1)} %get-tuple-element.161), channel_id=1, source_target_pairs={{0,1},{1,0},{2,3},{3,2},{4,5},{5,4},{6,7},{7,6},{8,9},{9,8},{10,11... | collective-permute-start | bytes 786440 | tf_op jit(solution)/shard_map/ppermute | solution.py:36
  68.8 7.6 %collective-permute-start.10 = (bf16[128,1024]{1,0:T(8,128)(2,1)S(1)}, bf16[128,1024]{1,0:T(8,128)(2,1)S(1)}, u32[]{:S(2)}, u32[]{:S(2)}) collective-permute-start(bf16[128,1024]{1,0:T(8,128)(2,1)S(1)} %get-tuple-element.167.n0), channel_id=1, source_target_pairs={{0,2},{2,0},{4,6},{6,4},{1,3},{3,1},{5,7},{7,5},{8,10},{10,8},{12,... | collective-permute-start | bytes 786440 | tf_op jit(solution)/shard_map/ppermute | solution.py:40
  69.2 7.2 %collective-permute-start.11 = (bf16[128,1024]{1,0:T(8,128)(2,1)S(1)}, bf16[128,1024]{1,0:T(8,128)(2,1)S(1)}, u32[]{:S(2)}, u32[]{:S(2)}) collective-permute-start(bf16[128,1024]{1,0:T(8,128)(2,1)S(1)} %get-tuple-element.167.n0), channel_id=1, source_target_pairs={{0,4},{2,6},{4,0},{6,2},{1,5},{3,7},{5,1},{7,3},{8,12},{10,14},{12... | collective-permute-start | bytes 786440 | tf_op jit(solution)/shard_map/ppermute | solution.py:40
  70.2 12.6 %collective-permute-start.12 = (bf16[128,1024]{1,0:T(8,128)(2,1)S(1)}, bf16[128,1024]{1,0:T(8,128)(2,1)S(1)}, u32[]{:S(2)}, u32[]{:S(2)}) collective-permute-start(bf16[128,1024]{1,0:T(8,128)(2,1)S(1)} %get-tuple-element.167.n0), channel_id=1, source_target_pairs={{0,6},{2,4},{4,2},{6,0},{1,7},{3,5},{5,3},{7,1},{8,14},{10,12},{12... | collective-permute-start | bytes 786440 | tf_op jit(solution)/shard_map/ppermute | solution.py:40
  87.1 10.7 %collective-permute-start.14 = (bf16[128,1024]{1,0:T(8,128)(2,1)S(1)}, bf16[128,1024]{1,0:T(8,128)(2,1)S(1)}, u32[]{:S(2)}, u32[]{:S(2)}) collective-permute-start(bf16[128,1024]{1,0:T(8,128)(2,1)S(1)} %get-tuple-element.174.y0.refs_1_), channel_id=1, source_target_pairs={{0,2},{2,0},{4,6},{6,4},{1,3},{3,1},{5,7},{7,5},{8,10},{10,8},{12,... | collective-permute-start | bytes 786440 | tf_op jit(solution)/shard_map/ppermute | solution.py:40
  88.6 11.8 %collective-permute-start.15 = (bf16[128,1024]{1,0:T(8,128)(2,1)S(1)}, bf16[128,1024]{1,0:T(8,128)(2,1)S(1)}, u32[]{:S(2)}, u32[]{:S(2)}) collective-permute-start(bf16[128,1024]{1,0:T(8,128)(2,1)S(1)} %get-tuple-element.174.y0.refs_1_), channel_id=1, source_target_pairs={{0,4},{2,6},{4,0},{6,2},{1,5},{3,7},{5,1},{7,3},{8,12},{10,14},{12... | collective-permute-start | bytes 786440 | tf_op jit(solution)/shard_map/ppermute | solution.py:40
  89.6 12.1 %collective-permute-start.16 = (bf16[128,1024]{1,0:T(8,128)(2,1)S(1)}, bf16[128,1024]{1,0:T(8,128)(2,1)S(1)}, u32[]{:S(2)}, u32[]{:S(2)}) collective-permute-start(bf16[128,1024]{1,0:T(8,128)(2,1)S(1)} %get-tuple-element.174.y0.refs_1_), channel_id=1, source_target_pairs={{0,6},{2,4},{4,2},{6,0},{1,7},{3,5},{5,3},{7,1},{8,14},{10,12},{12... | collective-permute-start | bytes 786440 | tf_op jit(solution)/shard_map/ppermute | solution.py:40
  101.6 6.6 %collective-permute-start.17 = (bf16[128,1024]{1,0:T(8,128)(2,1)S(1)}, bf16[128,1024]{1,0:T(8,128)(2,1)S(1)}, u32[]{:S(2)}, u32[]{:S(2)}) collective-permute-start(bf16[128,1024]{1,0:T(8,128)(2,1)S(1)} %get-tuple-element.176), channel_id=1, source_target_pairs={{0,2},{2,0},{4,6},{6,4},{1,3},{3,1},{5,7},{7,5},{8,10},{10,8},{12,... | collective-permute-start | bytes 786440 | tf_op jit(solution)/shard_map/ppermute | solution.py:40
  102.9 7.2 %collective-permute-start.18 = (bf16[128,1024]{1,0:T(8,128)(2,1)S(1)}, bf16[128,1024]{1,0:T(8,128)(2,1)S(1)}, u32[]{:S(2)}, u32[]{:S(2)}) collective-permute-start(bf16[128,1024]{1,0:T(8,128)(2,1)S(1)} %get-tuple-element.177), channel_id=1, source_target_pairs={{0,4},{2,6},{4,0},{6,2},{1,5},{3,7},{5,1},{7,3},{8,12},{10,14},{12... | collective-permute-start | bytes 786440 | tf_op jit(solution)/shard_map/ppermute | solution.py:40
  103.4 11.7 %collective-permute-start.19 = (bf16[128,1024]{1,0:T(8,128)(2,1)S(1)}, bf16[128,1024]{1,0:T(8,128)(2,1)S(1)}, u32[]{:S(2)}, u32[]{:S(2)}) collective-permute-start(bf16[128,1024]{1,0:T(8,128)(2,1)S(1)} %get-tuple-element.178), channel_id=1, source_target_pairs={{0,6},{2,4},{4,2},{6,0},{1,7},{3,5},{5,3},{7,1},{8,14},{10,12},{12... | collective-permute-start | bytes 786440 | tf_op jit(solution)/shard_map/ppermute | solution.py:40
  115.3 5.6 %collective-permute-start.20 = (bf16[128,1024]{1,0:T(8,128)(2,1)S(1)}, bf16[128,1024]{1,0:T(8,128)(2,1)S(1)}, u32[]{:S(2)}, u32[]{:S(2)}) collective-permute-start(bf16[128,1024]{1,0:T(8,128)(2,1)S(1)} %get-tuple-element.179.n0), channel_id=1, source_target_pairs={{0,2},{2,0},{4,6},{6,4},{1,3},{3,1},{5,7},{7,5},{8,10},{10,8},{12,... | collective-permute-start | bytes 786440 | tf_op jit(solution)/shard_map/ppermute | solution.py:40
  116.2 7.6 %collective-permute-start.21 = (bf16[128,1024]{1,0:T(8,128)(2,1)S(1)}, bf16[128,1024]{1,0:T(8,128)(2,1)S(1)}, u32[]{:S(2)}, u32[]{:S(2)}) collective-permute-start(bf16[128,1024]{1,0:T(8,128)(2,1)S(1)} %get-tuple-element.179.n0), channel_id=1, source_target_pairs={{0,4},{2,6},{4,0},{6,2},{1,5},{3,7},{5,1},{7,3},{8,12},{10,14},{12... | collective-permute-start | bytes 786440 | tf_op jit(solution)/shard_map/ppermute | solution.py:40
  117.3 9.4 %collective-permute-start.22 = (bf16[128,1024]{1,0:T(8,128)(2,1)S(1)}, bf16[128,1024]{1,0:T(8,128)(2,1)S(1)}, u32[]{:S(2)}, u32[]{:S(2)}) collective-permute-start(bf16[128,1024]{1,0:T(8,128)(2,1)S(1)} %get-tuple-element.179.n0), channel_id=1, source_target_pairs={{0,6},{2,4},{4,2},{6,0},{1,7},{3,5},{5,3},{7,1},{8,14},{10,12},{12... | collective-permute-start | bytes 786440 | tf_op jit(solution)/shard_map/ppermute | solution.py:40
  135.2 10.4 %collective-permute-start.24 = (bf16[128,1024]{1,0:T(8,128)(2,1)S(1)}, bf16[128,1024]{1,0:T(8,128)(2,1)S(1)}, u32[]{:S(2)}, u32[]{:S(2)}) collective-permute-start(bf16[128,1024]{1,0:T(8,128)(2,1)S(1)} %get-tuple-element.198), channel_id=1, source_target_pairs={{0,4},{2,6},{4,0},{6,2},{1,5},{3,7},{5,1},{7,3},{8,12},{10,14},{12... | collective-permute-start | bytes 786440 | tf_op jit(solution)/shard_map/ppermute | solution.py:40
  136.3 9.3 %collective-permute-start.25 = (bf16[128,1024]{1,0:T(8,128)(2,1)S(1)}, bf16[128,1024]{1,0:T(8,128)(2,1)S(1)}, u32[]{:S(2)}, u32[]{:S(2)}) collective-permute-start(bf16[128,1024]{1,0:T(8,128)(2,1)S(1)} %get-tuple-element.199), channel_id=1, source_target_pairs={{0,6},{2,4},{4,2},{6,0},{1,7},{3,5},{5,3},{7,1},{8,14},{10,12},{12... | collective-permute-start | bytes 786440 | tf_op jit(solution)/shard_map/ppermute | solution.py:40
  138.3 8.3 %collective-permute-start.23 = (bf16[128,1024]{1,0:T(8,128)(2,1)S(1)}, bf16[128,1024]{1,0:T(8,128)(2,1)S(1)}, u32[]{:S(2)}, u32[]{:S(2)}) collective-permute-start(bf16[128,1024]{1,0:T(8,128)(2,1)S(1)} %get-tuple-element.197), channel_id=1, source_target_pairs={{0,2},{2,0},{4,6},{6,4},{1,3},{3,1},{5,7},{7,5},{8,10},{10,8},{12,... | collective-permute-start | bytes 786440 | tf_op jit(solution)/shard_map/ppermute | solution.py:40
  146.9 8.7 %collective-permute-start.26 = (bf16[128,1024]{1,0:T(8,128)(2,1)S(1)}, bf16[128,1024]{1,0:T(8,128)(2,1)S(1)}, u32[]{:S(2)}, u32[]{:S(2)}) collective-permute-start(bf16[128,1024]{1,0:T(8,128)(2,1)S(1)} %get-tuple-element.200.g0), channel_id=1, source_target_pairs={{0,2},{2,0},{4,6},{6,4},{1,3},{3,1},{5,7},{7,5},{8,10},{10,8},{12,... | collective-permute-start | bytes 786440 | tf_op jit(solution)/shard_map/ppermute | solution.py:40
  149.3 7.5 %collective-permute-start.27 = (bf16[128,1024]{1,0:T(8,128)(2,1)S(1)}, bf16[128,1024]{1,0:T(8,128)(2,1)S(1)}, u32[]{:S(2)}, u32[]{:S(2)}) collective-permute-start(bf16[128,1024]{1,0:T(8,128)(2,1)S(1)} %get-tuple-element.200.g0), channel_id=1, source_target_pairs={{0,4},{2,6},{4,0},{6,2},{1,5},{3,7},{5,1},{7,3},{8,12},{10,14},{12... | collective-permute-start | bytes 786440 | tf_op jit(solution)/shard_map/ppermute | solution.py:40
  150.2 8.1 %collective-permute-start.28 = (bf16[128,1024]{1,0:T(8,128)(2,1)S(1)}, bf16[128,1024]{1,0:T(8,128)(2,1)S(1)}, u32[]{:S(2)}, u32[]{:S(2)}) collective-permute-start(bf16[128,1024]{1,0:T(8,128)(2,1)S(1)} %get-tuple-element.200.g0), channel_id=1, source_target_pairs={{0,6},{2,4},{4,2},{6,0},{1,7},{3,5},{5,3},{7,1},{8,14},{10,12},{12... | collective-permute-start | bytes 786440 | tf_op jit(solution)/shard_map/ppermute | solution.py:40
  153.3 11.1 %collective-permute-start.29 = (bf16[128,1024]{1,0:T(8,128)(2,1)S(1)}, bf16[128,1024]{1,0:T(8,128)(2,1)S(1)}, u32[]{:S(2)}, u32[]{:S(2)}) collective-permute-start(bf16[128,1024]{1,0:T(8,128)(2,1)S(1)} %get-tuple-element.216), channel_id=1, source_target_pairs={{0,2},{2,0},{4,6},{6,4},{1,3},{3,1},{5,7},{7,5},{8,10},{10,8},{12,... | collective-permute-start | bytes 786440 | tf_op jit(solution)/shard_map/ppermute | solution.py:40
  154.8 13.9 %collective-permute-start.30 = (bf16[128,1024]{1,0:T(8,128)(2,1)S(1)}, bf16[128,1024]{1,0:T(8,128)(2,1)S(1)}, u32[]{:S(2)}, u32[]{:S(2)}) collective-permute-start(bf16[128,1024]{1,0:T(8,128)(2,1)S(1)} %get-tuple-element.217), channel_id=1, source_target_pairs={{0,4},{2,6},{4,0},{6,2},{1,5},{3,7},{5,1},{7,3},{8,12},{10,14},{12... | collective-permute-start | bytes 786440 | tf_op jit(solution)/shard_map/ppermute | solution.py:40
  155.6 13.9 %collective-permute-start.31 = (bf16[128,1024]{1,0:T(8,128)(2,1)S(1)}, bf16[128,1024]{1,0:T(8,128)(2,1)S(1)}, u32[]{:S(2)}, u32[]{:S(2)}) collective-permute-start(bf16[128,1024]{1,0:T(8,128)(2,1)S(1)} %get-tuple-element.218), channel_id=1, source_target_pairs={{0,6},{2,4},{4,2},{6,0},{1,7},{3,5},{5,3},{7,1},{8,14},{10,12},{12... | collective-permute-start | bytes 786440 | tf_op jit(solution)/shard_map/ppermute | solution.py:40
  169.5 6.9 %collective-permute-start.32 = (bf16[512,512]{1,0:T(8,128)(2,1)S(1)}, bf16[512,512]{1,0:T(8,128)(2,1)S(1)}, u32[]{:S(2)}, u32[]{:S(2)}) collective-permute-start(bf16[512,512]{1,0:T(8,128)(2,1)S(1)} %get-tuple-element.219), channel_id=1, source_target_pairs={{0,1},{1,0},{2,3},{3,2},{4,5},{5,4},{6,7},{7,6},{8,9},{9,8},{10,11... | collective-permute-start | bytes 1572872 | tf_op jit(solution)/shard_map/ppermute | solution.py:36
  180.0 5.6 %collective-permute-start.33 = (bf16[1024,512]{1,0:T(8,128)(2,1)S(1)}, bf16[1024,512]{1,0:T(8,128)(2,1)S(1)}, u32[]{:S(2)}, u32[]{:S(2)}) collective-permute-start(bf16[1024,512]{1,0:T(8,128)(2,1)S(1)} %get-tuple-element.231), channel_id=1, source_target_pairs={{0,1},{1,0},{2,3},{3,2},{4,5},{5,4},{6,7},{7,6},{8,9},{9,8},{10,11... | collective-permute-start | bytes 3145736 | tf_op jit(solution)/shard_map/ppermute | solution.py:36
  180.4 7.8 %collective-permute-start.34 = (bf16[128,1024]{1,0:T(8,128)(2,1)S(1)}, bf16[128,1024]{1,0:T(8,128)(2,1)S(1)}, u32[]{:S(2)}, u32[]{:S(2)}) collective-permute-start(bf16[128,1024]{1,0:T(8,128)(2,1)S(1)} %get-tuple-element.237), channel_id=1, source_target_pairs={{0,2},{2,0},{4,6},{6,4},{1,3},{3,1},{5,7},{7,5},{8,10},{10,8},{12,... | collective-permute-start | bytes 786440 | tf_op jit(solution)/shard_map/ppermute | solution.py:40
  181.1 7.4 %collective-permute-start.35 = (bf16[128,1024]{1,0:T(8,128)(2,1)S(1)}, bf16[128,1024]{1,0:T(8,128)(2,1)S(1)}, u32[]{:S(2)}, u32[]{:S(2)}) collective-permute-start(bf16[128,1024]{1,0:T(8,128)(2,1)S(1)} %get-tuple-element.238), channel_id=1, source_target_pairs={{0,4},{2,6},{4,0},{6,2},{1,5},{3,7},{5,1},{7,3},{8,12},{10,14},{12... | collective-permute-start | bytes 786440 | tf_op jit(solution)/shard_map/ppermute | solution.py:40
  181.9 12.5 %collective-permute-start.36 = (bf16[128,1024]{1,0:T(8,128)(2,1)S(1)}, bf16[128,1024]{1,0:T(8,128)(2,1)S(1)}, u32[]{:S(2)}, u32[]{:S(2)}) collective-permute-start(bf16[128,1024]{1,0:T(8,128)(2,1)S(1)} %get-tuple-element.239), channel_id=1, source_target_pairs={{0,6},{2,4},{4,2},{6,0},{1,7},{3,5},{5,3},{7,1},{8,14},{10,12},{12... | collective-permute-start | bytes 786440 | tf_op jit(solution)/shard_map/ppermute | solution.py:40
  185.9 11.6 %collective-permute-start.38 = (bf16[256,512]{1,0:T(8,128)(2,1)S(1)}, bf16[256,512]{1,0:T(8,128)(2,1)S(1)}, u32[]{:S(2)}, u32[]{:S(2)}) collective-permute-start(bf16[256,512]{1,0:T(8,128)(2,1)S(1)} %get-tuple-element.233), channel_id=1, source_target_pairs={{0,8},{8,16},{16,24},{24,0},{1,9},{9,17},{17,25},{25,1},{2,10},{10... | collective-permute-start | bytes 786440 | tf_op jit(solution)/shard_map/ppermute | solution.py:534
  194.8 6.7 %collective-permute-start.37 = (bf16[128,1024]{1,0:T(8,128)(2,1)S(1)}, bf16[128,1024]{1,0:T(8,128)(2,1)S(1)}, u32[]{:S(2)}, u32[]{:S(2)}) collective-permute-start(bf16[128,1024]{1,0:T(8,128)(2,1)S(1)} %get-tuple-element.247), channel_id=1, source_target_pairs={{0,1},{1,0},{2,3},{3,2},{4,5},{5,4},{6,7},{7,6},{8,9},{9,8},{10,11... | collective-permute-start | bytes 786440 | tf_op jit(solution)/shard_map/ppermute | solution.py:36
  195.9 23.0 %collective-permute-start.42 = (bf16[256,512]{1,0:T(8,128)(2,1)S(1)}, bf16[256,512]{1,0:T(8,128)(2,1)S(1)}, u32[]{:S(2)}, u32[]{:S(2)}) collective-permute-start(bf16[256,512]{1,0:T(8,128)(2,1)S(1)} %get-tuple-element.234), channel_id=1, source_target_pairs={{0,16},{8,24},{16,0},{24,8},{1,17},{9,25},{17,1},{25,9},{2,18},{10... | collective-permute-start | bytes 786440 | tf_op jit(solution)/shard_map/ppermute | solution.py:534
  197.5 21.8 %collective-permute-start.43 = (bf16[256,512]{1,0:T(8,128)(2,1)S(1)}, bf16[256,512]{1,0:T(8,128)(2,1)S(1)}, u32[]{:S(2)}, u32[]{:S(2)}) collective-permute-start(bf16[256,512]{1,0:T(8,128)(2,1)S(1)} %get-tuple-element.235), channel_id=1, source_target_pairs={{0,24},{8,0},{16,8},{24,16},{1,25},{9,1},{17,9},{25,17},{2,26},{10... | collective-permute-start | bytes 786440 | tf_op jit(solution)/shard_map/ppermute | solution.py:534
  200.0 10.0 %collective-permute-start.39 = (bf16[64,1152]{1,0:T(8,128)(2,1)}, bf16[64,1152]{1,0:T(8,128)(2,1)S(1)}, u32[]{:S(2)}, u32[]{:S(2)}) collective-permute-start(bf16[64,1152]{1,0:T(8,128)(2,1)} %get-tuple-element.251), channel_id=1, source_target_pairs={{0,2},{2,0},{4,6},{6,4},{1,3},{3,1},{5,7},{7,5},{8,10},{10,8},{12,... | collective-permute-start | bytes 442376 | tf_op jit(solution)/shard_map/ppermute | solution.py:40
  201.3 8.6 %collective-permute-start.40 = (bf16[64,1152]{1,0:T(8,128)(2,1)S(1)}, bf16[64,1152]{1,0:T(8,128)(2,1)S(1)}, u32[]{:S(2)}, u32[]{:S(2)}) collective-permute-start(bf16[64,1152]{1,0:T(8,128)(2,1)S(1)} %get-tuple-element.252), channel_id=1, source_target_pairs={{0,4},{2,6},{4,0},{6,2},{1,5},{3,7},{5,1},{7,3},{8,12},{10,14},{12... | collective-permute-start | bytes 442376 | tf_op jit(solution)/shard_map/ppermute | solution.py:40
  201.5 8.5 %collective-permute-start.41 = (bf16[64,1152]{1,0:T(8,128)(2,1)S(1)}, bf16[64,1152]{1,0:T(8,128)(2,1)}, u32[]{:S(2)}, u32[]{:S(2)}) collective-permute-start(bf16[64,1152]{1,0:T(8,128)(2,1)S(1)} %get-tuple-element.253), channel_id=1, source_target_pairs={{0,6},{2,4},{4,2},{6,0},{1,7},{3,5},{5,3},{7,1},{8,14},{10,12},{12... | collective-permute-start | bytes 442376 | tf_op jit(solution)/shard_map/ppermute | solution.py:40
  204.5 32.6 %all-to-all-start.1 = ((bf16[16,32,1024]{2,1,0:T(8,128)(2,1)}), bf16[16,32,1024]{2,1,0:T(8,128)(2,1)S(1)}, u32[]{:S(2)}, u32[]{:S(2)}) async-start(bf16[16,32,1024]{2,1,0:T(8,128)(2,1)} %bitcast.18), calls=%async_computation.1 | async-start | bytes 2097152 | tf_op jit(solution)/shard_map/all_to_all | solution.py:759
  219.4 4.6 %collective-permute-start.44 = (bf16[64,512]{1,0:T(8,128)(2,1)S(1)}, bf16[64,512]{1,0:T(8,128)(2,1)S(1)}, u32[]{:S(2)}, u32[]{:S(2)}) collective-permute-start(bf16[64,512]{1,0:T(8,128)(2,1)S(1)} %get-tuple-element.259), channel_id=1, source_target_pairs={{0,2},{2,0},{4,6},{6,4},{1,3},{3,1},{5,7},{7,5},{8,10},{10,8},{12,... | collective-permute-start | bytes 196616 | tf_op jit(solution)/shard_map/ppermute | solution.py:40
  220.7 4.0 %collective-permute-start.45 = (bf16[64,512]{1,0:T(8,128)(2,1)S(1)}, bf16[64,512]{1,0:T(8,128)(2,1)S(1)}, u32[]{:S(2)}, u32[]{:S(2)}) collective-permute-start(bf16[64,512]{1,0:T(8,128)(2,1)S(1)} %get-tuple-element.260), channel_id=1, source_target_pairs={{0,4},{2,6},{4,0},{6,2},{1,5},{3,7},{5,1},{7,3},{8,12},{10,14},{12... | collective-permute-start | bytes 196616 | tf_op jit(solution)/shard_map/ppermute | solution.py:40
  222.5 5.9 %collective-permute-start.46 = (bf16[64,512]{1,0:T(8,128)(2,1)S(1)}, bf16[64,512]{1,0:T(8,128)(2,1)S(1)}, u32[]{:S(2)}, u32[]{:S(2)}) collective-permute-start(bf16[64,512]{1,0:T(8,128)(2,1)S(1)} %get-tuple-element.261), channel_id=1, source_target_pairs={{0,6},{2,4},{4,2},{6,0},{1,7},{3,5},{5,3},{7,1},{8,14},{10,12},{12... | collective-permute-start | bytes 196616 | tf_op jit(solution)/shard_map/ppermute | solution.py:40
  (32 other events, 229.9 us)
Sparse Core Ops, SparseCore 0:
  17.4 44.0 all-gather.2
  63.1 53.2 all-gather.4
  135.3 55.6 reduce-scatter.1

commit v5 on v4

--- a/solution.py
+++ b/solution.py
@@ -146,6 +146,12 @@
         plane = lax.rem(far[0] + (4 - k), 4)
         for i in range(4):
             out[plane * 4 + (me[0] ^ i)] = ref[i]
+
+
+def join_attn_kernel(core, own, other, both, far, sems):
+    both[core[0]] = own[...]
+    both[1 - core[0]] = other[...]
+    wait(bring([(both, far)], sems))
 
 
 def collect_kernel(core, slot_row, slots, own, give):
@@ -563,8 +569,14 @@
         flat = flat.reshape(4 * rows, cols)
         return flat, lambda operand: lax.all_gather(operand, (CORE,) + FAR, axis=0, tiled=True).reshape(2, width, cols)
 
-    attn_flat, gather_attn = gathered(packed(attn_weights, gain_a, hp, hp, both))
-    attn_w = gather_attn(attn_flat)
+    attn_pack = packed(attn_weights, gain_a, hp, hp, both)
+    if direct:
+        attn_flat = jnp.stack([attn_pack[0]] + scatter_near(attn_pack[1:]))
+        shifted = [attn_flat] + [far_shift(attn_flat, k) for k in range(1, far)]
+    else:
+        attn_flat, gather_attn = gathered(attn_pack)
+        attn_w = gather_attn(attn_flat)
+        shifted = attn_w
     ffn_flat, gather_ffn = gathered(packed(ffn_weights, gain_f, ff_part, ff_pad, attn_flat))
     doc_rows = jnp.concatenate(gather_near(after(doc_ids, attn_flat)), axis=0)
     my_counts = lax.dynamic_index_in_dim(counts, my_row, 0, keepdims=False)
@@ -572,11 +584,21 @@
     slots = jnp.arange(slot_cap, dtype=jnp.int32)
     slot_token = jnp.where(slots[None, :] < my_counts[:, None], offsets[:, None] + slots[None, :], -1).reshape(-1)
     slot_row, slot_col = slot_token[None, :], slot_token[:, None]
-    received, slot_row, slot_col, doc_rows, ffn_flat = lax.optimization_barrier(
-        (received, slot_row, slot_col, doc_rows, ffn_flat)
-    )
-    ffn_w = gather_ffn(ffn_flat)
-    if not direct:
+    received, slot_row, slot_col, doc_rows, ffn_flat, shifted = lax.optimization_barrier(
+        (received, slot_row, slot_col, doc_rows, ffn_flat, shifted)
+    )
+    ffn_w = gather_ffn(after(ffn_flat, shifted))
+    if direct:
+        (attn_own,) = call(place_far_kernel, [((16, rows, 4 * hp), bf16)], [near_ref, far_ref, *shifted])
+        attn_own = attn_own.reshape(width, 4 * hp)
+        attn_near, attn_w = call(
+            join_attn_kernel,
+            [((2, width, 4 * hp), bf16)] * 2,
+            [core_ref, attn_own, swap(attn_own)],
+            [pltpu.SemaphoreType.DMA((3,))],
+            far_outs=(1,),
+        )
+    else:
         attn_w, ffn_w = (jnp.stack([natural_rows(w[i], far_sizes, rows) for i in range(2)]) for w in (attn_w, ffn_w))
     doc_own = lax.dynamic_slice_in_dim(doc_rows, core * toks, toks, 1)
     doc_oth = lax.dynamic_slice_in_dim(doc_rows, (1 - core) * toks, toks, 1)
@@ -596,13 +618,14 @@
     probs_shape = ((head_count, 2 * toks, toks), bf16)
     ffn_w_shape = ((2, width, 3 * ff_pad), bf16)
 
-    own, give = call(collect_kernel, [token_low, token_low], [core_ref, slot_row, received])
+    own, give = call(collect_kernel, [token_low, token_low], [core_ref, slot_row, received], us=1)
     x, grad_low, norm, x_far = call(
         enter_kernel, [token_low] * 4, [core_ref, own, swap(give)], [sems((1,))], far_outs=(3,)
     )
     norm_a = gather_near(norm)
     grad_y = gather_near(grad_low)
-    (attn_near,) = fetch([attn_w])
+    if not direct:
+        (attn_near,) = fetch([attn_w])
     q, kv, norm_a_all = call(
         project_kernel,
         [q_shape, kv_shape, whole],

time: 251 us -> 250 us (level)
  waiting for transfers between devices: 100 us -> 93.8 us
  starting transfers between devices: 63.9 us -> 70.1 us
    all_to_all x1, waiting for transfers between devices: 24.9 us -> 0.01 us  [body(): lax.all_to_all(both, DP, 0, 0, tiled=True).reshape(slot_count, width)]
    ppermute x3 -> x6, waiting for transfers between devices: 5.16 us -> 22.6 us  [far_shift(): return lax.ppermute(value, FAR, [(i, (i + k) % far) for i in range(far)])]
    ppermute x3 -> x6, starting transfers between devices: 2.64 us -> 8.79 us  [far_shift(): return lax.ppermute(value, FAR, [(i, (i + k) % far) for i in range(far)])]
    ppermute x39, waiting for transfers between devices: 57.9 us -> 54.9 us  [near(): return lax.ppermute(value, NEAR, [(i, i ^ k) for i in range(4)])]
    all_to_all x1, waiting for transfers between devices: 7.68 us -> 10.5 us  [returned(): lax.all_to_all(spread.reshape(peers, slot_cap, width), DP, 0, 0, tiled=True)]
    ppermute x7 -> x8, waiting for transfers between devices: 4.75 us -> 5.71 us  [swap(): return lax.ppermute(value, CORE, [(0, 1), (1, 0)])]
    ppermute x7 -> x8, starting transfers between devices: 12.6 us -> 12.1 us  [swap(): return lax.ppermute(value, CORE, [(0, 1), (1, 0)])]
  transfers between devices with their start and end apart: 54 -> 57, of which waited for: 33 -> 27; matrix products, arithmetic and copies ran while one was open for 1% -> 1% of each run, Pallas kernels for 20% -> 20%
where the time goes in v5:
time: 250 us; the launch traced here: 249 us
  waiting for transfers between devices  93.8 us (38%)
  starting transfers between devices  70.1 us (28%)
  Pallas kernels  60.9 us (24%)
  between operations  14.7 us (6%)
  local copies, waits for them, and re-layouts  7.49 us (3%)
    pallas_call x33, Pallas kernels, call(): pl.pallas_call(kernel, out_shape=[pltpu.HBM(shape, kind) if i in far_outs...  60.9 us
    ppermute x39, waiting for transfers between devices, near(): return lax.ppermute(value, NEAR, [(i, i ^ k) for i in range(4)])  54.9 us
    ppermute x39, starting transfers between devices, near(): return lax.ppermute(value, NEAR, [(i, i ^ k) for i in range(4)])  36.5 us
    ppermute x6, waiting for transfers between devices, far_shift(): return lax.ppermute(value, FAR, [(i, (i + k) % far) for i in range(far)])  22.6 us
    ppermute x8, starting transfers between devices, swap(): return lax.ppermute(value, CORE, [(0, 1), (1, 0)])  12.1 us
    all_to_all x1, waiting for transfers between devices, returned(): lax.all_to_all(spread.reshape(peers, slot_cap, width), DP, 0, 0, tiled=True)  10.5 us
    ppermute x6, starting transfers between devices, far_shift(): return lax.ppermute(value, FAR, [(i, (i + k) % far) for i in range(far)])  8.79 us
    all_to_all x1, starting transfers between devices, body(): lax.all_to_all(both, DP, 0, 0, tiled=True).reshape(slot_count, width)  6.66 us
  transfers between devices with their start and end apart: 57, of which 27 were waited for; matrix products, arithmetic and copies ran while one was open for 1% of the time, Pallas kernels for 20%

profile of v5, /device:TPU:9, one launch (start us, length us, event | category | flops | bytes accessed | tf_op | source)
XLA Modules:
  0.0 249.1 jit_solution(8689828868190762728)
XLA Ops:
  9.6 6.7 %all-to-all-start = ((bf16[16,32,1024]{2,1,0:T(8,128)(2,1)}), bf16[16,32,1024]{2,1,0:T(8,128)(2,1)S(1)}, u32[]{:S(2)}, u32[]{:S(2)}) async-start(bf16[16,32,1024]{2,1,0:T(8,128)(2,1)} %pad_maximum_fusion), calls=%async_computation | async-start | bytes 2097152 | tf_op jit(solution)/shard_map/all_to_all | solution.py:546
  21.7 2.9 %collective-permute-done.1 = bf16[64,512]{1,0:T(8,128)(2,1)S(1)} collective-permute-done((bf16[64,512]{1,0:T(8,128)(2,1)S(1)}, bf16[64,512]{1,0:T(8,128)(2,1)S(1)}, u32[]{:S(2)}, u32[]{:S(2)}) %collective-permute-start.1) | collective-permute-done | bytes 65568 | tf_op jit(solution)/shard_map/ppermute | solution.py:40
  25.4 2.2 collective-permute-start.4
  29.8 5.9 %collective-permute-start.10 = (bf16[4,64,512]{2,1,0:T(8,128)(2,1)S(1)}, bf16[4,64,512]{2,1,0:T(8,128)(2,1)S(1)}, u32[]{:S(2)}, u32[]{:S(2)}) collective-permute-start(bf16[4,64,512]{2,1,0:T(8,128)(2,1)S(1)} %pad_maximum_fusion.1.b0), channel_id=1, source_target_pairs={{0,16},{8,24},{16,0},{24,8},{1,17},{9,25},{17,1},{25,9},{2,18},{10... | collective-permute-start | bytes 786440 | tf_op jit(solution)/shard_map/ppermute | solution.py:540
  37.4 2.3 collective-permute-start.8
  40.0 3.1 %collective-permute-done.7.b2 = bf16[64,1152]{1,0:T(8,128)(2,1)S(1)} collective-permute-done((bf16[64,1152]{1,0:T(8,128)(2,1)S(1)}, bf16[64,1152]{1,0:T(8,128)(2,1)S(1)}, u32[]{:S(2)}, u32[]{:S(2)}) %collective-permute-start.7) | collective-permute-done | bytes 147488 | tf_op jit(solution)/shard_map/ppermute | solution.py:40
  43.9 11.0 %collective-permute-done.10.b2 = bf16[4,64,512]{2,1,0:T(8,128)(2,1)S(1)} collective-permute-done((bf16[4,64,512]{2,1,0:T(8,128)(2,1)S(1)}, bf16[4,64,512]{2,1,0:T(8,128)(2,1)S(1)}, u32[]{:S(2)}, u32[]{:S(2)}) %collective-permute-start.10) | collective-permute-done | bytes 262176 | tf_op jit(solution)/shard_map/ppermute | solution.py:540
  54.9 8.0 %collective-permute-done.11.b3 = bf16[4,64,512]{2,1,0:T(8,128)(2,1)S(1)} collective-permute-done((bf16[4,64,512]{2,1,0:T(8,128)(2,1)S(1)}, bf16[4,64,512]{2,1,0:T(8,128)(2,1)S(1)}, u32[]{:S(2)}, u32[]{:S(2)}) %collective-permute-start.11) | collective-permute-done | bytes 262176 | tf_op jit(solution)/shard_map/ppermute | solution.py:540
  65.3 2.1 collective-permute-done.12.other
  71.1 2.7 %shard_map.218 = (bf16[2,1024,512]{2,1,0:T(8,128)(2,1)S(1)}, bf16[2,1024,512]{2,1,0:T(8,128)(2,1)}) custom-call(s32[1]{0:T(128)} %bitcast.core, bf16[1024,512]{1,0:T(8,128)(2,1)S(1)} %bitcast.52, bf16[1024,512]{1,0:T(8,128)(2,1)} %collective-permute-done.16.other), custom_call_target="tpu_custom_call" | custom-call | flops 1000000000 | bytes 1000000 | tf_op jit(solution)/shard_map/pallas_call | solution.py:66
  73.8 2.1 collective-permute-done.13.n1
  76.7 5.8 %collective-permute-done.15.n3 = bf16[128,1024]{1,0:T(8,128)(2,1)S(1)} collective-permute-done((bf16[128,1024]{1,0:T(8,128)(2,1)S(1)}, bf16[128,1024]{1,0:T(8,128)(2,1)S(1)}, u32[]{:S(2)}, u32[]{:S(2)}) %collective-permute-start.15) | collective-permute-done | bytes 262176 | tf_op jit(solution)/shard_map/ppermute | solution.py:40
  83.3 2.4 shard_map.219
  85.7 2.0 collective-permute-start.17
  90.4 8.0 %shard_map.220 = (bf16[16,256,128]{2,1,0:T(8,128)(2,1)}, bf16[512,256]{1,0:T(8,128)(2,1)}, bf16[512,512]{1,0:T(8,128)(2,1)}, bf16[512,512]{1,0:T(8,128)(2,1)}, b...) custom-call(s32[1]{0:T(128)} %bitcast.core, ...), custom_call_target="tpu_custom_call" | custom-call | tf_op jit(solution)/shard_map/pallas_call | solution.py:66
  98.4 3.9 %collective-permute-done.20.y3 = bf16[128,1024]{1,0:T(8,128)(2,1)} collective-permute-done((bf16[128,1024]{1,0:T(8,128)(2,1)S(1)}, bf16[128,1024]{1,0:T(8,128)(2,1)}, u32[]{:S(2)}, u32[]{:S(2)}) %collective-permute-start.20) | collective-permute-done | bytes 262176 | tf_op jit(solution)/shard_map/ppermute | solution.py:40
  105.0 4.3 %collective-permute-done.21.b1 = bf16[128,1024]{1,0:T(8,128)(2,1)S(1)} collective-permute-done((bf16[128,1024]{1,0:T(8,128)(2,1)S(1)}, bf16[128,1024]{1,0:T(8,128)(2,1)S(1)}, u32[]{:S(2)}, u32[]{:S(2)}) %collective-permute-start.21) | collective-permute-done | bytes 262176 | tf_op jit(solution)/shard_map/ppermute | solution.py:40
  109.6 4.8 %collective-permute-done.23.b3 = bf16[128,1024]{1,0:T(8,128)(2,1)S(1)} collective-permute-done((bf16[128,1024]{1,0:T(8,128)(2,1)S(1)}, bf16[128,1024]{1,0:T(8,128)(2,1)S(1)}, u32[]{:S(2)}, u32[]{:S(2)}) %collective-permute-start.23) | collective-permute-done | bytes 262176 | tf_op jit(solution)/shard_map/ppermute | solution.py:40
  117.7 2.7 %shard_map.222 = (bf16[256,1024]{1,0:T(8,128)(2,1)S(1)}, bf16[256,1024]{1,0:T(8,128)(2,1)S(1)}, bf16[2,1024,1152]{2,1,0:T(8,128)(2,1)S(1)}) custom-call(bf16[128,1024]{1,0:T(8,128)(2,1)} %copy-done, bf16[128,1024]{1,0:T(8,128)(2,1)} %copy-done.22, bf16[128,1024]{1,0:T(8,128)(2,1)} %collective-permute-done.19.y2, ...), custom_call_target="tpu_custom_call" | custom-call | flops 2000000000 | bytes 2000000 | tf_op jit(solution)/shard_map/pallas_call | solution.py:66
  120.4 2.9 %shard_map.223 = (bf16[512,2304]{1,0:T(8,128)(2,1)S(1)}, bf16[512,1024]{1,0:T(8,128)(2,1)S(1)}, f32[128,1024]{1,0:T(8,128)}, f32[128,1024]{1,0:T(8,128)S(1)}, bf16[128,1024]{1,0:T(8,128)(2,1)S(1)}) custom-call(bf16[128,1024]{1,0:T(8,128)(2,1)S(1)} %get-tuple-element.192.n0, bf16[128,1024]{1,0:T(8,128)(2,1)S(1)} %collective-permute-done.24.n1, ...), custom_call_target="tpu_custom_call" | custom-call | flops 3000000000 | bytes 3000000 | tf_op jit(solution)/shard_map/pallas_call | solution.py:66
  123.3 4.3 %collective-permute-done.26.n1 = bf16[128,1024]{1,0:T(8,128)(2,1)S(1)} collective-permute-done((bf16[128,1024]{1,0:T(8,128)(2,1)S(1)}, bf16[128,1024]{1,0:T(8,128)(2,1)S(1)}, u32[]{:S(2)}, u32[]{:S(2)}) %collective-permute-start.26) | collective-permute-done | bytes 262176 | tf_op jit(solution)/shard_map/ppermute | solution.py:40
  127.7 2.9 %shard_map.225 = (bf16[512,2304]{1,0:T(8,128)(2,1)S(1)}, bf16[512,1024]{1,0:T(8,128)(2,1)S(1)}, bf16[128,1024]{1,0:T(8,128)(2,1)S(1)}, bf16[128,1024]{1,0:T(8,128)(2,1)S(1)}) custom-call(bf16[128,1024]{1,0:T(8,128)(2,1)S(1)} %collective-permute-done.25.n0, ...), custom_call_target="tpu_custom_call", output_to_operand_aliasing={{0}: (4, {}), {1}: (5, {})} | custom-call | flops 3000000000 | bytes 3000000 | tf_op jit(solution)/shard_map/pallas_call | solution.py:66
  130.6 5.5 %shard_map.226 = (bf16[4,2,256,1152]{3,2,1,0:T(8,128)(2,1)}, f32[128,1024]{1,0:T(8,128)}) custom-call(bf16[512,1024]{1,0:T(8,128)(2,1)S(1)} %get-tuple-element.203.all_n, bf16[128,1024]{1,0:T(8,128)(2,1)} %copy-done, bf16[128,1024]{1,0:T(8,128)(2,1)} %copy-done.22, bf16[128,1024]{1,0:T(8,128)(2,1)} %collective-permute-done.19.y2, ...), custom_call_target="tpu_custom_call" | custom-call | flops 4000000000 | bytes 4000000 | tf_op jit(solution)/shard_map/pallas_call | solution.py:66
  138.8 1.7 copy-done.13
  140.5 3.3 %shard_map.227 = (f32[128,1024]{1,0:T(8,128)}, bf16[128,1024]{1,0:T(8,128)(2,1)S(1)}, bf16[128,1024]{1,0:T(8,128)(2,1)S(1)}, bf16[128,1024]{1,0:T(8,128)(2,1)S(1)}) custom-call(bf16[512,2304]{1,0:T(8,128)(2,1)S(1)} %copy-done.13, bf16[2,1024,1152]{2,1,0:T(8,128)(2,1)} %bitcast.60), custom_call_target="tpu_custom_call" | custom-call | flops 2000000000 | bytes 2000000 | tf_op jit(solution)/shard_map/pallas_call | solution.py:66
  146.0 3.1 %collective-permute-done.28.b2 = bf16[128,1024]{1,0:T(8,128)(2,1)S(1)} collective-permute-done((bf16[128,1024]{1,0:T(8,128)(2,1)S(1)}, bf16[128,1024]{1,0:T(8,128)(2,1)S(1)}, u32[]{:S(2)}, u32[]{:S(2)}) %collective-permute-start.28) | collective-permute-done | bytes 262176 | tf_op jit(solution)/shard_map/ppermute | solution.py:40
  149.6 2.6 %collective-permute-start.32 = (bf16[128,1024]{1,0:T(8,128)(2,1)S(1)}, bf16[128,1024]{1,0:T(8,128)(2,1)S(1)}, u32[]{:S(2)}, u32[]{:S(2)}) collective-permute-start(bf16[128,1024]{1,0:T(8,128)(2,1)S(1)} %get-tuple-element.214.g0), channel_id=1, source_target_pairs={{0,6},{2,4},{4,2},{6,0},{1,7},{3,5},{5,3},{7,1},{8,14},{10,12},{12... | collective-permute-start | bytes 786440 | tf_op jit(solution)/shard_map/ppermute | solution.py:40
  153.2 1.7 shard_map.231
  155.2 2.4 collective-permute-start.35
  158.7 6.2 %shard_map.232 = (bf16[512,256]{1,0:T(8,128)(2,1)S(1)}, f32[512,512]{1,0:T(8,128)S(1)}, bf16[512,512]{1,0:T(8,128)(2,1)S(1)}, bf16[2,1024,384]{2,1,0:T(8,128)(2,...) custom-call(bf16[128,1024]{1,0:T(8,128)(2,1)S(1)} %get-tuple-element.214.g0, ...), custom_call_target="tpu_custom_call" | custom-call | flops 7000000000 | bytes 7000000 | tf_op jit(solution)/shard_map/pallas_call | solution.py:66
  165.9 4.1 %collective-permute-done.34.b2 = bf16[128,1024]{1,0:T(8,128)(2,1)S(1)} collective-permute-done((bf16[128,1024]{1,0:T(8,128)(2,1)S(1)}, bf16[128,1024]{1,0:T(8,128)(2,1)S(1)}, u32[]{:S(2)}, u32[]{:S(2)}) %collective-permute-start.34) | collective-permute-done | bytes 262176 | tf_op jit(solution)/shard_map/ppermute | solution.py:40
  170.0 5.1 %collective-permute-start.36 = (bf16[512,512]{1,0:T(8,128)(2,1)S(1)}, bf16[512,512]{1,0:T(8,128)(2,1)S(1)}, u32[]{:S(2)}, u32[]{:S(2)}) collective-permute-start(bf16[512,512]{1,0:T(8,128)(2,1)S(1)} %get-tuple-element.233), channel_id=1, source_target_pairs={{0,1},{1,0},{2,3},{3,2},{4,5},{5,4},{6,7},{7,6},{8,9},{9,8},{10,11... | collective-permute-start | bytes 1572872 | tf_op jit(solution)/shard_map/ppermute | solution.py:36
  175.1 1.5 collective-permute-done.36.back
  176.7 1.6 shard_map.234
  178.3 1.9 shard_map.235
  186.2 2.2 collective-permute-done.38.b1
  189.7 5.2 %collective-permute-done.40.b3 = bf16[128,1024]{1,0:T(8,128)(2,1)S(1)} collective-permute-done((bf16[128,1024]{1,0:T(8,128)(2,1)S(1)}, bf16[128,1024]{1,0:T(8,128)(2,1)S(1)}, u32[]{:S(2)}, u32[]{:S(2)}) %collective-permute-start.40) | collective-permute-done | bytes 262176 | tf_op jit(solution)/shard_map/ppermute | solution.py:40
  195.2 1.5 collective-permute-start.41
  198.1 1.8 shard_map.240
  203.4 1.7 shard_map.239
  205.2 5.7 %all-to-all-start.1 = ((bf16[16,32,1024]{2,1,0:T(8,128)(2,1)}), bf16[16,32,1024]{2,1,0:T(8,128)(2,1)S(1)}, u32[]{:S(2)}, u32[]{:S(2)}) async-start(bf16[16,32,1024]{2,1,0:T(8,128)(2,1)} %bitcast.21), calls=%async_computation.1 | async-start | bytes 2097152 | tf_op jit(solution)/shard_map/all_to_all | solution.py:782
  211.8 3.2 %shard_map.241 = (f32[64,1408]{1,0:T(8,128)}, f32[64,1408]{1,0:T(8,128)}, f32[64,1408]{1,0:T(8,128)}, f32[64,1]{1,0:T(8,128)S(1)}) custom-call(s32[1]{0:T(128)} %bitcast.6.me, f32[64,1]{1,0:T(8,128)S(1)} %copy.49.gain, bf16[64,1152]{1,0:T(8,128)(2,1)S(1)} %copy-done.17, bf16[64,1152]{1,0:T(8,128)(2,1)S(1)} %collective-permute-done.43.s1, ...), custom_call_target="tpu_custom_call" | custom-call | flops 1000000000 | bytes 1000000 | tf_op jit(solution)/shard_map/pallas_call | solution.py:66
  215.0 3.7 %collective-permute-done.47.t3 = bf16[256,512]{1,0:T(8,128)(2,1)S(1)} collective-permute-done((bf16[256,512]{1,0:T(8,128)(2,1)S(1)}, bf16[256,512]{1,0:T(8,128)(2,1)S(1)}, u32[]{:S(2)}, u32[]{:S(2)}) %collective-permute-start.47) | collective-permute-done | bytes 262176 | tf_op jit(solution)/shard_map/ppermute | solution.py:540
  219.0 2.6 %collective-permute-start.50 = (bf16[64,512]{1,0:T(8,128)(2,1)S(1)}, bf16[64,512]{1,0:T(8,128)(2,1)S(1)}, u32[]{:S(2)}, u32[]{:S(2)}) collective-permute-start(bf16[64,512]{1,0:T(8,128)(2,1)S(1)} %get-tuple-element.275), channel_id=1, source_target_pairs={{0,6},{2,4},{4,2},{6,0},{1,7},{3,5},{5,3},{7,1},{8,14},{10,12},{12... | collective-permute-start | bytes 196616 | tf_op jit(solution)/shard_map/ppermute | solution.py:40
  222.6 2.3 collective-permute-done.50.s3
  226.0 10.5 %all-to-all-done.1 = bf16[16,32,1024]{2,1,0:T(8,128)(2,1)S(1)} async-done(((bf16[16,32,1024]{2,1,0:T(8,128)(2,1)}), bf16[16,32,1024]{2,1,0:T(8,128)(2,1)S(1)}, u32[]{:S(2)}, u32[]{:S(2)}) %all-to-all-start.1) | async-done | bytes 1048608 | tf_op jit(solution)/shard_map/all_to_all | solution.py:782
  238.1 2.0 collective-permute-done.52
  240.7 1.5 shard_map.244
  (176 shorter events, 56.7 us)
Async XLA Ops:
  9.6 53.2 %all-to-all-start = ((bf16[16,32,1024]{2,1,0:T(8,128)(2,1)}), bf16[16,32,1024]{2,1,0:T(8,128)(2,1)S(1)}, u32[]{:S(2)}, u32[]{:S(2)}) async-start(bf16[16,32,1024]{2,1,0:T(8,128)(2,1)} %pad_maximum_fusion), calls=%async_computation | async-start | bytes 2097152 | tf_op jit(solution)/shard_map/all_to_all | solution.py:546
  16.3 101.4 %all-gather.2.cloned.1.call-start = ((), (), s32[]{:S(2)}) async-start(), calls=%async_computation.3 | async-start | bytes 5308416 | tf_op jit(solution)/shard_map/all_gather | solution.py:570
  17.9 6.6 %collective-permute-start.1 = (bf16[64,512]{1,0:T(8,128)(2,1)S(1)}, bf16[64,512]{1,0:T(8,128)(2,1)S(1)}, u32[]{:S(2)}, u32[]{:S(2)}) collective-permute-start(bf16[64,512]{1,0:T(8,128)(2,1)S(1)} %get-tuple-element.154), channel_id=1, source_target_pairs={{0,4},{2,6},{4,0},{6,2},{1,5},{3,7},{5,1},{7,3},{8,12},{10,14},{12... | collective-permute-start | bytes 196616 | tf_op jit(solution)/shard_map/ppermute | solution.py:40
  24.6 11.1 %collective-permute-start.3 = (s32[1,256]{1,0:T(1,128)S(1)}, s32[1,256]{1,0:T(1,128)S(1)}, u32[]{:S(2)}, u32[]{:S(2)}) collective-permute-start(s32[1,256]{1,0:T(1,128)S(1)} %copy-done.21), channel_id=1, source_target_pairs={{0,2},{2,0},{4,6},{6,4},{1,3},{3,1},{5,7},{7,5},{8,10},{10,8},{12,... | collective-permute-start | bytes 3080 | tf_op jit(solution)/shard_map/ppermute | solution.py:40
  25.4 10.4 %collective-permute-start.4 = (s32[1,256]{1,0:T(1,128)S(1)}, s32[1,256]{1,0:T(1,128)S(1)}, u32[]{:S(2)}, u32[]{:S(2)}) collective-permute-start(s32[1,256]{1,0:T(1,128)S(1)} %copy-done.21), channel_id=1, source_target_pairs={{0,4},{2,6},{4,0},{6,2},{1,5},{3,7},{5,1},{7,3},{8,12},{10,14},{12... | collective-permute-start | bytes 3080 | tf_op jit(solution)/shard_map/ppermute | solution.py:40
  27.6 9.6 %collective-permute-start.5 = (s32[1,256]{1,0:T(1,128)S(1)}, s32[1,256]{1,0:T(1,128)S(1)}, u32[]{:S(2)}, u32[]{:S(2)}) collective-permute-start(s32[1,256]{1,0:T(1,128)S(1)} %copy-done.21), channel_id=1, source_target_pairs={{0,6},{2,4},{4,2},{6,0},{1,7},{3,5},{5,3},{7,1},{8,14},{10,12},{12... | collective-permute-start | bytes 3080 | tf_op jit(solution)/shard_map/ppermute | solution.py:40
  28.1 9.2 %collective-permute-start.6 = (bf16[64,1152]{1,0:T(8,128)(2,1)S(1)}, bf16[64,1152]{1,0:T(8,128)(2,1)S(1)}, u32[]{:S(2)}, u32[]{:S(2)}) collective-permute-start(bf16[64,1152]{1,0:T(8,128)(2,1)S(1)} %get-tuple-element.161), channel_id=1, source_target_pairs={{0,2},{2,0},{4,6},{6,4},{1,3},{3,1},{5,7},{7,5},{8,10},{10,8},{12,... | collective-permute-start | bytes 442376 | tf_op jit(solution)/shard_map/ppermute | solution.py:40
  29.8 25.0 %collective-permute-start.10 = (bf16[4,64,512]{2,1,0:T(8,128)(2,1)S(1)}, bf16[4,64,512]{2,1,0:T(8,128)(2,1)S(1)}, u32[]{:S(2)}, u32[]{:S(2)}) collective-permute-start(bf16[4,64,512]{2,1,0:T(8,128)(2,1)S(1)} %pad_maximum_fusion.1.b0), channel_id=1, source_target_pairs={{0,16},{8,24},{16,0},{24,8},{1,17},{9,25},{17,1},{25,9},{2,18},{10... | collective-permute-start | bytes 786440 | tf_op jit(solution)/shard_map/ppermute | solution.py:540
  35.7 27.1 %collective-permute-start.11 = (bf16[4,64,512]{2,1,0:T(8,128)(2,1)S(1)}, bf16[4,64,512]{2,1,0:T(8,128)(2,1)S(1)}, u32[]{:S(2)}, u32[]{:S(2)}) collective-permute-start(bf16[4,64,512]{2,1,0:T(8,128)(2,1)S(1)} %pad_maximum_fusion.1.b0), channel_id=1, source_target_pairs={{0,24},{8,0},{16,8},{24,16},{1,25},{9,1},{17,9},{25,17},{2,26},{10... | collective-permute-start | bytes 786440 | tf_op jit(solution)/shard_map/ppermute | solution.py:540
  35.7 27.1 %collective-permute-start.9 = (bf16[4,64,512]{2,1,0:T(8,128)(2,1)S(1)}, bf16[4,64,512]{2,1,0:T(8,128)(2,1)S(1)}, u32[]{:S(2)}, u32[]{:S(2)}) collective-permute-start(bf16[4,64,512]{2,1,0:T(8,128)(2,1)S(1)} %pad_maximum_fusion.1.b0), channel_id=1, source_target_pairs={{0,8},{8,16},{16,24},{24,0},{1,9},{9,17},{17,25},{25,1},{2,10},{10... | collective-permute-start | bytes 786440 | tf_op jit(solution)/shard_map/ppermute | solution.py:540
  37.2 5.9 %collective-permute-start.7 = (bf16[64,1152]{1,0:T(8,128)(2,1)S(1)}, bf16[64,1152]{1,0:T(8,128)(2,1)S(1)}, u32[]{:S(2)}, u32[]{:S(2)}) collective-permute-start(bf16[64,1152]{1,0:T(8,128)(2,1)S(1)} %get-tuple-element.162), channel_id=1, source_target_pairs={{0,4},{2,6},{4,0},{6,2},{1,5},{3,7},{5,1},{7,3},{8,12},{10,14},{12... | collective-permute-start | bytes 442376 | tf_op jit(solution)/shard_map/ppermute | solution.py:40
  37.4 5.7 %collective-permute-start.8 = (bf16[64,1152]{1,0:T(8,128)(2,1)S(1)}, bf16[64,1152]{1,0:T(8,128)(2,1)S(1)}, u32[]{:S(2)}, u32[]{:S(2)}) collective-permute-start(bf16[64,1152]{1,0:T(8,128)(2,1)S(1)} %get-tuple-element.163), channel_id=1, source_target_pairs={{0,6},{2,4},{4,2},{6,0},{1,7},{3,5},{5,3},{7,1},{8,14},{10,12},{12... | collective-permute-start | bytes 442376 | tf_op jit(solution)/shard_map/ppermute | solution.py:40
  62.9 135.2 %reduce-scatter.2.cloned.1.call-start = ((), (), s32[]{:S(2)}) async-start(), calls=%async_computation.4 | async-start | bytes 5308416 | tf_op jit(solution)/shard_map/reduce_scatter | solution.py:716
  63.2 7.9 %collective-permute-start.16 = (bf16[1024,512]{1,0:T(8,128)(2,1)S(1)}, bf16[1024,512]{1,0:T(8,128)(2,1)}, u32[]{:S(2)}, u32[]{:S(2)}) collective-permute-start(bf16[1024,512]{1,0:T(8,128)(2,1)S(1)} %bitcast.51), channel_id=1, source_target_pairs={{0,1},{1,0},{2,3},{3,2},{4,5},{5,4},{6,7},{7,6},{8,9},{9,8},{10,11... | collective-permute-start | bytes 3145736 | tf_op jit(solution)/shard_map/ppermute | solution.py:36
  68.2 7.7 %collective-permute-start.13 = (bf16[128,1024]{1,0:T(8,128)(2,1)S(1)}, bf16[128,1024]{1,0:T(8,128)(2,1)S(1)}, u32[]{:S(2)}, u32[]{:S(2)}) collective-permute-start(bf16[128,1024]{1,0:T(8,128)(2,1)S(1)} %get-tuple-element.174.n0), channel_id=1, source_target_pairs={{0,2},{2,0},{4,6},{6,4},{1,3},{3,1},{5,7},{7,5},{8,10},{10,8},{12,... | collective-permute-start | bytes 786440 | tf_op jit(solution)/shard_map/ppermute | solution.py:40
  69.4 7.3 %collective-permute-start.14 = (bf16[128,1024]{1,0:T(8,128)(2,1)S(1)}, bf16[128,1024]{1,0:T(8,128)(2,1)S(1)}, u32[]{:S(2)}, u32[]{:S(2)}) collective-permute-start(bf16[128,1024]{1,0:T(8,128)(2,1)S(1)} %get-tuple-element.174.n0), channel_id=1, source_target_pairs={{0,4},{2,6},{4,0},{6,2},{1,5},{3,7},{5,1},{7,3},{8,12},{10,14},{12... | collective-permute-start | bytes 786440 | tf_op jit(solution)/shard_map/ppermute | solution.py:40
  70.8 11.8 %collective-permute-start.15 = (bf16[128,1024]{1,0:T(8,128)(2,1)S(1)}, bf16[128,1024]{1,0:T(8,128)(2,1)S(1)}, u32[]{:S(2)}, u32[]{:S(2)}) collective-permute-start(bf16[128,1024]{1,0:T(8,128)(2,1)S(1)} %get-tuple-element.174.n0), channel_id=1, source_target_pairs={{0,6},{2,4},{4,2},{6,0},{1,7},{3,5},{5,3},{7,1},{8,14},{10,12},{12... | collective-permute-start | bytes 786440 | tf_op jit(solution)/shard_map/ppermute | solution.py:40
  87.6 10.7 %collective-permute-start.18 = (bf16[128,1024]{1,0:T(8,128)(2,1)S(1)}, bf16[128,1024]{1,0:T(8,128)(2,1)S(1)}, u32[]{:S(2)}, u32[]{:S(2)}) collective-permute-start(bf16[128,1024]{1,0:T(8,128)(2,1)S(1)} %get-tuple-element.187.y0.refs_1_), channel_id=1, source_target_pairs={{0,2},{2,0},{4,6},{6,4},{1,3},{3,1},{5,7},{7,5},{8,10},{10,8},{12,... | collective-permute-start | bytes 786440 | tf_op jit(solution)/shard_map/ppermute | solution.py:40
  88.1 10.3 %collective-permute-start.19 = (bf16[128,1024]{1,0:T(8,128)(2,1)S(1)}, bf16[128,1024]{1,0:T(8,128)(2,1)}, u32[]{:S(2)}, u32[]{:S(2)}) collective-permute-start(bf16[128,1024]{1,0:T(8,128)(2,1)S(1)} %get-tuple-element.187.y0.refs_1_), channel_id=1, source_target_pairs={{0,4},{2,6},{4,0},{6,2},{1,5},{3,7},{5,1},{7,3},{8,12},{10,14},{12... | collective-permute-start | bytes 786440 | tf_op jit(solution)/shard_map/ppermute | solution.py:40
  89.3 13.1 %collective-permute-start.20 = (bf16[128,1024]{1,0:T(8,128)(2,1)S(1)}, bf16[128,1024]{1,0:T(8,128)(2,1)}, u32[]{:S(2)}, u32[]{:S(2)}) collective-permute-start(bf16[128,1024]{1,0:T(8,128)(2,1)S(1)} %get-tuple-element.187.y0.refs_1_), channel_id=1, source_target_pairs={{0,6},{2,4},{4,2},{6,0},{1,7},{3,5},{5,3},{7,1},{8,14},{10,12},{12... | collective-permute-start | bytes 786440 | tf_op jit(solution)/shard_map/ppermute | solution.py:40
  102.3 7.0 %collective-permute-start.21 = (bf16[128,1024]{1,0:T(8,128)(2,1)S(1)}, bf16[128,1024]{1,0:T(8,128)(2,1)S(1)}, u32[]{:S(2)}, u32[]{:S(2)}) collective-permute-start(bf16[128,1024]{1,0:T(8,128)(2,1)S(1)} %get-tuple-element.189), channel_id=1, source_target_pairs={{0,2},{2,0},{4,6},{6,4},{1,3},{3,1},{5,7},{7,5},{8,10},{10,8},{12,... | collective-permute-start | bytes 786440 | tf_op jit(solution)/shard_map/ppermute | solution.py:40
  102.6 7.0 %collective-permute-start.22 = (bf16[128,1024]{1,0:T(8,128)(2,1)S(1)}, bf16[128,1024]{1,0:T(8,128)(2,1)S(1)}, u32[]{:S(2)}, u32[]{:S(2)}) collective-permute-start(bf16[128,1024]{1,0:T(8,128)(2,1)S(1)} %get-tuple-element.190), channel_id=1, source_target_pairs={{0,4},{2,6},{4,0},{6,2},{1,5},{3,7},{5,1},{7,3},{8,12},{10,14},{12... | collective-permute-start | bytes 786440 | tf_op jit(solution)/shard_map/ppermute | solution.py:40
  103.8 10.7 %collective-permute-start.23 = (bf16[128,1024]{1,0:T(8,128)(2,1)S(1)}, bf16[128,1024]{1,0:T(8,128)(2,1)S(1)}, u32[]{:S(2)}, u32[]{:S(2)}) collective-permute-start(bf16[128,1024]{1,0:T(8,128)(2,1)S(1)} %get-tuple-element.191), channel_id=1, source_target_pairs={{0,6},{2,4},{4,2},{6,0},{1,7},{3,5},{5,3},{7,1},{8,14},{10,12},{12... | collective-permute-start | bytes 786440 | tf_op jit(solution)/shard_map/ppermute | solution.py:40
  114.7 5.7 %collective-permute-start.24 = (bf16[128,1024]{1,0:T(8,128)(2,1)S(1)}, bf16[128,1024]{1,0:T(8,128)(2,1)S(1)}, u32[]{:S(2)}, u32[]{:S(2)}) collective-permute-start(bf16[128,1024]{1,0:T(8,128)(2,1)S(1)} %get-tuple-element.192.n0), channel_id=1, source_target_pairs={{0,2},{2,0},{4,6},{6,4},{1,3},{3,1},{5,7},{7,5},{8,10},{10,8},{12,... | collective-permute-start | bytes 786440 | tf_op jit(solution)/shard_map/ppermute | solution.py:40
  116.1 7.2 %collective-permute-start.25 = (bf16[128,1024]{1,0:T(8,128)(2,1)S(1)}, bf16[128,1024]{1,0:T(8,128)(2,1)S(1)}, u32[]{:S(2)}, u32[]{:S(2)}) collective-permute-start(bf16[128,1024]{1,0:T(8,128)(2,1)S(1)} %get-tuple-element.192.n0), channel_id=1, source_target_pairs={{0,4},{2,6},{4,0},{6,2},{1,5},{3,7},{5,1},{7,3},{8,12},{10,14},{12... | collective-permute-start | bytes 786440 | tf_op jit(solution)/shard_map/ppermute | solution.py:40
  116.6 11.0 %collective-permute-start.26 = (bf16[128,1024]{1,0:T(8,128)(2,1)S(1)}, bf16[128,1024]{1,0:T(8,128)(2,1)S(1)}, u32[]{:S(2)}, u32[]{:S(2)}) collective-permute-start(bf16[128,1024]{1,0:T(8,128)(2,1)S(1)} %get-tuple-element.192.n0), channel_id=1, source_target_pairs={{0,6},{2,4},{4,2},{6,0},{1,7},{3,5},{5,3},{7,1},{8,14},{10,12},{12... | collective-permute-start | bytes 786440 | tf_op jit(solution)/shard_map/ppermute | solution.py:40
  136.1 13.0 %collective-permute-start.28 = (bf16[128,1024]{1,0:T(8,128)(2,1)S(1)}, bf16[128,1024]{1,0:T(8,128)(2,1)S(1)}, u32[]{:S(2)}, u32[]{:S(2)}) collective-permute-start(bf16[128,1024]{1,0:T(8,128)(2,1)S(1)} %get-tuple-element.212), channel_id=1, source_target_pairs={{0,4},{2,6},{4,0},{6,2},{1,5},{3,7},{5,1},{7,3},{8,12},{10,14},{12... | collective-permute-start | bytes 786440 | tf_op jit(solution)/shard_map/ppermute | solution.py:40
  136.2 12.9 %collective-permute-start.29 = (bf16[128,1024]{1,0:T(8,128)(2,1)S(1)}, bf16[128,1024]{1,0:T(8,128)(2,1)S(1)}, u32[]{:S(2)}, u32[]{:S(2)}) collective-permute-start(bf16[128,1024]{1,0:T(8,128)(2,1)S(1)} %get-tuple-element.213), channel_id=1, source_target_pairs={{0,6},{2,4},{4,2},{6,0},{1,7},{3,5},{5,3},{7,1},{8,14},{10,12},{12... | collective-permute-start | bytes 786440 | tf_op jit(solution)/shard_map/ppermute | solution.py:40
  137.5 11.6 %collective-permute-start.27 = (bf16[128,1024]{1,0:T(8,128)(2,1)S(1)}, bf16[128,1024]{1,0:T(8,128)(2,1)S(1)}, u32[]{:S(2)}, u32[]{:S(2)}) collective-permute-start(bf16[128,1024]{1,0:T(8,128)(2,1)S(1)} %get-tuple-element.211), channel_id=1, source_target_pairs={{0,2},{2,0},{4,6},{6,4},{1,3},{3,1},{5,7},{7,5},{8,10},{10,8},{12,... | collective-permute-start | bytes 786440 | tf_op jit(solution)/shard_map/ppermute | solution.py:40
  149.4 5.8 %collective-permute-start.30 = (bf16[128,1024]{1,0:T(8,128)(2,1)S(1)}, bf16[128,1024]{1,0:T(8,128)(2,1)S(1)}, u32[]{:S(2)}, u32[]{:S(2)}) collective-permute-start(bf16[128,1024]{1,0:T(8,128)(2,1)S(1)} %get-tuple-element.214.g0), channel_id=1, source_target_pairs={{0,2},{2,0},{4,6},{6,4},{1,3},{3,1},{5,7},{7,5},{8,10},{10,8},{12,... | collective-permute-start | bytes 786440 | tf_op jit(solution)/shard_map/ppermute | solution.py:40
  149.5 9.3 %collective-permute-start.31 = (bf16[128,1024]{1,0:T(8,128)(2,1)S(1)}, bf16[128,1024]{1,0:T(8,128)(2,1)S(1)}, u32[]{:S(2)}, u32[]{:S(2)}) collective-permute-start(bf16[128,1024]{1,0:T(8,128)(2,1)S(1)} %get-tuple-element.214.g0), channel_id=1, source_target_pairs={{0,4},{2,6},{4,0},{6,2},{1,5},{3,7},{5,1},{7,3},{8,12},{10,14},{12... | collective-permute-start | bytes 786440 | tf_op jit(solution)/shard_map/ppermute | solution.py:40
  149.6 9.2 %collective-permute-start.32 = (bf16[128,1024]{1,0:T(8,128)(2,1)S(1)}, bf16[128,1024]{1,0:T(8,128)(2,1)S(1)}, u32[]{:S(2)}, u32[]{:S(2)}) collective-permute-start(bf16[128,1024]{1,0:T(8,128)(2,1)S(1)} %get-tuple-element.214.g0), channel_id=1, source_target_pairs={{0,6},{2,4},{4,2},{6,0},{1,7},{3,5},{5,3},{7,1},{8,14},{10,12},{12... | collective-permute-start | bytes 786440 | tf_op jit(solution)/shard_map/ppermute | solution.py:40
  154.9 11.0 %collective-permute-start.33 = (bf16[128,1024]{1,0:T(8,128)(2,1)S(1)}, bf16[128,1024]{1,0:T(8,128)(2,1)S(1)}, u32[]{:S(2)}, u32[]{:S(2)}) collective-permute-start(bf16[128,1024]{1,0:T(8,128)(2,1)S(1)} %get-tuple-element.230), channel_id=1, source_target_pairs={{0,2},{2,0},{4,6},{6,4},{1,3},{3,1},{5,7},{7,5},{8,10},{10,8},{12,... | collective-permute-start | bytes 786440 | tf_op jit(solution)/shard_map/ppermute | solution.py:40
  155.1 14.9 %collective-permute-start.34 = (bf16[128,1024]{1,0:T(8,128)(2,1)S(1)}, bf16[128,1024]{1,0:T(8,128)(2,1)S(1)}, u32[]{:S(2)}, u32[]{:S(2)}) collective-permute-start(bf16[128,1024]{1,0:T(8,128)(2,1)S(1)} %get-tuple-element.231), channel_id=1, source_target_pairs={{0,4},{2,6},{4,0},{6,2},{1,5},{3,7},{5,1},{7,3},{8,12},{10,14},{12... | collective-permute-start | bytes 786440 | tf_op jit(solution)/shard_map/ppermute | solution.py:40
  155.2 14.8 %collective-permute-start.35 = (bf16[128,1024]{1,0:T(8,128)(2,1)S(1)}, bf16[128,1024]{1,0:T(8,128)(2,1)S(1)}, u32[]{:S(2)}, u32[]{:S(2)}) collective-permute-start(bf16[128,1024]{1,0:T(8,128)(2,1)S(1)} %get-tuple-element.232), channel_id=1, source_target_pairs={{0,6},{2,4},{4,2},{6,0},{1,7},{3,5},{5,3},{7,1},{8,14},{10,12},{12... | collective-permute-start | bytes 786440 | tf_op jit(solution)/shard_map/ppermute | solution.py:40
  170.0 6.7 %collective-permute-start.36 = (bf16[512,512]{1,0:T(8,128)(2,1)S(1)}, bf16[512,512]{1,0:T(8,128)(2,1)S(1)}, u32[]{:S(2)}, u32[]{:S(2)}) collective-permute-start(bf16[512,512]{1,0:T(8,128)(2,1)S(1)} %get-tuple-element.233), channel_id=1, source_target_pairs={{0,1},{1,0},{2,3},{3,2},{4,5},{5,4},{6,7},{7,6},{8,9},{9,8},{10,11... | collective-permute-start | bytes 1572872 | tf_op jit(solution)/shard_map/ppermute | solution.py:36
  180.6 7.8 %collective-permute-start.38 = (bf16[128,1024]{1,0:T(8,128)(2,1)S(1)}, bf16[128,1024]{1,0:T(8,128)(2,1)S(1)}, u32[]{:S(2)}, u32[]{:S(2)}) collective-permute-start(bf16[128,1024]{1,0:T(8,128)(2,1)S(1)} %get-tuple-element.251), channel_id=1, source_target_pairs={{0,2},{2,0},{4,6},{6,4},{1,3},{3,1},{5,7},{7,5},{8,10},{10,8},{12,... | collective-permute-start | bytes 786440 | tf_op jit(solution)/shard_map/ppermute | solution.py:40
  182.0 7.7 %collective-permute-start.39 = (bf16[128,1024]{1,0:T(8,128)(2,1)S(1)}, bf16[128,1024]{1,0:T(8,128)(2,1)S(1)}, u32[]{:S(2)}, u32[]{:S(2)}) collective-permute-start(bf16[128,1024]{1,0:T(8,128)(2,1)S(1)} %get-tuple-element.252), channel_id=1, source_target_pairs={{0,4},{2,6},{4,0},{6,2},{1,5},{3,7},{5,1},{7,3},{8,12},{10,14},{12... | collective-permute-start | bytes 786440 | tf_op jit(solution)/shard_map/ppermute | solution.py:40
  182.1 12.8 %collective-permute-start.40 = (bf16[128,1024]{1,0:T(8,128)(2,1)S(1)}, bf16[128,1024]{1,0:T(8,128)(2,1)S(1)}, u32[]{:S(2)}, u32[]{:S(2)}) collective-permute-start(bf16[128,1024]{1,0:T(8,128)(2,1)S(1)} %get-tuple-element.253), channel_id=1, source_target_pairs={{0,6},{2,4},{4,2},{6,0},{1,7},{3,5},{5,3},{7,1},{8,14},{10,12},{12... | collective-permute-start | bytes 786440 | tf_op jit(solution)/shard_map/ppermute | solution.py:40
  186.1 12.0 %collective-permute-start.42 = (bf16[256,512]{1,0:T(8,128)(2,1)S(1)}, bf16[256,512]{1,0:T(8,128)(2,1)S(1)}, u32[]{:S(2)}, u32[]{:S(2)}) collective-permute-start(bf16[256,512]{1,0:T(8,128)(2,1)S(1)} %get-tuple-element.247), channel_id=1, source_target_pairs={{0,8},{8,16},{16,24},{24,0},{1,9},{9,17},{17,25},{25,1},{2,10},{10... | collective-permute-start | bytes 786440 | tf_op jit(solution)/shard_map/ppermute | solution.py:540
  195.2 6.6 %collective-permute-start.41 = (bf16[128,1024]{1,0:T(8,128)(2,1)S(1)}, bf16[128,1024]{1,0:T(8,128)(2,1)S(1)}, u32[]{:S(2)}, u32[]{:S(2)}) collective-permute-start(bf16[128,1024]{1,0:T(8,128)(2,1)S(1)} %get-tuple-element.261), channel_id=1, source_target_pairs={{0,1},{1,0},{2,3},{3,2},{4,5},{5,4},{6,7},{7,6},{8,9},{9,8},{10,11... | collective-permute-start | bytes 786440 | tf_op jit(solution)/shard_map/ppermute | solution.py:36
  196.8 18.3 %collective-permute-start.46 = (bf16[256,512]{1,0:T(8,128)(2,1)S(1)}, bf16[256,512]{1,0:T(8,128)(2,1)S(1)}, u32[]{:S(2)}, u32[]{:S(2)}) collective-permute-start(bf16[256,512]{1,0:T(8,128)(2,1)S(1)} %get-tuple-element.248), channel_id=1, source_target_pairs={{0,16},{8,24},{16,0},{24,8},{1,17},{9,25},{17,1},{25,9},{2,18},{10... | collective-permute-start | bytes 786440 | tf_op jit(solution)/shard_map/ppermute | solution.py:540
  196.8 21.9 %collective-permute-start.47 = (bf16[256,512]{1,0:T(8,128)(2,1)S(1)}, bf16[256,512]{1,0:T(8,128)(2,1)S(1)}, u32[]{:S(2)}, u32[]{:S(2)}) collective-permute-start(bf16[256,512]{1,0:T(8,128)(2,1)S(1)} %get-tuple-element.249), channel_id=1, source_target_pairs={{0,24},{8,0},{16,8},{24,16},{1,25},{9,1},{17,9},{25,17},{2,26},{10... | collective-permute-start | bytes 786440 | tf_op jit(solution)/shard_map/ppermute | solution.py:540
  200.6 10.2 %collective-permute-start.43 = (bf16[64,1152]{1,0:T(8,128)(2,1)}, bf16[64,1152]{1,0:T(8,128)(2,1)S(1)}, u32[]{:S(2)}, u32[]{:S(2)}) collective-permute-start(bf16[64,1152]{1,0:T(8,128)(2,1)} %get-tuple-element.265), channel_id=1, source_target_pairs={{0,2},{2,0},{4,6},{6,4},{1,3},{3,1},{5,7},{7,5},{8,10},{10,8},{12,... | collective-permute-start | bytes 442376 | tf_op jit(solution)/shard_map/ppermute | solution.py:40
  200.6 10.2 %collective-permute-start.44 = (bf16[64,1152]{1,0:T(8,128)(2,1)S(1)}, bf16[64,1152]{1,0:T(8,128)(2,1)S(1)}, u32[]{:S(2)}, u32[]{:S(2)}) collective-permute-start(bf16[64,1152]{1,0:T(8,128)(2,1)S(1)} %get-tuple-element.266), channel_id=1, source_target_pairs={{0,4},{2,6},{4,0},{6,2},{1,5},{3,7},{5,1},{7,3},{8,12},{10,14},{12... | collective-permute-start | bytes 442376 | tf_op jit(solution)/shard_map/ppermute | solution.py:40
  201.8 9.1 %collective-permute-start.45 = (bf16[64,1152]{1,0:T(8,128)(2,1)S(1)}, bf16[64,1152]{1,0:T(8,128)(2,1)}, u32[]{:S(2)}, u32[]{:S(2)}) collective-permute-start(bf16[64,1152]{1,0:T(8,128)(2,1)S(1)} %get-tuple-element.267), channel_id=1, source_target_pairs={{0,6},{2,4},{4,2},{6,0},{1,7},{3,5},{5,3},{7,1},{8,14},{10,12},{12... | collective-permute-start | bytes 442376 | tf_op jit(solution)/shard_map/ppermute | solution.py:40
  205.2 31.3 %all-to-all-start.1 = ((bf16[16,32,1024]{2,1,0:T(8,128)(2,1)}), bf16[16,32,1024]{2,1,0:T(8,128)(2,1)S(1)}, u32[]{:S(2)}, u32[]{:S(2)}) async-start(bf16[16,32,1024]{2,1,0:T(8,128)(2,1)} %bitcast.21), calls=%async_computation.1 | async-start | bytes 2097152 | tf_op jit(solution)/shard_map/all_to_all | solution.py:782
  219.0 5.9 %collective-permute-start.50 = (bf16[64,512]{1,0:T(8,128)(2,1)S(1)}, bf16[64,512]{1,0:T(8,128)(2,1)S(1)}, u32[]{:S(2)}, u32[]{:S(2)}) collective-permute-start(bf16[64,512]{1,0:T(8,128)(2,1)S(1)} %get-tuple-element.275), channel_id=1, source_target_pairs={{0,6},{2,4},{4,2},{6,0},{1,7},{3,5},{5,3},{7,1},{8,14},{10,12},{12... | collective-permute-start | bytes 196616 | tf_op jit(solution)/shard_map/ppermute | solution.py:40
  (34 other events, 241.7 us)
Sparse Core Ops, SparseCore 0:
  63.0 50.6 all-gather.1
  136.2 56.8 reduce-scatter.1

commit v6 on v5

--- a/solution.py
+++ b/solution.py
@@ -790,7 +790,7 @@
             pieces = call(pick_kernel, [((rows, part.shape[1]), bf16)] * 4, [near_ref, part], [sems((4,))], far_args=(1,))
             return [pieces[0]] + scatter_near(pieces[1:])
 
-        *ffn_grads, sum_f = finished(pieces_of(after(ffn_part, planes[1])), ffn_weights, gain_f, ff_part, ff_pad)
+        *ffn_grads, sum_f = finished(pieces_of(after(ffn_part, planes[3])), ffn_weights, gain_f, ff_part, ff_pad)
         planes[0] = after(planes[0], ffn_grads)
         pieces = call(far_sum_kernel, [((rows, 4 * hp), bf16)] * 4, [near_ref, *planes], us=23)
         pieces = [pieces[0]] + scatter_near(pieces[1:])

time: 250 us -> 250 us (level)
    ppermute x39, waiting for transfers between devices: 54.9 us -> 57.6 us  [near(): return lax.ppermute(value, NEAR, [(i, i ^ k) for i in range(4)])]
  transfers between devices with their start and end apart: 57 -> 57, of which waited for: 27 -> 27; matrix products, arithmetic and copies ran while one was open for 1% -> 1% of each run, Pallas kernels for 20% -> 21%
where the time goes in v6:
time: 250 us; the launch traced here: 248 us
  waiting for transfers between devices  95.1 us (38%)
  starting transfers between devices  68.2 us (27%)
  Pallas kernels  60.9 us (24%)
  between operations  14.7 us (6%)
  local copies, waits for them, and re-layouts  7.49 us (3%)
    pallas_call x33, Pallas kernels, call(): pl.pallas_call(kernel, out_shape=[pltpu.HBM(shape, kind) if i in far_outs...  60.9 us
    ppermute x39, waiting for transfers between devices, near(): return lax.ppermute(value, NEAR, [(i, i ^ k) for i in range(4)])  57.6 us
    ppermute x39, starting transfers between devices, near(): return lax.ppermute(value, NEAR, [(i, i ^ k) for i in range(4)])  36.6 us
    ppermute x6, waiting for transfers between devices, far_shift(): return lax.ppermute(value, FAR, [(i, (i + k) % far) for i in range(far)])  23.3 us
    ppermute x8, starting transfers between devices, swap(): return lax.ppermute(value, CORE, [(0, 1), (1, 0)])  11.6 us
    all_to_all x1, waiting for transfers between devices, returned(): lax.all_to_all(spread.reshape(peers, slot_cap, width), DP, 0, 0, tiled=True)  8.51 us
    ppermute x6, starting transfers between devices, far_shift(): return lax.ppermute(value, FAR, [(i, (i + k) % far) for i in range(far)])  7.53 us
    all_to_all x1, starting transfers between devices, body(): lax.all_to_all(both, DP, 0, 0, tiled=True).reshape(slot_count, width)  6.66 us
  transfers between devices with their start and end apart: 57, of which 27 were waited for; matrix products, arithmetic and copies ran while one was open for 1% of the time, Pallas kernels for 21%

profile of v6, /device:TPU:9, one launch (start us, length us, event | category | flops | bytes accessed | tf_op | source)
XLA Modules:
  0.0 248.5 jit_solution(5868164190984110697)
XLA Ops:
  9.6 6.7 %all-to-all-start = ((bf16[16,32,1024]{2,1,0:T(8,128)(2,1)}), bf16[16,32,1024]{2,1,0:T(8,128)(2,1)S(1)}, u32[]{:S(2)}, u32[]{:S(2)}) async-start(bf16[16,32,1024]{2,1,0:T(8,128)(2,1)} %pad_maximum_fusion), calls=%async_computation | async-start | bytes 2097152 | tf_op jit(solution)/shard_map/all_to_all | solution.py:546
  21.7 2.9 %collective-permute-done.1 = bf16[64,512]{1,0:T(8,128)(2,1)S(1)} collective-permute-done((bf16[64,512]{1,0:T(8,128)(2,1)S(1)}, bf16[64,512]{1,0:T(8,128)(2,1)S(1)}, u32[]{:S(2)}, u32[]{:S(2)}) %collective-permute-start.1) | collective-permute-done | bytes 65568 | tf_op jit(solution)/shard_map/ppermute | solution.py:40
  25.4 2.2 collective-permute-start.4
  29.8 5.9 %collective-permute-start.10 = (bf16[4,64,512]{2,1,0:T(8,128)(2,1)S(1)}, bf16[4,64,512]{2,1,0:T(8,128)(2,1)S(1)}, u32[]{:S(2)}, u32[]{:S(2)}) collective-permute-start(bf16[4,64,512]{2,1,0:T(8,128)(2,1)S(1)} %pad_maximum_fusion.1.b0), channel_id=1, source_target_pairs={{0,16},{8,24},{16,0},{24,8},{1,17},{9,25},{17,1},{25,9},{2,18},{10... | collective-permute-start | bytes 786440 | tf_op jit(solution)/shard_map/ppermute | solution.py:540
  37.4 2.3 collective-permute-start.8
  40.0 3.1 %collective-permute-done.7.b2 = bf16[64,1152]{1,0:T(8,128)(2,1)S(1)} collective-permute-done((bf16[64,1152]{1,0:T(8,128)(2,1)S(1)}, bf16[64,1152]{1,0:T(8,128)(2,1)S(1)}, u32[]{:S(2)}, u32[]{:S(2)}) %collective-permute-start.7) | collective-permute-done | bytes 147488 | tf_op jit(solution)/shard_map/ppermute | solution.py:40
  43.9 11.0 %collective-permute-done.10.b2 = bf16[4,64,512]{2,1,0:T(8,128)(2,1)S(1)} collective-permute-done((bf16[4,64,512]{2,1,0:T(8,128)(2,1)S(1)}, bf16[4,64,512]{2,1,0:T(8,128)(2,1)S(1)}, u32[]{:S(2)}, u32[]{:S(2)}) %collective-permute-start.10) | collective-permute-done | bytes 262176 | tf_op jit(solution)/shard_map/ppermute | solution.py:540
  54.9 8.0 %collective-permute-done.11.b3 = bf16[4,64,512]{2,1,0:T(8,128)(2,1)S(1)} collective-permute-done((bf16[4,64,512]{2,1,0:T(8,128)(2,1)S(1)}, bf16[4,64,512]{2,1,0:T(8,128)(2,1)S(1)}, u32[]{:S(2)}, u32[]{:S(2)}) %collective-permute-start.11) | collective-permute-done | bytes 262176 | tf_op jit(solution)/shard_map/ppermute | solution.py:540
  65.3 2.1 collective-permute-done.12.other
  71.1 2.7 %shard_map.218 = (bf16[2,1024,512]{2,1,0:T(8,128)(2,1)S(1)}, bf16[2,1024,512]{2,1,0:T(8,128)(2,1)}) custom-call(s32[1]{0:T(128)} %bitcast.core, bf16[1024,512]{1,0:T(8,128)(2,1)S(1)} %bitcast.52, bf16[1024,512]{1,0:T(8,128)(2,1)} %collective-permute-done.16.other), custom_call_target="tpu_custom_call" | custom-call | flops 1000000000 | bytes 1000000 | tf_op jit(solution)/shard_map/pallas_call | solution.py:66
  73.8 2.1 collective-permute-done.13.n1
  76.7 5.8 %collective-permute-done.15.n3 = bf16[128,1024]{1,0:T(8,128)(2,1)S(1)} collective-permute-done((bf16[128,1024]{1,0:T(8,128)(2,1)S(1)}, bf16[128,1024]{1,0:T(8,128)(2,1)S(1)}, u32[]{:S(2)}, u32[]{:S(2)}) %collective-permute-start.15) | collective-permute-done | bytes 262176 | tf_op jit(solution)/shard_map/ppermute | solution.py:40
  83.3 2.4 shard_map.219
  85.7 2.0 collective-permute-start.17
  90.4 8.0 %shard_map.220 = (bf16[16,256,128]{2,1,0:T(8,128)(2,1)}, bf16[512,256]{1,0:T(8,128)(2,1)}, bf16[512,512]{1,0:T(8,128)(2,1)}, bf16[512,512]{1,0:T(8,128)(2,1)}, b...) custom-call(s32[1]{0:T(128)} %bitcast.core, ...), custom_call_target="tpu_custom_call" | custom-call | tf_op jit(solution)/shard_map/pallas_call | solution.py:66
  98.4 3.9 %collective-permute-done.20.y3 = bf16[128,1024]{1,0:T(8,128)(2,1)} collective-permute-done((bf16[128,1024]{1,0:T(8,128)(2,1)S(1)}, bf16[128,1024]{1,0:T(8,128)(2,1)}, u32[]{:S(2)}, u32[]{:S(2)}) %collective-permute-start.20) | collective-permute-done | bytes 262176 | tf_op jit(solution)/shard_map/ppermute | solution.py:40
  105.0 4.3 %collective-permute-done.21.b1 = bf16[128,1024]{1,0:T(8,128)(2,1)S(1)} collective-permute-done((bf16[128,1024]{1,0:T(8,128)(2,1)S(1)}, bf16[128,1024]{1,0:T(8,128)(2,1)S(1)}, u32[]{:S(2)}, u32[]{:S(2)}) %collective-permute-start.21) | collective-permute-done | bytes 262176 | tf_op jit(solution)/shard_map/ppermute | solution.py:40
  109.6 4.8 %collective-permute-done.23.b3 = bf16[128,1024]{1,0:T(8,128)(2,1)S(1)} collective-permute-done((bf16[128,1024]{1,0:T(8,128)(2,1)S(1)}, bf16[128,1024]{1,0:T(8,128)(2,1)S(1)}, u32[]{:S(2)}, u32[]{:S(2)}) %collective-permute-start.23) | collective-permute-done | bytes 262176 | tf_op jit(solution)/shard_map/ppermute | solution.py:40
  117.7 2.7 %shard_map.222 = (bf16[256,1024]{1,0:T(8,128)(2,1)S(1)}, bf16[256,1024]{1,0:T(8,128)(2,1)S(1)}, bf16[2,1024,1152]{2,1,0:T(8,128)(2,1)S(1)}) custom-call(bf16[128,1024]{1,0:T(8,128)(2,1)} %copy-done, bf16[128,1024]{1,0:T(8,128)(2,1)} %copy-done.22, bf16[128,1024]{1,0:T(8,128)(2,1)} %collective-permute-done.19.y2, ...), custom_call_target="tpu_custom_call" | custom-call | flops 2000000000 | bytes 2000000 | tf_op jit(solution)/shard_map/pallas_call | solution.py:66
  120.4 2.9 %shard_map.223 = (bf16[512,2304]{1,0:T(8,128)(2,1)S(1)}, bf16[512,1024]{1,0:T(8,128)(2,1)S(1)}, f32[128,1024]{1,0:T(8,128)}, f32[128,1024]{1,0:T(8,128)S(1)}, bf16[128,1024]{1,0:T(8,128)(2,1)S(1)}) custom-call(bf16[128,1024]{1,0:T(8,128)(2,1)S(1)} %get-tuple-element.192.n0, bf16[128,1024]{1,0:T(8,128)(2,1)S(1)} %collective-permute-done.24.n1, ...), custom_call_target="tpu_custom_call" | custom-call | flops 3000000000 | bytes 3000000 | tf_op jit(solution)/shard_map/pallas_call | solution.py:66
  123.3 4.3 %collective-permute-done.26.n1 = bf16[128,1024]{1,0:T(8,128)(2,1)S(1)} collective-permute-done((bf16[128,1024]{1,0:T(8,128)(2,1)S(1)}, bf16[128,1024]{1,0:T(8,128)(2,1)S(1)}, u32[]{:S(2)}, u32[]{:S(2)}) %collective-permute-start.26) | collective-permute-done | bytes 262176 | tf_op jit(solution)/shard_map/ppermute | solution.py:40
  127.7 2.9 %shard_map.225 = (bf16[512,2304]{1,0:T(8,128)(2,1)S(1)}, bf16[512,1024]{1,0:T(8,128)(2,1)S(1)}, bf16[128,1024]{1,0:T(8,128)(2,1)S(1)}, bf16[128,1024]{1,0:T(8,128)(2,1)S(1)}) custom-call(bf16[128,1024]{1,0:T(8,128)(2,1)S(1)} %collective-permute-done.25.n0, ...), custom_call_target="tpu_custom_call", output_to_operand_aliasing={{0}: (4, {}), {1}: (5, {})} | custom-call | flops 3000000000 | bytes 3000000 | tf_op jit(solution)/shard_map/pallas_call | solution.py:66
  130.6 5.5 %shard_map.226 = (bf16[4,2,256,1152]{3,2,1,0:T(8,128)(2,1)}, f32[128,1024]{1,0:T(8,128)}) custom-call(bf16[512,1024]{1,0:T(8,128)(2,1)S(1)} %get-tuple-element.203.all_n, bf16[128,1024]{1,0:T(8,128)(2,1)} %copy-done, bf16[128,1024]{1,0:T(8,128)(2,1)} %copy-done.22, bf16[128,1024]{1,0:T(8,128)(2,1)} %collective-permute-done.19.y2, ...), custom_call_target="tpu_custom_call" | custom-call | flops 4000000000 | bytes 4000000 | tf_op jit(solution)/shard_map/pallas_call | solution.py:66
  138.8 1.7 copy-done.13
  140.5 3.3 %shard_map.227 = (f32[128,1024]{1,0:T(8,128)}, bf16[128,1024]{1,0:T(8,128)(2,1)S(1)}, bf16[128,1024]{1,0:T(8,128)(2,1)S(1)}, bf16[128,1024]{1,0:T(8,128)(2,1)S(1)}) custom-call(bf16[512,2304]{1,0:T(8,128)(2,1)S(1)} %copy-done.13, bf16[2,1024,1152]{2,1,0:T(8,128)(2,1)} %bitcast.60), custom_call_target="tpu_custom_call" | custom-call | flops 2000000000 | bytes 2000000 | tf_op jit(solution)/shard_map/pallas_call | solution.py:66
  146.0 3.1 %collective-permute-done.28.b2 = bf16[128,1024]{1,0:T(8,128)(2,1)S(1)} collective-permute-done((bf16[128,1024]{1,0:T(8,128)(2,1)S(1)}, bf16[128,1024]{1,0:T(8,128)(2,1)S(1)}, u32[]{:S(2)}, u32[]{:S(2)}) %collective-permute-start.28) | collective-permute-done | bytes 262176 | tf_op jit(solution)/shard_map/ppermute | solution.py:40
  149.6 2.6 %collective-permute-start.32 = (bf16[128,1024]{1,0:T(8,128)(2,1)S(1)}, bf16[128,1024]{1,0:T(8,128)(2,1)S(1)}, u32[]{:S(2)}, u32[]{:S(2)}) collective-permute-start(bf16[128,1024]{1,0:T(8,128)(2,1)S(1)} %get-tuple-element.214.g0), channel_id=1, source_target_pairs={{0,6},{2,4},{4,2},{6,0},{1,7},{3,5},{5,3},{7,1},{8,14},{10,12},{12... | collective-permute-start | bytes 786440 | tf_op jit(solution)/shard_map/ppermute | solution.py:40
  153.2 1.7 shard_map.231
  155.2 2.4 collective-permute-start.35
  158.7 6.2 %shard_map.232 = (bf16[512,256]{1,0:T(8,128)(2,1)S(1)}, f32[512,512]{1,0:T(8,128)S(1)}, bf16[512,512]{1,0:T(8,128)(2,1)S(1)}, bf16[2,1024,384]{2,1,0:T(8,128)(2,...) custom-call(bf16[128,1024]{1,0:T(8,128)(2,1)S(1)} %get-tuple-element.214.g0, ...), custom_call_target="tpu_custom_call" | custom-call | flops 7000000000 | bytes 7000000 | tf_op jit(solution)/shard_map/pallas_call | solution.py:66
  165.9 4.1 %collective-permute-done.34.b2 = bf16[128,1024]{1,0:T(8,128)(2,1)S(1)} collective-permute-done((bf16[128,1024]{1,0:T(8,128)(2,1)S(1)}, bf16[128,1024]{1,0:T(8,128)(2,1)S(1)}, u32[]{:S(2)}, u32[]{:S(2)}) %collective-permute-start.34) | collective-permute-done | bytes 262176 | tf_op jit(solution)/shard_map/ppermute | solution.py:40
  170.0 5.1 %collective-permute-start.36 = (bf16[512,512]{1,0:T(8,128)(2,1)S(1)}, bf16[512,512]{1,0:T(8,128)(2,1)S(1)}, u32[]{:S(2)}, u32[]{:S(2)}) collective-permute-start(bf16[512,512]{1,0:T(8,128)(2,1)S(1)} %get-tuple-element.233), channel_id=1, source_target_pairs={{0,1},{1,0},{2,3},{3,2},{4,5},{5,4},{6,7},{7,6},{8,9},{9,8},{10,11... | collective-permute-start | bytes 1572872 | tf_op jit(solution)/shard_map/ppermute | solution.py:36
  175.1 1.5 collective-permute-done.36.back
  176.7 1.6 shard_map.234
  178.3 1.9 shard_map.235
  186.2 2.3 collective-permute-done.38.b1
  189.8 5.1 %collective-permute-done.40.b3 = bf16[128,1024]{1,0:T(8,128)(2,1)S(1)} collective-permute-done((bf16[128,1024]{1,0:T(8,128)(2,1)S(1)}, bf16[128,1024]{1,0:T(8,128)(2,1)S(1)}, u32[]{:S(2)}, u32[]{:S(2)}) %collective-permute-start.40) | collective-permute-done | bytes 262176 | tf_op jit(solution)/shard_map/ppermute | solution.py:40
  195.2 1.5 collective-permute-start.41
  197.0 1.8 shard_map.240
  202.3 1.7 shard_map.239
  204.0 5.6 %all-to-all-start.1 = ((bf16[16,32,1024]{2,1,0:T(8,128)(2,1)}), bf16[16,32,1024]{2,1,0:T(8,128)(2,1)S(1)}, u32[]{:S(2)}, u32[]{:S(2)}) async-start(bf16[16,32,1024]{2,1,0:T(8,128)(2,1)} %bitcast.21), calls=%async_computation.1 | async-start | bytes 2097152 | tf_op jit(solution)/shard_map/all_to_all | solution.py:782
  210.6 3.2 %shard_map.241 = (f32[64,1408]{1,0:T(8,128)}, f32[64,1408]{1,0:T(8,128)}, f32[64,1408]{1,0:T(8,128)}, f32[64,1]{1,0:T(8,128)S(1)}) custom-call(s32[1]{0:T(128)} %bitcast.6.me, f32[64,1]{1,0:T(8,128)S(1)} %copy.49.gain, bf16[64,1152]{1,0:T(8,128)(2,1)S(1)} %copy-done.17, bf16[64,1152]{1,0:T(8,128)(2,1)S(1)} %collective-permute-done.43.s1, ...), custom_call_target="tpu_custom_call" | custom-call | flops 1000000000 | bytes 1000000 | tf_op jit(solution)/shard_map/pallas_call | solution.py:66
  213.7 4.3 %collective-permute-done.47.t2 = bf16[256,512]{1,0:T(8,128)(2,1)S(1)} collective-permute-done((bf16[256,512]{1,0:T(8,128)(2,1)S(1)}, bf16[256,512]{1,0:T(8,128)(2,1)S(1)}, u32[]{:S(2)}, u32[]{:S(2)}) %collective-permute-start.47) | collective-permute-done | bytes 262176 | tf_op jit(solution)/shard_map/ppermute | solution.py:540
  219.1 1.8 collective-permute-start.50
  221.5 5.4 %collective-permute-done.50.s3 = bf16[64,512]{1,0:T(8,128)(2,1)S(1)} collective-permute-done((bf16[64,512]{1,0:T(8,128)(2,1)S(1)}, bf16[64,512]{1,0:T(8,128)(2,1)S(1)}, u32[]{:S(2)}, u32[]{:S(2)}) %collective-permute-start.50) | collective-permute-done | bytes 65568 | tf_op jit(solution)/shard_map/ppermute | solution.py:40
  227.9 8.5 %all-to-all-done.1 = bf16[16,32,1024]{2,1,0:T(8,128)(2,1)S(1)} async-done(((bf16[16,32,1024]{2,1,0:T(8,128)(2,1)}), bf16[16,32,1024]{2,1,0:T(8,128)(2,1)S(1)}, u32[]{:S(2)}, u32[]{:S(2)}) %all-to-all-start.1) | async-done | bytes 1048608 | tf_op jit(solution)/shard_map/all_to_all | solution.py:782
  237.5 2.0 collective-permute-done.52
  240.1 1.5 shard_map.244
  (176 shorter events, 55.2 us)
Async XLA Ops:
  9.6 53.2 %all-to-all-start = ((bf16[16,32,1024]{2,1,0:T(8,128)(2,1)}), bf16[16,32,1024]{2,1,0:T(8,128)(2,1)S(1)}, u32[]{:S(2)}, u32[]{:S(2)}) async-start(bf16[16,32,1024]{2,1,0:T(8,128)(2,1)} %pad_maximum_fusion), calls=%async_computation | async-start | bytes 2097152 | tf_op jit(solution)/shard_map/all_to_all | solution.py:546
  16.3 101.4 %all-gather.2.cloned.1.call-start = ((), (), s32[]{:S(2)}) async-start(), calls=%async_computation.3 | async-start | bytes 5308416 | tf_op jit(solution)/shard_map/all_gather | solution.py:570
  17.9 6.6 %collective-permute-start.1 = (bf16[64,512]{1,0:T(8,128)(2,1)S(1)}, bf16[64,512]{1,0:T(8,128)(2,1)S(1)}, u32[]{:S(2)}, u32[]{:S(2)}) collective-permute-start(bf16[64,512]{1,0:T(8,128)(2,1)S(1)} %get-tuple-element.154), channel_id=1, source_target_pairs={{0,4},{2,6},{4,0},{6,2},{1,5},{3,7},{5,1},{7,3},{8,12},{10,14},{12... | collective-permute-start | bytes 196616 | tf_op jit(solution)/shard_map/ppermute | solution.py:40
  24.6 11.1 %collective-permute-start.3 = (s32[1,256]{1,0:T(1,128)S(1)}, s32[1,256]{1,0:T(1,128)S(1)}, u32[]{:S(2)}, u32[]{:S(2)}) collective-permute-start(s32[1,256]{1,0:T(1,128)S(1)} %copy-done.21), channel_id=1, source_target_pairs={{0,2},{2,0},{4,6},{6,4},{1,3},{3,1},{5,7},{7,5},{8,10},{10,8},{12,... | collective-permute-start | bytes 3080 | tf_op jit(solution)/shard_map/ppermute | solution.py:40
  25.4 10.4 %collective-permute-start.4 = (s32[1,256]{1,0:T(1,128)S(1)}, s32[1,256]{1,0:T(1,128)S(1)}, u32[]{:S(2)}, u32[]{:S(2)}) collective-permute-start(s32[1,256]{1,0:T(1,128)S(1)} %copy-done.21), channel_id=1, source_target_pairs={{0,4},{2,6},{4,0},{6,2},{1,5},{3,7},{5,1},{7,3},{8,12},{10,14},{12... | collective-permute-start | bytes 3080 | tf_op jit(solution)/shard_map/ppermute | solution.py:40
  27.6 9.6 %collective-permute-start.5 = (s32[1,256]{1,0:T(1,128)S(1)}, s32[1,256]{1,0:T(1,128)S(1)}, u32[]{:S(2)}, u32[]{:S(2)}) collective-permute-start(s32[1,256]{1,0:T(1,128)S(1)} %copy-done.21), channel_id=1, source_target_pairs={{0,6},{2,4},{4,2},{6,0},{1,7},{3,5},{5,3},{7,1},{8,14},{10,12},{12... | collective-permute-start | bytes 3080 | tf_op jit(solution)/shard_map/ppermute | solution.py:40
  28.1 9.2 %collective-permute-start.6 = (bf16[64,1152]{1,0:T(8,128)(2,1)S(1)}, bf16[64,1152]{1,0:T(8,128)(2,1)S(1)}, u32[]{:S(2)}, u32[]{:S(2)}) collective-permute-start(bf16[64,1152]{1,0:T(8,128)(2,1)S(1)} %get-tuple-element.161), channel_id=1, source_target_pairs={{0,2},{2,0},{4,6},{6,4},{1,3},{3,1},{5,7},{7,5},{8,10},{10,8},{12,... | collective-permute-start | bytes 442376 | tf_op jit(solution)/shard_map/ppermute | solution.py:40
  29.8 25.0 %collective-permute-start.10 = (bf16[4,64,512]{2,1,0:T(8,128)(2,1)S(1)}, bf16[4,64,512]{2,1,0:T(8,128)(2,1)S(1)}, u32[]{:S(2)}, u32[]{:S(2)}) collective-permute-start(bf16[4,64,512]{2,1,0:T(8,128)(2,1)S(1)} %pad_maximum_fusion.1.b0), channel_id=1, source_target_pairs={{0,16},{8,24},{16,0},{24,8},{1,17},{9,25},{17,1},{25,9},{2,18},{10... | collective-permute-start | bytes 786440 | tf_op jit(solution)/shard_map/ppermute | solution.py:540
  35.7 27.1 %collective-permute-start.11 = (bf16[4,64,512]{2,1,0:T(8,128)(2,1)S(1)}, bf16[4,64,512]{2,1,0:T(8,128)(2,1)S(1)}, u32[]{:S(2)}, u32[]{:S(2)}) collective-permute-start(bf16[4,64,512]{2,1,0:T(8,128)(2,1)S(1)} %pad_maximum_fusion.1.b0), channel_id=1, source_target_pairs={{0,24},{8,0},{16,8},{24,16},{1,25},{9,1},{17,9},{25,17},{2,26},{10... | collective-permute-start | bytes 786440 | tf_op jit(solution)/shard_map/ppermute | solution.py:540
  35.7 27.1 %collective-permute-start.9 = (bf16[4,64,512]{2,1,0:T(8,128)(2,1)S(1)}, bf16[4,64,512]{2,1,0:T(8,128)(2,1)S(1)}, u32[]{:S(2)}, u32[]{:S(2)}) collective-permute-start(bf16[4,64,512]{2,1,0:T(8,128)(2,1)S(1)} %pad_maximum_fusion.1.b0), channel_id=1, source_target_pairs={{0,8},{8,16},{16,24},{24,0},{1,9},{9,17},{17,25},{25,1},{2,10},{10... | collective-permute-start | bytes 786440 | tf_op jit(solution)/shard_map/ppermute | solution.py:540
  37.2 5.9 %collective-permute-start.7 = (bf16[64,1152]{1,0:T(8,128)(2,1)S(1)}, bf16[64,1152]{1,0:T(8,128)(2,1)S(1)}, u32[]{:S(2)}, u32[]{:S(2)}) collective-permute-start(bf16[64,1152]{1,0:T(8,128)(2,1)S(1)} %get-tuple-element.162), channel_id=1, source_target_pairs={{0,4},{2,6},{4,0},{6,2},{1,5},{3,7},{5,1},{7,3},{8,12},{10,14},{12... | collective-permute-start | bytes 442376 | tf_op jit(solution)/shard_map/ppermute | solution.py:40
  37.4 5.7 %collective-permute-start.8 = (bf16[64,1152]{1,0:T(8,128)(2,1)S(1)}, bf16[64,1152]{1,0:T(8,128)(2,1)S(1)}, u32[]{:S(2)}, u32[]{:S(2)}) collective-permute-start(bf16[64,1152]{1,0:T(8,128)(2,1)S(1)} %get-tuple-element.163), channel_id=1, source_target_pairs={{0,6},{2,4},{4,2},{6,0},{1,7},{3,5},{5,3},{7,1},{8,14},{10,12},{12... | collective-permute-start | bytes 442376 | tf_op jit(solution)/shard_map/ppermute | solution.py:40
  62.9 134.1 %reduce-scatter.2.cloned.1.call-start = ((), (), s32[]{:S(2)}) async-start(), calls=%async_computation.4 | async-start | bytes 5308416 | tf_op jit(solution)/shard_map/reduce_scatter | solution.py:716
  63.2 7.9 %collective-permute-start.16 = (bf16[1024,512]{1,0:T(8,128)(2,1)S(1)}, bf16[1024,512]{1,0:T(8,128)(2,1)}, u32[]{:S(2)}, u32[]{:S(2)}) collective-permute-start(bf16[1024,512]{1,0:T(8,128)(2,1)S(1)} %bitcast.51), channel_id=1, source_target_pairs={{0,1},{1,0},{2,3},{3,2},{4,5},{5,4},{6,7},{7,6},{8,9},{9,8},{10,11... | collective-permute-start | bytes 3145736 | tf_op jit(solution)/shard_map/ppermute | solution.py:36
  68.2 7.7 %collective-permute-start.13 = (bf16[128,1024]{1,0:T(8,128)(2,1)S(1)}, bf16[128,1024]{1,0:T(8,128)(2,1)S(1)}, u32[]{:S(2)}, u32[]{:S(2)}) collective-permute-start(bf16[128,1024]{1,0:T(8,128)(2,1)S(1)} %get-tuple-element.174.n0), channel_id=1, source_target_pairs={{0,2},{2,0},{4,6},{6,4},{1,3},{3,1},{5,7},{7,5},{8,10},{10,8},{12,... | collective-permute-start | bytes 786440 | tf_op jit(solution)/shard_map/ppermute | solution.py:40
  69.4 7.3 %collective-permute-start.14 = (bf16[128,1024]{1,0:T(8,128)(2,1)S(1)}, bf16[128,1024]{1,0:T(8,128)(2,1)S(1)}, u32[]{:S(2)}, u32[]{:S(2)}) collective-permute-start(bf16[128,1024]{1,0:T(8,128)(2,1)S(1)} %get-tuple-element.174.n0), channel_id=1, source_target_pairs={{0,4},{2,6},{4,0},{6,2},{1,5},{3,7},{5,1},{7,3},{8,12},{10,14},{12... | collective-permute-start | bytes 786440 | tf_op jit(solution)/shard_map/ppermute | solution.py:40
  70.8 11.8 %collective-permute-start.15 = (bf16[128,1024]{1,0:T(8,128)(2,1)S(1)}, bf16[128,1024]{1,0:T(8,128)(2,1)S(1)}, u32[]{:S(2)}, u32[]{:S(2)}) collective-permute-start(bf16[128,1024]{1,0:T(8,128)(2,1)S(1)} %get-tuple-element.174.n0), channel_id=1, source_target_pairs={{0,6},{2,4},{4,2},{6,0},{1,7},{3,5},{5,3},{7,1},{8,14},{10,12},{12... | collective-permute-start | bytes 786440 | tf_op jit(solution)/shard_map/ppermute | solution.py:40
  87.6 10.7 %collective-permute-start.18 = (bf16[128,1024]{1,0:T(8,128)(2,1)S(1)}, bf16[128,1024]{1,0:T(8,128)(2,1)S(1)}, u32[]{:S(2)}, u32[]{:S(2)}) collective-permute-start(bf16[128,1024]{1,0:T(8,128)(2,1)S(1)} %get-tuple-element.187.y0.refs_1_), channel_id=1, source_target_pairs={{0,2},{2,0},{4,6},{6,4},{1,3},{3,1},{5,7},{7,5},{8,10},{10,8},{12,... | collective-permute-start | bytes 786440 | tf_op jit(solution)/shard_map/ppermute | solution.py:40
  88.1 10.3 %collective-permute-start.19 = (bf16[128,1024]{1,0:T(8,128)(2,1)S(1)}, bf16[128,1024]{1,0:T(8,128)(2,1)}, u32[]{:S(2)}, u32[]{:S(2)}) collective-permute-start(bf16[128,1024]{1,0:T(8,128)(2,1)S(1)} %get-tuple-element.187.y0.refs_1_), channel_id=1, source_target_pairs={{0,4},{2,6},{4,0},{6,2},{1,5},{3,7},{5,1},{7,3},{8,12},{10,14},{12... | collective-permute-start | bytes 786440 | tf_op jit(solution)/shard_map/ppermute | solution.py:40
  89.3 13.1 %collective-permute-start.20 = (bf16[128,1024]{1,0:T(8,128)(2,1)S(1)}, bf16[128,1024]{1,0:T(8,128)(2,1)}, u32[]{:S(2)}, u32[]{:S(2)}) collective-permute-start(bf16[128,1024]{1,0:T(8,128)(2,1)S(1)} %get-tuple-element.187.y0.refs_1_), channel_id=1, source_target_pairs={{0,6},{2,4},{4,2},{6,0},{1,7},{3,5},{5,3},{7,1},{8,14},{10,12},{12... | collective-permute-start | bytes 786440 | tf_op jit(solution)/shard_map/ppermute | solution.py:40
  102.3 7.0 %collective-permute-start.21 = (bf16[128,1024]{1,0:T(8,128)(2,1)S(1)}, bf16[128,1024]{1,0:T(8,128)(2,1)S(1)}, u32[]{:S(2)}, u32[]{:S(2)}) collective-permute-start(bf16[128,1024]{1,0:T(8,128)(2,1)S(1)} %get-tuple-element.189), channel_id=1, source_target_pairs={{0,2},{2,0},{4,6},{6,4},{1,3},{3,1},{5,7},{7,5},{8,10},{10,8},{12,... | collective-permute-start | bytes 786440 | tf_op jit(solution)/shard_map/ppermute | solution.py:40
  102.6 7.0 %collective-permute-start.22 = (bf16[128,1024]{1,0:T(8,128)(2,1)S(1)}, bf16[128,1024]{1,0:T(8,128)(2,1)S(1)}, u32[]{:S(2)}, u32[]{:S(2)}) collective-permute-start(bf16[128,1024]{1,0:T(8,128)(2,1)S(1)} %get-tuple-element.190), channel_id=1, source_target_pairs={{0,4},{2,6},{4,0},{6,2},{1,5},{3,7},{5,1},{7,3},{8,12},{10,14},{12... | collective-permute-start | bytes 786440 | tf_op jit(solution)/shard_map/ppermute | solution.py:40
  103.8 10.7 %collective-permute-start.23 = (bf16[128,1024]{1,0:T(8,128)(2,1)S(1)}, bf16[128,1024]{1,0:T(8,128)(2,1)S(1)}, u32[]{:S(2)}, u32[]{:S(2)}) collective-permute-start(bf16[128,1024]{1,0:T(8,128)(2,1)S(1)} %get-tuple-element.191), channel_id=1, source_target_pairs={{0,6},{2,4},{4,2},{6,0},{1,7},{3,5},{5,3},{7,1},{8,14},{10,12},{12... | collective-permute-start | bytes 786440 | tf_op jit(solution)/shard_map/ppermute | solution.py:40
  114.7 5.7 %collective-permute-start.24 = (bf16[128,1024]{1,0:T(8,128)(2,1)S(1)}, bf16[128,1024]{1,0:T(8,128)(2,1)S(1)}, u32[]{:S(2)}, u32[]{:S(2)}) collective-permute-start(bf16[128,1024]{1,0:T(8,128)(2,1)S(1)} %get-tuple-element.192.n0), channel_id=1, source_target_pairs={{0,2},{2,0},{4,6},{6,4},{1,3},{3,1},{5,7},{7,5},{8,10},{10,8},{12,... | collective-permute-start | bytes 786440 | tf_op jit(solution)/shard_map/ppermute | solution.py:40
  116.1 7.2 %collective-permute-start.25 = (bf16[128,1024]{1,0:T(8,128)(2,1)S(1)}, bf16[128,1024]{1,0:T(8,128)(2,1)S(1)}, u32[]{:S(2)}, u32[]{:S(2)}) collective-permute-start(bf16[128,1024]{1,0:T(8,128)(2,1)S(1)} %get-tuple-element.192.n0), channel_id=1, source_target_pairs={{0,4},{2,6},{4,0},{6,2},{1,5},{3,7},{5,1},{7,3},{8,12},{10,14},{12... | collective-permute-start | bytes 786440 | tf_op jit(solution)/shard_map/ppermute | solution.py:40
  116.6 11.0 %collective-permute-start.26 = (bf16[128,1024]{1,0:T(8,128)(2,1)S(1)}, bf16[128,1024]{1,0:T(8,128)(2,1)S(1)}, u32[]{:S(2)}, u32[]{:S(2)}) collective-permute-start(bf16[128,1024]{1,0:T(8,128)(2,1)S(1)} %get-tuple-element.192.n0), channel_id=1, source_target_pairs={{0,6},{2,4},{4,2},{6,0},{1,7},{3,5},{5,3},{7,1},{8,14},{10,12},{12... | collective-permute-start | bytes 786440 | tf_op jit(solution)/shard_map/ppermute | solution.py:40
  136.1 13.0 %collective-permute-start.28 = (bf16[128,1024]{1,0:T(8,128)(2,1)S(1)}, bf16[128,1024]{1,0:T(8,128)(2,1)S(1)}, u32[]{:S(2)}, u32[]{:S(2)}) collective-permute-start(bf16[128,1024]{1,0:T(8,128)(2,1)S(1)} %get-tuple-element.212), channel_id=1, source_target_pairs={{0,4},{2,6},{4,0},{6,2},{1,5},{3,7},{5,1},{7,3},{8,12},{10,14},{12... | collective-permute-start | bytes 786440 | tf_op jit(solution)/shard_map/ppermute | solution.py:40
  136.2 12.9 %collective-permute-start.29 = (bf16[128,1024]{1,0:T(8,128)(2,1)S(1)}, bf16[128,1024]{1,0:T(8,128)(2,1)S(1)}, u32[]{:S(2)}, u32[]{:S(2)}) collective-permute-start(bf16[128,1024]{1,0:T(8,128)(2,1)S(1)} %get-tuple-element.213), channel_id=1, source_target_pairs={{0,6},{2,4},{4,2},{6,0},{1,7},{3,5},{5,3},{7,1},{8,14},{10,12},{12... | collective-permute-start | bytes 786440 | tf_op jit(solution)/shard_map/ppermute | solution.py:40
  137.5 11.6 %collective-permute-start.27 = (bf16[128,1024]{1,0:T(8,128)(2,1)S(1)}, bf16[128,1024]{1,0:T(8,128)(2,1)S(1)}, u32[]{:S(2)}, u32[]{:S(2)}) collective-permute-start(bf16[128,1024]{1,0:T(8,128)(2,1)S(1)} %get-tuple-element.211), channel_id=1, source_target_pairs={{0,2},{2,0},{4,6},{6,4},{1,3},{3,1},{5,7},{7,5},{8,10},{10,8},{12,... | collective-permute-start | bytes 786440 | tf_op jit(solution)/shard_map/ppermute | solution.py:40
  149.4 5.8 %collective-permute-start.30 = (bf16[128,1024]{1,0:T(8,128)(2,1)S(1)}, bf16[128,1024]{1,0:T(8,128)(2,1)S(1)}, u32[]{:S(2)}, u32[]{:S(2)}) collective-permute-start(bf16[128,1024]{1,0:T(8,128)(2,1)S(1)} %get-tuple-element.214.g0), channel_id=1, source_target_pairs={{0,2},{2,0},{4,6},{6,4},{1,3},{3,1},{5,7},{7,5},{8,10},{10,8},{12,... | collective-permute-start | bytes 786440 | tf_op jit(solution)/shard_map/ppermute | solution.py:40
  149.5 9.3 %collective-permute-start.31 = (bf16[128,1024]{1,0:T(8,128)(2,1)S(1)}, bf16[128,1024]{1,0:T(8,128)(2,1)S(1)}, u32[]{:S(2)}, u32[]{:S(2)}) collective-permute-start(bf16[128,1024]{1,0:T(8,128)(2,1)S(1)} %get-tuple-element.214.g0), channel_id=1, source_target_pairs={{0,4},{2,6},{4,0},{6,2},{1,5},{3,7},{5,1},{7,3},{8,12},{10,14},{12... | collective-permute-start | bytes 786440 | tf_op jit(solution)/shard_map/ppermute | solution.py:40
  149.6 9.2 %collective-permute-start.32 = (bf16[128,1024]{1,0:T(8,128)(2,1)S(1)}, bf16[128,1024]{1,0:T(8,128)(2,1)S(1)}, u32[]{:S(2)}, u32[]{:S(2)}) collective-permute-start(bf16[128,1024]{1,0:T(8,128)(2,1)S(1)} %get-tuple-element.214.g0), channel_id=1, source_target_pairs={{0,6},{2,4},{4,2},{6,0},{1,7},{3,5},{5,3},{7,1},{8,14},{10,12},{12... | collective-permute-start | bytes 786440 | tf_op jit(solution)/shard_map/ppermute | solution.py:40
  154.9 11.0 %collective-permute-start.33 = (bf16[128,1024]{1,0:T(8,128)(2,1)S(1)}, bf16[128,1024]{1,0:T(8,128)(2,1)S(1)}, u32[]{:S(2)}, u32[]{:S(2)}) collective-permute-start(bf16[128,1024]{1,0:T(8,128)(2,1)S(1)} %get-tuple-element.230), channel_id=1, source_target_pairs={{0,2},{2,0},{4,6},{6,4},{1,3},{3,1},{5,7},{7,5},{8,10},{10,8},{12,... | collective-permute-start | bytes 786440 | tf_op jit(solution)/shard_map/ppermute | solution.py:40
  155.1 14.9 %collective-permute-start.34 = (bf16[128,1024]{1,0:T(8,128)(2,1)S(1)}, bf16[128,1024]{1,0:T(8,128)(2,1)S(1)}, u32[]{:S(2)}, u32[]{:S(2)}) collective-permute-start(bf16[128,1024]{1,0:T(8,128)(2,1)S(1)} %get-tuple-element.231), channel_id=1, source_target_pairs={{0,4},{2,6},{4,0},{6,2},{1,5},{3,7},{5,1},{7,3},{8,12},{10,14},{12... | collective-permute-start | bytes 786440 | tf_op jit(solution)/shard_map/ppermute | solution.py:40
  155.2 14.8 %collective-permute-start.35 = (bf16[128,1024]{1,0:T(8,128)(2,1)S(1)}, bf16[128,1024]{1,0:T(8,128)(2,1)S(1)}, u32[]{:S(2)}, u32[]{:S(2)}) collective-permute-start(bf16[128,1024]{1,0:T(8,128)(2,1)S(1)} %get-tuple-element.232), channel_id=1, source_target_pairs={{0,6},{2,4},{4,2},{6,0},{1,7},{3,5},{5,3},{7,1},{8,14},{10,12},{12... | collective-permute-start | bytes 786440 | tf_op jit(solution)/shard_map/ppermute | solution.py:40
  170.0 6.7 %collective-permute-start.36 = (bf16[512,512]{1,0:T(8,128)(2,1)S(1)}, bf16[512,512]{1,0:T(8,128)(2,1)S(1)}, u32[]{:S(2)}, u32[]{:S(2)}) collective-permute-start(bf16[512,512]{1,0:T(8,128)(2,1)S(1)} %get-tuple-element.233), channel_id=1, source_target_pairs={{0,1},{1,0},{2,3},{3,2},{4,5},{5,4},{6,7},{7,6},{8,9},{9,8},{10,11... | collective-permute-start | bytes 1572872 | tf_op jit(solution)/shard_map/ppermute | solution.py:36
  180.2 5.6 %collective-permute-start.37 = (bf16[1024,512]{1,0:T(8,128)(2,1)S(1)}, bf16[1024,512]{1,0:T(8,128)(2,1)S(1)}, u32[]{:S(2)}, u32[]{:S(2)}) collective-permute-start(bf16[1024,512]{1,0:T(8,128)(2,1)S(1)} %get-tuple-element.245), channel_id=1, source_target_pairs={{0,1},{1,0},{2,3},{3,2},{4,5},{5,4},{6,7},{7,6},{8,9},{9,8},{10,11... | collective-permute-start | bytes 3145736 | tf_op jit(solution)/shard_map/ppermute | solution.py:36
  180.6 7.9 %collective-permute-start.38 = (bf16[128,1024]{1,0:T(8,128)(2,1)S(1)}, bf16[128,1024]{1,0:T(8,128)(2,1)S(1)}, u32[]{:S(2)}, u32[]{:S(2)}) collective-permute-start(bf16[128,1024]{1,0:T(8,128)(2,1)S(1)} %get-tuple-element.251), channel_id=1, source_target_pairs={{0,2},{2,0},{4,6},{6,4},{1,3},{3,1},{5,7},{7,5},{8,10},{10,8},{12,... | collective-permute-start | bytes 786440 | tf_op jit(solution)/shard_map/ppermute | solution.py:40
  182.0 7.8 %collective-permute-start.39 = (bf16[128,1024]{1,0:T(8,128)(2,1)S(1)}, bf16[128,1024]{1,0:T(8,128)(2,1)S(1)}, u32[]{:S(2)}, u32[]{:S(2)}) collective-permute-start(bf16[128,1024]{1,0:T(8,128)(2,1)S(1)} %get-tuple-element.252), channel_id=1, source_target_pairs={{0,4},{2,6},{4,0},{6,2},{1,5},{3,7},{5,1},{7,3},{8,12},{10,14},{12... | collective-permute-start | bytes 786440 | tf_op jit(solution)/shard_map/ppermute | solution.py:40
  182.1 12.8 %collective-permute-start.40 = (bf16[128,1024]{1,0:T(8,128)(2,1)S(1)}, bf16[128,1024]{1,0:T(8,128)(2,1)S(1)}, u32[]{:S(2)}, u32[]{:S(2)}) collective-permute-start(bf16[128,1024]{1,0:T(8,128)(2,1)S(1)} %get-tuple-element.253), channel_id=1, source_target_pairs={{0,6},{2,4},{4,2},{6,0},{1,7},{3,5},{5,3},{7,1},{8,14},{10,12},{12... | collective-permute-start | bytes 786440 | tf_op jit(solution)/shard_map/ppermute | solution.py:40
  186.1 10.8 %collective-permute-start.42 = (bf16[256,512]{1,0:T(8,128)(2,1)S(1)}, bf16[256,512]{1,0:T(8,128)(2,1)S(1)}, u32[]{:S(2)}, u32[]{:S(2)}) collective-permute-start(bf16[256,512]{1,0:T(8,128)(2,1)S(1)} %get-tuple-element.249), channel_id=1, source_target_pairs={{0,24},{8,0},{16,8},{24,16},{1,25},{9,1},{17,9},{25,17},{2,26},{10... | collective-permute-start | bytes 786440 | tf_op jit(solution)/shard_map/ppermute | solution.py:540
  196.8 17.0 %collective-permute-start.46 = (bf16[256,512]{1,0:T(8,128)(2,1)S(1)}, bf16[256,512]{1,0:T(8,128)(2,1)S(1)}, u32[]{:S(2)}, u32[]{:S(2)}) collective-permute-start(bf16[256,512]{1,0:T(8,128)(2,1)S(1)} %get-tuple-element.247), channel_id=1, source_target_pairs={{0,8},{8,16},{16,24},{24,0},{1,9},{9,17},{17,25},{25,1},{2,10},{10... | collective-permute-start | bytes 786440 | tf_op jit(solution)/shard_map/ppermute | solution.py:540
  196.9 21.1 %collective-permute-start.47 = (bf16[256,512]{1,0:T(8,128)(2,1)S(1)}, bf16[256,512]{1,0:T(8,128)(2,1)S(1)}, u32[]{:S(2)}, u32[]{:S(2)}) collective-permute-start(bf16[256,512]{1,0:T(8,128)(2,1)S(1)} %get-tuple-element.248), channel_id=1, source_target_pairs={{0,16},{8,24},{16,0},{24,8},{1,17},{9,25},{17,1},{25,9},{2,18},{10... | collective-permute-start | bytes 786440 | tf_op jit(solution)/shard_map/ppermute | solution.py:540
  199.5 10.1 %collective-permute-start.43 = (bf16[64,1152]{1,0:T(8,128)(2,1)}, bf16[64,1152]{1,0:T(8,128)(2,1)S(1)}, u32[]{:S(2)}, u32[]{:S(2)}) collective-permute-start(bf16[64,1152]{1,0:T(8,128)(2,1)} %get-tuple-element.265), channel_id=1, source_target_pairs={{0,2},{2,0},{4,6},{6,4},{1,3},{3,1},{5,7},{7,5},{8,10},{10,8},{12,... | collective-permute-start | bytes 442376 | tf_op jit(solution)/shard_map/ppermute | solution.py:40
  199.5 10.1 %collective-permute-start.44 = (bf16[64,1152]{1,0:T(8,128)(2,1)S(1)}, bf16[64,1152]{1,0:T(8,128)(2,1)S(1)}, u32[]{:S(2)}, u32[]{:S(2)}) collective-permute-start(bf16[64,1152]{1,0:T(8,128)(2,1)S(1)} %get-tuple-element.266), channel_id=1, source_target_pairs={{0,4},{2,6},{4,0},{6,2},{1,5},{3,7},{5,1},{7,3},{8,12},{10,14},{12... | collective-permute-start | bytes 442376 | tf_op jit(solution)/shard_map/ppermute | solution.py:40
  200.6 8.9 %collective-permute-start.45 = (bf16[64,1152]{1,0:T(8,128)(2,1)S(1)}, bf16[64,1152]{1,0:T(8,128)(2,1)}, u32[]{:S(2)}, u32[]{:S(2)}) collective-permute-start(bf16[64,1152]{1,0:T(8,128)(2,1)S(1)} %get-tuple-element.267), channel_id=1, source_target_pairs={{0,6},{2,4},{4,2},{6,0},{1,7},{3,5},{5,3},{7,1},{8,14},{10,12},{12... | collective-permute-start | bytes 442376 | tf_op jit(solution)/shard_map/ppermute | solution.py:40
  204.0 32.4 %all-to-all-start.1 = ((bf16[16,32,1024]{2,1,0:T(8,128)(2,1)}), bf16[16,32,1024]{2,1,0:T(8,128)(2,1)S(1)}, u32[]{:S(2)}, u32[]{:S(2)}) async-start(bf16[16,32,1024]{2,1,0:T(8,128)(2,1)} %bitcast.21), calls=%async_computation.1 | async-start | bytes 2097152 | tf_op jit(solution)/shard_map/all_to_all | solution.py:782
  219.1 7.7 %collective-permute-start.50 = (bf16[64,512]{1,0:T(8,128)(2,1)S(1)}, bf16[64,512]{1,0:T(8,128)(2,1)S(1)}, u32[]{:S(2)}, u32[]{:S(2)}) collective-permute-start(bf16[64,512]{1,0:T(8,128)(2,1)S(1)} %get-tuple-element.275), channel_id=1, source_target_pairs={{0,6},{2,4},{4,2},{6,0},{1,7},{3,5},{5,3},{7,1},{8,14},{10,12},{12... | collective-permute-start | bytes 196616 | tf_op jit(solution)/shard_map/ppermute | solution.py:40
  (34 other events, 249.0 us)
Sparse Core Ops, SparseCore 0:
  63.0 50.6 all-gather.1
  136.2 58.0 reduce-scatter.1
